TPU v7x, 1024 devices: a whole 4x4x32 slice. The times are simulated.
1024 devices in a mesh: dp: 64 (over x, z_lo), tensor: 16 (over y, z_hi, core).
Axes of the slice: x: 4, y: 4, z: 32 (z_hi: 2, z_lo: 16; z = z_hi * 16 + z_lo), core: 2. Of those that a mesh axis runs over, the one named last changes fastest.
Arguments:
- tokens: bfloat16 [16384, 4096], P(('dp', 'tensor')), may hold values from -24 to 24
- q_weight: bfloat16 [4096, 2048], P('dp', 'tensor'), may hold values from -3.90625 to 3.90625
- k_weight: bfloat16 [4096, 1024], P('dp', 'tensor'), may hold values from -0.125 to 0.125, as said below
- v_weight: bfloat16 [4096, 1024], P('dp', 'tensor'), may hold values from -0.09375 to 0.09375
- d_context: bfloat16 [16384, 2048], P('dp', 'tensor'), may hold values from -6 to 6
Outputs:
- context: bfloat16 [16384, 2048], P('dp', 'tensor')
- grad_tokens: bfloat16 [16384, 4096], P(('dp', 'tensor'))
- grad_q: float32 [4096, 2048], P('dp', 'tensor')
- grad_k: float32 [4096, 1024], P('dp', 'tensor')
- grad_v: float32 [4096, 1024], P('dp', 'tensor')
Inputs may be any that keep to these rules, and one draw needn't show every extreme that they name: k_weight has independent entries.
All inputs are finite; a program needn't handle non-finite values.
Results may differ from a plain program's by a relative error of at most 0.02.
Values may be sent and summed in bfloat16 or wider, within the bound.
No kernel may reach another device: no remote copies, remote signals or barrier semaphores. Data moves between devices by JAX's collectives and lax.ppermute only.
A program may use at most 32 MiB of HBM per device.

v0:
```python
import math

import jax
import jax.numpy as jnp
from jax import lax
from jax.sharding import PartitionSpec as P

SEQ = 16


def swapped(value, axis, apart):
    mask = 2**apart
    pairs = [(source, source ^ mask) for source in range(lax.axis_size(axis))]
    return lax.ppermute(value, axis, pairs)


def rope_tables(count, head_size):
    position = (jnp.arange(count) % SEQ).astype(jnp.float32)
    exponent = jnp.arange(head_size // 2).astype(jnp.float32) * (2.0 / head_size)
    inverse = jnp.exp(-exponent * jnp.log(500000.0))
    angles = position[:, None] * inverse[None, :]
    return (jnp.cos(angles), jnp.sin(angles))


def rotate(values, cosine, sine):
    half_size = values.shape[-1] // 2
    first = values[..., :half_size]
    second = values[..., half_size:]
    return jnp.concatenate(
        [first * cosine - second * sine, second * cosine + first * sine], axis=-1
    )


def unrotate(grads, cosine, sine):
    half_size = grads.shape[-1] // 2
    first = grads[..., :half_size]
    second = grads[..., half_size:]
    return jnp.concatenate(
        [first * cosine + second * sine, second * cosine - first * sine], axis=-1
    )


def partner(pieces):
    return swapped((pieces[0], pieces[1]), "tensor", 0)


def shards(tokens, q_weight, k_weight, v_weight, d_context):
    head_size = q_weight.shape[1]
    half_size = head_size // 2
    scale = 1.0 / math.sqrt(head_size)
    inputs = tokens.astype(jnp.float32)
    inv_rms = lax.rsqrt(jnp.mean(inputs * inputs, axis=-1, keepdims=True) + 1e-05)
    normed = lax.all_gather((inputs * inv_rms).astype(jnp.bfloat16), "tensor", axis=0, tiled=True)
    w_query, w_key, w_value = (
        lax.all_gather(q_weight, "dp", axis=0, tiled=True),
        lax.all_gather(k_weight, "dp", axis=0, tiled=True),
        lax.all_gather(v_weight, "dp", axis=0, tiled=True),
    )
    w_joined = jnp.concatenate([w_query, w_key, w_value], axis=1)
    projected = jnp.dot(normed, w_joined, preferred_element_type=jnp.float32)
    group_rows = normed.shape[0]
    sequences = group_rows // SEQ
    cosine, sine = rope_tables(group_rows, head_size)
    query = rotate(projected[:, :head_size], cosine, sine).astype(jnp.bfloat16)
    key_mine = projected[:, head_size : head_size + half_size].astype(jnp.bfloat16)
    value_mine = projected[:, head_size + half_size :].astype(jnp.bfloat16)
    key_other, value_other = partner((key_mine, value_mine))
    is_first = lax.axis_index("tensor") % 2 == 0
    key_raw = jnp.where(
        is_first,
        jnp.concatenate([key_mine, key_other], axis=1),
        jnp.concatenate([key_other, key_mine], axis=1),
    )
    value_full = jnp.where(
        is_first,
        jnp.concatenate([value_mine, value_other], axis=1),
        jnp.concatenate([value_other, value_mine], axis=1),
    )
    key_rot = rotate(key_raw.astype(jnp.float32), cosine, sine).astype(jnp.bfloat16)
    query_b = query.reshape(sequences, SEQ, head_size)
    key_b = key_rot.reshape(sequences, SEQ, head_size)
    value_b = value_full.reshape(sequences, SEQ, head_size)
    places = jnp.arange(SEQ)
    allowed = places[None, :] <= places[:, None]
    scores = jnp.einsum("bid,bjd->bij", query_b, key_b, preferred_element_type=jnp.float32) * scale
    masked = jnp.where(allowed[None], scores, -1e30)
    largest = jnp.max(masked, axis=-1, keepdims=True)
    expd = jnp.exp(masked - largest)
    probs = expd / jnp.sum(expd, axis=-1, keepdims=True)
    probs_b = probs.astype(jnp.bfloat16)
    context = jnp.einsum("bij,bjd->bid", probs_b, value_b, preferred_element_type=jnp.float32)
    context = context.reshape(group_rows, head_size).astype(jnp.bfloat16)
    grad_out = d_context.reshape(sequences, SEQ, head_size)
    d_probs = jnp.einsum("bid,bjd->bij", grad_out, value_b, preferred_element_type=jnp.float32)
    d_scores = (
        probs * (d_probs - jnp.sum(probs * d_probs, axis=-1, keepdims=True)) * scale
    ).astype(jnp.bfloat16)
    value_term = jnp.einsum("bij,bid->bjd", probs_b, grad_out, preferred_element_type=jnp.float32)
    dq_rot = jnp.einsum("bij,bjd->bid", d_scores, key_b, preferred_element_type=jnp.float32)
    dk_rot = jnp.einsum("bij,bid->bjd", d_scores, query_b, preferred_element_type=jnp.float32)
    d_query = unrotate(dq_rot.reshape(group_rows, head_size), cosine, sine).astype(jnp.bfloat16)
    key_term = unrotate(dk_rot.reshape(group_rows, head_size), cosine, sine).astype(jnp.bfloat16)
    value_term = value_term.reshape(group_rows, head_size).astype(jnp.bfloat16)
    keep_key = jnp.where(is_first, key_term[:, :half_size], key_term[:, half_size:])
    send_key = jnp.where(is_first, key_term[:, half_size:], key_term[:, :half_size])
    keep_value = jnp.where(is_first, value_term[:, :half_size], value_term[:, half_size:])
    send_value = jnp.where(is_first, value_term[:, half_size:], value_term[:, :half_size])
    got_key, got_value = partner((send_key, send_value))
    d_key = (keep_key.astype(jnp.float32) + got_key.astype(jnp.float32)).astype(jnp.bfloat16)
    d_value = (keep_value.astype(jnp.float32) + got_value.astype(jnp.float32)).astype(jnp.bfloat16)
    d_joined = jnp.concatenate([d_query, d_key, d_value], axis=1)
    grads = lax.psum_scatter(
        lax.dot_general(
            normed, d_joined, (((0,), (0,)), ((), ())), preferred_element_type=jnp.float32
        ),
        "dp",
        scatter_dimension=0,
        tiled=True,
    )
    partial_sum = lax.dot_general(
        d_joined, w_joined, (((1,), (1,)), ((), ())), preferred_element_type=jnp.float32
    )
    d_normed = lax.psum_scatter(
        lax.optimization_barrier(partial_sum.astype(jnp.bfloat16))
        .astype(jnp.float32)
        .astype(jnp.bfloat16),
        "tensor",
        scatter_dimension=0,
        tiled=True,
    ).astype(jnp.float32)
    cubed = inv_rms * inv_rms * inv_rms
    grad_tokens = inv_rms * d_normed - inputs * cubed * jnp.mean(
        inputs * d_normed, axis=-1, keepdims=True
    )
    grad_q = grads[:, :head_size]
    grad_k = grads[:, head_size : head_size + half_size]
    grad_v = grads[:, head_size + half_size :]
    return (context, grad_tokens.astype(jnp.bfloat16), grad_q, grad_k, grad_v)


def solution(mesh):
    placed = (
        P(("dp", "tensor"), None),
        P("dp", "tensor"),
        P("dp", "tensor"),
        P("dp", "tensor"),
        P("dp", "tensor"),
    )
    return jax.shard_map(
        shards,
        mesh=mesh,
        in_specs=placed,
        out_specs=(
            P("dp", "tensor"),
            P(("dp", "tensor"), None),
            P("dp", "tensor"),
            P("dp", "tensor"),
            P("dp", "tensor"),
        ),
        check_vma=False,
    )
```

profile of v0, /device:TPU:24, one launch (start us, length us, event | category | flops | bytes accessed | tf_op | source)
XLA Modules:
  0.0 1859.3 jit_solution(10220149632697170241)
XLA Ops:
  7.2 0.0 copy-start
  7.2 0.0 all-gather.5.cloned.1.call-start
  7.2 0.7 all-gather.5.cloned.1.call-update
  7.9 0.0 all-gather.3.cloned.1.call-start
  8.0 1.1 fusion.14
  9.0 1.7 fusion.15
  10.7 0.0 all-gather.3.cloned.1.call-update
  10.7 0.0 reduce-scatter.3.cloned.1.call-start
  10.8 412.3 %all_gather.14 = bf16[4096,64]{1,0:T(8,128)(2,1)S(1)} all-gather(bf16[64,64]{1,0:T(8,128)(2,1)} %param.7), channel_id=1, replica_groups=mesh['dp'=64,'tensor'=16] {'dp'}, dimensions={0}, use_global_device_ids=true | all-gather | bytes 532480 | tf_op jit(solution)/shard_map/all_gather | solution.py:56
  423.0 387.2 %all_gather.15 = bf16[4096,64]{1,0:T(8,128)(2,1)S(1)} all-gather(bf16[64,64]{1,0:T(8,128)(2,1)} %param.8), channel_id=1, replica_groups=mesh['dp'=64,'tensor'=16] {'dp'}, dimensions={0}, use_global_device_ids=true | all-gather | bytes 532480 | tf_op jit(solution)/shard_map/all_gather | solution.py:57
  810.3 0.0 all-gather.5.cloned.1.call-done
  810.3 69.2 %all-gather.3.cloned.1.call-done = bf16[256,4096]{1,0:T(8,128)(2,1)} async-done(((bf16[16,4096]{1,0:T(8,128)(2,1)}), bf16[256,4096]{1,0:T(8,128)(2,1)}) %all-gather.3.cloned.1.call-update) | async-done | bytes 2097168 | tf_op jit(solution)/shard_map/all_gather | solution.py:53
  879.5 3.2 fusion.83
  882.7 2.1 collective-permute-start
  884.9 2.2 collective-permute-start.1
  887.1 0.1 copy.27
  887.2 0.0 collective-permute-done
  887.3 0.3 fusion.39
  887.6 0.1 copy.23
  887.7 0.1 copy.24
  887.8 0.1 copy.26
  888.0 0.1 copy.25
  888.1 0.3 fusion.84
  888.4 0.0 copy-done
  888.4 0.4 convolution_convert_fusion.1
  888.8 0.0 collective-permute-done.1
  888.8 0.1 copy.28
  888.9 0.2 convolution_bitcast_fusion
  889.2 0.3 fusion.10
  889.4 0.2 fusion.9
  889.7 0.1 fusion.82
  889.8 0.1 copy.43
  889.9 0.1 copy.44
  890.0 2.1 collective-permute-start.3
  892.1 0.1 fusion.78
  892.2 0.1 copy.40
  892.3 0.1 copy.39
  892.4 0.1 fusion.79
  892.5 0.1 copy.41
  892.6 0.1 copy.42
  892.7 0.3 broadcast_select_fusion.1
  893.0 2.2 collective-permute-start.2
  895.2 0.3 fusion.47
  895.5 0.0 collective-permute-done.3
  895.6 0.5 collective-permute-done.2
  896.1 3.7 convolution_convert_fusion
  899.8 0.0 copy-start.1
  899.8 0.0 reduce-scatter.3.cloned.1.call-update
  899.9 0.0 reduce-scatter.5.cloned.1.call-start
  899.9 1.5 copy-done.1
  901.4 2.7 fusion.59
  904.1 0.0 copy-start.2
  904.1 0.0 reduce-scatter.5.cloned.1.call-update
  904.2 1.1 convolution_convert_fusion.2
  905.3 166.6 %reduce-scatter.3.cloned.1.call-done = bf16[16,4096]{1,0:T(8,128)(2,1)} async-done(((bf16[256,4096]{1,0:T(8,128)(2,1)}), bf16[16,4096]{1,0:T(8,128)(2,1)}) %reduce-scatter.3.cloned.1.call-update) | async-done | bytes 131088 | tf_op jit(solution)/shard_map/reduce_scatter | solution.py:123
  1071.9 0.0 copy-done.2
  1071.9 1.1 fusion.17
  1073.0 1.7 fusion.13
  1074.7 775.2 %reduce-scatter.5.cloned.1.call-done = f32[64,256]{1,0:T(8,128)} async-done(((f32[4096,256]{1,0:T(8,128)}), f32[64,256]{1,0:T(8,128)}) %reduce-scatter.5.cloned.1.call-update) | async-done | bytes 65552 | tf_op jit(solution)/shard_map/reduce_scatter | solution.py:112
  1849.9 1.4 slice.89
  1851.2 1.5 fusion.81
  (10 shorter events, 0.1 us)
Async XLA Ops:
  7.2 881.2 %copy-start = (bf16[256,128]{1,0:T(8,128)(2,1)S(1)}, bf16[256,128]{1,0:T(8,128)(2,1)}, u32[]{:S(2)}) copy-start(bf16[256,128]{1,0:T(8,128)(2,1)} %param.9) | copy-start | bytes 196612
  7.2 803.1 %all-gather.5.cloned.1.call-start = ((), (), s32[]{:S(2)}) async-start(), calls=%async_computation.3 | async-start | bytes 1064960 | tf_op jit(solution)/shard_map/all_gather | solution.py:55
  7.9 871.6 %all-gather.3.cloned.1.call-start = ((), (), s32[]{:S(2)}) async-start(), calls=%async_computation.2 | async-start | bytes 2228224 | tf_op jit(solution)/shard_map/all_gather | solution.py:53
  10.7 1061.2 %reduce-scatter.3.cloned.1.call-start = ((), (), s32[]{:S(2)}) async-start(), calls=%async_computation.4 | async-start | bytes 2228224 | tf_op jit(solution)/shard_map/reduce_scatter | solution.py:123
  882.7 4.5 collective-permute-start
  884.9 3.9 collective-permute-start.1
  890.0 5.6 collective-permute-start.3
  893.0 3.1 collective-permute-start.2
  899.8 1.6 copy-start.1
  899.9 950.0 %reduce-scatter.5.cloned.1.call-start = ((), (), s32[]{:S(2)}) async-start(), calls=%async_computation.5 | async-start | bytes 4259840 | tf_op jit(solution)/shard_map/reduce_scatter | solution.py:112
  904.1 167.8 %copy-start.2 = (bf16[16,4096]{1,0:T(8,128)(2,1)S(1)}, bf16[16,4096]{1,0:T(8,128)(2,1)}, u32[]{:S(2)}) copy-start(bf16[16,4096]{1,0:T(8,128)(2,1)} %param.5) | copy-start | bytes 393220
Sparse Core Ops, SparseCore 0:
  10.7 716.5 all-gather.4
  732.3 147.1 all-gather.2
  900.0 171.8 reduce-scatter.2
  1075.1 774.6 reduce-scatter.4
where the time goes:
time: 1860 us
  waiting for transfers between devices  1010 us (54%)
  blocking collectives  800 us (43%)
    reduce_scatter x1, waiting for transfers between devices, shards(): lax.psum_scatter(lax.dot_general(normed, d_joined, (((0,), (0,)), ((), ()...  775 us
    all_gather x1, blocking collectives, shards(): lax.all_gather(k_weight, 'dp', axis=0, tiled=True)  412 us
    all_gather x1, blocking collectives, shards(): lax.all_gather(v_weight, 'dp', axis=0, tiled=True)  387 us
    reduce_scatter x1, waiting for transfers between devices, shards(): lax.psum_scatter(lax.optimization_barrier(partial_sum.astype(jnp.bfloat16...  167 us
    all_gather x1, waiting for transfers between devices, shards(): lax.all_gather((inputs * inv_rms).astype(jnp.bfloat16), 'tensor', axis=0,...  69.2 us
  transfers between devices with their start and end apart: 8, of which 4 were waited for; matrix products, arithmetic and copies ran while one was open for 1% of the time, Pallas kernels for 0%

commit v1 on v0

v1 whole, which is shorter than its diff:
```python
import functools
import math

import jax
import jax.numpy as jnp
import numpy as np
from jax import lax
from jax.experimental import pallas as pl
from jax.experimental.pallas import tpu as pltpu
from jax.sharding import Mesh
from jax.sharding import PartitionSpec as P

SEQ = 16
SHIFTS = (0, -1, 1, 2)
VMEM_LIMIT = 40 * 1024 * 1024

AXES = ("x", "zl", "y", "zh", "co")
SIZES = (4, 16, 4, 2, 2)
DP = ("x", "zl")
TENSOR = ("y", "zh", "co")


def flipped(value, axis, mask):
    size = lax.axis_size(axis)
    return lax.ppermute(value, axis, [(s, s ^ mask) for s in range(size)])


def shifted(value, axis, step):
    size = lax.axis_size(axis)
    return lax.ppermute(value, axis, [(s, (s + step) % size) for s in range(size)])


def z_masks():
    masks = []
    mask = SIZES[1] // 2
    while mask:
        masks.append(mask)
        mask //= 2
    return masks


def z_offset(place):
    return sum(m for bit, m in enumerate(z_masks()) if place >> bit & 1)


def ring_gather(block, axis):
    half = block.shape[0] // 2
    left = shifted(block, axis, 1)
    right = shifted(block, axis, -1)
    far_a = shifted(left[:half], axis, 1)
    far_b = shifted(right[half:], axis, -1)
    return left, right, far_a, far_b


def added(*terms):
    total = terms[0].astype(jnp.float32)
    for term in terms[1:]:
        total = total + term.astype(jnp.float32)
    return total


def ring_scatter(own, left, right, far_a, far_b, axis):
    half = own.shape[0] // 2
    got_a = shifted(far_a, axis, 1)
    got_b = shifted(far_b, axis, -1)
    to_right = jnp.concatenate(
        [added(right[:half], got_a).astype(jnp.bfloat16), right[half:]], axis=0
    )
    to_left = jnp.concatenate(
        [left[:half], added(left[half:], got_b).astype(jnp.bfloat16)], axis=0
    )
    from_left = shifted(to_right, axis, 1)
    from_right = shifted(to_left, axis, -1)
    return added(own, from_left, from_right)


def rope_tables(rows, head_size):
    position = (np.arange(rows) % SEQ).astype(np.float32)
    exponent = np.arange(head_size // 2).astype(np.float32) * np.float32(2.0 / head_size)
    inverse = np.exp(-exponent * np.log(np.float32(500000.0)))
    angles = position[:, None] * inverse[None, :]
    cosine, sine = np.cos(angles), np.sin(angles)
    return (
        np.concatenate([cosine, cosine], axis=1).astype(np.float32),
        np.concatenate([-sine, sine], axis=1).astype(np.float32),
    )


def half_roll(value):
    return pltpu.roll(value, value.shape[-1] // 2, 1)


def sequence_at(place, ids):
    co, yq, zh = place // 8, place // 2 % 4, place % 2
    y = (ids[2] + SHIFTS[yq] + 4) % 4
    return y * 4 + (ids[3] ^ zh) * 2 + (ids[4] ^ co)


def project_kernel(zs, ids, t0, t1, w_own, w_left, w_right, w_fa, w_fb, cos, sin, w_out, q_out, kv_out):
    rows = w_own.shape[0]
    unit = rows // zs
    pieces = ((w_own, 0, 0, zs), (w_left, 1, 0, zs), (w_right, 2, 0, zs), (w_fa, 3, 0, zs // 2), (w_fb, 3, zs // 2, zs))
    for ref, ring, first, last in pieces:
        block = (ids[0] + SHIFTS[ring] + 4) % 4
        for place in range(first, last):
            z = ids[1] ^ z_offset(place)
            at = pl.multiple_of(block * rows + z * unit, unit)
            w_out[pl.ds(at, unit), :] = ref[(place - first) * unit : (place - first + 1) * unit, :]
    totals = []
    for ref in (t0, t1):
        total = None
        for k in range(4):
            cut = slice(k * rows, (k + 1) * rows)
            term = jnp.dot(ref[:, cut], w_out[cut, :], preferred_element_type=jnp.float32)
            total = term if total is None else total + term
        totals.append(total)
    projected = jnp.concatenate(totals, axis=0)
    head = projected.shape[1] // 2
    query = projected[:, :head]
    q_out[...] = (query * cos[...] + half_roll(query) * sin[...]).astype(jnp.bfloat16)
    kv_out[...] = projected[:, head:].astype(jnp.bfloat16)


def attend_kernel(ids, q_ref, mine_ref, other_ref, d_ctx_ref, cos, sin, ctx_out, dq_out, keep_out, send_out, d_ctx, ctx):
    rows, head = q_ref.shape
    half = rows // 2
    scale = 1.0 / math.sqrt(head)
    is_first = ids[4] == 0
    low = lax.broadcasted_iota(jnp.int32, (rows, head), 1) < head // 2
    mine = mine_ref[...].astype(jnp.float32)
    other = jnp.concatenate([other_ref[half:, :], other_ref[:half, :]], axis=0).astype(jnp.float32)
    a = jnp.where(is_first, mine, other)
    b = jnp.where(is_first, other, mine)
    key_raw = jnp.where(low, a, half_roll(b))
    value = jnp.where(low, half_roll(a), b).astype(jnp.bfloat16)
    key = (key_raw * cos[...] + half_roll(key_raw) * sin[...]).astype(jnp.bfloat16)
    query = q_ref[...]
    for place in range(rows // SEQ):
        at = pl.multiple_of(sequence_at(place, ids) * SEQ, SEQ)
        d_ctx[place * SEQ : (place + 1) * SEQ, :] = d_ctx_ref[pl.ds(at, SEQ), :]
    grad_out = d_ctx[...]
    row = lax.broadcasted_iota(jnp.int32, (rows, rows), 0)
    col = lax.broadcasted_iota(jnp.int32, (rows, rows), 1)
    allowed = (row // SEQ == col // SEQ) & (col <= row)
    last = (((1,), (1,)), ((), ()))
    first = (((0,), (0,)), ((), ()))
    dot = functools.partial(lax.dot_general, preferred_element_type=jnp.float32)
    scores = dot(query, key, last) * scale
    masked = jnp.where(allowed, scores, -1e30)
    expd = jnp.exp(masked - jnp.max(masked, axis=-1, keepdims=True))
    probs = expd / jnp.sum(expd, axis=-1, keepdims=True)
    probs_b = probs.astype(jnp.bfloat16)
    ctx[...] = jnp.dot(probs_b, value, preferred_element_type=jnp.float32).astype(jnp.bfloat16)
    for place in range(rows // SEQ):
        at = pl.multiple_of(sequence_at(place, ids) * SEQ, SEQ)
        ctx_out[pl.ds(at, SEQ), :] = ctx[place * SEQ : (place + 1) * SEQ, :]
    d_probs = dot(grad_out, value, last)
    d_scores = probs * (d_probs - jnp.sum(probs * d_probs, axis=-1, keepdims=True)) * scale
    d_scores = d_scores.astype(jnp.bfloat16)
    value_term = dot(probs_b, grad_out, first)
    dq_rot = jnp.dot(d_scores, key, preferred_element_type=jnp.float32)
    dk_rot = dot(d_scores, query, first)
    dq_out[...] = (dq_rot * cos[...] - half_roll(dq_rot) * sin[...]).astype(jnp.bfloat16)
    key_term = dk_rot * cos[...] - half_roll(dk_rot) * sin[...]
    lows = jnp.where(low, key_term, half_roll(value_term))
    highs = jnp.where(low, half_roll(key_term), value_term)
    keep_out[...] = jnp.where(is_first, lows, highs).astype(jnp.bfloat16)
    send_out[...] = jnp.where(is_first, highs, lows).astype(jnp.bfloat16)


def joined_grads(dq_ref, keep_ref, got_ref):
    half = dq_ref.shape[0] // 2
    got = jnp.concatenate([got_ref[half:, :], got_ref[:half, :]], axis=0)
    d_kv = (keep_ref[...].astype(jnp.float32) + got.astype(jnp.float32)).astype(jnp.bfloat16)
    return jnp.concatenate([dq_ref[...], d_kv], axis=1)


def weight_grad_kernel(zs, ids, t0, t1, dq_ref, keep_ref, got_ref, own, left, right, far_a, far_b, dj_out, natural):
    joined = joined_grads(dq_ref, keep_ref, got_ref)
    dj_out[...] = joined
    half = joined.shape[0] // 2
    rows = own.shape[0]
    unit = rows // zs
    dims = (((0,), (0,)), ((), ()))
    pieces = ((far_a, far_b, 3), (left, None, 1), (right, None, 2), (own, None, 0))
    for ref, second, ring in pieces:
        block = (ids[0] + SHIFTS[ring] + 4) % 4
        cut = pl.ds(pl.multiple_of(block * rows, rows), rows)
        total = lax.dot_general(t0[:, cut], joined[:half], dims, preferred_element_type=jnp.float32)
        total += lax.dot_general(t1[:, cut], joined[half:], dims, preferred_element_type=jnp.float32)
        natural[...] = total.astype(jnp.bfloat16)
        for place in range(zs):
            at = pl.multiple_of((ids[1] ^ z_offset(place)) * unit, unit)
            target, where = ref, place
            if second is not None and place >= zs // 2:
                target, where = second, place - zs // 2
            target[where * unit : (where + 1) * unit, :] = natural[pl.ds(at, unit), :]


def token_grad_kernel(dj_ref, w_ref, mine_out, send_out):
    half, width = mine_out.shape
    step = width // 4
    dims = (((1,), (1,)), ((), ()))
    for ref, rows in ((send_out, slice(half, None)), (mine_out, slice(0, half))):
        for k in range(4):
            cut = slice(k * step, (k + 1) * step)
            ref[:, cut] = lax.dot_general(
                dj_ref[rows, :], w_ref[cut, :], dims, preferred_element_type=jnp.float32
            ).astype(jnp.bfloat16)


def call(kernel, out_shapes, *args, scratch=(), flops=0, moved=0):
    vmem = pl.BlockSpec(memory_space=pltpu.VMEM)
    smem = pl.BlockSpec(memory_space=pltpu.SMEM)
    return pl.pallas_call(
        kernel,
        out_shape=[jax.ShapeDtypeStruct(s, jnp.bfloat16) for s in out_shapes],
        in_specs=[smem if a.dtype == jnp.int32 else vmem for a in args],
        out_specs=[vmem] * len(out_shapes),
        scratch_shapes=[pltpu.VMEM(s, jnp.bfloat16) for s in scratch],
        compiler_params=pltpu.CompilerParams(vmem_limit_bytes=VMEM_LIMIT),
        cost_estimate=pl.CostEstimate(flops=flops, bytes_accessed=moved, transcendentals=0),
    )(*args)


def shards(tokens, q_weight, k_weight, v_weight, d_context):
    head = q_weight.shape[1]
    width = tokens.shape[1]
    zs = SIZES[1]
    ids = jnp.stack([lax.axis_index(a) for a in AXES]).astype(jnp.int32)

    weights = jnp.concatenate([q_weight, k_weight, v_weight], axis=1)
    for mask in z_masks():
        weights = jnp.concatenate([weights, flipped(weights, "zl", mask)], axis=0)
    w_pieces = (weights, *ring_gather(weights, "x"))

    inputs = tokens.astype(jnp.float32)
    inv_rms = lax.rsqrt(jnp.mean(inputs * inputs, axis=-1, keepdims=True) + 1e-05)
    normed = (inputs * inv_rms).astype(jnp.bfloat16)
    normed = jnp.concatenate([normed, flipped(normed, "zh", 1)], axis=0)
    t0 = jnp.concatenate([normed, *ring_gather(normed, "y")], axis=0)
    t1 = flipped(t0, "co", 1)

    half = t0.shape[0]
    rows = 2 * half
    cosine, sine = (jnp.asarray(t) for t in rope_tables(rows, head))
    product = 2 * rows * width * 2 * head
    w_natural, query, kv_mine = call(
        functools.partial(project_kernel, zs),
        [(width, 2 * head), (rows, head), (rows, head)],
        ids, t0, t1, *w_pieces, cosine, sine,
        flops=product, moved=6 * width * rows,
    )
    kv_other = flipped(kv_mine, "co", 1)
    context, d_query, keep, send = call(
        attend_kernel,
        [(rows, head)] * 4,
        ids, query, kv_mine, kv_other, d_context, cosine, sine,
        scratch=[(rows, head)] * 2,
        flops=14 * rows * rows * head, moved=24 * rows * head,
    )
    got = flipped(send, "co", 1)
    block = width // SIZES[0]
    *g_pieces, joined = call(
        functools.partial(weight_grad_kernel, zs),
        [(block, 2 * head)] * 3 + [(block // 2, 2 * head)] * 2 + [(rows, 2 * head)],
        ids, t0, t1, d_query, keep, got,
        scratch=[(block, 2 * head)],
        flops=product, moved=4 * width * rows,
    )
    p_mine, p_send = call(
        token_grad_kernel,
        [(half, width)] * 2,
        joined, w_natural,
        flops=product, moved=4 * width * rows,
    )

    grads = ring_scatter(*g_pieces, "x")
    for mask in reversed(z_masks()):
        cut = grads.shape[0] // 2
        grads = grads[:cut] + flipped(grads[cut:].astype(jnp.bfloat16), "zl", mask).astype(jnp.float32)

    part = added(p_mine, flipped(p_send, "co", 1)).astype(jnp.bfloat16)
    quarter = half // 4
    far = part[3 * quarter :]
    part = ring_scatter(
        part[:quarter], part[quarter : 2 * quarter], part[2 * quarter : 3 * quarter],
        far[: quarter // 2], far[quarter // 2 :], "y",
    )
    cut = part.shape[0] // 2
    d_normed = part[:cut] + flipped(part[cut:].astype(jnp.bfloat16), "zh", 1).astype(jnp.float32)
    cubed = inv_rms * inv_rms * inv_rms
    grad_tokens = inv_rms * d_normed - inputs * cubed * jnp.mean(
        inputs * d_normed, axis=-1, keepdims=True
    )
    quart = head + head // 2
    return (context, grad_tokens.astype(jnp.bfloat16), grads[:, :head], grads[:, head:quart], grads[:, quart:])


def solution(mesh):
    split = P(DP, TENSOR)
    rows = P(DP + TENSOR, None)
    return jax.shard_map(
        shards,
        mesh=Mesh(mesh.devices.reshape(SIZES), AXES),
        in_specs=(rows, split, split, split, split),
        out_specs=(split, rows, split, split, split),
        check_vma=False,
    )
```

time: 1860 us -> 262 us (0.14)
  the two profiles are of different devices: /device:TPU:24 before, /device:TPU:64 now
where the time goes in v1:
time: 262 us; the launch traced here: 260 us
  starting transfers between devices  141 us (54%)
  waiting for transfers between devices  98.7 us (38%)
  Pallas kernels  7.43 us (3%)
  other arithmetic  7.28 us (3%)
  local copies, waits for them, and re-layouts  4.18 us (2%)
    ppermute x14, starting transfers between devices, flipped(): return lax.ppermute(value, axis, [(s, s ^ mask) for s in range(size)])  86.6 us
    ppermute x14, waiting for transfers between devices, flipped(): return lax.ppermute(value, axis, [(s, s ^ mask) for s in range(size)])  57.9 us
    ppermute x16, starting transfers between devices, shifted(): lax.ppermute(value, axis, [(s, (s + step) % size) for s in range(size)])  54.7 us
    ppermute x16, waiting for transfers between devices, shifted(): lax.ppermute(value, axis, [(s, (s + step) % size) for s in range(size)])  40.8 us
    pallas_call x4, Pallas kernels, call(): pl.pallas_call(kernel, out_shape=[jax.ShapeDtypeStruct(s, jnp.bfloat16) f...  7.43 us
  transfers between devices with their start and end apart: 30, of which 16 were waited for; matrix products, arithmetic and copies ran while one was open for 3% of the time, Pallas kernels for 1%

profile of v1, /device:TPU:64, one launch (start us, length us, event | category | flops | bytes accessed | tf_op | source)
XLA Modules:
  0.0 260.2 jit_solution(2558248277626460216)
XLA Ops:
  0.6 0.8 constant_dynamic-update-slice_fusion.10
  1.5 15.7 %collective-permute-start.6 = (bf16[64,256]{1,0:T(8,128)(2,1)S(1)}, bf16[64,256]{1,0:T(8,128)(2,1)S(1)}, u32[]{:S(2)}, u32[]{:S(2)}) collective-permute-start(bf16[64,256]{1,0:T(8,128)(2,1)S(1)} %get-tuple-element.36), channel_id=1, source_target_pairs={{0,128},{16,144},{32,160},{48,176},{64,192},{80,208},{96,224},{112... | collective-permute-start | bytes 98312 | tf_op jit(solution)/shard_map/ppermute | solution.py:25
  17.2 1.1 fusion
  18.2 1.0 constant_dynamic-update-slice_fusion.5
  19.3 17.6 %collective-permute-start = (bf16[16,4096]{1,0:T(8,128)(2,1)S(1)}, bf16[16,4096]{1,0:T(8,128)(2,1)S(1)}, u32[]{:S(2)}, u32[]{:S(2)}) collective-permute-start(bf16[16,4096]{1,0:T(8,128)(2,1)S(1)} %get-tuple-element.38), channel_id=1, source_target_pairs={{0,2},{2,0},{1,3},{3,1},{4,6},{6,4},{5,7},{7,5},{8,10},{10,8},{9,1... | collective-permute-start | bytes 393224 | tf_op jit(solution)/shard_map/ppermute | solution.py:25
  36.8 0.8 pad_maximum_fusion.7
  37.7 4.3 %collective-permute-start.7 = (bf16[128,256]{1,0:T(8,128)(2,1)S(1)}, bf16[128,256]{1,0:T(8,128)(2,1)S(1)}, u32[]{:S(2)}, u32[]{:S(2)}) collective-permute-start(bf16[128,256]{1,0:T(8,128)(2,1)S(1)} %pad_maximum_fusion.7), channel_id=1, source_target_pairs={{0,64},{16,80},{32,96},{48,112},{64,0},{80,16},{96,32},{112,48},{1... | collective-permute-start | bytes 196616 | tf_op jit(solution)/shard_map/ppermute | solution.py:25
  42.0 20.3 %collective-permute-done.7 = bf16[128,256]{1,0:T(8,128)(2,1)S(1)} collective-permute-done((bf16[128,256]{1,0:T(8,128)(2,1)S(1)}, bf16[128,256]{1,0:T(8,128)(2,1)S(1)}, u32[]{:S(2)}, u32[]{:S(2)}) %collective-permute-start.7) | collective-permute-done | bytes 65568 | tf_op jit(solution)/shard_map/ppermute | solution.py:25
  62.3 0.8 pad_maximum_fusion.6
  63.1 8.9 %collective-permute-start.8 = (bf16[256,256]{1,0:T(8,128)(2,1)S(1)}, bf16[256,256]{1,0:T(8,128)(2,1)S(1)}, u32[]{:S(2)}, u32[]{:S(2)}) collective-permute-start(bf16[256,256]{1,0:T(8,128)(2,1)S(1)} %pad_maximum_fusion.6), channel_id=1, source_target_pairs={{0,32},{16,48},{32,0},{48,16},{64,96},{80,112},{96,64},{112,80},{1... | collective-permute-start | bytes 393224 | tf_op jit(solution)/shard_map/ppermute | solution.py:25
  72.1 4.9 %collective-permute-start.2 = (bf16[32,4096]{1,0:T(8,128)(2,1)S(1)}, bf16[32,4096]{1,0:T(8,128)(2,1)S(1)}, u32[]{:S(2)}, u32[]{:S(2)}) collective-permute-start(bf16[32,4096]{1,0:T(8,128)(2,1)S(1)} %pad_maximum_fusion.2), channel_id=1, source_target_pairs={{0,12},{4,0},{8,4},{12,8},{1,13},{5,1},{9,5},{13,9},{2,14},{6,2},{... | collective-permute-start | bytes 786440 | tf_op jit(solution)/shard_map/ppermute | solution.py:30
  77.0 1.9 collective-permute-start.1
  79.0 0.8 pad_maximum_fusion.3
  79.9 2.1 collective-permute-start.9
  81.9 0.6 collective-permute-done.2
  82.5 5.6 %collective-permute-start.4 = (bf16[16,4096]{1,0:T(8,128)(2,1)S(1)}, bf16[16,4096]{1,0:T(8,128)(2,1)S(1)}, u32[]{:S(2)}, u32[]{:S(2)}) collective-permute-start(bf16[16,4096]{1,0:T(8,128)(2,1)S(1)} %slice.127), channel_id=1, source_target_pairs={{0,12},{4,0},{8,4},{12,8},{1,13},{5,1},{9,5},{13,9},{2,14},{6,2},{... | collective-permute-start | bytes 393224 | tf_op jit(solution)/shard_map/ppermute | solution.py:30
  88.1 1.9 collective-permute-start.3
  90.1 6.1 %collective-permute-done.3 = bf16[16,4096]{1,0:T(8,128)(2,1)S(1)} collective-permute-done((bf16[16,4096]{1,0:T(8,128)(2,1)S(1)}, bf16[16,4096]{1,0:T(8,128)(2,1)S(1)}, u32[]{:S(2)}, u32[]{:S(2)}) %collective-permute-start.3) | collective-permute-done | bytes 131104 | tf_op jit(solution)/shard_map/ppermute | solution.py:30
  96.3 1.9 collective-permute-start.5
  98.3 4.7 %collective-permute-start.11 = (bf16[1024,256]{1,0:T(8,128)(2,1)S(1)}, bf16[1024,256]{1,0:T(8,128)(2,1)S(1)}, u32[]{:S(2)}, u32[]{:S(2)}) collective-permute-start(bf16[1024,256]{1,0:T(8,128)(2,1)S(1)} %constant_dynamic-update-slice_fusion.6.w_own), channel_id=1, source_target_pairs={{0,768},{256,0},{512,256},{768,512},{1,769},{257,1},{513,257},{769... | collective-permute-start | bytes 1572872 | tf_op jit(solution)/shard_map/ppermute | solution.py:30
  102.9 1.9 collective-permute-start.10
  104.9 9.9 %collective-permute-done.11.w_right = bf16[1024,256]{1,0:T(8,128)(2,1)S(1)} collective-permute-done((bf16[1024,256]{1,0:T(8,128)(2,1)S(1)}, bf16[1024,256]{1,0:T(8,128)(2,1)S(1)}, u32[]{:S(2)}, u32[]{:S(2)}) %collective-permute-start.11) | collective-permute-done | bytes 524320 | tf_op jit(solution)/shard_map/ppermute | solution.py:30
  114.8 0.7 slice.129
  115.5 5.6 %collective-permute-start.13 = (bf16[512,256]{1,0:T(8,128)(2,1)}, bf16[512,256]{1,0:T(8,128)(2,1)}, u32[]{:S(2)}, u32[]{:S(2)}) collective-permute-start(bf16[512,256]{1,0:T(8,128)(2,1)} %slice.129), channel_id=1, source_target_pairs={{0,768},{256,0},{512,256},{768,512},{1,769},{257,1},{513,257},{769... | collective-permute-start | bytes 786440 | tf_op jit(solution)/shard_map/ppermute | solution.py:30
  121.1 0.7 slice.128
  121.8 1.9 collective-permute-start.12
  123.8 3.0 %collective-permute-done.13.w_fb = bf16[512,256]{1,0:T(8,128)(2,1)} collective-permute-done((bf16[512,256]{1,0:T(8,128)(2,1)}, bf16[512,256]{1,0:T(8,128)(2,1)}, u32[]{:S(2)}, u32[]{:S(2)}) %collective-permute-start.13) | collective-permute-done | bytes 262176 | tf_op jit(solution)/shard_map/ppermute | solution.py:30
  126.8 6.1 %collective-permute-done.12.w_fa = bf16[512,256]{1,0:T(8,128)(2,1)} collective-permute-done((bf16[512,256]{1,0:T(8,128)(2,1)}, bf16[512,256]{1,0:T(8,128)(2,1)}, u32[]{:S(2)}, u32[]{:S(2)}) %collective-permute-start.12) | collective-permute-done | bytes 262176 | tf_op jit(solution)/shard_map/ppermute | solution.py:30
  132.9 1.0 copy-done.1
  133.9 2.0 shard_map.110
  136.0 1.9 collective-permute-start.14
  137.9 1.2 collective-permute-done.14.other_ref
  139.1 1.9 shard_map.111
  141.0 2.1 collective-permute-start.15
  143.1 1.1 collective-permute-done.15.got_ref
  144.2 2.0 shard_map.112
  146.2 1.9 collective-permute-start.24
  148.2 3.9 %collective-permute-start.22 = (bf16[512,256]{1,0:T(8,128)(2,1)S(1)}, bf16[512,256]{1,0:T(8,128)(2,1)S(1)}, u32[]{:S(2)}, u32[]{:S(2)}) collective-permute-start(bf16[512,256]{1,0:T(8,128)(2,1)S(1)} %get-tuple-element.32), channel_id=1, source_target_pairs={{0,256},{256,512},{512,768},{768,0},{1,257},{257,513},{513,769},{7... | collective-permute-start | bytes 786440 | tf_op jit(solution)/shard_map/ppermute | solution.py:30
  152.1 4.4 %collective-permute-done.24 = bf16[512,256]{1,0:T(8,128)(2,1)S(1)} collective-permute-done((bf16[512,256]{1,0:T(8,128)(2,1)S(1)}, bf16[512,256]{1,0:T(8,128)(2,1)S(1)}, u32[]{:S(2)}, u32[]{:S(2)}) %collective-permute-start.24) | collective-permute-done | bytes 262176 | tf_op jit(solution)/shard_map/ppermute | solution.py:30
  156.6 3.4 %collective-permute-start.25 = (bf16[1024,256]{1,0:T(8,128)(2,1)S(1)}, bf16[1024,256]{1,0:T(8,128)(2,1)S(1)}, u32[]{:S(2)}, u32[]{:S(2)}) collective-permute-start(bf16[1024,256]{1,0:T(8,128)(2,1)S(1)} %pad_maximum_fusion.1), channel_id=1, source_target_pairs={{0,768},{256,0},{512,256},{768,512},{1,769},{257,1},{513,257},{769... | collective-permute-start | bytes 1572872 | tf_op jit(solution)/shard_map/ppermute | solution.py:30
  160.1 2.4 collective-permute-start.23
  162.5 1.5 shard_map.113
  164.0 1.9 collective-permute-start.16
  166.0 5.6 %collective-permute-done.25 = bf16[1024,256]{1,0:T(8,128)(2,1)S(1)} collective-permute-done((bf16[1024,256]{1,0:T(8,128)(2,1)S(1)}, bf16[1024,256]{1,0:T(8,128)(2,1)S(1)}, u32[]{:S(2)}, u32[]{:S(2)}) %collective-permute-start.25) | collective-permute-done | bytes 524320 | tf_op jit(solution)/shard_map/ppermute | solution.py:30
  171.6 4.8 %collective-permute-done.23 = bf16[1024,256]{1,0:T(8,128)(2,1)S(1)} collective-permute-done((bf16[1024,256]{1,0:T(8,128)(2,1)S(1)}, bf16[1024,256]{1,0:T(8,128)(2,1)S(1)}, u32[]{:S(2)}, u32[]{:S(2)}) %collective-permute-start.23) | collective-permute-done | bytes 524320 | tf_op jit(solution)/shard_map/ppermute | solution.py:30
  176.4 0.2 convert_add_fusion
  176.6 2.9 %collective-permute-start.26 = (bf16[512,256]{1,0:T(8,128)(2,1)S(1)}, bf16[512,256]{1,0:T(8,128)(2,1)S(1)}, u32[]{:S(2)}, u32[]{:S(2)}) collective-permute-start(bf16[512,256]{1,0:T(8,128)(2,1)S(1)} %slice.169), channel_id=1, source_target_pairs={{0,16},{16,0},{32,48},{48,32},{64,80},{80,64},{96,112},{112,96},{1... | collective-permute-start | bytes 786440 | tf_op jit(solution)/shard_map/ppermute | solution.py:25
  179.5 5.6 %collective-permute-done.26 = bf16[512,256]{1,0:T(8,128)(2,1)S(1)} collective-permute-done((bf16[512,256]{1,0:T(8,128)(2,1)S(1)}, bf16[512,256]{1,0:T(8,128)(2,1)S(1)}, u32[]{:S(2)}, u32[]{:S(2)}) %collective-permute-start.26) | collective-permute-done | bytes 262176 | tf_op jit(solution)/shard_map/ppermute | solution.py:25
  185.3 2.2 collective-permute-start.27
  187.5 0.2 add_convert_fusion
  187.8 1.9 collective-permute-start.17
  189.7 5.1 %collective-permute-start.19 = (bf16[16,4096]{1,0:T(8,128)(2,1)S(1)}, bf16[16,4096]{1,0:T(8,128)(2,1)S(1)}, u32[]{:S(2)}, u32[]{:S(2)}) collective-permute-start(bf16[16,4096]{1,0:T(8,128)(2,1)S(1)} %get-tuple-element.42), channel_id=1, source_target_pairs={{0,12},{4,0},{8,4},{12,8},{1,13},{5,1},{9,5},{13,9},{2,14},{6,2},{... | collective-permute-start | bytes 393224 | tf_op jit(solution)/shard_map/ppermute | solution.py:30
  194.9 2.1 collective-permute-start.28
  197.0 0.4 collective-permute-done.19
  197.4 5.6 %collective-permute-start.20 = (bf16[32,4096]{1,0:T(8,128)(2,1)S(1)}, bf16[32,4096]{1,0:T(8,128)(2,1)S(1)}, u32[]{:S(2)}, u32[]{:S(2)}) collective-permute-start(bf16[32,4096]{1,0:T(8,128)(2,1)S(1)} %pad_maximum_fusion.5), channel_id=1, source_target_pairs={{0,12},{4,0},{8,4},{12,8},{1,13},{5,1},{9,5},{13,9},{2,14},{6,2},{... | collective-permute-start | bytes 786440 | tf_op jit(solution)/shard_map/ppermute | solution.py:30
  203.0 1.9 collective-permute-start.18
  205.0 1.0 collective-permute-done.28
  206.0 9.3 %collective-permute-start.29 = (bf16[64,256]{1,0:T(8,128)(2,1)S(1)}, bf16[64,256]{1,0:T(8,128)(2,1)S(1)}, u32[]{:S(2)}, u32[]{:S(2)}) collective-permute-start(bf16[64,256]{1,0:T(8,128)(2,1)S(1)} %slice.173), channel_id=1, source_target_pairs={{0,128},{16,144},{32,160},{48,176},{64,192},{80,208},{96,224},{112... | collective-permute-start | bytes 98312 | tf_op jit(solution)/shard_map/ppermute | solution.py:25
  215.3 5.3 %collective-permute-done.29 = bf16[64,256]{1,0:T(8,128)(2,1)S(1)} collective-permute-done((bf16[64,256]{1,0:T(8,128)(2,1)S(1)}, bf16[64,256]{1,0:T(8,128)(2,1)S(1)}, u32[]{:S(2)}, u32[]{:S(2)}) %collective-permute-start.29) | collective-permute-done | bytes 32800 | tf_op jit(solution)/shard_map/ppermute | solution.py:25
  220.6 0.6 slice.147
  221.4 13.9 %collective-permute-start.21 = (bf16[16,4096]{1,0:T(8,128)(2,1)S(1)}, bf16[16,4096]{1,0:T(8,128)(2,1)S(1)}, u32[]{:S(2)}, u32[]{:S(2)}) collective-permute-start(bf16[16,4096]{1,0:T(8,128)(2,1)S(1)} %slice.171), channel_id=1, source_target_pairs={{0,2},{2,0},{1,3},{3,1},{4,6},{6,4},{5,7},{7,5},{8,10},{10,8},{9,1... | collective-permute-start | bytes 393224 | tf_op jit(solution)/shard_map/ppermute | solution.py:25
  235.2 0.7 fusion.8
  235.9 23.3 %collective-permute-done.21 = bf16[16,4096]{1,0:T(8,128)(2,1)S(1)} collective-permute-done((bf16[16,4096]{1,0:T(8,128)(2,1)S(1)}, bf16[16,4096]{1,0:T(8,128)(2,1)S(1)}, u32[]{:S(2)}, u32[]{:S(2)}) %collective-permute-start.21) | collective-permute-done | bytes 131104 | tf_op jit(solution)/shard_map/ppermute | solution.py:25
  259.4 0.8 fusion.4
  (61 shorter events, 1.1 us)
Async XLA Ops:
  1.5 35.4 %collective-permute-start.6 = (bf16[64,256]{1,0:T(8,128)(2,1)S(1)}, bf16[64,256]{1,0:T(8,128)(2,1)S(1)}, u32[]{:S(2)}, u32[]{:S(2)}) collective-permute-start(bf16[64,256]{1,0:T(8,128)(2,1)S(1)} %get-tuple-element.36), channel_id=1, source_target_pairs={{0,128},{16,144},{32,160},{48,176},{64,192},{80,208},{96,224},{112... | collective-permute-start | bytes 98312 | tf_op jit(solution)/shard_map/ppermute | solution.py:25
  19.3 52.8 %collective-permute-start = (bf16[16,4096]{1,0:T(8,128)(2,1)S(1)}, bf16[16,4096]{1,0:T(8,128)(2,1)S(1)}, u32[]{:S(2)}, u32[]{:S(2)}) collective-permute-start(bf16[16,4096]{1,0:T(8,128)(2,1)S(1)} %get-tuple-element.38), channel_id=1, source_target_pairs={{0,2},{2,0},{1,3},{3,1},{4,6},{6,4},{5,7},{7,5},{8,10},{10,8},{9,1... | collective-permute-start | bytes 393224 | tf_op jit(solution)/shard_map/ppermute | solution.py:25
  37.7 24.6 %collective-permute-start.7 = (bf16[128,256]{1,0:T(8,128)(2,1)S(1)}, bf16[128,256]{1,0:T(8,128)(2,1)S(1)}, u32[]{:S(2)}, u32[]{:S(2)}) collective-permute-start(bf16[128,256]{1,0:T(8,128)(2,1)S(1)} %pad_maximum_fusion.7), channel_id=1, source_target_pairs={{0,64},{16,80},{32,96},{48,112},{64,0},{80,16},{96,32},{112,48},{1... | collective-permute-start | bytes 196616 | tf_op jit(solution)/shard_map/ppermute | solution.py:25
  63.1 15.9 %collective-permute-start.8 = (bf16[256,256]{1,0:T(8,128)(2,1)S(1)}, bf16[256,256]{1,0:T(8,128)(2,1)S(1)}, u32[]{:S(2)}, u32[]{:S(2)}) collective-permute-start(bf16[256,256]{1,0:T(8,128)(2,1)S(1)} %pad_maximum_fusion.6), channel_id=1, source_target_pairs={{0,32},{16,48},{32,0},{48,16},{64,96},{80,112},{96,64},{112,80},{1... | collective-permute-start | bytes 393224 | tf_op jit(solution)/shard_map/ppermute | solution.py:25
  72.1 10.4 %collective-permute-start.2 = (bf16[32,4096]{1,0:T(8,128)(2,1)S(1)}, bf16[32,4096]{1,0:T(8,128)(2,1)S(1)}, u32[]{:S(2)}, u32[]{:S(2)}) collective-permute-start(bf16[32,4096]{1,0:T(8,128)(2,1)S(1)} %pad_maximum_fusion.2), channel_id=1, source_target_pairs={{0,12},{4,0},{8,4},{12,8},{1,13},{5,1},{9,5},{13,9},{2,14},{6,2},{... | collective-permute-start | bytes 786440 | tf_op jit(solution)/shard_map/ppermute | solution.py:30
  77.0 11.1 %collective-permute-start.1 = (bf16[32,4096]{1,0:T(8,128)(2,1)S(1)}, bf16[32,4096]{1,0:T(8,128)(2,1)S(1)}, u32[]{:S(2)}, u32[]{:S(2)}) collective-permute-start(bf16[32,4096]{1,0:T(8,128)(2,1)S(1)} %pad_maximum_fusion.2), channel_id=1, source_target_pairs={{0,4},{4,8},{8,12},{12,0},{1,5},{5,9},{9,13},{13,1},{2,6},{6,10},{... | collective-permute-start | bytes 786440 | tf_op jit(solution)/shard_map/ppermute | solution.py:30
  79.8 53.0 %copy-start.2 = (f32[256,128]{1,0:T(8,128)S(1)}, f32[256,128]{1,0:T(8,128)}, u32[]{:S(2)}) copy-start(f32[256,128]{1,0:T(8,128)} %constant.33.clone.sin) | copy-start | bytes 393220
  79.8 53.0 %copy-start.3 = (f32[256,128]{1,0:T(8,128)S(1)}, f32[256,128]{1,0:T(8,128)}, u32[]{:S(2)}) copy-start(f32[256,128]{1,0:T(8,128)} %constant.32.clone.cos) | copy-start | bytes 393220
  79.9 18.4 %collective-permute-start.9 = (bf16[512,256]{1,0:T(8,128)(2,1)S(1)}, bf16[512,256]{1,0:T(8,128)(2,1)S(1)}, u32[]{:S(2)}, u32[]{:S(2)}) collective-permute-start(bf16[512,256]{1,0:T(8,128)(2,1)S(1)} %pad_maximum_fusion.3), channel_id=1, source_target_pairs={{0,16},{16,0},{32,48},{48,32},{64,80},{80,64},{96,112},{112,96},{1... | collective-permute-start | bytes 786440 | tf_op jit(solution)/shard_map/ppermute | solution.py:25
  82.5 13.7 %collective-permute-start.4 = (bf16[16,4096]{1,0:T(8,128)(2,1)S(1)}, bf16[16,4096]{1,0:T(8,128)(2,1)S(1)}, u32[]{:S(2)}, u32[]{:S(2)}) collective-permute-start(bf16[16,4096]{1,0:T(8,128)(2,1)S(1)} %slice.127), channel_id=1, source_target_pairs={{0,12},{4,0},{8,4},{12,8},{1,13},{5,1},{9,5},{13,9},{2,14},{6,2},{... | collective-permute-start | bytes 393224 | tf_op jit(solution)/shard_map/ppermute | solution.py:30
  88.1 8.1 %collective-permute-start.3 = (bf16[16,4096]{1,0:T(8,128)(2,1)S(1)}, bf16[16,4096]{1,0:T(8,128)(2,1)S(1)}, u32[]{:S(2)}, u32[]{:S(2)}) collective-permute-start(bf16[16,4096]{1,0:T(8,128)(2,1)S(1)} %slice.126), channel_id=1, source_target_pairs={{0,4},{4,8},{8,12},{12,0},{1,5},{5,9},{9,13},{13,1},{2,6},{6,10},{... | collective-permute-start | bytes 393224 | tf_op jit(solution)/shard_map/ppermute | solution.py:30
  96.3 36.6 %collective-permute-start.5 = (bf16[128,4096]{1,0:T(8,128)(2,1)S(1)}, bf16[128,4096]{1,0:T(8,128)(2,1)S(1)}, u32[]{:S(2)}, u32[]{:S(2)}) collective-permute-start(bf16[128,4096]{1,0:T(8,128)(2,1)S(1)} %constant_dynamic-update-slice_fusion.t0), channel_id=1, source_target_pairs={{0,1},{1,0},{2,3},{3,2},{4,5},{5,4},{6,7},{7,6},{8,9},{9,8},{10,11... | collective-permute-start | bytes 3145736 | tf_op jit(solution)/shard_map/ppermute | solution.py:25
  98.3 22.8 %copy-start = (bf16[1024,256]{1,0:T(8,128)(2,1)}, bf16[1024,256]{1,0:T(8,128)(2,1)S(1)}, u32[]{:S(2)}) copy-start(bf16[1024,256]{1,0:T(8,128)(2,1)S(1)} %constant_dynamic-update-slice_fusion.6.w_own) | copy-start | bytes 1572868
  98.3 16.5 %collective-permute-start.11 = (bf16[1024,256]{1,0:T(8,128)(2,1)S(1)}, bf16[1024,256]{1,0:T(8,128)(2,1)S(1)}, u32[]{:S(2)}, u32[]{:S(2)}) collective-permute-start(bf16[1024,256]{1,0:T(8,128)(2,1)S(1)} %constant_dynamic-update-slice_fusion.6.w_own), channel_id=1, source_target_pairs={{0,768},{256,0},{512,256},{768,512},{1,769},{257,1},{513,257},{769... | collective-permute-start | bytes 1572872 | tf_op jit(solution)/shard_map/ppermute | solution.py:30
  102.9 18.1 %collective-permute-start.10 = (bf16[1024,256]{1,0:T(8,128)(2,1)S(1)}, bf16[1024,256]{1,0:T(8,128)(2,1)S(1)}, u32[]{:S(2)}, u32[]{:S(2)}) collective-permute-start(bf16[1024,256]{1,0:T(8,128)(2,1)S(1)} %constant_dynamic-update-slice_fusion.6.w_own), channel_id=1, source_target_pairs={{0,256},{256,512},{512,768},{768,0},{1,257},{257,513},{513,769},{7... | collective-permute-start | bytes 1572872 | tf_op jit(solution)/shard_map/ppermute | solution.py:30
  115.5 11.3 %collective-permute-start.13 = (bf16[512,256]{1,0:T(8,128)(2,1)}, bf16[512,256]{1,0:T(8,128)(2,1)}, u32[]{:S(2)}, u32[]{:S(2)}) collective-permute-start(bf16[512,256]{1,0:T(8,128)(2,1)} %slice.129), channel_id=1, source_target_pairs={{0,768},{256,0},{512,256},{768,512},{1,769},{257,1},{513,257},{769... | collective-permute-start | bytes 786440 | tf_op jit(solution)/shard_map/ppermute | solution.py:30
  121.8 11.1 %collective-permute-start.12 = (bf16[512,256]{1,0:T(8,128)(2,1)}, bf16[512,256]{1,0:T(8,128)(2,1)}, u32[]{:S(2)}, u32[]{:S(2)}) collective-permute-start(bf16[512,256]{1,0:T(8,128)(2,1)} %slice.128), channel_id=1, source_target_pairs={{0,256},{256,512},{512,768},{768,0},{1,257},{257,513},{513,769},{7... | collective-permute-start | bytes 786440 | tf_op jit(solution)/shard_map/ppermute | solution.py:30
  132.9 1.0 copy-start.1
  133.9 5.2 %copy-start.4 = (bf16[256,128]{1,0:T(8,128)(2,1)S(1)}, bf16[256,128]{1,0:T(8,128)(2,1)}, u32[]{:S(2)}) copy-start(bf16[256,128]{1,0:T(8,128)(2,1)} %d_ctx_ref.1) | copy-start | bytes 196612
  136.0 3.1 %collective-permute-start.14 = (bf16[256,128]{1,0:T(8,128)(2,1)S(1)}, bf16[256,128]{1,0:T(8,128)(2,1)S(1)}, u32[]{:S(2)}, u32[]{:S(2)}) collective-permute-start(bf16[256,128]{1,0:T(8,128)(2,1)S(1)} %get-tuple-element.21.mine_ref), channel_id=1, source_target_pairs={{0,1},{1,0},{2,3},{3,2},{4,5},{5,4},{6,7},{7,6},{8,9},{9,8},{10,11... | collective-permute-start | bytes 196616 | tf_op jit(solution)/shard_map/ppermute | solution.py:25
  141.0 3.1 %collective-permute-start.15 = (bf16[256,128]{1,0:T(8,128)(2,1)S(1)}, bf16[256,128]{1,0:T(8,128)(2,1)S(1)}, u32[]{:S(2)}, u32[]{:S(2)}) collective-permute-start(bf16[256,128]{1,0:T(8,128)(2,1)S(1)} %get-tuple-element.25), channel_id=1, source_target_pairs={{0,1},{1,0},{2,3},{3,2},{4,5},{5,4},{6,7},{7,6},{8,9},{9,8},{10,11... | collective-permute-start | bytes 196616 | tf_op jit(solution)/shard_map/ppermute | solution.py:25
  146.2 10.3 %collective-permute-start.24 = (bf16[512,256]{1,0:T(8,128)(2,1)S(1)}, bf16[512,256]{1,0:T(8,128)(2,1)S(1)}, u32[]{:S(2)}, u32[]{:S(2)}) collective-permute-start(bf16[512,256]{1,0:T(8,128)(2,1)S(1)} %get-tuple-element.34), channel_id=1, source_target_pairs={{0,768},{256,0},{512,256},{768,512},{1,769},{257,1},{513,257},{769... | collective-permute-start | bytes 786440 | tf_op jit(solution)/shard_map/ppermute | solution.py:30
  148.2 11.8 %collective-permute-start.22 = (bf16[512,256]{1,0:T(8,128)(2,1)S(1)}, bf16[512,256]{1,0:T(8,128)(2,1)S(1)}, u32[]{:S(2)}, u32[]{:S(2)}) collective-permute-start(bf16[512,256]{1,0:T(8,128)(2,1)S(1)} %get-tuple-element.32), channel_id=1, source_target_pairs={{0,256},{256,512},{512,768},{768,0},{1,257},{257,513},{513,769},{7... | collective-permute-start | bytes 786440 | tf_op jit(solution)/shard_map/ppermute | solution.py:30
  156.6 15.1 %collective-permute-start.25 = (bf16[1024,256]{1,0:T(8,128)(2,1)S(1)}, bf16[1024,256]{1,0:T(8,128)(2,1)S(1)}, u32[]{:S(2)}, u32[]{:S(2)}) collective-permute-start(bf16[1024,256]{1,0:T(8,128)(2,1)S(1)} %pad_maximum_fusion.1), channel_id=1, source_target_pairs={{0,768},{256,0},{512,256},{768,512},{1,769},{257,1},{513,257},{769... | collective-permute-start | bytes 1572872 | tf_op jit(solution)/shard_map/ppermute | solution.py:30
  160.1 16.3 %collective-permute-start.23 = (bf16[1024,256]{1,0:T(8,128)(2,1)S(1)}, bf16[1024,256]{1,0:T(8,128)(2,1)S(1)}, u32[]{:S(2)}, u32[]{:S(2)}) collective-permute-start(bf16[1024,256]{1,0:T(8,128)(2,1)S(1)} %pad_maximum_fusion), channel_id=1, source_target_pairs={{0,256},{256,512},{512,768},{768,0},{1,257},{257,513},{513,769},{7... | collective-permute-start | bytes 1572872 | tf_op jit(solution)/shard_map/ppermute | solution.py:30
  164.0 23.4 %collective-permute-start.16 = (bf16[128,4096]{1,0:T(8,128)(2,1)S(1)}, bf16[128,4096]{1,0:T(8,128)(2,1)S(1)}, u32[]{:S(2)}, u32[]{:S(2)}) collective-permute-start(bf16[128,4096]{1,0:T(8,128)(2,1)S(1)} %get-tuple-element.29), channel_id=1, source_target_pairs={{0,1},{1,0},{2,3},{3,2},{4,5},{5,4},{6,7},{7,6},{8,9},{9,8},{10,11... | collective-permute-start | bytes 3145736 | tf_op jit(solution)/shard_map/ppermute | solution.py:25
  176.6 8.6 %collective-permute-start.26 = (bf16[512,256]{1,0:T(8,128)(2,1)S(1)}, bf16[512,256]{1,0:T(8,128)(2,1)S(1)}, u32[]{:S(2)}, u32[]{:S(2)}) collective-permute-start(bf16[512,256]{1,0:T(8,128)(2,1)S(1)} %slice.169), channel_id=1, source_target_pairs={{0,16},{16,0},{32,48},{48,32},{64,80},{80,64},{96,112},{112,96},{1... | collective-permute-start | bytes 786440 | tf_op jit(solution)/shard_map/ppermute | solution.py:25
  185.3 9.6 %collective-permute-start.27 = (bf16[256,256]{1,0:T(8,128)(2,1)S(1)}, bf16[256,256]{1,0:T(8,128)(2,1)S(1)}, u32[]{:S(2)}, u32[]{:S(2)}) collective-permute-start(bf16[256,256]{1,0:T(8,128)(2,1)S(1)} %slice.170), channel_id=1, source_target_pairs={{0,32},{16,48},{32,0},{48,16},{64,96},{80,112},{96,64},{112,80},{1... | collective-permute-start | bytes 393224 | tf_op jit(solution)/shard_map/ppermute | solution.py:25
  187.8 9.2 %collective-permute-start.17 = (bf16[16,4096]{1,0:T(8,128)(2,1)S(1)}, bf16[16,4096]{1,0:T(8,128)(2,1)S(1)}, u32[]{:S(2)}, u32[]{:S(2)}) collective-permute-start(bf16[16,4096]{1,0:T(8,128)(2,1)S(1)} %get-tuple-element.41), channel_id=1, source_target_pairs={{0,4},{4,8},{8,12},{12,0},{1,5},{5,9},{9,13},{13,1},{2,6},{6,10},{... | collective-permute-start | bytes 393224 | tf_op jit(solution)/shard_map/ppermute | solution.py:30
  189.7 7.6 %collective-permute-start.19 = (bf16[16,4096]{1,0:T(8,128)(2,1)S(1)}, bf16[16,4096]{1,0:T(8,128)(2,1)S(1)}, u32[]{:S(2)}, u32[]{:S(2)}) collective-permute-start(bf16[16,4096]{1,0:T(8,128)(2,1)S(1)} %get-tuple-element.42), channel_id=1, source_target_pairs={{0,12},{4,0},{8,4},{12,8},{1,13},{5,1},{9,5},{13,9},{2,14},{6,2},{... | collective-permute-start | bytes 393224 | tf_op jit(solution)/shard_map/ppermute | solution.py:30
  194.9 64.3 %copy-start.5 = (bf16[16,4096]{1,0:T(8,128)(2,1)S(1)}, bf16[16,4096]{1,0:T(8,128)(2,1)}, u32[]{:S(2)}) copy-start(bf16[16,4096]{1,0:T(8,128)(2,1)} %param.7) | copy-start | bytes 393220
  194.9 11.1 %collective-permute-start.28 = (bf16[128,256]{1,0:T(8,128)(2,1)S(1)}, bf16[128,256]{1,0:T(8,128)(2,1)S(1)}, u32[]{:S(2)}, u32[]{:S(2)}) collective-permute-start(bf16[128,256]{1,0:T(8,128)(2,1)S(1)} %slice.172), channel_id=1, source_target_pairs={{0,64},{16,80},{32,96},{48,112},{64,0},{80,16},{96,32},{112,48},{1... | collective-permute-start | bytes 196616 | tf_op jit(solution)/shard_map/ppermute | solution.py:25
  197.4 23.8 %collective-permute-start.20 = (bf16[32,4096]{1,0:T(8,128)(2,1)S(1)}, bf16[32,4096]{1,0:T(8,128)(2,1)S(1)}, u32[]{:S(2)}, u32[]{:S(2)}) collective-permute-start(bf16[32,4096]{1,0:T(8,128)(2,1)S(1)} %pad_maximum_fusion.5), channel_id=1, source_target_pairs={{0,12},{4,0},{8,4},{12,8},{1,13},{5,1},{9,5},{13,9},{2,14},{6,2},{... | collective-permute-start | bytes 786440 | tf_op jit(solution)/shard_map/ppermute | solution.py:30
  203.0 18.2 %collective-permute-start.18 = (bf16[32,4096]{1,0:T(8,128)(2,1)S(1)}, bf16[32,4096]{1,0:T(8,128)(2,1)S(1)}, u32[]{:S(2)}, u32[]{:S(2)}) collective-permute-start(bf16[32,4096]{1,0:T(8,128)(2,1)S(1)} %pad_maximum_fusion.4), channel_id=1, source_target_pairs={{0,4},{4,8},{8,12},{12,0},{1,5},{5,9},{9,13},{13,1},{2,6},{6,10},{... | collective-permute-start | bytes 786440 | tf_op jit(solution)/shard_map/ppermute | solution.py:30
  206.0 14.6 %collective-permute-start.29 = (bf16[64,256]{1,0:T(8,128)(2,1)S(1)}, bf16[64,256]{1,0:T(8,128)(2,1)S(1)}, u32[]{:S(2)}, u32[]{:S(2)}) collective-permute-start(bf16[64,256]{1,0:T(8,128)(2,1)S(1)} %slice.173), channel_id=1, source_target_pairs={{0,128},{16,144},{32,160},{48,176},{64,192},{80,208},{96,224},{112... | collective-permute-start | bytes 98312 | tf_op jit(solution)/shard_map/ppermute | solution.py:25
  221.4 37.9 %collective-permute-start.21 = (bf16[16,4096]{1,0:T(8,128)(2,1)S(1)}, bf16[16,4096]{1,0:T(8,128)(2,1)S(1)}, u32[]{:S(2)}, u32[]{:S(2)}) collective-permute-start(bf16[16,4096]{1,0:T(8,128)(2,1)S(1)} %slice.171), channel_id=1, source_target_pairs={{0,2},{2,0},{1,3},{3,1},{4,6},{6,4},{5,7},{7,5},{8,10},{10,8},{9,1... | collective-permute-start | bytes 393224 | tf_op jit(solution)/shard_map/ppermute | solution.py:25

commit v2 on v1

v2 whole, which is shorter than its diff:
```python
import functools
import math

import jax
import jax.numpy as jnp
import numpy as np
from jax import lax
from jax.experimental import pallas as pl
from jax.experimental.pallas import tpu as pltpu
from jax.sharding import Mesh
from jax.sharding import PartitionSpec as P

SEQ = 16
SHIFTS = (0, -1, 1, 2)
VMEM_LIMIT = 40 * 1024 * 1024

AXES = ("x", "zl", "y", "zh", "co")
SIZES = (4, 16, 4, 2, 2)
DP = ("x", "zl")
TENSOR = ("y", "zh", "co")


def flipped(value, axis, mask):
    size = lax.axis_size(axis)
    return lax.ppermute(value, axis, [(s, s ^ mask) for s in range(size)])


def shifted(value, axis, step):
    size = lax.axis_size(axis)
    return lax.ppermute(value, axis, [(s, (s + step) % size) for s in range(size)])


RADIX = 4


def z_offset(place):
    return place % RADIX * RADIX + place // RADIX


def spread(block, axis, step):
    return tuple(flipped(block, axis, k * step) for k in range(1, RADIX))


def collect(blocks, axis, step):
    return tuple(flipped(block, axis, k * step) for k, block in enumerate(blocks, 1))


def ring_gather(block, axis):
    return tuple(shifted(block, axis, -shift) for shift in SHIFTS[1:])


def added(*terms):
    total = terms[0].astype(jnp.float32)
    for term in terms[1:]:
        total = total + term.astype(jnp.float32)
    return total


def ring_scatter(blocks, axis):
    return (blocks[0], *(shifted(block, axis, shift) for block, shift in zip(blocks[1:], SHIFTS[1:])))


def rope_tables(rows, head_size):
    position = (np.arange(rows) % SEQ).astype(np.float32)
    exponent = np.arange(head_size // 2).astype(np.float32) * np.float32(2.0 / head_size)
    inverse = np.exp(-exponent * np.log(np.float32(500000.0)))
    angles = position[:, None] * inverse[None, :]
    cosine, sine = np.cos(angles), np.sin(angles)
    return (
        np.concatenate([cosine, cosine], axis=1).astype(np.float32),
        np.concatenate([-sine, sine], axis=1).astype(np.float32),
    )


def half_roll(value):
    return pltpu.roll(value, value.shape[-1] // 2, 1)


def sequence_at(place, ids):
    co, yq, zh = place // 8, place // 2 % 4, place % 2
    y = (ids[2] + SHIFTS[yq] + 4) % 4
    return y * 4 + (ids[3] ^ zh) * 2 + (ids[4] ^ co)


def norm_kernel(tokens, inv_out, normed_out):
    inputs = tokens[...].astype(jnp.float32)
    inv = lax.rsqrt(jnp.mean(inputs * inputs, axis=-1, keepdims=True) + 1e-05)
    inv_out[...] = jnp.broadcast_to(inv, inv_out.shape)
    normed_out[...] = (inputs * inv).astype(jnp.bfloat16)


def rows_kernel(first, *refs):
    *parts, out = refs[first:]
    count = parts[0].shape[0]
    for place, ref in enumerate(parts):
        out[place * count : (place + 1) * count, :] = ref[...]


def scatter_sum_kernel(first, terms, *refs):
    parts, outs = refs[first : first + terms], refs[first + terms :]
    count = outs[0].shape[0]
    for place, out in enumerate(outs):
        cut = slice(place * count, (place + 1) * count)
        out[...] = added(*(part[cut, :] for part in parts)).astype(out.dtype)


def weights_out_kernel(own, a, b, c, q_out, k_out, v_out):
    total = added(own[...], a[...], b[...], c[...])
    head, half = q_out.shape[1], k_out.shape[1]
    q_out[...] = total[:, :head]
    k_out[...] = total[:, head : head + half]
    v_out[...] = total[:, head + half :]


def tokens_out_kernel(tokens, inv_wide, kept, got, out):
    inputs = tokens[...].astype(jnp.float32)
    d_normed = kept[...] + got[...].astype(jnp.float32)
    inv = inv_wide[:, :1]
    mean = jnp.mean(inputs * d_normed, axis=-1, keepdims=True)
    out[...] = (inv * d_normed - inputs * (inv * inv * inv) * mean).astype(jnp.bfloat16)


def project_kernel(zs, ids, t0, t1, w_own, w_left, w_right, w_far, cos, sin, w_out, q_out, kv_out):
    rows = w_own.shape[0]
    unit = rows // zs
    for ring, ref in enumerate((w_own, w_left, w_right, w_far)):
        block = (ids[0] + SHIFTS[ring] + 4) % 4
        for place in range(zs):
            z = ids[1] ^ z_offset(place)
            at = pl.multiple_of(block * rows + z * unit, unit)
            w_out[pl.ds(at, unit), :] = ref[place * unit : (place + 1) * unit, :]
    totals = []
    for ref in (t0, t1):
        total = None
        for k in range(4):
            cut = slice(k * rows, (k + 1) * rows)
            term = jnp.dot(ref[:, cut], w_out[cut, :], preferred_element_type=jnp.float32)
            total = term if total is None else total + term
        totals.append(total)
    projected = jnp.concatenate(totals, axis=0)
    head = projected.shape[1] // 2
    query = projected[:, :head]
    q_out[...] = (query * cos[...] + half_roll(query) * sin[...]).astype(jnp.bfloat16)
    kv_out[...] = projected[:, head:].astype(jnp.bfloat16)


def attend_kernel(ids, q_ref, mine_ref, other_ref, d_ctx_ref, cos, sin, ctx_out, dq_out, keep_out, send_out, d_ctx, ctx):
    rows, head = q_ref.shape
    half = rows // 2
    scale = 1.0 / math.sqrt(head)
    is_first = ids[4] == 0
    low = lax.broadcasted_iota(jnp.int32, (rows, head), 1) < head // 2
    mine = mine_ref[...].astype(jnp.float32)
    other = jnp.concatenate([other_ref[half:, :], other_ref[:half, :]], axis=0).astype(jnp.float32)
    a = jnp.where(is_first, mine, other)
    b = jnp.where(is_first, other, mine)
    key_raw = jnp.where(low, a, half_roll(b))
    value = jnp.where(low, half_roll(a), b).astype(jnp.bfloat16)
    key = (key_raw * cos[...] + half_roll(key_raw) * sin[...]).astype(jnp.bfloat16)
    query = q_ref[...]
    for place in range(rows // SEQ):
        at = pl.multiple_of(sequence_at(place, ids) * SEQ, SEQ)
        d_ctx[place * SEQ : (place + 1) * SEQ, :] = d_ctx_ref[pl.ds(at, SEQ), :]
    grad_out = d_ctx[...]
    row = lax.broadcasted_iota(jnp.int32, (rows, rows), 0)
    col = lax.broadcasted_iota(jnp.int32, (rows, rows), 1)
    allowed = (row // SEQ == col // SEQ) & (col <= row)
    last = (((1,), (1,)), ((), ()))
    first = (((0,), (0,)), ((), ()))
    dot = functools.partial(lax.dot_general, preferred_element_type=jnp.float32)
    scores = dot(query, key, last) * scale
    masked = jnp.where(allowed, scores, -1e30)
    expd = jnp.exp(masked - jnp.max(masked, axis=-1, keepdims=True))
    probs = expd / jnp.sum(expd, axis=-1, keepdims=True)
    probs_b = probs.astype(jnp.bfloat16)
    ctx[...] = jnp.dot(probs_b, value, preferred_element_type=jnp.float32).astype(jnp.bfloat16)
    for place in range(rows // SEQ):
        at = pl.multiple_of(sequence_at(place, ids) * SEQ, SEQ)
        ctx_out[pl.ds(at, SEQ), :] = ctx[place * SEQ : (place + 1) * SEQ, :]
    d_probs = dot(grad_out, value, last)
    d_scores = probs * (d_probs - jnp.sum(probs * d_probs, axis=-1, keepdims=True)) * scale
    d_scores = d_scores.astype(jnp.bfloat16)
    value_term = dot(probs_b, grad_out, first)
    dq_rot = jnp.dot(d_scores, key, preferred_element_type=jnp.float32)
    dk_rot = dot(d_scores, query, first)
    dq_out[...] = (dq_rot * cos[...] - half_roll(dq_rot) * sin[...]).astype(jnp.bfloat16)
    key_term = dk_rot * cos[...] - half_roll(dk_rot) * sin[...]
    lows = jnp.where(low, key_term, half_roll(value_term))
    highs = jnp.where(low, half_roll(key_term), value_term)
    keep_out[...] = jnp.where(is_first, lows, highs).astype(jnp.bfloat16)
    send_out[...] = jnp.where(is_first, highs, lows).astype(jnp.bfloat16)


def joined_grads(dq_ref, keep_ref, got_ref):
    half = dq_ref.shape[0] // 2
    got = jnp.concatenate([got_ref[half:, :], got_ref[:half, :]], axis=0)
    d_kv = (keep_ref[...].astype(jnp.float32) + got.astype(jnp.float32)).astype(jnp.bfloat16)
    return jnp.concatenate([dq_ref[...], d_kv], axis=1)


def weight_grad_kernel(zs, ids, t0, t1, dj_ref, own, left, right, far, natural):
    half = dj_ref.shape[0] // 2
    rows = own.shape[0]
    unit = rows // zs
    dims = (((0,), (0,)), ((), ()))
    for ref, ring in ((far, 3), (left, 1), (right, 2), (own, 0)):
        block = (ids[0] + SHIFTS[ring] + 4) % 4
        cut = pl.ds(pl.multiple_of(block * rows, rows), rows)
        total = lax.dot_general(t0[:, cut], dj_ref[:half, :], dims, preferred_element_type=jnp.float32)
        total += lax.dot_general(t1[:, cut], dj_ref[half:, :], dims, preferred_element_type=jnp.float32)
        natural[...] = total.astype(jnp.bfloat16)
        for place in range(zs):
            at = pl.multiple_of((ids[1] ^ z_offset(place)) * unit, unit)
            ref[place * unit : (place + 1) * unit, :] = natural[pl.ds(at, unit), :]


def token_grad_kernel(dq_ref, keep_ref, got_ref, w_ref, mine_out, send_out, dj_out):
    dj_out[...] = joined_grads(dq_ref, keep_ref, got_ref)
    half, width = mine_out.shape
    step = width // 4
    dims = (((1,), (1,)), ((), ()))
    for ref, rows in ((send_out, slice(half, None)), (mine_out, slice(0, half))):
        for k in range(4):
            cut = slice(k * step, (k + 1) * step)
            ref[:, cut] = lax.dot_general(
                dj_out[rows, :], w_ref[cut, :], dims, preferred_element_type=jnp.float32
            ).astype(jnp.bfloat16)


def call(kernel, out_shapes, *args, after=(), scratch=(), flops=0, moved=0):
    vmem = pl.BlockSpec(memory_space=pltpu.VMEM)
    smem = pl.BlockSpec(memory_space=pltpu.SMEM)
    in_specs = [smem if a.dtype == jnp.int32 else vmem for a in args]
    in_specs = [pl.BlockSpec(memory_space=pl.ANY)] * len(after) + in_specs
    return pl.pallas_call(
        kernel,
        out_shape=[jax.ShapeDtypeStruct(s, t) for s, t in out_shapes],
        in_specs=in_specs,
        out_specs=[vmem] * len(out_shapes),
        scratch_shapes=[pltpu.VMEM(s, jnp.bfloat16) for s in scratch],
        compiler_params=pltpu.CompilerParams(vmem_limit_bytes=VMEM_LIMIT),
        cost_estimate=pl.CostEstimate(flops=flops, bytes_accessed=moved, transcendentals=0),
    )(*after, *args)


def rows(*parts, after=(), flops=0):
    shape = (len(parts) * parts[0].shape[0], parts[0].shape[1])
    (out,) = call(
        functools.partial(rows_kernel, len(after)), [(shape, parts[0].dtype)], *parts, after=after,
        flops=flops, moved=4 * shape[0] * shape[1],
    )
    return out


def scatter_sum(blocks, *parts, after=()):
    shape = (parts[0].shape[0] // blocks, parts[0].shape[1])
    return call(
        functools.partial(scatter_sum_kernel, len(after), len(parts)),
        [(shape, jnp.float32)] + [(shape, jnp.bfloat16)] * (blocks - 1),
        *parts, after=after, moved=4 * len(parts) * parts[0].shape[0] * shape[1],
    )


def shards(tokens, q_weight, k_weight, v_weight, d_context):
    head = q_weight.shape[1]
    count, width = tokens.shape
    zs = SIZES[1]
    b16, f32 = jnp.bfloat16, jnp.float32
    product = 64 * count * width * head
    ids = jnp.stack([lax.axis_index(a) for a in AXES]).astype(jnp.int32)

    weights = jnp.concatenate([q_weight, k_weight, v_weight], axis=1)
    inv_wide, normed = call(
        norm_kernel, [((count, 128), f32), ((count, width), b16)], tokens,
        flops=4 * count * width, moved=4 * count * width,
    )
    near = rows(weights, *spread(weights, "zl", RADIX), after=(normed,))
    whole = rows(near, *spread(near, "zl", 1))
    w_pieces = (whole, *ring_gather(whole, "x"))
    far = rows(flipped(normed, "zh", 1), after=(whole,), flops=40 * product)
    pair = rows(normed, far, after=w_pieces[1:3])
    t0 = rows(pair, *ring_gather(pair, "y"), after=w_pieces[3:])
    t1 = flipped(t0, "co", 1)

    half = t0.shape[0]
    held = 2 * half
    cosine, sine = (jnp.asarray(t) for t in rope_tables(held, head))
    one_head = ((held, head), b16)
    w_natural, query, kv_mine = call(
        functools.partial(project_kernel, zs),
        [((width, 2 * head), b16), one_head, one_head],
        ids, t0, t1, *w_pieces, cosine, sine,
        flops=product, moved=6 * width * held,
    )
    kv_other = flipped(kv_mine, "co", 1)
    context, d_query, keep, send = call(
        attend_kernel,
        [one_head] * 4,
        ids, query, kv_mine, kv_other, d_context, cosine, sine,
        scratch=[(held, head)] * 2,
        flops=14 * held * held * head, moved=24 * held * head,
    )
    got = flipped(send, "co", 1)
    block = width // SIZES[0]
    p_mine, p_send, joined = call(
        token_grad_kernel,
        [((half, width), b16)] * 2 + [((held, 2 * head), b16)],
        d_query, keep, got, w_natural,
        flops=product, moved=4 * width * held,
    )
    g_blocks = call(
        functools.partial(weight_grad_kernel, zs),
        [((block, 2 * head), b16)] * 4,
        ids, t0, t1, joined,
        scratch=[(block, 2 * head)],
        flops=product, moved=4 * width * held,
    )

    y_blocks = scatter_sum(SIZES[2], p_mine, flipped(p_send, "co", 1), after=(g_blocks[0],))
    kept_t, sent_t = scatter_sum(2, *ring_scatter(y_blocks, "y"))
    from_zh = flipped(sent_t, "zh", 1)
    (grad_tokens,) = call(
        tokens_out_kernel, [((count, width), b16)], tokens, inv_wide, kept_t, from_zh,
        flops=8 * count * width, moved=12 * count * width,
    )

    kept, *sent = scatter_sum(RADIX, *ring_scatter(g_blocks, "x"), after=(y_blocks[0],))
    kept, *sent = scatter_sum(RADIX, kept, *collect(sent, "zl", 1))
    cut = kept.shape[0]
    grads = call(
        weights_out_kernel,
        [((cut, head), f32), ((cut, head // 2), f32), ((cut, head // 2), f32)],
        kept, *collect(sent, "zl", RADIX),
        moved=24 * cut * head,
    )
    return (context, grad_tokens, *grads)


def solution(mesh):
    split = P(DP, TENSOR)
    rows = P(DP + TENSOR, None)
    return jax.shard_map(
        shards,
        mesh=Mesh(mesh.devices.reshape(SIZES), AXES),
        in_specs=(rows, split, split, split, split),
        out_specs=(split, rows, split, split, split),
        check_vma=False,
    )
```

time: 262 us -> 233 us (0.89)
  the two profiles are of different devices: /device:TPU:64 before, /device:TPU:78 now
where the time goes in v2:
time: 233 us; the launch traced here: 232 us
  starting transfers between devices  150 us (64%)
  waiting for transfers between devices  66 us (28%)
  Pallas kernels  9.44 us (4%)
  local copies, waits for them, and re-layouts  3.91 us (2%)
    ppermute x18, starting transfers between devices, flipped(): return lax.ppermute(value, axis, [(s, s ^ mask) for s in range(size)])  111 us
    ppermute x18, waiting for transfers between devices, flipped(): return lax.ppermute(value, axis, [(s, s ^ mask) for s in range(size)])  47.8 us
    ppermute x12, starting transfers between devices, shifted(): lax.ppermute(value, axis, [(s, (s + step) % size) for s in range(size)])  39.4 us
    ppermute x12, waiting for transfers between devices, shifted(): lax.ppermute(value, axis, [(s, (s + step) % size) for s in range(size)])  18.3 us
    pallas_call x16, Pallas kernels, call(): pl.pallas_call(kernel, out_shape=[jax.ShapeDtypeStruct(s, t) for s, t in...  9.44 us
  transfers between devices with their start and end apart: 30, of which 14 were waited for; matrix products, arithmetic and copies ran while one was open for 0% of the time, Pallas kernels for 2%

profile of v2, /device:TPU:78, one launch (start us, length us, event | category | flops | bytes accessed | tf_op | source)
XLA Modules:
  0.0 231.5 jit_solution(3364044388122971442)
XLA Ops:
  0.6 0.8 pad_maximum_fusion.refs_1_
  1.5 22.3 %collective-permute-start.2 = (bf16[64,256]{1,0:T(8,128)(2,1)S(1)}, bf16[64,256]{1,0:T(8,128)(2,1)S(1)}, u32[]{:S(2)}, u32[]{:S(2)}) collective-permute-start(bf16[64,256]{1,0:T(8,128)(2,1)S(1)} %pad_maximum_fusion.refs_1_), channel_id=1, source_target_pairs={{0,192},{16,208},{32,224},{48,240},{64,128},{80,144},{96,160},{112... | collective-permute-start | bytes 98312 | tf_op jit(solution)/shard_map/ppermute | solution.py:25
  23.8 1.9 collective-permute-start.1
  25.7 2.5 %collective-permute-start = (bf16[64,256]{1,0:T(8,128)(2,1)S(1)}, bf16[64,256]{1,0:T(8,128)(2,1)S(1)}, u32[]{:S(2)}, u32[]{:S(2)}) collective-permute-start(bf16[64,256]{1,0:T(8,128)(2,1)S(1)} %pad_maximum_fusion.refs_1_), channel_id=1, source_target_pairs={{0,64},{16,80},{32,96},{48,112},{64,0},{80,16},{96,32},{112,48},{1... | collective-permute-start | bytes 98312 | tf_op jit(solution)/shard_map/ppermute | solution.py:25
  28.2 0.9 copy-done.6
  29.1 0.1 shard_map.110
  29.3 9.4 %collective-permute-done.1.refs_3_ = bf16[64,256]{1,0:T(8,128)(2,1)S(1)} collective-permute-done((bf16[64,256]{1,0:T(8,128)(2,1)S(1)}, bf16[64,256]{1,0:T(8,128)(2,1)S(1)}, u32[]{:S(2)}, u32[]{:S(2)}) %collective-permute-start.1) | collective-permute-done | bytes 32800 | tf_op jit(solution)/shard_map/ppermute | solution.py:25
  38.7 2.1 collective-permute-start.5
  40.8 5.8 %collective-permute-start.4 = (bf16[256,256]{1,0:T(8,128)(2,1)S(1)}, bf16[256,256]{1,0:T(8,128)(2,1)S(1)}, u32[]{:S(2)}, u32[]{:S(2)}) collective-permute-start(bf16[256,256]{1,0:T(8,128)(2,1)S(1)} %shard_map.111.refs_0_), channel_id=1, source_target_pairs={{0,32},{16,48},{32,0},{48,16},{64,96},{80,112},{96,64},{112,80},{1... | collective-permute-start | bytes 393224 | tf_op jit(solution)/shard_map/ppermute | solution.py:25
  46.6 1.9 collective-permute-start.3
  48.5 16.3 %collective-permute-start.9 = (bf16[16,4096]{1,0:T(8,128)(2,1)S(1)}, bf16[16,4096]{1,0:T(8,128)(2,1)S(1)}, u32[]{:S(2)}, u32[]{:S(2)}) collective-permute-start(bf16[16,4096]{1,0:T(8,128)(2,1)S(1)} %get-tuple-element.38.refs_0_.refs_2_), channel_id=1, source_target_pairs={{0,2},{2,0},{1,3},{3,1},{4,6},{6,4},{5,7},{7,5},{8,10},{10,8},{9,1... | collective-permute-start | bytes 393224 | tf_op jit(solution)/shard_map/ppermute | solution.py:25
  64.9 2.7 %collective-permute-start.8 = (bf16[1024,256]{1,0:T(8,128)(2,1)S(1)}, bf16[1024,256]{1,0:T(8,128)(2,1)S(1)}, u32[]{:S(2)}, u32[]{:S(2)}) collective-permute-start(bf16[1024,256]{1,0:T(8,128)(2,1)S(1)} %shard_map.112.refs_0_.w_own), channel_id=1, source_target_pairs={{0,768},{256,0},{512,256},{768,512},{1,769},{257,1},{513,257},{769... | collective-permute-start | bytes 1572872 | tf_op jit(solution)/shard_map/ppermute | solution.py:30
  67.6 4.3 %collective-permute-start.7 = (bf16[1024,256]{1,0:T(8,128)(2,1)S(1)}, bf16[1024,256]{1,0:T(8,128)(2,1)S(1)}, u32[]{:S(2)}, u32[]{:S(2)}) collective-permute-start(bf16[1024,256]{1,0:T(8,128)(2,1)S(1)} %shard_map.112.refs_0_.w_own), channel_id=1, source_target_pairs={{0,256},{256,512},{512,768},{768,0},{1,257},{257,513},{513,769},{7... | collective-permute-start | bytes 1572872 | tf_op jit(solution)/shard_map/ppermute | solution.py:30
  71.9 2.1 collective-permute-start.6
  74.0 16.2 %collective-permute-done.9.refs_1_ = bf16[16,4096]{1,0:T(8,128)(2,1)S(1)} collective-permute-done((bf16[16,4096]{1,0:T(8,128)(2,1)S(1)}, bf16[16,4096]{1,0:T(8,128)(2,1)S(1)}, u32[]{:S(2)}, u32[]{:S(2)}) %collective-permute-start.9) | collective-permute-done | bytes 131104 | tf_op jit(solution)/shard_map/ppermute | solution.py:25
  90.3 0.0 copy-start.4
  90.3 0.0 copy-start.5
  90.3 1.5 collective-permute-done.8.refs_1_.w_right
  91.8 1.2 collective-permute-done.7.refs_0_.w_left
  93.1 4.2 %collective-permute-start.12 = (bf16[32,4096]{1,0:T(8,128)(2,1)S(1)}, bf16[32,4096]{1,0:T(8,128)(2,1)S(1)}, u32[]{:S(2)}, u32[]{:S(2)}) collective-permute-start(bf16[32,4096]{1,0:T(8,128)(2,1)S(1)} %shard_map.114.refs_1_), channel_id=1, source_target_pairs={{0,8},{4,12},{8,0},{12,4},{1,9},{5,13},{9,1},{13,5},{2,10},{6,14},... | collective-permute-start | bytes 786440 | tf_op jit(solution)/shard_map/ppermute | solution.py:30
  97.3 3.3 %collective-permute-start.11 = (bf16[32,4096]{1,0:T(8,128)(2,1)S(1)}, bf16[32,4096]{1,0:T(8,128)(2,1)S(1)}, u32[]{:S(2)}, u32[]{:S(2)}) collective-permute-start(bf16[32,4096]{1,0:T(8,128)(2,1)S(1)} %shard_map.114.refs_1_), channel_id=1, source_target_pairs={{0,12},{4,0},{8,4},{12,8},{1,13},{5,1},{9,5},{13,9},{2,14},{6,2},{... | collective-permute-start | bytes 786440 | tf_op jit(solution)/shard_map/ppermute | solution.py:30
  100.5 2.6 %collective-permute-start.10 = (bf16[32,4096]{1,0:T(8,128)(2,1)S(1)}, bf16[32,4096]{1,0:T(8,128)(2,1)S(1)}, u32[]{:S(2)}, u32[]{:S(2)}) collective-permute-start(bf16[32,4096]{1,0:T(8,128)(2,1)S(1)} %shard_map.114.refs_1_), channel_id=1, source_target_pairs={{0,4},{4,8},{8,12},{12,0},{1,5},{5,9},{9,13},{13,1},{2,6},{6,10},{... | collective-permute-start | bytes 786440 | tf_op jit(solution)/shard_map/ppermute | solution.py:30
  103.2 2.5 %collective-permute-done.11.refs_3_ = bf16[32,4096]{1,0:T(8,128)(2,1)S(1)} collective-permute-done((bf16[32,4096]{1,0:T(8,128)(2,1)S(1)}, bf16[32,4096]{1,0:T(8,128)(2,1)S(1)}, u32[]{:S(2)}, u32[]{:S(2)}) %collective-permute-start.11) | collective-permute-done | bytes 262176 | tf_op jit(solution)/shard_map/ppermute | solution.py:30
  105.6 3.2 %collective-permute-done.10.refs_2_ = bf16[32,4096]{1,0:T(8,128)(2,1)S(1)} collective-permute-done((bf16[32,4096]{1,0:T(8,128)(2,1)S(1)}, bf16[32,4096]{1,0:T(8,128)(2,1)S(1)}, u32[]{:S(2)}, u32[]{:S(2)}) %collective-permute-start.10) | collective-permute-done | bytes 262176 | tf_op jit(solution)/shard_map/ppermute | solution.py:30
  108.8 0.1 shard_map.115.t0
  108.9 0.8 copy-done
  109.7 1.9 collective-permute-start.13
  111.6 0.1 stack.23.ids
  111.7 2.5 %collective-permute-done.13.t1 = bf16[128,4096]{1,0:T(8,128)(2,1)S(1)} collective-permute-done((bf16[128,4096]{1,0:T(8,128)(2,1)S(1)}, bf16[128,4096]{1,0:T(8,128)(2,1)S(1)}, u32[]{:S(2)}, u32[]{:S(2)}) %collective-permute-start.13) | collective-permute-done | bytes 1048608 | tf_op jit(solution)/shard_map/ppermute | solution.py:25
  114.3 1.0 copy-done.1
  115.3 1.0 copy-done.3
  116.3 1.5 shard_map.116
  117.8 2.0 collective-permute-start.14
  119.9 1.1 collective-permute-done.14.other_ref
  121.0 1.9 shard_map.117
  122.9 2.1 collective-permute-start.15
  125.0 1.1 collective-permute-done.15.got_ref
  126.0 1.5 shard_map.118
  127.5 2.1 collective-permute-start.16
  129.6 2.0 shard_map.119
  131.6 1.9 collective-permute-start.21
  133.6 5.6 %collective-permute-start.22 = (bf16[1024,256]{1,0:T(8,128)(2,1)S(1)}, bf16[1024,256]{1,0:T(8,128)(2,1)S(1)}, u32[]{:S(2)}, u32[]{:S(2)}) collective-permute-start(bf16[1024,256]{1,0:T(8,128)(2,1)S(1)} %get-tuple-element.58), channel_id=1, source_target_pairs={{0,256},{256,512},{512,768},{768,0},{1,257},{257,513},{513,769},{7... | collective-permute-start | bytes 1572872 | tf_op jit(solution)/shard_map/ppermute | solution.py:30
  139.2 3.4 %collective-permute-start.23 = (bf16[1024,256]{1,0:T(8,128)(2,1)S(1)}, bf16[1024,256]{1,0:T(8,128)(2,1)S(1)}, u32[]{:S(2)}, u32[]{:S(2)}) collective-permute-start(bf16[1024,256]{1,0:T(8,128)(2,1)S(1)} %get-tuple-element.59), channel_id=1, source_target_pairs={{0,512},{256,768},{512,0},{768,256},{1,513},{257,769},{513,1},{769... | collective-permute-start | bytes 1572872 | tf_op jit(solution)/shard_map/ppermute | solution.py:30
  142.5 0.3 shard_map.120
  142.8 4.2 %collective-permute-start.17 = (bf16[32,4096]{1,0:T(8,128)(2,1)S(1)}, bf16[32,4096]{1,0:T(8,128)(2,1)S(1)}, u32[]{:S(2)}, u32[]{:S(2)}) collective-permute-start(bf16[32,4096]{1,0:T(8,128)(2,1)S(1)} %get-tuple-element.52), channel_id=1, source_target_pairs={{0,12},{4,0},{8,4},{12,8},{1,13},{5,1},{9,5},{13,9},{2,14},{6,2},{... | collective-permute-start | bytes 786440 | tf_op jit(solution)/shard_map/ppermute | solution.py:30
  147.0 1.9 collective-permute-start.18
  148.9 0.7 collective-permute-done.21.refs_2_
  149.6 3.3 %collective-permute-start.19 = (bf16[32,4096]{1,0:T(8,128)(2,1)S(1)}, bf16[32,4096]{1,0:T(8,128)(2,1)S(1)}, u32[]{:S(2)}, u32[]{:S(2)}) collective-permute-start(bf16[32,4096]{1,0:T(8,128)(2,1)S(1)} %get-tuple-element.54), channel_id=1, source_target_pairs={{0,8},{4,12},{8,0},{12,4},{1,9},{5,13},{9,1},{13,5},{2,10},{6,14},... | collective-permute-start | bytes 786440 | tf_op jit(solution)/shard_map/ppermute | solution.py:30
  152.9 9.2 %collective-permute-done.22.refs_3_ = bf16[1024,256]{1,0:T(8,128)(2,1)S(1)} collective-permute-done((bf16[1024,256]{1,0:T(8,128)(2,1)S(1)}, bf16[1024,256]{1,0:T(8,128)(2,1)S(1)}, u32[]{:S(2)}, u32[]{:S(2)}) %collective-permute-start.22) | collective-permute-done | bytes 524320 | tf_op jit(solution)/shard_map/ppermute | solution.py:30
  162.1 0.3 shard_map.123
  162.3 2.9 %collective-permute-start.24 = (bf16[256,256]{1,0:T(8,128)(2,1)S(1)}, bf16[256,256]{1,0:T(8,128)(2,1)S(1)}, u32[]{:S(2)}, u32[]{:S(2)}) collective-permute-start(bf16[256,256]{1,0:T(8,128)(2,1)S(1)} %get-tuple-element.61), channel_id=1, source_target_pairs={{0,16},{16,0},{32,48},{48,32},{64,80},{80,64},{96,112},{112,96},{1... | collective-permute-start | bytes 393224 | tf_op jit(solution)/shard_map/ppermute | solution.py:25
  165.2 3.3 %collective-permute-start.25 = (bf16[256,256]{1,0:T(8,128)(2,1)S(1)}, bf16[256,256]{1,0:T(8,128)(2,1)S(1)}, u32[]{:S(2)}, u32[]{:S(2)}) collective-permute-start(bf16[256,256]{1,0:T(8,128)(2,1)S(1)} %get-tuple-element.62), channel_id=1, source_target_pairs={{0,32},{16,48},{32,0},{48,16},{64,96},{80,112},{96,64},{112,80},{1... | collective-permute-start | bytes 393224 | tf_op jit(solution)/shard_map/ppermute | solution.py:25
  168.6 3.0 %collective-permute-start.26 = (bf16[256,256]{1,0:T(8,128)(2,1)S(1)}, bf16[256,256]{1,0:T(8,128)(2,1)S(1)}, u32[]{:S(2)}, u32[]{:S(2)}) collective-permute-start(bf16[256,256]{1,0:T(8,128)(2,1)S(1)} %get-tuple-element.63), channel_id=1, source_target_pairs={{0,48},{16,32},{32,16},{48,0},{64,112},{80,96},{96,80},{112,64},{1... | collective-permute-start | bytes 393224 | tf_op jit(solution)/shard_map/ppermute | solution.py:25
  171.6 0.1 shard_map.121
  171.7 18.7 %collective-permute-start.20 = (bf16[16,4096]{1,0:T(8,128)(2,1)S(1)}, bf16[16,4096]{1,0:T(8,128)(2,1)S(1)}, u32[]{:S(2)}, u32[]{:S(2)}) collective-permute-start(bf16[16,4096]{1,0:T(8,128)(2,1)S(1)} %get-tuple-element.56), channel_id=1, source_target_pairs={{0,2},{2,0},{1,3},{3,1},{4,6},{6,4},{5,7},{7,5},{8,10},{10,8},{9,1... | collective-permute-start | bytes 393224 | tf_op jit(solution)/shard_map/ppermute | solution.py:25
  190.4 0.1 shard_map.124
  190.5 1.9 collective-permute-start.27
  192.4 18.2 %collective-permute-start.28 = (bf16[64,256]{1,0:T(8,128)(2,1)S(1)}, bf16[64,256]{1,0:T(8,128)(2,1)S(1)}, u32[]{:S(2)}, u32[]{:S(2)}) collective-permute-start(bf16[64,256]{1,0:T(8,128)(2,1)S(1)} %get-tuple-element.66), channel_id=1, source_target_pairs={{0,128},{16,144},{32,160},{48,176},{64,192},{80,208},{96,224},{112... | collective-permute-start | bytes 98312 | tf_op jit(solution)/shard_map/ppermute | solution.py:25
  210.6 1.9 collective-permute-start.29
  212.6 2.6 %collective-permute-done.27.a = bf16[64,256]{1,0:T(8,128)(2,1)S(1)} collective-permute-done((bf16[64,256]{1,0:T(8,128)(2,1)S(1)}, bf16[64,256]{1,0:T(8,128)(2,1)S(1)}, u32[]{:S(2)}, u32[]{:S(2)}) %collective-permute-start.27) | collective-permute-done | bytes 32800 | tf_op jit(solution)/shard_map/ppermute | solution.py:25
  215.2 0.7 collective-permute-done.28.b
  215.9 14.1 %collective-permute-done.29.c = bf16[64,256]{1,0:T(8,128)(2,1)S(1)} collective-permute-done((bf16[64,256]{1,0:T(8,128)(2,1)S(1)}, bf16[64,256]{1,0:T(8,128)(2,1)S(1)}, u32[]{:S(2)}, u32[]{:S(2)}) %collective-permute-start.29) | collective-permute-done | bytes 32800 | tf_op jit(solution)/shard_map/ppermute | solution.py:25
  230.0 0.7 shard_map.125
  230.7 0.8 shard_map.122
  (32 shorter events, 0.1 us)
Async XLA Ops:
  1.5 27.8 %collective-permute-start.2 = (bf16[64,256]{1,0:T(8,128)(2,1)S(1)}, bf16[64,256]{1,0:T(8,128)(2,1)S(1)}, u32[]{:S(2)}, u32[]{:S(2)}) collective-permute-start(bf16[64,256]{1,0:T(8,128)(2,1)S(1)} %pad_maximum_fusion.refs_1_), channel_id=1, source_target_pairs={{0,192},{16,208},{32,224},{48,240},{64,128},{80,144},{96,160},{112... | collective-permute-start | bytes 98312 | tf_op jit(solution)/shard_map/ppermute | solution.py:25
  23.8 14.9 %collective-permute-start.1 = (bf16[64,256]{1,0:T(8,128)(2,1)S(1)}, bf16[64,256]{1,0:T(8,128)(2,1)S(1)}, u32[]{:S(2)}, u32[]{:S(2)}) collective-permute-start(bf16[64,256]{1,0:T(8,128)(2,1)S(1)} %pad_maximum_fusion.refs_1_), channel_id=1, source_target_pairs={{0,128},{16,144},{32,160},{48,176},{64,192},{80,208},{96,224},{112... | collective-permute-start | bytes 98312 | tf_op jit(solution)/shard_map/ppermute | solution.py:25
  25.7 12.9 %collective-permute-start = (bf16[64,256]{1,0:T(8,128)(2,1)S(1)}, bf16[64,256]{1,0:T(8,128)(2,1)S(1)}, u32[]{:S(2)}, u32[]{:S(2)}) collective-permute-start(bf16[64,256]{1,0:T(8,128)(2,1)S(1)} %pad_maximum_fusion.refs_1_), channel_id=1, source_target_pairs={{0,64},{16,80},{32,96},{48,112},{64,0},{80,16},{96,32},{112,48},{1... | collective-permute-start | bytes 98312 | tf_op jit(solution)/shard_map/ppermute | solution.py:25
  28.2 0.9 copy-start.6
  38.7 26.1 %collective-permute-start.5 = (bf16[256,256]{1,0:T(8,128)(2,1)S(1)}, bf16[256,256]{1,0:T(8,128)(2,1)S(1)}, u32[]{:S(2)}, u32[]{:S(2)}) collective-permute-start(bf16[256,256]{1,0:T(8,128)(2,1)S(1)} %shard_map.111.refs_0_), channel_id=1, source_target_pairs={{0,48},{16,32},{32,16},{48,0},{64,112},{80,96},{96,80},{112,64},{1... | collective-permute-start | bytes 393224 | tf_op jit(solution)/shard_map/ppermute | solution.py:25
  40.8 24.0 %collective-permute-start.4 = (bf16[256,256]{1,0:T(8,128)(2,1)S(1)}, bf16[256,256]{1,0:T(8,128)(2,1)S(1)}, u32[]{:S(2)}, u32[]{:S(2)}) collective-permute-start(bf16[256,256]{1,0:T(8,128)(2,1)S(1)} %shard_map.111.refs_0_), channel_id=1, source_target_pairs={{0,32},{16,48},{32,0},{48,16},{64,96},{80,112},{96,64},{112,80},{1... | collective-permute-start | bytes 393224 | tf_op jit(solution)/shard_map/ppermute | solution.py:25
  46.6 18.2 %collective-permute-start.3 = (bf16[256,256]{1,0:T(8,128)(2,1)S(1)}, bf16[256,256]{1,0:T(8,128)(2,1)S(1)}, u32[]{:S(2)}, u32[]{:S(2)}) collective-permute-start(bf16[256,256]{1,0:T(8,128)(2,1)S(1)} %shard_map.111.refs_0_), channel_id=1, source_target_pairs={{0,16},{16,0},{32,48},{48,32},{64,80},{80,64},{96,112},{112,96},{1... | collective-permute-start | bytes 393224 | tf_op jit(solution)/shard_map/ppermute | solution.py:25
  48.5 41.8 %collective-permute-start.9 = (bf16[16,4096]{1,0:T(8,128)(2,1)S(1)}, bf16[16,4096]{1,0:T(8,128)(2,1)S(1)}, u32[]{:S(2)}, u32[]{:S(2)}) collective-permute-start(bf16[16,4096]{1,0:T(8,128)(2,1)S(1)} %get-tuple-element.38.refs_0_.refs_2_), channel_id=1, source_target_pairs={{0,2},{2,0},{1,3},{3,1},{4,6},{6,4},{5,7},{7,5},{8,10},{10,8},{9,1... | collective-permute-start | bytes 393224 | tf_op jit(solution)/shard_map/ppermute | solution.py:25
  64.8 25.4 %copy-start.2 = (bf16[1024,256]{1,0:T(8,128)(2,1)}, bf16[1024,256]{1,0:T(8,128)(2,1)S(1)}, u32[]{:S(2)}) copy-start(bf16[1024,256]{1,0:T(8,128)(2,1)S(1)} %shard_map.112.refs_0_.w_own) | copy-start | bytes 1572868
  64.9 27.0 %collective-permute-start.8 = (bf16[1024,256]{1,0:T(8,128)(2,1)S(1)}, bf16[1024,256]{1,0:T(8,128)(2,1)S(1)}, u32[]{:S(2)}, u32[]{:S(2)}) collective-permute-start(bf16[1024,256]{1,0:T(8,128)(2,1)S(1)} %shard_map.112.refs_0_.w_own), channel_id=1, source_target_pairs={{0,768},{256,0},{512,256},{768,512},{1,769},{257,1},{513,257},{769... | collective-permute-start | bytes 1572872 | tf_op jit(solution)/shard_map/ppermute | solution.py:30
  67.6 25.4 %collective-permute-start.7 = (bf16[1024,256]{1,0:T(8,128)(2,1)S(1)}, bf16[1024,256]{1,0:T(8,128)(2,1)S(1)}, u32[]{:S(2)}, u32[]{:S(2)}) collective-permute-start(bf16[1024,256]{1,0:T(8,128)(2,1)S(1)} %shard_map.112.refs_0_.w_own), channel_id=1, source_target_pairs={{0,256},{256,512},{512,768},{768,0},{1,257},{257,513},{513,769},{7... | collective-permute-start | bytes 1572872 | tf_op jit(solution)/shard_map/ppermute | solution.py:30
  71.9 31.2 %collective-permute-start.6 = (bf16[1024,256]{1,0:T(8,128)(2,1)S(1)}, bf16[1024,256]{1,0:T(8,128)(2,1)S(1)}, u32[]{:S(2)}, u32[]{:S(2)}) collective-permute-start(bf16[1024,256]{1,0:T(8,128)(2,1)S(1)} %shard_map.112.refs_0_.w_own), channel_id=1, source_target_pairs={{0,512},{256,768},{512,0},{768,256},{1,513},{257,769},{513,1},{769... | collective-permute-start | bytes 1572872 | tf_op jit(solution)/shard_map/ppermute | solution.py:30
  90.3 24.0 %copy-start.4 = (f32[256,128]{1,0:T(8,128)S(1)}, f32[256,128]{1,0:T(8,128)}, u32[]{:S(2)}) copy-start(f32[256,128]{1,0:T(8,128)} %constant.25.clone.sin) | copy-start | bytes 393220
  90.3 23.9 %copy-start.5 = (f32[256,128]{1,0:T(8,128)S(1)}, f32[256,128]{1,0:T(8,128)}, u32[]{:S(2)}) copy-start(f32[256,128]{1,0:T(8,128)} %constant.24.clone.cos) | copy-start | bytes 393220
  93.1 10.1 %collective-permute-start.12 = (bf16[32,4096]{1,0:T(8,128)(2,1)S(1)}, bf16[32,4096]{1,0:T(8,128)(2,1)S(1)}, u32[]{:S(2)}, u32[]{:S(2)}) collective-permute-start(bf16[32,4096]{1,0:T(8,128)(2,1)S(1)} %shard_map.114.refs_1_), channel_id=1, source_target_pairs={{0,8},{4,12},{8,0},{12,4},{1,9},{5,13},{9,1},{13,5},{2,10},{6,14},... | collective-permute-start | bytes 786440 | tf_op jit(solution)/shard_map/ppermute | solution.py:30
  97.3 8.4 %collective-permute-start.11 = (bf16[32,4096]{1,0:T(8,128)(2,1)S(1)}, bf16[32,4096]{1,0:T(8,128)(2,1)S(1)}, u32[]{:S(2)}, u32[]{:S(2)}) collective-permute-start(bf16[32,4096]{1,0:T(8,128)(2,1)S(1)} %shard_map.114.refs_1_), channel_id=1, source_target_pairs={{0,12},{4,0},{8,4},{12,8},{1,13},{5,1},{9,5},{13,9},{2,14},{6,2},{... | collective-permute-start | bytes 786440 | tf_op jit(solution)/shard_map/ppermute | solution.py:30
  100.5 8.3 %collective-permute-start.10 = (bf16[32,4096]{1,0:T(8,128)(2,1)S(1)}, bf16[32,4096]{1,0:T(8,128)(2,1)S(1)}, u32[]{:S(2)}, u32[]{:S(2)}) collective-permute-start(bf16[32,4096]{1,0:T(8,128)(2,1)S(1)} %shard_map.114.refs_1_), channel_id=1, source_target_pairs={{0,4},{4,8},{8,12},{12,0},{1,5},{5,9},{9,13},{13,1},{2,6},{6,10},{... | collective-permute-start | bytes 786440 | tf_op jit(solution)/shard_map/ppermute | solution.py:30
  108.9 0.8 copy-start
  109.7 4.5 %collective-permute-start.13 = (bf16[128,4096]{1,0:T(8,128)(2,1)S(1)}, bf16[128,4096]{1,0:T(8,128)(2,1)S(1)}, u32[]{:S(2)}, u32[]{:S(2)}) collective-permute-start(bf16[128,4096]{1,0:T(8,128)(2,1)S(1)} %shard_map.115.t0), channel_id=1, source_target_pairs={{0,1},{1,0},{2,3},{3,2},{4,5},{5,4},{6,7},{7,6},{8,9},{9,8},{10,11... | collective-permute-start | bytes 3145736 | tf_op jit(solution)/shard_map/ppermute | solution.py:25
  114.2 1.0 copy-start.1
  115.3 1.0 copy-start.3
  116.3 4.7 %copy-start.8 = (bf16[256,128]{1,0:T(8,128)(2,1)S(1)}, bf16[256,128]{1,0:T(8,128)(2,1)}, u32[]{:S(2)}) copy-start(bf16[256,128]{1,0:T(8,128)(2,1)} %d_ctx_ref.1) | copy-start | bytes 196612
  117.8 3.1 %collective-permute-start.14 = (bf16[256,128]{1,0:T(8,128)(2,1)S(1)}, bf16[256,128]{1,0:T(8,128)(2,1)S(1)}, u32[]{:S(2)}, u32[]{:S(2)}) collective-permute-start(bf16[256,128]{1,0:T(8,128)(2,1)S(1)} %get-tuple-element.40.mine_ref), channel_id=1, source_target_pairs={{0,1},{1,0},{2,3},{3,2},{4,5},{5,4},{6,7},{7,6},{8,9},{9,8},{10,11... | collective-permute-start | bytes 196616 | tf_op jit(solution)/shard_map/ppermute | solution.py:25
  122.9 3.1 %collective-permute-start.15 = (bf16[256,128]{1,0:T(8,128)(2,1)S(1)}, bf16[256,128]{1,0:T(8,128)(2,1)S(1)}, u32[]{:S(2)}, u32[]{:S(2)}) collective-permute-start(bf16[256,128]{1,0:T(8,128)(2,1)S(1)} %get-tuple-element.45), channel_id=1, source_target_pairs={{0,1},{1,0},{2,3},{3,2},{4,5},{5,4},{6,7},{7,6},{8,9},{9,8},{10,11... | collective-permute-start | bytes 196616 | tf_op jit(solution)/shard_map/ppermute | solution.py:25
  127.5 15.0 %collective-permute-start.16 = (bf16[128,4096]{1,0:T(8,128)(2,1)S(1)}, bf16[128,4096]{1,0:T(8,128)(2,1)S(1)}, u32[]{:S(2)}, u32[]{:S(2)}) collective-permute-start(bf16[128,4096]{1,0:T(8,128)(2,1)S(1)} %get-tuple-element.50), channel_id=1, source_target_pairs={{0,1},{1,0},{2,3},{3,2},{4,5},{5,4},{6,7},{7,6},{8,9},{9,8},{10,11... | collective-permute-start | bytes 3145736 | tf_op jit(solution)/shard_map/ppermute | solution.py:25
  131.6 18.0 %collective-permute-start.21 = (bf16[1024,256]{1,0:T(8,128)(2,1)S(1)}, bf16[1024,256]{1,0:T(8,128)(2,1)S(1)}, u32[]{:S(2)}, u32[]{:S(2)}) collective-permute-start(bf16[1024,256]{1,0:T(8,128)(2,1)S(1)} %get-tuple-element.57), channel_id=1, source_target_pairs={{0,768},{256,0},{512,256},{768,512},{1,769},{257,1},{513,257},{769... | collective-permute-start | bytes 1572872 | tf_op jit(solution)/shard_map/ppermute | solution.py:30
  133.6 28.5 %collective-permute-start.22 = (bf16[1024,256]{1,0:T(8,128)(2,1)S(1)}, bf16[1024,256]{1,0:T(8,128)(2,1)S(1)}, u32[]{:S(2)}, u32[]{:S(2)}) collective-permute-start(bf16[1024,256]{1,0:T(8,128)(2,1)S(1)} %get-tuple-element.58), channel_id=1, source_target_pairs={{0,256},{256,512},{512,768},{768,0},{1,257},{257,513},{513,769},{7... | collective-permute-start | bytes 1572872 | tf_op jit(solution)/shard_map/ppermute | solution.py:30
  139.2 22.9 %collective-permute-start.23 = (bf16[1024,256]{1,0:T(8,128)(2,1)S(1)}, bf16[1024,256]{1,0:T(8,128)(2,1)S(1)}, u32[]{:S(2)}, u32[]{:S(2)}) collective-permute-start(bf16[1024,256]{1,0:T(8,128)(2,1)S(1)} %get-tuple-element.59), channel_id=1, source_target_pairs={{0,512},{256,768},{512,0},{768,256},{1,513},{257,769},{513,1},{769... | collective-permute-start | bytes 1572872 | tf_op jit(solution)/shard_map/ppermute | solution.py:30
  142.8 25.8 %collective-permute-start.17 = (bf16[32,4096]{1,0:T(8,128)(2,1)S(1)}, bf16[32,4096]{1,0:T(8,128)(2,1)S(1)}, u32[]{:S(2)}, u32[]{:S(2)}) collective-permute-start(bf16[32,4096]{1,0:T(8,128)(2,1)S(1)} %get-tuple-element.52), channel_id=1, source_target_pairs={{0,12},{4,0},{8,4},{12,8},{1,13},{5,1},{9,5},{13,9},{2,14},{6,2},{... | collective-permute-start | bytes 786440 | tf_op jit(solution)/shard_map/ppermute | solution.py:30
  147.0 24.6 %collective-permute-start.18 = (bf16[32,4096]{1,0:T(8,128)(2,1)S(1)}, bf16[32,4096]{1,0:T(8,128)(2,1)S(1)}, u32[]{:S(2)}, u32[]{:S(2)}) collective-permute-start(bf16[32,4096]{1,0:T(8,128)(2,1)S(1)} %get-tuple-element.53), channel_id=1, source_target_pairs={{0,4},{4,8},{8,12},{12,0},{1,5},{5,9},{9,13},{13,1},{2,6},{6,10},{... | collective-permute-start | bytes 786440 | tf_op jit(solution)/shard_map/ppermute | solution.py:30
  149.6 21.9 %collective-permute-start.19 = (bf16[32,4096]{1,0:T(8,128)(2,1)S(1)}, bf16[32,4096]{1,0:T(8,128)(2,1)S(1)}, u32[]{:S(2)}, u32[]{:S(2)}) collective-permute-start(bf16[32,4096]{1,0:T(8,128)(2,1)S(1)} %get-tuple-element.54), channel_id=1, source_target_pairs={{0,8},{4,12},{8,0},{12,4},{1,9},{5,13},{9,1},{13,5},{2,10},{6,14},... | collective-permute-start | bytes 786440 | tf_op jit(solution)/shard_map/ppermute | solution.py:30
  162.1 68.6 %copy-start.7 = (bf16[16,4096]{1,0:T(8,128)(2,1)S(1)}, bf16[16,4096]{1,0:T(8,128)(2,1)}, u32[]{:S(2)}) copy-start(bf16[16,4096]{1,0:T(8,128)(2,1)} %tokens.3) | copy-start | bytes 393220
  162.3 28.1 %collective-permute-start.24 = (bf16[256,256]{1,0:T(8,128)(2,1)S(1)}, bf16[256,256]{1,0:T(8,128)(2,1)S(1)}, u32[]{:S(2)}, u32[]{:S(2)}) collective-permute-start(bf16[256,256]{1,0:T(8,128)(2,1)S(1)} %get-tuple-element.61), channel_id=1, source_target_pairs={{0,16},{16,0},{32,48},{48,32},{64,80},{80,64},{96,112},{112,96},{1... | collective-permute-start | bytes 393224 | tf_op jit(solution)/shard_map/ppermute | solution.py:25
  165.2 25.2 %collective-permute-start.25 = (bf16[256,256]{1,0:T(8,128)(2,1)S(1)}, bf16[256,256]{1,0:T(8,128)(2,1)S(1)}, u32[]{:S(2)}, u32[]{:S(2)}) collective-permute-start(bf16[256,256]{1,0:T(8,128)(2,1)S(1)} %get-tuple-element.62), channel_id=1, source_target_pairs={{0,32},{16,48},{32,0},{48,16},{64,96},{80,112},{96,64},{112,80},{1... | collective-permute-start | bytes 393224 | tf_op jit(solution)/shard_map/ppermute | solution.py:25
  168.6 21.8 %collective-permute-start.26 = (bf16[256,256]{1,0:T(8,128)(2,1)S(1)}, bf16[256,256]{1,0:T(8,128)(2,1)S(1)}, u32[]{:S(2)}, u32[]{:S(2)}) collective-permute-start(bf16[256,256]{1,0:T(8,128)(2,1)S(1)} %get-tuple-element.63), channel_id=1, source_target_pairs={{0,48},{16,32},{32,16},{48,0},{64,112},{80,96},{96,80},{112,64},{1... | collective-permute-start | bytes 393224 | tf_op jit(solution)/shard_map/ppermute | solution.py:25
  171.7 58.9 %collective-permute-start.20 = (bf16[16,4096]{1,0:T(8,128)(2,1)S(1)}, bf16[16,4096]{1,0:T(8,128)(2,1)S(1)}, u32[]{:S(2)}, u32[]{:S(2)}) collective-permute-start(bf16[16,4096]{1,0:T(8,128)(2,1)S(1)} %get-tuple-element.56), channel_id=1, source_target_pairs={{0,2},{2,0},{1,3},{3,1},{4,6},{6,4},{5,7},{7,5},{8,10},{10,8},{9,1... | collective-permute-start | bytes 393224 | tf_op jit(solution)/shard_map/ppermute | solution.py:25
  190.5 24.7 %collective-permute-start.27 = (bf16[64,256]{1,0:T(8,128)(2,1)S(1)}, bf16[64,256]{1,0:T(8,128)(2,1)S(1)}, u32[]{:S(2)}, u32[]{:S(2)}) collective-permute-start(bf16[64,256]{1,0:T(8,128)(2,1)S(1)} %get-tuple-element.65), channel_id=1, source_target_pairs={{0,64},{16,80},{32,96},{48,112},{64,0},{80,16},{96,32},{112,48},{1... | collective-permute-start | bytes 98312 | tf_op jit(solution)/shard_map/ppermute | solution.py:25
  192.4 23.5 %collective-permute-start.28 = (bf16[64,256]{1,0:T(8,128)(2,1)S(1)}, bf16[64,256]{1,0:T(8,128)(2,1)S(1)}, u32[]{:S(2)}, u32[]{:S(2)}) collective-permute-start(bf16[64,256]{1,0:T(8,128)(2,1)S(1)} %get-tuple-element.66), channel_id=1, source_target_pairs={{0,128},{16,144},{32,160},{48,176},{64,192},{80,208},{96,224},{112... | collective-permute-start | bytes 98312 | tf_op jit(solution)/shard_map/ppermute | solution.py:25
  210.6 19.3 %collective-permute-start.29 = (bf16[64,256]{1,0:T(8,128)(2,1)S(1)}, bf16[64,256]{1,0:T(8,128)(2,1)S(1)}, u32[]{:S(2)}, u32[]{:S(2)}) collective-permute-start(bf16[64,256]{1,0:T(8,128)(2,1)S(1)} %get-tuple-element.67), channel_id=1, source_target_pairs={{0,192},{16,208},{32,224},{48,240},{64,128},{80,144},{96,160},{112... | collective-permute-start | bytes 98312 | tf_op jit(solution)/shard_map/ppermute | solution.py:25

commit v3 on v2

--- a/solution.py
+++ b/solution.py
@@ -12,7 +12,7 @@
 
 SEQ = 16
 SHIFTS = (0, -1, 1, 2)
-VMEM_LIMIT = 40 * 1024 * 1024
+VMEM_LIMIT = 20 * 1024 * 1024
 
 AXES = ("x", "zl", "y", "zh", "co")
 SIZES = (4, 16, 4, 2, 2)
@@ -42,7 +42,7 @@
 
 
 def collect(blocks, axis, step):
-    return tuple(flipped(block, axis, k * step) for k, block in enumerate(blocks, 1))
+    return [flipped(block, axis, k * step) for k, block in reversed(list(enumerate(blocks, 1)))]
 
 
 def ring_gather(block, axis):
@@ -54,10 +54,6 @@
     for term in terms[1:]:
         total = total + term.astype(jnp.float32)
     return total
-
-
-def ring_scatter(blocks, axis):
-    return (blocks[0], *(shifted(block, axis, shift) for block, shift in zip(blocks[1:], SHIFTS[1:])))
 
 
 def rope_tables(rows, head_size):
@@ -79,7 +75,7 @@
 def sequence_at(place, ids):
     co, yq, zh = place // 8, place // 2 % 4, place % 2
     y = (ids[2] + SHIFTS[yq] + 4) % 4
-    return y * 4 + (ids[3] ^ zh) * 2 + (ids[4] ^ co)
+    return y * 4 + zh * 2 + (ids[4] ^ co)
 
 
 def norm_kernel(tokens, inv_out, normed_out):
@@ -96,8 +92,24 @@
         out[place * count : (place + 1) * count, :] = ref[...]
 
 
-def scatter_sum_kernel(first, terms, *refs):
-    parts, outs = refs[first : first + terms], refs[first + terms :]
+def part_kernel(after, mine, got, *outs):
+    count = outs[0].shape[0]
+    for place, out in enumerate(outs):
+        cut = slice(place * count, (place + 1) * count)
+        out[...] = added(mine[cut, :], got[cut, :]).astype(out.dtype)
+
+
+def pair_kernel(ids, own, left, right, far, keep_out, send_out):
+    count = keep_out.shape[0]
+    for zh, out in ((ids[3], keep_out), (1 - ids[3], send_out)):
+        cut = pl.ds(pl.multiple_of(zh * count, count), count)
+        out[...] = added(own[cut, :], left[cut, :], right[cut, :], far[cut, :]).astype(out.dtype)
+
+
+def scatter_sum_kernel(first, blocks, *refs):
+    parts, outs = refs[first:-blocks], refs[-blocks:]
+    if len(parts) == 1:
+        parts = [parts[0].at[entry] for entry in range(parts[0].shape[0])]
     count = outs[0].shape[0]
     for place, out in enumerate(outs):
         cut = slice(place * count, (place + 1) * count)
@@ -114,7 +126,7 @@
 
 def tokens_out_kernel(tokens, inv_wide, kept, got, out):
     inputs = tokens[...].astype(jnp.float32)
-    d_normed = kept[...] + got[...].astype(jnp.float32)
+    d_normed = added(kept[...], got[...])
     inv = inv_wide[:, :1]
     mean = jnp.mean(inputs * d_normed, axis=-1, keepdims=True)
     out[...] = (inv * d_normed - inputs * (inv * inv * inv) * mean).astype(jnp.bfloat16)
@@ -198,20 +210,19 @@
     return jnp.concatenate([dq_ref[...], d_kv], axis=1)
 
 
-def weight_grad_kernel(zs, ids, t0, t1, dj_ref, own, left, right, far, natural):
+def weight_grad_kernel(zs, ids, t0, t1, dj_ref, out, natural):
     half = dj_ref.shape[0] // 2
-    rows = own.shape[0]
+    blocks, rows = out.shape[:2]
     unit = rows // zs
     dims = (((0,), (0,)), ((), ()))
-    for ref, ring in ((far, 3), (left, 1), (right, 2), (own, 0)):
-        block = (ids[0] + SHIFTS[ring] + 4) % 4
-        cut = pl.ds(pl.multiple_of(block * rows, rows), rows)
+    for block in range(blocks):
+        cut = slice(block * rows, (block + 1) * rows)
         total = lax.dot_general(t0[:, cut], dj_ref[:half, :], dims, preferred_element_type=jnp.float32)
         total += lax.dot_general(t1[:, cut], dj_ref[half:, :], dims, preferred_element_type=jnp.float32)
         natural[...] = total.astype(jnp.bfloat16)
         for place in range(zs):
             at = pl.multiple_of((ids[1] ^ z_offset(place)) * unit, unit)
-            ref[place * unit : (place + 1) * unit, :] = natural[pl.ds(at, unit), :]
+            out[block, place * unit : (place + 1) * unit, :] = natural[pl.ds(at, unit), :]
 
 
 def token_grad_kernel(dq_ref, keep_ref, got_ref, w_ref, mine_out, send_out, dj_out):
@@ -253,11 +264,11 @@
 
 
 def scatter_sum(blocks, *parts, after=()):
-    shape = (parts[0].shape[0] // blocks, parts[0].shape[1])
+    shape = (parts[0].shape[-2] // blocks, parts[0].shape[-1])
     return call(
-        functools.partial(scatter_sum_kernel, len(after), len(parts)),
+        functools.partial(scatter_sum_kernel, len(after), blocks),
         [(shape, jnp.float32)] + [(shape, jnp.bfloat16)] * (blocks - 1),
-        *parts, after=after, moved=4 * len(parts) * parts[0].shape[0] * shape[1],
+        *parts, after=after, moved=16 * blocks * shape[0] * shape[1],
     )
 
 
@@ -277,9 +288,9 @@
     near = rows(weights, *spread(weights, "zl", RADIX), after=(normed,))
     whole = rows(near, *spread(near, "zl", 1))
     w_pieces = (whole, *ring_gather(whole, "x"))
-    far = rows(flipped(normed, "zh", 1), after=(whole,), flops=40 * product)
-    pair = rows(normed, far, after=w_pieces[1:3])
-    t0 = rows(pair, *ring_gather(pair, "y"), after=w_pieces[3:])
+    both = lax.all_to_all(jnp.stack([normed, normed]), "zh", 0, 0).reshape(2 * count, width)
+    pair = rows(both, after=(whole,), flops=40 * product)
+    t0 = rows(pair, *ring_gather(pair, "y"), after=w_pieces[1:])
     t1 = flipped(t0, "co", 1)
 
     half = t0.shape[0]
@@ -308,23 +319,29 @@
         d_query, keep, got, w_natural,
         flops=product, moved=4 * width * held,
     )
-    g_blocks = call(
+    (g_blocks,) = call(
         functools.partial(weight_grad_kernel, zs),
-        [((block, 2 * head), b16)] * 4,
+        [((SIZES[0], block, 2 * head), b16)],
         ids, t0, t1, joined,
         scratch=[(block, 2 * head)],
         flops=product, moved=4 * width * held,
     )
 
-    y_blocks = scatter_sum(SIZES[2], p_mine, flipped(p_send, "co", 1), after=(g_blocks[0],))
-    kept_t, sent_t = scatter_sum(2, *ring_scatter(y_blocks, "y"))
+    y_own, *y_sent = call(
+        part_kernel, [((2 * count, width), f32)] + [((2 * count, width), b16)] * 3, p_mine, flipped(p_send, "co", 1),
+        after=(g_blocks,), moved=24 * half * width,
+    )
+    y_got = [shifted(sent, "y", shift) for sent, shift in zip(y_sent, SHIFTS[1:])]
+    kept_t, sent_t = call(
+        pair_kernel, [((count, width), f32), ((count, width), b16)], ids, y_own, *y_got, moved=24 * count * width,
+    )
     from_zh = flipped(sent_t, "zh", 1)
     (grad_tokens,) = call(
         tokens_out_kernel, [((count, width), b16)], tokens, inv_wide, kept_t, from_zh,
-        flops=8 * count * width, moved=12 * count * width,
-    )
-
-    kept, *sent = scatter_sum(RADIX, *ring_scatter(g_blocks, "x"), after=(y_blocks[0],))
+        flops=40 * product, moved=12 * count * width,
+    )
+
+    kept, *sent = scatter_sum(RADIX, lax.all_to_all(g_blocks, "x", 0, 0), after=(sent_t,))
     kept, *sent = scatter_sum(RADIX, kept, *collect(sent, "zl", 1))
     cut = kept.shape[0]
     grads = call(

time: 233 us -> 234 us (level)
  the two profiles are of different devices: /device:TPU:78 before, /device:TPU:1 now
where the time goes in v3:
time: 234 us; the launch traced here: 233 us
  starting transfers between devices  163 us (70%)
  waiting for transfers between devices  50.8 us (22%)
  Pallas kernels  11.3 us (5%)
  local copies, waits for them, and re-layouts  4.88 us (2%)
    ppermute x17, starting transfers between devices, flipped(): return lax.ppermute(value, axis, [(s, s ^ mask) for s in range(size)])  102 us
    ppermute x17, waiting for transfers between devices, flipped(): return lax.ppermute(value, axis, [(s, s ^ mask) for s in range(size)])  33.9 us
    ppermute x9, starting transfers between devices, shifted(): lax.ppermute(value, axis, [(s, (s + step) % size) for s in range(size)])  29.1 us
    all_to_all x1, starting transfers between devices, shards(): lax.all_to_all(jnp.stack([normed, normed]), 'zh', 0, 0)  28.9 us
    ppermute x9, waiting for transfers between devices, shifted(): lax.ppermute(value, axis, [(s, (s + step) % size) for s in range(size)])  14.8 us
    pallas_call x15, Pallas kernels, call(): pl.pallas_call(kernel, out_shape=[jax.ShapeDtypeStruct(s, t) for s, t in...  11.3 us
    unnamed x20, local copies, waits for them, and re-layouts  4.79 us
  transfers between devices with their start and end apart: 28, of which 15 were waited for; matrix products, arithmetic and copies ran while one was open for 0% of the time, Pallas kernels for 1%

profile of v3, /device:TPU:1, one launch (start us, length us, event | category | flops | bytes accessed | tf_op | source)
XLA Modules:
  0.0 232.9 jit_solution(11536059551380853280)
XLA Ops:
  0.6 0.9 copy-done.6
  1.5 0.1 shard_map.110
  1.7 0.7 pad_maximum_fusion
  2.4 28.9 %all-to-all-start = ((bf16[2,16,4096]{2,1,0:T(8,128)(2,1)}), bf16[2,16,4096]{2,1,0:T(8,128)(2,1)S(1)}, u32[]{:S(2)}, u32[]{:S(2)}) async-start(bf16[2,16,4096]{2,1,0:T(8,128)(2,1)} %pad_maximum_fusion), calls=%async_computation | async-start | bytes 524288 | tf_op jit(solution)/shard_map/all_to_all | solution.py:291
  31.3 0.8 pad_maximum_fusion.1.refs_1_
  32.1 4.0 %collective-permute-start = (bf16[64,256]{1,0:T(8,128)(2,1)S(1)}, bf16[64,256]{1,0:T(8,128)(2,1)S(1)}, u32[]{:S(2)}, u32[]{:S(2)}) collective-permute-start(bf16[64,256]{1,0:T(8,128)(2,1)S(1)} %pad_maximum_fusion.1.refs_1_), channel_id=1, source_target_pairs={{0,64},{16,80},{32,96},{48,112},{64,0},{80,16},{96,32},{112,48},{1... | collective-permute-start | bytes 98312 | tf_op jit(solution)/shard_map/ppermute | solution.py:25
  36.1 5.8 %collective-permute-start.1 = (bf16[64,256]{1,0:T(8,128)(2,1)S(1)}, bf16[64,256]{1,0:T(8,128)(2,1)S(1)}, u32[]{:S(2)}, u32[]{:S(2)}) collective-permute-start(bf16[64,256]{1,0:T(8,128)(2,1)S(1)} %pad_maximum_fusion.1.refs_1_), channel_id=1, source_target_pairs={{0,128},{16,144},{32,160},{48,176},{64,192},{80,208},{96,224},{112... | collective-permute-start | bytes 98312 | tf_op jit(solution)/shard_map/ppermute | solution.py:25
  42.0 11.2 %collective-permute-start.2 = (bf16[64,256]{1,0:T(8,128)(2,1)S(1)}, bf16[64,256]{1,0:T(8,128)(2,1)S(1)}, u32[]{:S(2)}, u32[]{:S(2)}) collective-permute-start(bf16[64,256]{1,0:T(8,128)(2,1)S(1)} %pad_maximum_fusion.1.refs_1_), channel_id=1, source_target_pairs={{0,192},{16,208},{32,224},{48,240},{64,128},{80,144},{96,160},{112... | collective-permute-start | bytes 98312 | tf_op jit(solution)/shard_map/ppermute | solution.py:25
  53.1 5.4 %collective-permute-done.refs_2_ = bf16[64,256]{1,0:T(8,128)(2,1)S(1)} collective-permute-done((bf16[64,256]{1,0:T(8,128)(2,1)S(1)}, bf16[64,256]{1,0:T(8,128)(2,1)S(1)}, u32[]{:S(2)}, u32[]{:S(2)}) %collective-permute-start) | collective-permute-done | bytes 32800 | tf_op jit(solution)/shard_map/ppermute | solution.py:25
  58.6 5.6 %collective-permute-done.2.refs_4_ = bf16[64,256]{1,0:T(8,128)(2,1)S(1)} collective-permute-done((bf16[64,256]{1,0:T(8,128)(2,1)S(1)}, bf16[64,256]{1,0:T(8,128)(2,1)S(1)}, u32[]{:S(2)}, u32[]{:S(2)}) %collective-permute-start.2) | collective-permute-done | bytes 32800 | tf_op jit(solution)/shard_map/ppermute | solution.py:25
  64.2 1.9 collective-permute-start.3
  66.1 1.9 collective-permute-start.4
  68.1 5.4 %collective-permute-start.5 = (bf16[256,256]{1,0:T(8,128)(2,1)S(1)}, bf16[256,256]{1,0:T(8,128)(2,1)S(1)}, u32[]{:S(2)}, u32[]{:S(2)}) collective-permute-start(bf16[256,256]{1,0:T(8,128)(2,1)S(1)} %shard_map.111.refs_0_), channel_id=1, source_target_pairs={{0,48},{16,32},{32,16},{48,0},{64,112},{80,96},{96,80},{112,64},{1... | collective-permute-start | bytes 393224 | tf_op jit(solution)/shard_map/ppermute | solution.py:25
  73.5 2.7 %collective-permute-done.4.refs_2_ = bf16[256,256]{1,0:T(8,128)(2,1)S(1)} collective-permute-done((bf16[256,256]{1,0:T(8,128)(2,1)S(1)}, bf16[256,256]{1,0:T(8,128)(2,1)S(1)}, u32[]{:S(2)}, u32[]{:S(2)}) %collective-permute-start.4) | collective-permute-done | bytes 131104 | tf_op jit(solution)/shard_map/ppermute | solution.py:25
  76.3 3.1 %collective-permute-start.6 = (bf16[1024,256]{1,0:T(8,128)(2,1)S(1)}, bf16[1024,256]{1,0:T(8,128)(2,1)S(1)}, u32[]{:S(2)}, u32[]{:S(2)}) collective-permute-start(bf16[1024,256]{1,0:T(8,128)(2,1)S(1)} %shard_map.112.refs_0_.w_own), channel_id=1, source_target_pairs={{0,256},{256,512},{512,768},{768,0},{1,257},{257,513},{513,769},{7... | collective-permute-start | bytes 1572872 | tf_op jit(solution)/shard_map/ppermute | solution.py:30
  79.4 3.4 %collective-permute-start.7 = (bf16[1024,256]{1,0:T(8,128)(2,1)S(1)}, bf16[1024,256]{1,0:T(8,128)(2,1)S(1)}, u32[]{:S(2)}, u32[]{:S(2)}) collective-permute-start(bf16[1024,256]{1,0:T(8,128)(2,1)S(1)} %shard_map.112.refs_0_.w_own), channel_id=1, source_target_pairs={{0,768},{256,0},{512,256},{768,512},{1,769},{257,1},{513,257},{769... | collective-permute-start | bytes 1572872 | tf_op jit(solution)/shard_map/ppermute | solution.py:30
  82.8 3.4 %collective-permute-start.8 = (bf16[1024,256]{1,0:T(8,128)(2,1)S(1)}, bf16[1024,256]{1,0:T(8,128)(2,1)S(1)}, u32[]{:S(2)}, u32[]{:S(2)}) collective-permute-start(bf16[1024,256]{1,0:T(8,128)(2,1)S(1)} %shard_map.112.refs_0_.w_own), channel_id=1, source_target_pairs={{0,512},{256,768},{512,0},{768,256},{1,513},{257,769},{513,1},{769... | collective-permute-start | bytes 1572872 | tf_op jit(solution)/shard_map/ppermute | solution.py:30
  86.3 0.0 copy-start.4
  86.3 3.3 %collective-permute-start.9 = (bf16[32,4096]{1,0:T(8,128)(2,1)S(1)}, bf16[32,4096]{1,0:T(8,128)(2,1)S(1)}, u32[]{:S(2)}, u32[]{:S(2)}) collective-permute-start(bf16[32,4096]{1,0:T(8,128)(2,1)S(1)} %shard_map.113.refs_3_), channel_id=1, source_target_pairs={{0,4},{4,8},{8,12},{12,0},{1,5},{5,9},{9,13},{13,1},{2,6},{6,10},{... | collective-permute-start | bytes 786440 | tf_op jit(solution)/shard_map/ppermute | solution.py:30
  89.6 3.4 %collective-permute-start.10 = (bf16[32,4096]{1,0:T(8,128)(2,1)S(1)}, bf16[32,4096]{1,0:T(8,128)(2,1)S(1)}, u32[]{:S(2)}, u32[]{:S(2)}) collective-permute-start(bf16[32,4096]{1,0:T(8,128)(2,1)S(1)} %shard_map.113.refs_3_), channel_id=1, source_target_pairs={{0,12},{4,0},{8,4},{12,8},{1,13},{5,1},{9,5},{13,9},{2,14},{6,2},{... | collective-permute-start | bytes 786440 | tf_op jit(solution)/shard_map/ppermute | solution.py:30
  93.0 3.5 %collective-permute-start.11 = (bf16[32,4096]{1,0:T(8,128)(2,1)S(1)}, bf16[32,4096]{1,0:T(8,128)(2,1)S(1)}, u32[]{:S(2)}, u32[]{:S(2)}) collective-permute-start(bf16[32,4096]{1,0:T(8,128)(2,1)S(1)} %shard_map.113.refs_3_), channel_id=1, source_target_pairs={{0,8},{4,12},{8,0},{12,4},{1,9},{5,13},{9,1},{13,5},{2,10},{6,14},... | collective-permute-start | bytes 786440 | tf_op jit(solution)/shard_map/ppermute | solution.py:30
  96.6 0.5 collective-permute-done.10.refs_5_
  97.0 4.9 %collective-permute-done.11.refs_6_ = bf16[32,4096]{1,0:T(8,128)(2,1)S(1)} collective-permute-done((bf16[32,4096]{1,0:T(8,128)(2,1)S(1)}, bf16[32,4096]{1,0:T(8,128)(2,1)S(1)}, u32[]{:S(2)}, u32[]{:S(2)}) %collective-permute-start.11) | collective-permute-done | bytes 262176 | tf_op jit(solution)/shard_map/ppermute | solution.py:30
  101.9 0.1 shard_map.114.t0
  102.0 0.8 copy-done
  102.8 14.8 %collective-permute-start.12 = (bf16[128,4096]{1,0:T(8,128)(2,1)S(1)}, bf16[128,4096]{1,0:T(8,128)(2,1)S(1)}, u32[]{:S(2)}, u32[]{:S(2)}) collective-permute-start(bf16[128,4096]{1,0:T(8,128)(2,1)S(1)} %shard_map.114.t0), channel_id=1, source_target_pairs={{0,1},{1,0},{2,3},{3,2},{4,5},{5,4},{6,7},{7,6},{8,9},{9,8},{10,11... | collective-permute-start | bytes 3145736 | tf_op jit(solution)/shard_map/ppermute | solution.py:25
  117.7 0.1 stack.30.ids
  117.8 2.2 collective-permute-done.12.t1
  120.0 1.0 copy-done.1
  121.0 1.0 copy-done.3
  122.0 1.5 shard_map.115
  123.5 2.3 collective-permute-start.13
  125.8 0.9 collective-permute-done.13.other_ref
  126.7 1.9 shard_map.116
  128.6 2.2 collective-permute-start.14
  130.9 0.9 collective-permute-done.14.got_ref
  131.8 1.5 shard_map.117
  133.3 1.0 copy-done.9
  134.2 3.4 %shard_map.118.after = bf16[4,1024,256]{2,1,0:T(8,128)(2,1)} custom-call(s32[5]{0:T(128)S(1)} %stack.30.ids, bf16[128,4096]{1,0:T(8,128)(2,1)S(1)} %shard_map.114.t0, bf16[128,4096]{1,0:T(8,128)(2,1)S(1)} %collective-permute-done.12.t1, bf16[256,256]{1,0:T(8,128)(2,1)S(1)} %get-tuple-element.43.dj_ref), custom_call_target="tpu_custom_call" | custom-call | flops 536870912 | bytes 4194304 | tf_op jit(solution)/shard_map/pallas_call | solution.py:246
  137.6 3.6 %all-to-all-start.1 = ((bf16[4,1024,256]{2,1,0:T(8,128)(2,1)}), bf16[4,1024,256]{2,1,0:T(8,128)(2,1)S(1)}, u32[]{:S(2)}, u32[]{:S(2)}) async-start(bf16[4,1024,256]{2,1,0:T(8,128)(2,1)} %shard_map.118.after), calls=%async_computation.1 | async-start | bytes 4194304 | tf_op jit(solution)/shard_map/all_to_all | solution.py:344
  141.2 2.3 collective-permute-start.15
  143.5 2.5 %collective-permute-done.15.got = bf16[128,4096]{1,0:T(8,128)(2,1)S(1)} collective-permute-done((bf16[128,4096]{1,0:T(8,128)(2,1)}, bf16[128,4096]{1,0:T(8,128)(2,1)S(1)}, u32[]{:S(2)}, u32[]{:S(2)}) %collective-permute-start.15) | collective-permute-done | bytes 1048608 | tf_op jit(solution)/shard_map/ppermute | solution.py:25
  146.0 0.2 shard_map.119
  146.2 3.4 %collective-permute-start.16 = (bf16[32,4096]{1,0:T(8,128)(2,1)S(1)}, bf16[32,4096]{1,0:T(8,128)(2,1)S(1)}, u32[]{:S(2)}, u32[]{:S(2)}) collective-permute-start(bf16[32,4096]{1,0:T(8,128)(2,1)S(1)} %get-tuple-element.47), channel_id=1, source_target_pairs={{0,12},{4,0},{8,4},{12,8},{1,13},{5,1},{9,5},{13,9},{2,14},{6,2},{... | collective-permute-start | bytes 786440 | tf_op jit(solution)/shard_map/ppermute | solution.py:30
  149.7 1.9 collective-permute-start.17
  151.6 3.5 %collective-permute-start.18 = (bf16[32,4096]{1,0:T(8,128)(2,1)S(1)}, bf16[32,4096]{1,0:T(8,128)(2,1)S(1)}, u32[]{:S(2)}, u32[]{:S(2)}) collective-permute-start(bf16[32,4096]{1,0:T(8,128)(2,1)S(1)} %get-tuple-element.49), channel_id=1, source_target_pairs={{0,8},{4,12},{8,0},{12,4},{1,9},{5,13},{9,1},{13,5},{2,10},{6,14},... | collective-permute-start | bytes 786440 | tf_op jit(solution)/shard_map/ppermute | solution.py:30
  155.1 0.5 collective-permute-done.16.left
  155.6 5.4 %collective-permute-done.17.right = bf16[32,4096]{1,0:T(8,128)(2,1)S(1)} collective-permute-done((bf16[32,4096]{1,0:T(8,128)(2,1)S(1)}, bf16[32,4096]{1,0:T(8,128)(2,1)S(1)}, u32[]{:S(2)}, u32[]{:S(2)}) %collective-permute-start.17) | collective-permute-done | bytes 262176 | tf_op jit(solution)/shard_map/ppermute | solution.py:30
  161.0 3.6 %collective-permute-done.18.far = bf16[32,4096]{1,0:T(8,128)(2,1)S(1)} collective-permute-done((bf16[32,4096]{1,0:T(8,128)(2,1)S(1)}, bf16[32,4096]{1,0:T(8,128)(2,1)S(1)}, u32[]{:S(2)}, u32[]{:S(2)}) %collective-permute-start.18) | collective-permute-done | bytes 262176 | tf_op jit(solution)/shard_map/ppermute | solution.py:30
  164.6 0.7 shard_map.120
  165.3 2.0 all-to-all-done.1.refs_1_
  167.3 0.3 shard_map.122
  167.5 1.9 collective-permute-start.20
  169.5 1.9 collective-permute-start.21
  171.4 5.4 %collective-permute-start.22 = (bf16[256,256]{1,0:T(8,128)(2,1)S(1)}, bf16[256,256]{1,0:T(8,128)(2,1)S(1)}, u32[]{:S(2)}, u32[]{:S(2)}) collective-permute-start(bf16[256,256]{1,0:T(8,128)(2,1)S(1)} %get-tuple-element.55), channel_id=1, source_target_pairs={{0,16},{16,0},{32,48},{48,32},{64,80},{80,64},{96,112},{112,96},{1... | collective-permute-start | bytes 393224 | tf_op jit(solution)/shard_map/ppermute | solution.py:25
  176.8 19.7 %collective-permute-start.19 = (bf16[16,4096]{1,0:T(8,128)(2,1)S(1)}, bf16[16,4096]{1,0:T(8,128)(2,1)S(1)}, u32[]{:S(2)}, u32[]{:S(2)}) collective-permute-start(bf16[16,4096]{1,0:T(8,128)(2,1)S(1)} %get-tuple-element.51.refs_0_), channel_id=1, source_target_pairs={{0,2},{2,0},{1,3},{3,1},{4,6},{6,4},{5,7},{7,5},{8,10},{10,8},{9,1... | collective-permute-start | bytes 393224 | tf_op jit(solution)/shard_map/ppermute | solution.py:25
  196.5 0.1 shard_map.123
  196.6 4.8 %collective-permute-start.23 = (bf16[64,256]{1,0:T(8,128)(2,1)S(1)}, bf16[64,256]{1,0:T(8,128)(2,1)S(1)}, u32[]{:S(2)}, u32[]{:S(2)}) collective-permute-start(bf16[64,256]{1,0:T(8,128)(2,1)S(1)} %get-tuple-element.57), channel_id=1, source_target_pairs={{0,192},{16,208},{32,224},{48,240},{64,128},{80,144},{96,160},{112... | collective-permute-start | bytes 98312 | tf_op jit(solution)/shard_map/ppermute | solution.py:25
  201.4 5.3 %collective-permute-start.24 = (bf16[64,256]{1,0:T(8,128)(2,1)S(1)}, bf16[64,256]{1,0:T(8,128)(2,1)S(1)}, u32[]{:S(2)}, u32[]{:S(2)}) collective-permute-start(bf16[64,256]{1,0:T(8,128)(2,1)S(1)} %get-tuple-element.58), channel_id=1, source_target_pairs={{0,128},{16,144},{32,160},{48,176},{64,192},{80,208},{96,224},{112... | collective-permute-start | bytes 98312 | tf_op jit(solution)/shard_map/ppermute | solution.py:25
  206.7 10.9 %collective-permute-start.25 = (bf16[64,256]{1,0:T(8,128)(2,1)S(1)}, bf16[64,256]{1,0:T(8,128)(2,1)S(1)}, u32[]{:S(2)}, u32[]{:S(2)}) collective-permute-start(bf16[64,256]{1,0:T(8,128)(2,1)S(1)} %get-tuple-element.59), channel_id=1, source_target_pairs={{0,64},{16,80},{32,96},{48,112},{64,0},{80,16},{96,32},{112,48},{1... | collective-permute-start | bytes 98312 | tf_op jit(solution)/shard_map/ppermute | solution.py:25
  217.7 0.8 shard_map.121
  218.5 11.0 %collective-permute-done.23.a = bf16[64,256]{1,0:T(8,128)(2,1)S(1)} collective-permute-done((bf16[64,256]{1,0:T(8,128)(2,1)S(1)}, bf16[64,256]{1,0:T(8,128)(2,1)S(1)}, u32[]{:S(2)}, u32[]{:S(2)}) %collective-permute-start.23) | collective-permute-done | bytes 32800 | tf_op jit(solution)/shard_map/ppermute | solution.py:25
  229.5 2.8 %collective-permute-done.24.b = bf16[64,256]{1,0:T(8,128)(2,1)S(1)} collective-permute-done((bf16[64,256]{1,0:T(8,128)(2,1)S(1)}, bf16[64,256]{1,0:T(8,128)(2,1)S(1)}, u32[]{:S(2)}, u32[]{:S(2)}) %collective-permute-start.24) | collective-permute-done | bytes 32800 | tf_op jit(solution)/shard_map/ppermute | solution.py:25
  232.2 0.7 shard_map.124
  (30 shorter events, 0.1 us)
Async XLA Ops:
  0.6 0.9 copy-start.6
  2.4 83.8 %all-to-all-start = ((bf16[2,16,4096]{2,1,0:T(8,128)(2,1)}), bf16[2,16,4096]{2,1,0:T(8,128)(2,1)S(1)}, u32[]{:S(2)}, u32[]{:S(2)}) async-start(bf16[2,16,4096]{2,1,0:T(8,128)(2,1)} %pad_maximum_fusion), calls=%async_computation | async-start | bytes 524288 | tf_op jit(solution)/shard_map/all_to_all | solution.py:291
  32.1 26.4 %collective-permute-start = (bf16[64,256]{1,0:T(8,128)(2,1)S(1)}, bf16[64,256]{1,0:T(8,128)(2,1)S(1)}, u32[]{:S(2)}, u32[]{:S(2)}) collective-permute-start(bf16[64,256]{1,0:T(8,128)(2,1)S(1)} %pad_maximum_fusion.1.refs_1_), channel_id=1, source_target_pairs={{0,64},{16,80},{32,96},{48,112},{64,0},{80,16},{96,32},{112,48},{1... | collective-permute-start | bytes 98312 | tf_op jit(solution)/shard_map/ppermute | solution.py:25
  36.1 22.4 %collective-permute-start.1 = (bf16[64,256]{1,0:T(8,128)(2,1)S(1)}, bf16[64,256]{1,0:T(8,128)(2,1)S(1)}, u32[]{:S(2)}, u32[]{:S(2)}) collective-permute-start(bf16[64,256]{1,0:T(8,128)(2,1)S(1)} %pad_maximum_fusion.1.refs_1_), channel_id=1, source_target_pairs={{0,128},{16,144},{32,160},{48,176},{64,192},{80,208},{96,224},{112... | collective-permute-start | bytes 98312 | tf_op jit(solution)/shard_map/ppermute | solution.py:25
  42.0 22.2 %collective-permute-start.2 = (bf16[64,256]{1,0:T(8,128)(2,1)S(1)}, bf16[64,256]{1,0:T(8,128)(2,1)S(1)}, u32[]{:S(2)}, u32[]{:S(2)}) collective-permute-start(bf16[64,256]{1,0:T(8,128)(2,1)S(1)} %pad_maximum_fusion.1.refs_1_), channel_id=1, source_target_pairs={{0,192},{16,208},{32,224},{48,240},{64,128},{80,144},{96,160},{112... | collective-permute-start | bytes 98312 | tf_op jit(solution)/shard_map/ppermute | solution.py:25
  64.2 9.3 %collective-permute-start.3 = (bf16[256,256]{1,0:T(8,128)(2,1)S(1)}, bf16[256,256]{1,0:T(8,128)(2,1)S(1)}, u32[]{:S(2)}, u32[]{:S(2)}) collective-permute-start(bf16[256,256]{1,0:T(8,128)(2,1)S(1)} %shard_map.111.refs_0_), channel_id=1, source_target_pairs={{0,16},{16,0},{32,48},{48,32},{64,80},{80,64},{96,112},{112,96},{1... | collective-permute-start | bytes 393224 | tf_op jit(solution)/shard_map/ppermute | solution.py:25
  66.1 10.1 %collective-permute-start.4 = (bf16[256,256]{1,0:T(8,128)(2,1)S(1)}, bf16[256,256]{1,0:T(8,128)(2,1)S(1)}, u32[]{:S(2)}, u32[]{:S(2)}) collective-permute-start(bf16[256,256]{1,0:T(8,128)(2,1)S(1)} %shard_map.111.refs_0_), channel_id=1, source_target_pairs={{0,32},{16,48},{32,0},{48,16},{64,96},{80,112},{96,64},{112,80},{1... | collective-permute-start | bytes 393224 | tf_op jit(solution)/shard_map/ppermute | solution.py:25
  68.1 8.1 %collective-permute-start.5 = (bf16[256,256]{1,0:T(8,128)(2,1)S(1)}, bf16[256,256]{1,0:T(8,128)(2,1)S(1)}, u32[]{:S(2)}, u32[]{:S(2)}) collective-permute-start(bf16[256,256]{1,0:T(8,128)(2,1)S(1)} %shard_map.111.refs_0_), channel_id=1, source_target_pairs={{0,48},{16,32},{32,16},{48,0},{64,112},{80,96},{96,80},{112,64},{1... | collective-permute-start | bytes 393224 | tf_op jit(solution)/shard_map/ppermute | solution.py:25
  76.3 10.0 %copy-start.2 = (bf16[1024,256]{1,0:T(8,128)(2,1)}, bf16[1024,256]{1,0:T(8,128)(2,1)S(1)}, u32[]{:S(2)}) copy-start(bf16[1024,256]{1,0:T(8,128)(2,1)S(1)} %shard_map.112.refs_0_.w_own) | copy-start | bytes 1572868
  76.3 16.7 %collective-permute-start.6 = (bf16[1024,256]{1,0:T(8,128)(2,1)S(1)}, bf16[1024,256]{1,0:T(8,128)(2,1)S(1)}, u32[]{:S(2)}, u32[]{:S(2)}) collective-permute-start(bf16[1024,256]{1,0:T(8,128)(2,1)S(1)} %shard_map.112.refs_0_.w_own), channel_id=1, source_target_pairs={{0,256},{256,512},{512,768},{768,0},{1,257},{257,513},{513,769},{7... | collective-permute-start | bytes 1572872 | tf_op jit(solution)/shard_map/ppermute | solution.py:30
  79.4 17.2 %collective-permute-start.7 = (bf16[1024,256]{1,0:T(8,128)(2,1)S(1)}, bf16[1024,256]{1,0:T(8,128)(2,1)S(1)}, u32[]{:S(2)}, u32[]{:S(2)}) collective-permute-start(bf16[1024,256]{1,0:T(8,128)(2,1)S(1)} %shard_map.112.refs_0_.w_own), channel_id=1, source_target_pairs={{0,768},{256,0},{512,256},{768,512},{1,769},{257,1},{513,257},{769... | collective-permute-start | bytes 1572872 | tf_op jit(solution)/shard_map/ppermute | solution.py:30
  82.8 13.8 %collective-permute-start.8 = (bf16[1024,256]{1,0:T(8,128)(2,1)S(1)}, bf16[1024,256]{1,0:T(8,128)(2,1)S(1)}, u32[]{:S(2)}, u32[]{:S(2)}) collective-permute-start(bf16[1024,256]{1,0:T(8,128)(2,1)S(1)} %shard_map.112.refs_0_.w_own), channel_id=1, source_target_pairs={{0,512},{256,768},{512,0},{768,256},{1,513},{257,769},{513,1},{769... | collective-permute-start | bytes 1572872 | tf_op jit(solution)/shard_map/ppermute | solution.py:30
  86.3 33.7 %copy-start.4 = (f32[256,128]{1,0:T(8,128)S(1)}, f32[256,128]{1,0:T(8,128)}, u32[]{:S(2)}) copy-start(f32[256,128]{1,0:T(8,128)} %constant.24.clone.cos) | copy-start | bytes 393220
  86.3 33.7 %copy-start.5 = (f32[256,128]{1,0:T(8,128)S(1)}, f32[256,128]{1,0:T(8,128)}, u32[]{:S(2)}) copy-start(f32[256,128]{1,0:T(8,128)} %constant.25.clone.sin) | copy-start | bytes 393220
  86.3 10.3 %collective-permute-start.9 = (bf16[32,4096]{1,0:T(8,128)(2,1)S(1)}, bf16[32,4096]{1,0:T(8,128)(2,1)S(1)}, u32[]{:S(2)}, u32[]{:S(2)}) collective-permute-start(bf16[32,4096]{1,0:T(8,128)(2,1)S(1)} %shard_map.113.refs_3_), channel_id=1, source_target_pairs={{0,4},{4,8},{8,12},{12,0},{1,5},{5,9},{9,13},{13,1},{2,6},{6,10},{... | collective-permute-start | bytes 786440 | tf_op jit(solution)/shard_map/ppermute | solution.py:30
  89.6 7.4 %collective-permute-start.10 = (bf16[32,4096]{1,0:T(8,128)(2,1)S(1)}, bf16[32,4096]{1,0:T(8,128)(2,1)S(1)}, u32[]{:S(2)}, u32[]{:S(2)}) collective-permute-start(bf16[32,4096]{1,0:T(8,128)(2,1)S(1)} %shard_map.113.refs_3_), channel_id=1, source_target_pairs={{0,12},{4,0},{8,4},{12,8},{1,13},{5,1},{9,5},{13,9},{2,14},{6,2},{... | collective-permute-start | bytes 786440 | tf_op jit(solution)/shard_map/ppermute | solution.py:30
  93.0 8.9 %collective-permute-start.11 = (bf16[32,4096]{1,0:T(8,128)(2,1)S(1)}, bf16[32,4096]{1,0:T(8,128)(2,1)S(1)}, u32[]{:S(2)}, u32[]{:S(2)}) collective-permute-start(bf16[32,4096]{1,0:T(8,128)(2,1)S(1)} %shard_map.113.refs_3_), channel_id=1, source_target_pairs={{0,8},{4,12},{8,0},{12,4},{1,9},{5,13},{9,1},{13,5},{2,10},{6,14},... | collective-permute-start | bytes 786440 | tf_op jit(solution)/shard_map/ppermute | solution.py:30
  102.0 0.8 copy-start
  102.8 17.1 %collective-permute-start.12 = (bf16[128,4096]{1,0:T(8,128)(2,1)S(1)}, bf16[128,4096]{1,0:T(8,128)(2,1)S(1)}, u32[]{:S(2)}, u32[]{:S(2)}) collective-permute-start(bf16[128,4096]{1,0:T(8,128)(2,1)S(1)} %shard_map.114.t0), channel_id=1, source_target_pairs={{0,1},{1,0},{2,3},{3,2},{4,5},{5,4},{6,7},{7,6},{8,9},{9,8},{10,11... | collective-permute-start | bytes 3145736 | tf_op jit(solution)/shard_map/ppermute | solution.py:25
  120.0 1.0 copy-start.1
  121.0 1.0 copy-start.3
  122.0 4.7 %copy-start.8 = (bf16[256,128]{1,0:T(8,128)(2,1)S(1)}, bf16[256,128]{1,0:T(8,128)(2,1)}, u32[]{:S(2)}) copy-start(bf16[256,128]{1,0:T(8,128)(2,1)} %d_ctx_ref.1) | copy-start | bytes 196612
  123.5 3.2 %collective-permute-start.13 = (bf16[256,128]{1,0:T(8,128)(2,1)S(1)}, bf16[256,128]{1,0:T(8,128)(2,1)S(1)}, u32[]{:S(2)}, u32[]{:S(2)}) collective-permute-start(bf16[256,128]{1,0:T(8,128)(2,1)S(1)} %get-tuple-element.36.mine_ref), channel_id=1, source_target_pairs={{0,1},{1,0},{2,3},{3,2},{4,5},{5,4},{6,7},{7,6},{8,9},{9,8},{10,11... | collective-permute-start | bytes 196616 | tf_op jit(solution)/shard_map/ppermute | solution.py:25
  128.6 3.1 %collective-permute-start.14 = (bf16[256,128]{1,0:T(8,128)(2,1)S(1)}, bf16[256,128]{1,0:T(8,128)(2,1)S(1)}, u32[]{:S(2)}, u32[]{:S(2)}) collective-permute-start(bf16[256,128]{1,0:T(8,128)(2,1)S(1)} %get-tuple-element.41), channel_id=1, source_target_pairs={{0,1},{1,0},{2,3},{3,2},{4,5},{5,4},{6,7},{7,6},{8,9},{9,8},{10,11... | collective-permute-start | bytes 196616 | tf_op jit(solution)/shard_map/ppermute | solution.py:25
  133.3 1.0 copy-start.9
  137.6 29.7 %all-to-all-start.1 = ((bf16[4,1024,256]{2,1,0:T(8,128)(2,1)}), bf16[4,1024,256]{2,1,0:T(8,128)(2,1)S(1)}, u32[]{:S(2)}, u32[]{:S(2)}) async-start(bf16[4,1024,256]{2,1,0:T(8,128)(2,1)} %shard_map.118.after), calls=%async_computation.1 | async-start | bytes 4194304 | tf_op jit(solution)/shard_map/all_to_all | solution.py:344
  141.2 4.8 %collective-permute-start.15 = (bf16[128,4096]{1,0:T(8,128)(2,1)}, bf16[128,4096]{1,0:T(8,128)(2,1)S(1)}, u32[]{:S(2)}, u32[]{:S(2)}) collective-permute-start(bf16[128,4096]{1,0:T(8,128)(2,1)} %copy-done.9), channel_id=1, source_target_pairs={{0,1},{1,0},{2,3},{3,2},{4,5},{5,4},{6,7},{7,6},{8,9},{9,8},{10,11... | collective-permute-start | bytes 3145736 | tf_op jit(solution)/shard_map/ppermute | solution.py:25
  146.2 9.4 %collective-permute-start.16 = (bf16[32,4096]{1,0:T(8,128)(2,1)S(1)}, bf16[32,4096]{1,0:T(8,128)(2,1)S(1)}, u32[]{:S(2)}, u32[]{:S(2)}) collective-permute-start(bf16[32,4096]{1,0:T(8,128)(2,1)S(1)} %get-tuple-element.47), channel_id=1, source_target_pairs={{0,12},{4,0},{8,4},{12,8},{1,13},{5,1},{9,5},{13,9},{2,14},{6,2},{... | collective-permute-start | bytes 786440 | tf_op jit(solution)/shard_map/ppermute | solution.py:30
  149.7 11.3 %collective-permute-start.17 = (bf16[32,4096]{1,0:T(8,128)(2,1)S(1)}, bf16[32,4096]{1,0:T(8,128)(2,1)S(1)}, u32[]{:S(2)}, u32[]{:S(2)}) collective-permute-start(bf16[32,4096]{1,0:T(8,128)(2,1)S(1)} %get-tuple-element.48), channel_id=1, source_target_pairs={{0,4},{4,8},{8,12},{12,0},{1,5},{5,9},{9,13},{13,1},{2,6},{6,10},{... | collective-permute-start | bytes 786440 | tf_op jit(solution)/shard_map/ppermute | solution.py:30
  151.6 13.0 %collective-permute-start.18 = (bf16[32,4096]{1,0:T(8,128)(2,1)S(1)}, bf16[32,4096]{1,0:T(8,128)(2,1)S(1)}, u32[]{:S(2)}, u32[]{:S(2)}) collective-permute-start(bf16[32,4096]{1,0:T(8,128)(2,1)S(1)} %get-tuple-element.49), channel_id=1, source_target_pairs={{0,8},{4,12},{8,0},{12,4},{1,9},{5,13},{9,1},{13,5},{2,10},{6,14},... | collective-permute-start | bytes 786440 | tf_op jit(solution)/shard_map/ppermute | solution.py:30
  164.6 53.0 %copy-start.7 = (bf16[16,4096]{1,0:T(8,128)(2,1)S(1)}, bf16[16,4096]{1,0:T(8,128)(2,1)}, u32[]{:S(2)}) copy-start(bf16[16,4096]{1,0:T(8,128)(2,1)} %tokens.3) | copy-start | bytes 393220
  167.5 29.0 %collective-permute-start.20 = (bf16[256,256]{1,0:T(8,128)(2,1)S(1)}, bf16[256,256]{1,0:T(8,128)(2,1)S(1)}, u32[]{:S(2)}, u32[]{:S(2)}) collective-permute-start(bf16[256,256]{1,0:T(8,128)(2,1)S(1)} %get-tuple-element.53), channel_id=1, source_target_pairs={{0,48},{16,32},{32,16},{48,0},{64,112},{80,96},{96,80},{112,64},{1... | collective-permute-start | bytes 393224 | tf_op jit(solution)/shard_map/ppermute | solution.py:25
  169.5 27.1 %collective-permute-start.21 = (bf16[256,256]{1,0:T(8,128)(2,1)S(1)}, bf16[256,256]{1,0:T(8,128)(2,1)S(1)}, u32[]{:S(2)}, u32[]{:S(2)}) collective-permute-start(bf16[256,256]{1,0:T(8,128)(2,1)S(1)} %get-tuple-element.54), channel_id=1, source_target_pairs={{0,32},{16,48},{32,0},{48,16},{64,96},{80,112},{96,64},{112,80},{1... | collective-permute-start | bytes 393224 | tf_op jit(solution)/shard_map/ppermute | solution.py:25
  171.4 25.1 %collective-permute-start.22 = (bf16[256,256]{1,0:T(8,128)(2,1)S(1)}, bf16[256,256]{1,0:T(8,128)(2,1)S(1)}, u32[]{:S(2)}, u32[]{:S(2)}) collective-permute-start(bf16[256,256]{1,0:T(8,128)(2,1)S(1)} %get-tuple-element.55), channel_id=1, source_target_pairs={{0,16},{16,0},{32,48},{48,32},{64,80},{80,64},{96,112},{112,96},{1... | collective-permute-start | bytes 393224 | tf_op jit(solution)/shard_map/ppermute | solution.py:25
  176.8 40.8 %collective-permute-start.19 = (bf16[16,4096]{1,0:T(8,128)(2,1)S(1)}, bf16[16,4096]{1,0:T(8,128)(2,1)S(1)}, u32[]{:S(2)}, u32[]{:S(2)}) collective-permute-start(bf16[16,4096]{1,0:T(8,128)(2,1)S(1)} %get-tuple-element.51.refs_0_), channel_id=1, source_target_pairs={{0,2},{2,0},{1,3},{3,1},{4,6},{6,4},{5,7},{7,5},{8,10},{10,8},{9,1... | collective-permute-start | bytes 393224 | tf_op jit(solution)/shard_map/ppermute | solution.py:25
  196.6 32.9 %collective-permute-start.23 = (bf16[64,256]{1,0:T(8,128)(2,1)S(1)}, bf16[64,256]{1,0:T(8,128)(2,1)S(1)}, u32[]{:S(2)}, u32[]{:S(2)}) collective-permute-start(bf16[64,256]{1,0:T(8,128)(2,1)S(1)} %get-tuple-element.57), channel_id=1, source_target_pairs={{0,192},{16,208},{32,224},{48,240},{64,128},{80,144},{96,160},{112... | collective-permute-start | bytes 98312 | tf_op jit(solution)/shard_map/ppermute | solution.py:25
  201.4 30.8 %collective-permute-start.24 = (bf16[64,256]{1,0:T(8,128)(2,1)S(1)}, bf16[64,256]{1,0:T(8,128)(2,1)S(1)}, u32[]{:S(2)}, u32[]{:S(2)}) collective-permute-start(bf16[64,256]{1,0:T(8,128)(2,1)S(1)} %get-tuple-element.58), channel_id=1, source_target_pairs={{0,128},{16,144},{32,160},{48,176},{64,192},{80,208},{96,224},{112... | collective-permute-start | bytes 98312 | tf_op jit(solution)/shard_map/ppermute | solution.py:25
  206.7 25.5 %collective-permute-start.25 = (bf16[64,256]{1,0:T(8,128)(2,1)S(1)}, bf16[64,256]{1,0:T(8,128)(2,1)S(1)}, u32[]{:S(2)}, u32[]{:S(2)}) collective-permute-start(bf16[64,256]{1,0:T(8,128)(2,1)S(1)} %get-tuple-element.59), channel_id=1, source_target_pairs={{0,64},{16,80},{32,96},{48,112},{64,0},{80,16},{96,32},{112,48},{1... | collective-permute-start | bytes 98312 | tf_op jit(solution)/shard_map/ppermute | solution.py:25

commit v4 on v3

--- a/solution.py
+++ b/solution.py
@@ -34,7 +34,8 @@
 
 
 def z_offset(place):
-    return place % RADIX * RADIX + place // RADIX
+    far = place % RADIX
+    return (far & 1) * 2 * RADIX + (far >> 1) * RADIX + place // RADIX
 
 
 def spread(block, axis, step):
@@ -75,7 +76,7 @@
 def sequence_at(place, ids):
     co, yq, zh = place // 8, place // 2 % 4, place % 2
     y = (ids[2] + SHIFTS[yq] + 4) % 4
-    return y * 4 + zh * 2 + (ids[4] ^ co)
+    return y * 4 + (ids[3] ^ zh) * 2 + (ids[4] ^ co)
 
 
 def norm_kernel(tokens, inv_out, normed_out):
@@ -99,10 +100,10 @@
         out[...] = added(mine[cut, :], got[cut, :]).astype(out.dtype)
 
 
-def pair_kernel(ids, own, left, right, far, keep_out, send_out):
+def pair_kernel(own, left, right, far, keep_out, send_out):
     count = keep_out.shape[0]
-    for zh, out in ((ids[3], keep_out), (1 - ids[3], send_out)):
-        cut = pl.ds(pl.multiple_of(zh * count, count), count)
+    for place, out in enumerate((keep_out, send_out)):
+        cut = slice(place * count, (place + 1) * count)
         out[...] = added(own[cut, :], left[cut, :], right[cut, :], far[cut, :]).astype(out.dtype)
 
 
@@ -116,8 +117,8 @@
         out[...] = added(*(part[cut, :] for part in parts)).astype(out.dtype)
 
 
-def weights_out_kernel(own, a, b, c, q_out, k_out, v_out):
-    total = added(own[...], a[...], b[...], c[...])
+def weights_out_kernel(own, got, q_out, k_out, v_out):
+    total = added(own[...], got[...])
     head, half = q_out.shape[1], k_out.shape[1]
     q_out[...] = total[:, :head]
     k_out[...] = total[:, head : head + half]
@@ -285,12 +286,13 @@
         norm_kernel, [((count, 128), f32), ((count, width), b16)], tokens,
         flops=4 * count * width, moved=4 * count * width,
     )
-    near = rows(weights, *spread(weights, "zl", RADIX), after=(normed,))
+    near = rows(weights, flipped(weights, "zl", 2 * RADIX), after=(normed,))
+    near = rows(near, flipped(near, "zl", RADIX))
     whole = rows(near, *spread(near, "zl", 1))
     w_pieces = (whole, *ring_gather(whole, "x"))
-    both = lax.all_to_all(jnp.stack([normed, normed]), "zh", 0, 0).reshape(2 * count, width)
-    pair = rows(both, after=(whole,), flops=40 * product)
-    t0 = rows(pair, *ring_gather(pair, "y"), after=w_pieces[1:])
+    far = rows(flipped(normed, "zh", 1), after=(whole,), flops=40 * product)
+    pair = rows(normed, far, after=w_pieces[1:3])
+    t0 = rows(pair, *ring_gather(pair, "y"), after=w_pieces[3:])
     t1 = flipped(t0, "co", 1)
 
     half = t0.shape[0]
@@ -333,7 +335,7 @@
     )
     y_got = [shifted(sent, "y", shift) for sent, shift in zip(y_sent, SHIFTS[1:])]
     kept_t, sent_t = call(
-        pair_kernel, [((count, width), f32), ((count, width), b16)], ids, y_own, *y_got, moved=24 * count * width,
+        pair_kernel, [((count, width), f32), ((count, width), b16)], y_own, *y_got, moved=24 * count * width,
     )
     from_zh = flipped(sent_t, "zh", 1)
     (grad_tokens,) = call(
@@ -342,13 +344,14 @@
     )
 
     kept, *sent = scatter_sum(RADIX, lax.all_to_all(g_blocks, "x", 0, 0), after=(sent_t,))
-    kept, *sent = scatter_sum(RADIX, kept, *collect(sent, "zl", 1))
+    kept, sent = scatter_sum(2, kept, *collect(sent, "zl", 1))
+    kept, sent = scatter_sum(2, kept, flipped(sent, "zl", RADIX))
     cut = kept.shape[0]
     grads = call(
         weights_out_kernel,
         [((cut, head), f32), ((cut, head // 2), f32), ((cut, head // 2), f32)],
-        kept, *collect(sent, "zl", RADIX),
-        moved=24 * cut * head,
+        kept, flipped(sent, "zl", 2 * RADIX),
+        moved=12 * cut * head,
     )
     return (context, grad_tokens, *grads)
 

time: 234 us -> 237 us (1.013)
  waiting for transfers between devices: 50.8 us -> 57.9 us
  starting transfers between devices: 163 us -> 160 us
    all_to_all x1 -> x0, starting transfers between devices: 28.9 us -> none  [shards(): lax.all_to_all(jnp.stack([normed, normed]), 'zh', 0, 0)]
    ppermute x17 -> x16, starting transfers between devices: 102 us -> 126 us  [flipped(): return lax.ppermute(value, axis, [(s, s ^ mask) for s in range(size)])]
    ppermute x9, waiting for transfers between devices: 14.8 us -> 30.7 us  [shifted(): lax.ppermute(value, axis, [(s, (s + step) % size) for s in range(size)])]
    ppermute x17 -> x16, waiting for transfers between devices: 33.9 us -> 26.5 us  [flipped(): return lax.ppermute(value, axis, [(s, s ^ mask) for s in range(size)])]
    pallas_call x15 -> x18, Pallas kernels: 11.3 us -> 10.7 us  [call(): pl.pallas_call(kernel, out_shape=[jax.ShapeDtypeStruct(s, t) for s, t in...]
  transfers between devices with their start and end apart: 28 -> 26, of which waited for: 15 -> 15; matrix products, arithmetic and copies ran while one was open for 0% -> 0% of each run, Pallas kernels for 1% -> 1%
where the time goes in v4:
time: 237 us; the launch traced here: 235 us
  starting transfers between devices  160 us (68%)
  waiting for transfers between devices  57.9 us (24%)
  Pallas kernels  10.7 us (5%)
  local copies, waits for them, and re-layouts  4.06 us (2%)
    ppermute x16, starting transfers between devices, flipped(): return lax.ppermute(value, axis, [(s, s ^ mask) for s in range(size)])  126 us
    ppermute x9, waiting for transfers between devices, shifted(): lax.ppermute(value, axis, [(s, (s + step) % size) for s in range(size)])  30.7 us
    ppermute x9, starting transfers between devices, shifted(): lax.ppermute(value, axis, [(s, (s + step) % size) for s in range(size)])  30.1 us
    ppermute x16, waiting for transfers between devices, flipped(): return lax.ppermute(value, axis, [(s, s ^ mask) for s in range(size)])  26.5 us
    pallas_call x18, Pallas kernels, call(): pl.pallas_call(kernel, out_shape=[jax.ShapeDtypeStruct(s, t) for s, t in...  10.7 us
  transfers between devices with their start and end apart: 26, of which 15 were waited for; matrix products, arithmetic and copies ran while one was open for 0% of the time, Pallas kernels for 1%

profile of v4, /device:TPU:1, one launch (start us, length us, event | category | flops | bytes accessed | tf_op | source)
XLA Modules:
  0.0 234.8 jit_solution(8411403781495622894)
XLA Ops:
  0.6 0.8 pad_maximum_fusion.refs_1_
  1.5 16.3 %collective-permute-start = (bf16[64,256]{1,0:T(8,128)(2,1)S(1)}, bf16[64,256]{1,0:T(8,128)(2,1)S(1)}, u32[]{:S(2)}, u32[]{:S(2)}) collective-permute-start(bf16[64,256]{1,0:T(8,128)(2,1)S(1)} %pad_maximum_fusion.refs_1_), channel_id=1, source_target_pairs={{0,128},{16,144},{32,160},{48,176},{64,192},{80,208},{96,224},{112... | collective-permute-start | bytes 98312 | tf_op jit(solution)/shard_map/ppermute | solution.py:25
  17.7 0.0 copy-start.6
  17.7 0.9 copy-done.6
  18.6 0.1 shard_map.110
  18.8 0.2 collective-permute-done.refs_2_
  19.0 9.7 %collective-permute-start.1 = (bf16[128,256]{1,0:T(8,128)(2,1)S(1)}, bf16[128,256]{1,0:T(8,128)(2,1)S(1)}, u32[]{:S(2)}, u32[]{:S(2)}) collective-permute-start(bf16[128,256]{1,0:T(8,128)(2,1)S(1)} %shard_map.111.refs_0_), channel_id=1, source_target_pairs={{0,64},{16,80},{32,96},{48,112},{64,0},{80,16},{96,32},{112,48},{1... | collective-permute-start | bytes 196616 | tf_op jit(solution)/shard_map/ppermute | solution.py:25
  28.7 1.8 collective-permute-done.1.refs_1_
  30.6 3.6 %collective-permute-start.2 = (bf16[256,256]{1,0:T(8,128)(2,1)S(1)}, bf16[256,256]{1,0:T(8,128)(2,1)S(1)}, u32[]{:S(2)}, u32[]{:S(2)}) collective-permute-start(bf16[256,256]{1,0:T(8,128)(2,1)S(1)} %shard_map.112.refs_0_), channel_id=1, source_target_pairs={{0,16},{16,0},{32,48},{48,32},{64,80},{80,64},{96,112},{112,96},{1... | collective-permute-start | bytes 393224 | tf_op jit(solution)/shard_map/ppermute | solution.py:25
  34.2 7.5 %collective-permute-start.3 = (bf16[256,256]{1,0:T(8,128)(2,1)S(1)}, bf16[256,256]{1,0:T(8,128)(2,1)S(1)}, u32[]{:S(2)}, u32[]{:S(2)}) collective-permute-start(bf16[256,256]{1,0:T(8,128)(2,1)S(1)} %shard_map.112.refs_0_), channel_id=1, source_target_pairs={{0,32},{16,48},{32,0},{48,16},{64,96},{80,112},{96,64},{112,80},{1... | collective-permute-start | bytes 393224 | tf_op jit(solution)/shard_map/ppermute | solution.py:25
  41.7 1.9 collective-permute-start.4
  43.6 21.1 %collective-permute-start.8 = (bf16[16,4096]{1,0:T(8,128)(2,1)S(1)}, bf16[16,4096]{1,0:T(8,128)(2,1)S(1)}, u32[]{:S(2)}, u32[]{:S(2)}) collective-permute-start(bf16[16,4096]{1,0:T(8,128)(2,1)S(1)} %get-tuple-element.34.refs_0_.refs_2_), channel_id=1, source_target_pairs={{0,2},{2,0},{1,3},{3,1},{4,6},{6,4},{5,7},{7,5},{8,10},{10,8},{9,1... | collective-permute-start | bytes 393224 | tf_op jit(solution)/shard_map/ppermute | solution.py:25
  64.7 0.0 collective-permute-done.2.refs_1_
  64.7 0.0 collective-permute-done.3.refs_2_
  64.8 4.7 %collective-permute-start.5 = (bf16[1024,256]{1,0:T(8,128)(2,1)S(1)}, bf16[1024,256]{1,0:T(8,128)(2,1)S(1)}, u32[]{:S(2)}, u32[]{:S(2)}) collective-permute-start(bf16[1024,256]{1,0:T(8,128)(2,1)S(1)} %shard_map.113.refs_0_.w_own), channel_id=1, source_target_pairs={{0,512},{256,768},{512,0},{768,256},{1,513},{257,769},{513,1},{769... | collective-permute-start | bytes 1572872 | tf_op jit(solution)/shard_map/ppermute | solution.py:30
  69.4 2.2 collective-permute-start.6
  71.7 4.3 %collective-permute-start.7 = (bf16[1024,256]{1,0:T(8,128)(2,1)S(1)}, bf16[1024,256]{1,0:T(8,128)(2,1)S(1)}, u32[]{:S(2)}, u32[]{:S(2)}) collective-permute-start(bf16[1024,256]{1,0:T(8,128)(2,1)S(1)} %shard_map.113.refs_0_.w_own), channel_id=1, source_target_pairs={{0,768},{256,0},{512,256},{768,512},{1,769},{257,1},{513,257},{769... | collective-permute-start | bytes 1572872 | tf_op jit(solution)/shard_map/ppermute | solution.py:30
  76.0 0.0 copy-start.4
  76.0 0.0 copy-start.5
  76.0 12.2 %collective-permute-done.6.refs_0_.w_left = bf16[1024,256]{1,0:T(8,128)(2,1)S(1)} collective-permute-done((bf16[1024,256]{1,0:T(8,128)(2,1)S(1)}, bf16[1024,256]{1,0:T(8,128)(2,1)S(1)}, u32[]{:S(2)}, u32[]{:S(2)}) %collective-permute-start.6) | collective-permute-done | bytes 524320 | tf_op jit(solution)/shard_map/ppermute | solution.py:30
  88.2 0.2 collective-permute-done.7.refs_1_.w_right
  88.4 3.2 %collective-permute-start.9 = (bf16[32,4096]{1,0:T(8,128)(2,1)S(1)}, bf16[32,4096]{1,0:T(8,128)(2,1)S(1)}, u32[]{:S(2)}, u32[]{:S(2)}) collective-permute-start(bf16[32,4096]{1,0:T(8,128)(2,1)S(1)} %shard_map.115.refs_1_), channel_id=1, source_target_pairs={{0,4},{4,8},{8,12},{12,0},{1,5},{5,9},{9,13},{13,1},{2,6},{6,10},{... | collective-permute-start | bytes 786440 | tf_op jit(solution)/shard_map/ppermute | solution.py:30
  91.6 3.4 %collective-permute-start.10 = (bf16[32,4096]{1,0:T(8,128)(2,1)S(1)}, bf16[32,4096]{1,0:T(8,128)(2,1)S(1)}, u32[]{:S(2)}, u32[]{:S(2)}) collective-permute-start(bf16[32,4096]{1,0:T(8,128)(2,1)S(1)} %shard_map.115.refs_1_), channel_id=1, source_target_pairs={{0,12},{4,0},{8,4},{12,8},{1,13},{5,1},{9,5},{13,9},{2,14},{6,2},{... | collective-permute-start | bytes 786440 | tf_op jit(solution)/shard_map/ppermute | solution.py:30
  95.0 3.5 %collective-permute-start.11 = (bf16[32,4096]{1,0:T(8,128)(2,1)S(1)}, bf16[32,4096]{1,0:T(8,128)(2,1)S(1)}, u32[]{:S(2)}, u32[]{:S(2)}) collective-permute-start(bf16[32,4096]{1,0:T(8,128)(2,1)S(1)} %shard_map.115.refs_1_), channel_id=1, source_target_pairs={{0,8},{4,12},{8,0},{12,4},{1,9},{5,13},{9,1},{13,5},{2,10},{6,14},... | collective-permute-start | bytes 786440 | tf_op jit(solution)/shard_map/ppermute | solution.py:30
  98.5 0.2 collective-permute-done.10.refs_3_
  98.7 7.3 %collective-permute-done.11.refs_4_ = bf16[32,4096]{1,0:T(8,128)(2,1)S(1)} collective-permute-done((bf16[32,4096]{1,0:T(8,128)(2,1)S(1)}, bf16[32,4096]{1,0:T(8,128)(2,1)S(1)}, u32[]{:S(2)}, u32[]{:S(2)}) %collective-permute-start.11) | collective-permute-done | bytes 262176 | tf_op jit(solution)/shard_map/ppermute | solution.py:30
  106.0 0.1 shard_map.116.t0
  106.1 6.6 %collective-permute-start.12 = (bf16[128,4096]{1,0:T(8,128)(2,1)S(1)}, bf16[128,4096]{1,0:T(8,128)(2,1)S(1)}, u32[]{:S(2)}, u32[]{:S(2)}) collective-permute-start(bf16[128,4096]{1,0:T(8,128)(2,1)S(1)} %shard_map.116.t0), channel_id=1, source_target_pairs={{0,1},{1,0},{2,3},{3,2},{4,5},{5,4},{6,7},{7,6},{8,9},{9,8},{10,11... | collective-permute-start | bytes 3145736 | tf_op jit(solution)/shard_map/ppermute | solution.py:25
  112.7 0.1 stack.23.ids
  112.8 2.2 collective-permute-done.12.t1
  115.0 1.0 copy-done.1
  116.1 1.0 copy-done.3
  117.1 1.5 shard_map.117
  118.6 2.3 collective-permute-start.13
  120.9 0.9 collective-permute-done.13.other_ref
  121.8 1.9 shard_map.118
  123.7 2.2 collective-permute-start.14
  125.9 0.9 collective-permute-done.14.got_ref
  126.8 1.5 shard_map.119
  128.3 1.0 copy-done.9
  129.3 3.4 %shard_map.120.after = bf16[4,1024,256]{2,1,0:T(8,128)(2,1)} custom-call(s32[5]{0:T(128)S(1)} %stack.23.ids, bf16[128,4096]{1,0:T(8,128)(2,1)S(1)} %shard_map.116.t0, bf16[128,4096]{1,0:T(8,128)(2,1)S(1)} %collective-permute-done.12.t1, bf16[256,256]{1,0:T(8,128)(2,1)S(1)} %get-tuple-element.43.dj_ref), custom_call_target="tpu_custom_call" | custom-call | flops 536870912 | bytes 4194304 | tf_op jit(solution)/shard_map/pallas_call | solution.py:247
  132.7 4.5 %all-to-all-start = ((bf16[4,1024,256]{2,1,0:T(8,128)(2,1)}), bf16[4,1024,256]{2,1,0:T(8,128)(2,1)S(1)}, u32[]{:S(2)}, u32[]{:S(2)}) async-start(bf16[4,1024,256]{2,1,0:T(8,128)(2,1)} %shard_map.120.after), calls=%async_computation | async-start | bytes 4194304 | tf_op jit(solution)/shard_map/all_to_all | solution.py:346
  137.1 2.5 %collective-permute-start.15 = (bf16[128,4096]{1,0:T(8,128)(2,1)}, bf16[128,4096]{1,0:T(8,128)(2,1)S(1)}, u32[]{:S(2)}, u32[]{:S(2)}) collective-permute-start(bf16[128,4096]{1,0:T(8,128)(2,1)} %copy-done.9), channel_id=1, source_target_pairs={{0,1},{1,0},{2,3},{3,2},{4,5},{5,4},{6,7},{7,6},{8,9},{9,8},{10,11... | collective-permute-start | bytes 3145736 | tf_op jit(solution)/shard_map/ppermute | solution.py:25
  139.7 2.5 %collective-permute-done.15.got = bf16[128,4096]{1,0:T(8,128)(2,1)S(1)} collective-permute-done((bf16[128,4096]{1,0:T(8,128)(2,1)}, bf16[128,4096]{1,0:T(8,128)(2,1)S(1)}, u32[]{:S(2)}, u32[]{:S(2)}) %collective-permute-start.15) | collective-permute-done | bytes 1048608 | tf_op jit(solution)/shard_map/ppermute | solution.py:25
  142.2 0.2 shard_map.121
  142.4 3.8 %collective-permute-start.16 = (bf16[32,4096]{1,0:T(8,128)(2,1)S(1)}, bf16[32,4096]{1,0:T(8,128)(2,1)S(1)}, u32[]{:S(2)}, u32[]{:S(2)}) collective-permute-start(bf16[32,4096]{1,0:T(8,128)(2,1)S(1)} %get-tuple-element.47), channel_id=1, source_target_pairs={{0,12},{4,0},{8,4},{12,8},{1,13},{5,1},{9,5},{13,9},{2,14},{6,2},{... | collective-permute-start | bytes 786440 | tf_op jit(solution)/shard_map/ppermute | solution.py:30
  146.2 1.9 collective-permute-start.17
  148.1 3.2 %collective-permute-start.18 = (bf16[32,4096]{1,0:T(8,128)(2,1)S(1)}, bf16[32,4096]{1,0:T(8,128)(2,1)S(1)}, u32[]{:S(2)}, u32[]{:S(2)}) collective-permute-start(bf16[32,4096]{1,0:T(8,128)(2,1)S(1)} %get-tuple-element.49), channel_id=1, source_target_pairs={{0,8},{4,12},{8,0},{12,4},{1,9},{5,13},{9,1},{13,5},{2,10},{6,14},... | collective-permute-start | bytes 786440 | tf_op jit(solution)/shard_map/ppermute | solution.py:30
  151.3 0.5 collective-permute-done.16.left
  151.8 10.3 %collective-permute-done.17.right = bf16[32,4096]{1,0:T(8,128)(2,1)S(1)} collective-permute-done((bf16[32,4096]{1,0:T(8,128)(2,1)S(1)}, bf16[32,4096]{1,0:T(8,128)(2,1)S(1)}, u32[]{:S(2)}, u32[]{:S(2)}) %collective-permute-start.17) | collective-permute-done | bytes 262176 | tf_op jit(solution)/shard_map/ppermute | solution.py:30
  162.1 0.1 shard_map.122
  162.2 0.7 all-to-all-done.refs_1_
  162.9 0.3 shard_map.124
  163.2 1.9 collective-permute-start.20
  165.1 2.3 collective-permute-start.21
  167.4 5.1 %collective-permute-start.22 = (bf16[256,256]{1,0:T(8,128)(2,1)S(1)}, bf16[256,256]{1,0:T(8,128)(2,1)S(1)}, u32[]{:S(2)}, u32[]{:S(2)}) collective-permute-start(bf16[256,256]{1,0:T(8,128)(2,1)S(1)} %get-tuple-element.55), channel_id=1, source_target_pairs={{0,16},{16,0},{32,48},{48,32},{64,80},{80,64},{96,112},{112,96},{1... | collective-permute-start | bytes 393224 | tf_op jit(solution)/shard_map/ppermute | solution.py:25
  172.5 18.9 %collective-permute-start.19 = (bf16[16,4096]{1,0:T(8,128)(2,1)S(1)}, bf16[16,4096]{1,0:T(8,128)(2,1)S(1)}, u32[]{:S(2)}, u32[]{:S(2)}) collective-permute-start(bf16[16,4096]{1,0:T(8,128)(2,1)S(1)} %get-tuple-element.51.refs_0_), channel_id=1, source_target_pairs={{0,2},{2,0},{1,3},{3,1},{4,6},{6,4},{5,7},{7,5},{8,10},{10,8},{9,1... | collective-permute-start | bytes 393224 | tf_op jit(solution)/shard_map/ppermute | solution.py:25
  191.5 0.1 shard_map.125
  191.5 1.9 collective-permute-start.23
  193.5 17.5 %collective-permute-done.23.refs_1_ = bf16[128,256]{1,0:T(8,128)(2,1)S(1)} collective-permute-done((bf16[128,256]{1,0:T(8,128)(2,1)S(1)}, bf16[128,256]{1,0:T(8,128)(2,1)S(1)}, u32[]{:S(2)}, u32[]{:S(2)}) %collective-permute-start.23) | collective-permute-done | bytes 65568 | tf_op jit(solution)/shard_map/ppermute | solution.py:25
  211.0 21.8 %collective-permute-start.24 = (bf16[64,256]{1,0:T(8,128)(2,1)S(1)}, bf16[64,256]{1,0:T(8,128)(2,1)S(1)}, u32[]{:S(2)}, u32[]{:S(2)}) collective-permute-start(bf16[64,256]{1,0:T(8,128)(2,1)S(1)} %get-tuple-element.59), channel_id=1, source_target_pairs={{0,128},{16,144},{32,160},{48,176},{64,192},{80,208},{96,224},{112... | collective-permute-start | bytes 98312 | tf_op jit(solution)/shard_map/ppermute | solution.py:25
  232.8 0.8 shard_map.123
  233.6 0.5 collective-permute-done.24.got
  234.1 0.7 shard_map.127
  (28 shorter events, 0.1 us)
Async XLA Ops:
  1.5 17.6 %collective-permute-start = (bf16[64,256]{1,0:T(8,128)(2,1)S(1)}, bf16[64,256]{1,0:T(8,128)(2,1)S(1)}, u32[]{:S(2)}, u32[]{:S(2)}) collective-permute-start(bf16[64,256]{1,0:T(8,128)(2,1)S(1)} %pad_maximum_fusion.refs_1_), channel_id=1, source_target_pairs={{0,128},{16,144},{32,160},{48,176},{64,192},{80,208},{96,224},{112... | collective-permute-start | bytes 98312 | tf_op jit(solution)/shard_map/ppermute | solution.py:25
  17.7 0.9 copy-start.6
  19.0 11.5 %collective-permute-start.1 = (bf16[128,256]{1,0:T(8,128)(2,1)S(1)}, bf16[128,256]{1,0:T(8,128)(2,1)S(1)}, u32[]{:S(2)}, u32[]{:S(2)}) collective-permute-start(bf16[128,256]{1,0:T(8,128)(2,1)S(1)} %shard_map.111.refs_0_), channel_id=1, source_target_pairs={{0,64},{16,80},{32,96},{48,112},{64,0},{80,16},{96,32},{112,48},{1... | collective-permute-start | bytes 196616 | tf_op jit(solution)/shard_map/ppermute | solution.py:25
  30.6 34.1 %collective-permute-start.2 = (bf16[256,256]{1,0:T(8,128)(2,1)S(1)}, bf16[256,256]{1,0:T(8,128)(2,1)S(1)}, u32[]{:S(2)}, u32[]{:S(2)}) collective-permute-start(bf16[256,256]{1,0:T(8,128)(2,1)S(1)} %shard_map.112.refs_0_), channel_id=1, source_target_pairs={{0,16},{16,0},{32,48},{48,32},{64,80},{80,64},{96,112},{112,96},{1... | collective-permute-start | bytes 393224 | tf_op jit(solution)/shard_map/ppermute | solution.py:25
  34.2 30.5 %collective-permute-start.3 = (bf16[256,256]{1,0:T(8,128)(2,1)S(1)}, bf16[256,256]{1,0:T(8,128)(2,1)S(1)}, u32[]{:S(2)}, u32[]{:S(2)}) collective-permute-start(bf16[256,256]{1,0:T(8,128)(2,1)S(1)} %shard_map.112.refs_0_), channel_id=1, source_target_pairs={{0,32},{16,48},{32,0},{48,16},{64,96},{80,112},{96,64},{112,80},{1... | collective-permute-start | bytes 393224 | tf_op jit(solution)/shard_map/ppermute | solution.py:25
  41.7 23.0 %collective-permute-start.4 = (bf16[256,256]{1,0:T(8,128)(2,1)S(1)}, bf16[256,256]{1,0:T(8,128)(2,1)S(1)}, u32[]{:S(2)}, u32[]{:S(2)}) collective-permute-start(bf16[256,256]{1,0:T(8,128)(2,1)S(1)} %shard_map.112.refs_0_), channel_id=1, source_target_pairs={{0,48},{16,32},{32,16},{48,0},{64,112},{80,96},{96,80},{112,64},{1... | collective-permute-start | bytes 393224 | tf_op jit(solution)/shard_map/ppermute | solution.py:25
  43.6 32.3 %collective-permute-start.8 = (bf16[16,4096]{1,0:T(8,128)(2,1)S(1)}, bf16[16,4096]{1,0:T(8,128)(2,1)S(1)}, u32[]{:S(2)}, u32[]{:S(2)}) collective-permute-start(bf16[16,4096]{1,0:T(8,128)(2,1)S(1)} %get-tuple-element.34.refs_0_.refs_2_), channel_id=1, source_target_pairs={{0,2},{2,0},{1,3},{3,1},{4,6},{6,4},{5,7},{7,5},{8,10},{10,8},{9,1... | collective-permute-start | bytes 393224 | tf_op jit(solution)/shard_map/ppermute | solution.py:25
  64.8 11.2 %copy-start.2 = (bf16[1024,256]{1,0:T(8,128)(2,1)}, bf16[1024,256]{1,0:T(8,128)(2,1)S(1)}, u32[]{:S(2)}) copy-start(bf16[1024,256]{1,0:T(8,128)(2,1)S(1)} %shard_map.113.refs_0_.w_own) | copy-start | bytes 1572868
  64.8 33.7 %collective-permute-start.5 = (bf16[1024,256]{1,0:T(8,128)(2,1)S(1)}, bf16[1024,256]{1,0:T(8,128)(2,1)S(1)}, u32[]{:S(2)}, u32[]{:S(2)}) collective-permute-start(bf16[1024,256]{1,0:T(8,128)(2,1)S(1)} %shard_map.113.refs_0_.w_own), channel_id=1, source_target_pairs={{0,512},{256,768},{512,0},{768,256},{1,513},{257,769},{513,1},{769... | collective-permute-start | bytes 1572872 | tf_op jit(solution)/shard_map/ppermute | solution.py:30
  69.4 18.8 %collective-permute-start.6 = (bf16[1024,256]{1,0:T(8,128)(2,1)S(1)}, bf16[1024,256]{1,0:T(8,128)(2,1)S(1)}, u32[]{:S(2)}, u32[]{:S(2)}) collective-permute-start(bf16[1024,256]{1,0:T(8,128)(2,1)S(1)} %shard_map.113.refs_0_.w_own), channel_id=1, source_target_pairs={{0,256},{256,512},{512,768},{768,0},{1,257},{257,513},{513,769},{7... | collective-permute-start | bytes 1572872 | tf_op jit(solution)/shard_map/ppermute | solution.py:30
  71.7 16.7 %collective-permute-start.7 = (bf16[1024,256]{1,0:T(8,128)(2,1)S(1)}, bf16[1024,256]{1,0:T(8,128)(2,1)S(1)}, u32[]{:S(2)}, u32[]{:S(2)}) collective-permute-start(bf16[1024,256]{1,0:T(8,128)(2,1)S(1)} %shard_map.113.refs_0_.w_own), channel_id=1, source_target_pairs={{0,768},{256,0},{512,256},{768,512},{1,769},{257,1},{513,257},{769... | collective-permute-start | bytes 1572872 | tf_op jit(solution)/shard_map/ppermute | solution.py:30
  76.0 39.0 %copy-start.4 = (f32[256,128]{1,0:T(8,128)S(1)}, f32[256,128]{1,0:T(8,128)}, u32[]{:S(2)}) copy-start(f32[256,128]{1,0:T(8,128)} %constant.24.clone.cos) | copy-start | bytes 393220
  76.0 39.0 %copy-start.5 = (f32[256,128]{1,0:T(8,128)S(1)}, f32[256,128]{1,0:T(8,128)}, u32[]{:S(2)}) copy-start(f32[256,128]{1,0:T(8,128)} %constant.25.clone.sin) | copy-start | bytes 393220
  88.4 17.8 %copy-start = (bf16[1024,256]{1,0:T(8,128)(2,1)}, bf16[1024,256]{1,0:T(8,128)(2,1)S(1)}, u32[]{:S(2)}) copy-start(bf16[1024,256]{1,0:T(8,128)(2,1)S(1)} %collective-permute-done.7.refs_1_.w_right) | copy-start | bytes 1572868
  88.4 10.1 %collective-permute-start.9 = (bf16[32,4096]{1,0:T(8,128)(2,1)S(1)}, bf16[32,4096]{1,0:T(8,128)(2,1)S(1)}, u32[]{:S(2)}, u32[]{:S(2)}) collective-permute-start(bf16[32,4096]{1,0:T(8,128)(2,1)S(1)} %shard_map.115.refs_1_), channel_id=1, source_target_pairs={{0,4},{4,8},{8,12},{12,0},{1,5},{5,9},{9,13},{13,1},{2,6},{6,10},{... | collective-permute-start | bytes 786440 | tf_op jit(solution)/shard_map/ppermute | solution.py:30
  91.6 7.1 %collective-permute-start.10 = (bf16[32,4096]{1,0:T(8,128)(2,1)S(1)}, bf16[32,4096]{1,0:T(8,128)(2,1)S(1)}, u32[]{:S(2)}, u32[]{:S(2)}) collective-permute-start(bf16[32,4096]{1,0:T(8,128)(2,1)S(1)} %shard_map.115.refs_1_), channel_id=1, source_target_pairs={{0,12},{4,0},{8,4},{12,8},{1,13},{5,1},{9,5},{13,9},{2,14},{6,2},{... | collective-permute-start | bytes 786440 | tf_op jit(solution)/shard_map/ppermute | solution.py:30
  95.0 11.1 %collective-permute-start.11 = (bf16[32,4096]{1,0:T(8,128)(2,1)S(1)}, bf16[32,4096]{1,0:T(8,128)(2,1)S(1)}, u32[]{:S(2)}, u32[]{:S(2)}) collective-permute-start(bf16[32,4096]{1,0:T(8,128)(2,1)S(1)} %shard_map.115.refs_1_), channel_id=1, source_target_pairs={{0,8},{4,12},{8,0},{12,4},{1,9},{5,13},{9,1},{13,5},{2,10},{6,14},... | collective-permute-start | bytes 786440 | tf_op jit(solution)/shard_map/ppermute | solution.py:30
  106.1 8.9 %collective-permute-start.12 = (bf16[128,4096]{1,0:T(8,128)(2,1)S(1)}, bf16[128,4096]{1,0:T(8,128)(2,1)S(1)}, u32[]{:S(2)}, u32[]{:S(2)}) collective-permute-start(bf16[128,4096]{1,0:T(8,128)(2,1)S(1)} %shard_map.116.t0), channel_id=1, source_target_pairs={{0,1},{1,0},{2,3},{3,2},{4,5},{5,4},{6,7},{7,6},{8,9},{9,8},{10,11... | collective-permute-start | bytes 3145736 | tf_op jit(solution)/shard_map/ppermute | solution.py:25
  115.0 1.0 copy-start.1
  116.0 1.0 copy-start.3
  117.1 4.7 %copy-start.8 = (bf16[256,128]{1,0:T(8,128)(2,1)S(1)}, bf16[256,128]{1,0:T(8,128)(2,1)}, u32[]{:S(2)}) copy-start(bf16[256,128]{1,0:T(8,128)(2,1)} %d_ctx_ref.1) | copy-start | bytes 196612
  118.6 3.2 %collective-permute-start.13 = (bf16[256,128]{1,0:T(8,128)(2,1)S(1)}, bf16[256,128]{1,0:T(8,128)(2,1)S(1)}, u32[]{:S(2)}, u32[]{:S(2)}) collective-permute-start(bf16[256,128]{1,0:T(8,128)(2,1)S(1)} %get-tuple-element.36.mine_ref), channel_id=1, source_target_pairs={{0,1},{1,0},{2,3},{3,2},{4,5},{5,4},{6,7},{7,6},{8,9},{9,8},{10,11... | collective-permute-start | bytes 196616 | tf_op jit(solution)/shard_map/ppermute | solution.py:25
  123.7 3.1 %collective-permute-start.14 = (bf16[256,128]{1,0:T(8,128)(2,1)S(1)}, bf16[256,128]{1,0:T(8,128)(2,1)S(1)}, u32[]{:S(2)}, u32[]{:S(2)}) collective-permute-start(bf16[256,128]{1,0:T(8,128)(2,1)S(1)} %get-tuple-element.41), channel_id=1, source_target_pairs={{0,1},{1,0},{2,3},{3,2},{4,5},{5,4},{6,7},{7,6},{8,9},{9,8},{10,11... | collective-permute-start | bytes 196616 | tf_op jit(solution)/shard_map/ppermute | solution.py:25
  128.3 1.0 copy-start.9
  132.7 30.3 %all-to-all-start = ((bf16[4,1024,256]{2,1,0:T(8,128)(2,1)}), bf16[4,1024,256]{2,1,0:T(8,128)(2,1)S(1)}, u32[]{:S(2)}, u32[]{:S(2)}) async-start(bf16[4,1024,256]{2,1,0:T(8,128)(2,1)} %shard_map.120.after), calls=%async_computation | async-start | bytes 4194304 | tf_op jit(solution)/shard_map/all_to_all | solution.py:346
  137.1 5.0 %collective-permute-start.15 = (bf16[128,4096]{1,0:T(8,128)(2,1)}, bf16[128,4096]{1,0:T(8,128)(2,1)S(1)}, u32[]{:S(2)}, u32[]{:S(2)}) collective-permute-start(bf16[128,4096]{1,0:T(8,128)(2,1)} %copy-done.9), channel_id=1, source_target_pairs={{0,1},{1,0},{2,3},{3,2},{4,5},{5,4},{6,7},{7,6},{8,9},{9,8},{10,11... | collective-permute-start | bytes 3145736 | tf_op jit(solution)/shard_map/ppermute | solution.py:25
  142.4 9.4 %collective-permute-start.16 = (bf16[32,4096]{1,0:T(8,128)(2,1)S(1)}, bf16[32,4096]{1,0:T(8,128)(2,1)S(1)}, u32[]{:S(2)}, u32[]{:S(2)}) collective-permute-start(bf16[32,4096]{1,0:T(8,128)(2,1)S(1)} %get-tuple-element.47), channel_id=1, source_target_pairs={{0,12},{4,0},{8,4},{12,8},{1,13},{5,1},{9,5},{13,9},{2,14},{6,2},{... | collective-permute-start | bytes 786440 | tf_op jit(solution)/shard_map/ppermute | solution.py:30
  146.2 15.9 %collective-permute-start.17 = (bf16[32,4096]{1,0:T(8,128)(2,1)S(1)}, bf16[32,4096]{1,0:T(8,128)(2,1)S(1)}, u32[]{:S(2)}, u32[]{:S(2)}) collective-permute-start(bf16[32,4096]{1,0:T(8,128)(2,1)S(1)} %get-tuple-element.48), channel_id=1, source_target_pairs={{0,4},{4,8},{8,12},{12,0},{1,5},{5,9},{9,13},{13,1},{2,6},{6,10},{... | collective-permute-start | bytes 786440 | tf_op jit(solution)/shard_map/ppermute | solution.py:30
  148.1 14.0 %collective-permute-start.18 = (bf16[32,4096]{1,0:T(8,128)(2,1)S(1)}, bf16[32,4096]{1,0:T(8,128)(2,1)S(1)}, u32[]{:S(2)}, u32[]{:S(2)}) collective-permute-start(bf16[32,4096]{1,0:T(8,128)(2,1)S(1)} %get-tuple-element.49), channel_id=1, source_target_pairs={{0,8},{4,12},{8,0},{12,4},{1,9},{5,13},{9,1},{13,5},{2,10},{6,14},... | collective-permute-start | bytes 786440 | tf_op jit(solution)/shard_map/ppermute | solution.py:30
  162.1 70.7 %copy-start.7 = (bf16[16,4096]{1,0:T(8,128)(2,1)S(1)}, bf16[16,4096]{1,0:T(8,128)(2,1)}, u32[]{:S(2)}) copy-start(bf16[16,4096]{1,0:T(8,128)(2,1)} %tokens.3) | copy-start | bytes 393220
  163.2 28.2 %collective-permute-start.20 = (bf16[256,256]{1,0:T(8,128)(2,1)S(1)}, bf16[256,256]{1,0:T(8,128)(2,1)S(1)}, u32[]{:S(2)}, u32[]{:S(2)}) collective-permute-start(bf16[256,256]{1,0:T(8,128)(2,1)S(1)} %get-tuple-element.53), channel_id=1, source_target_pairs={{0,48},{16,32},{32,16},{48,0},{64,112},{80,96},{96,80},{112,64},{1... | collective-permute-start | bytes 393224 | tf_op jit(solution)/shard_map/ppermute | solution.py:25
  165.1 26.3 %collective-permute-start.21 = (bf16[256,256]{1,0:T(8,128)(2,1)S(1)}, bf16[256,256]{1,0:T(8,128)(2,1)S(1)}, u32[]{:S(2)}, u32[]{:S(2)}) collective-permute-start(bf16[256,256]{1,0:T(8,128)(2,1)S(1)} %get-tuple-element.54), channel_id=1, source_target_pairs={{0,32},{16,48},{32,0},{48,16},{64,96},{80,112},{96,64},{112,80},{1... | collective-permute-start | bytes 393224 | tf_op jit(solution)/shard_map/ppermute | solution.py:25
  167.4 24.0 %collective-permute-start.22 = (bf16[256,256]{1,0:T(8,128)(2,1)S(1)}, bf16[256,256]{1,0:T(8,128)(2,1)S(1)}, u32[]{:S(2)}, u32[]{:S(2)}) collective-permute-start(bf16[256,256]{1,0:T(8,128)(2,1)S(1)} %get-tuple-element.55), channel_id=1, source_target_pairs={{0,16},{16,0},{32,48},{48,32},{64,80},{80,64},{96,112},{112,96},{1... | collective-permute-start | bytes 393224 | tf_op jit(solution)/shard_map/ppermute | solution.py:25
  172.5 60.3 %collective-permute-start.19 = (bf16[16,4096]{1,0:T(8,128)(2,1)S(1)}, bf16[16,4096]{1,0:T(8,128)(2,1)S(1)}, u32[]{:S(2)}, u32[]{:S(2)}) collective-permute-start(bf16[16,4096]{1,0:T(8,128)(2,1)S(1)} %get-tuple-element.51.refs_0_), channel_id=1, source_target_pairs={{0,2},{2,0},{1,3},{3,1},{4,6},{6,4},{5,7},{7,5},{8,10},{10,8},{9,1... | collective-permute-start | bytes 393224 | tf_op jit(solution)/shard_map/ppermute | solution.py:25
  191.5 19.5 %collective-permute-start.23 = (bf16[128,256]{1,0:T(8,128)(2,1)S(1)}, bf16[128,256]{1,0:T(8,128)(2,1)S(1)}, u32[]{:S(2)}, u32[]{:S(2)}) collective-permute-start(bf16[128,256]{1,0:T(8,128)(2,1)S(1)} %get-tuple-element.57), channel_id=1, source_target_pairs={{0,64},{16,80},{32,96},{48,112},{64,0},{80,16},{96,32},{112,48},{1... | collective-permute-start | bytes 196616 | tf_op jit(solution)/shard_map/ppermute | solution.py:25
  211.0 23.1 %collective-permute-start.24 = (bf16[64,256]{1,0:T(8,128)(2,1)S(1)}, bf16[64,256]{1,0:T(8,128)(2,1)S(1)}, u32[]{:S(2)}, u32[]{:S(2)}) collective-permute-start(bf16[64,256]{1,0:T(8,128)(2,1)S(1)} %get-tuple-element.59), channel_id=1, source_target_pairs={{0,128},{16,144},{32,160},{48,176},{64,192},{80,208},{96,224},{112... | collective-permute-start | bytes 98312 | tf_op jit(solution)/shard_map/ppermute | solution.py:25

commit v5 on v4

--- a/solution.py
+++ b/solution.py
@@ -34,8 +34,7 @@
 
 
 def z_offset(place):
-    far = place % RADIX
-    return (far & 1) * 2 * RADIX + (far >> 1) * RADIX + place // RADIX
+    return place % RADIX * RADIX + place // RADIX
 
 
 def spread(block, axis, step):
@@ -86,10 +85,10 @@
     normed_out[...] = (inputs * inv).astype(jnp.bfloat16)
 
 
-def rows_kernel(first, *refs):
+def rows_kernel(first, order, *refs):
     *parts, out = refs[first:]
     count = parts[0].shape[0]
-    for place, ref in enumerate(parts):
+    for place, ref in enumerate(parts[::order]):
         out[place * count : (place + 1) * count, :] = ref[...]
 
 
@@ -117,8 +116,8 @@
         out[...] = added(*(part[cut, :] for part in parts)).astype(out.dtype)
 
 
-def weights_out_kernel(own, got, q_out, k_out, v_out):
-    total = added(own[...], got[...])
+def weights_out_kernel(own, a, b, c, q_out, k_out, v_out):
+    total = added(own[...], a[...], b[...], c[...])
     head, half = q_out.shape[1], k_out.shape[1]
     q_out[...] = total[:, :head]
     k_out[...] = total[:, head : head + half]
@@ -255,10 +254,10 @@
     )(*after, *args)
 
 
-def rows(*parts, after=(), flops=0):
+def rows(*parts, after=(), last_first=False, flops=0):
     shape = (len(parts) * parts[0].shape[0], parts[0].shape[1])
     (out,) = call(
-        functools.partial(rows_kernel, len(after)), [(shape, parts[0].dtype)], *parts, after=after,
+        functools.partial(rows_kernel, len(after), -1 if last_first else 1), [(shape, parts[0].dtype)], *parts, after=after,
         flops=flops, moved=4 * shape[0] * shape[1],
     )
     return out
@@ -286,8 +285,7 @@
         norm_kernel, [((count, 128), f32), ((count, width), b16)], tokens,
         flops=4 * count * width, moved=4 * count * width,
     )
-    near = rows(weights, flipped(weights, "zl", 2 * RADIX), after=(normed,))
-    near = rows(near, flipped(near, "zl", RADIX))
+    near = rows(*spread(weights, "zl", RADIX)[::-1], weights, after=(normed,), last_first=True)
     whole = rows(near, *spread(near, "zl", 1))
     w_pieces = (whole, *ring_gather(whole, "x"))
     far = rows(flipped(normed, "zh", 1), after=(whole,), flops=40 * product)
@@ -344,14 +342,13 @@
     )
 
     kept, *sent = scatter_sum(RADIX, lax.all_to_all(g_blocks, "x", 0, 0), after=(sent_t,))
-    kept, sent = scatter_sum(2, kept, *collect(sent, "zl", 1))
-    kept, sent = scatter_sum(2, kept, flipped(sent, "zl", RADIX))
+    kept, *sent = scatter_sum(RADIX, kept, *collect(sent, "zl", 1))
     cut = kept.shape[0]
     grads = call(
         weights_out_kernel,
         [((cut, head), f32), ((cut, head // 2), f32), ((cut, head // 2), f32)],
-        kept, flipped(sent, "zl", 2 * RADIX),
-        moved=12 * cut * head,
+        kept, *collect(sent, "zl", RADIX),
+        moved=24 * cut * head,
     )
     return (context, grad_tokens, *grads)
 

time: 237 us -> 231 us (0.975)
  starting transfers between devices: 160 us -> 150 us
  waiting for transfers between devices: 57.9 us -> 62.4 us
    ppermute x16 -> x18, starting transfers between devices: 126 us -> 115 us  [flipped(): return lax.ppermute(value, axis, [(s, s ^ mask) for s in range(size)])]
    ppermute x9, waiting for transfers between devices: 30.7 us -> 34.7 us  [shifted(): lax.ppermute(value, axis, [(s, (s + step) % size) for s in range(size)])]
    ppermute x16 -> x18, waiting for transfers between devices: 26.5 us -> 27.8 us  [flipped(): return lax.ppermute(value, axis, [(s, s ^ mask) for s in range(size)])]
    pallas_call x18 -> x16, Pallas kernels: 10.7 us -> 10.7 us  [call(): pl.pallas_call(kernel, out_shape=[jax.ShapeDtypeStruct(s, t) for s, t in...]
  transfers between devices with their start and end apart: 26 -> 28, of which waited for: 15 -> 12; matrix products, arithmetic and copies ran while one was open for 0% -> 0% of each run, Pallas kernels for 1% -> 1%
where the time goes in v5:
time: 231 us; the launch traced here: 230 us
  starting transfers between devices  150 us (65%)
  waiting for transfers between devices  62.4 us (27%)
  Pallas kernels  10.7 us (5%)
  local copies, waits for them, and re-layouts  4.06 us (2%)
    ppermute x18, starting transfers between devices, flipped(): return lax.ppermute(value, axis, [(s, s ^ mask) for s in range(size)])  115 us
    ppermute x9, waiting for transfers between devices, shifted(): lax.ppermute(value, axis, [(s, (s + step) % size) for s in range(size)])  34.7 us
    ppermute x9, starting transfers between devices, shifted(): lax.ppermute(value, axis, [(s, (s + step) % size) for s in range(size)])  31.6 us
    ppermute x18, waiting for transfers between devices, flipped(): return lax.ppermute(value, axis, [(s, s ^ mask) for s in range(size)])  27.8 us
    pallas_call x16, Pallas kernels, call(): pl.pallas_call(kernel, out_shape=[jax.ShapeDtypeStruct(s, t) for s, t in...  10.7 us
  transfers between devices with their start and end apart: 28, of which 12 were waited for; matrix products, arithmetic and copies ran while one was open for 0% of the time, Pallas kernels for 1%

profile of v5, /device:TPU:1, one launch (start us, length us, event | category | flops | bytes accessed | tf_op | source)
XLA Modules:
  0.0 229.5 jit_solution(16104443056580296608)
XLA Ops:
  0.6 0.8 pad_maximum_fusion.refs_4_
  1.5 22.9 %collective-permute-start = (bf16[64,256]{1,0:T(8,128)(2,1)S(1)}, bf16[64,256]{1,0:T(8,128)(2,1)S(1)}, u32[]{:S(2)}, u32[]{:S(2)}) collective-permute-start(bf16[64,256]{1,0:T(8,128)(2,1)S(1)} %pad_maximum_fusion.refs_4_), channel_id=1, source_target_pairs={{0,192},{16,208},{32,224},{48,240},{64,128},{80,144},{96,160},{112... | collective-permute-start | bytes 98312 | tf_op jit(solution)/shard_map/ppermute | solution.py:25
  24.4 1.9 collective-permute-start.1
  26.3 2.2 collective-permute-start.2
  28.5 0.0 copy-start.6
  28.5 0.9 copy-done.6
  29.4 0.1 shard_map.110
  29.5 0.0 collective-permute-done.refs_1_
  29.5 8.3 %collective-permute-done.1.refs_2_ = bf16[64,256]{1,0:T(8,128)(2,1)S(1)} collective-permute-done((bf16[64,256]{1,0:T(8,128)(2,1)S(1)}, bf16[64,256]{1,0:T(8,128)(2,1)S(1)}, u32[]{:S(2)}, u32[]{:S(2)}) %collective-permute-start.1) | collective-permute-done | bytes 32800 | tf_op jit(solution)/shard_map/ppermute | solution.py:25
  37.9 3.7 %collective-permute-start.3 = (bf16[256,256]{1,0:T(8,128)(2,1)S(1)}, bf16[256,256]{1,0:T(8,128)(2,1)S(1)}, u32[]{:S(2)}, u32[]{:S(2)}) collective-permute-start(bf16[256,256]{1,0:T(8,128)(2,1)S(1)} %shard_map.111.refs_0_), channel_id=1, source_target_pairs={{0,16},{16,0},{32,48},{48,32},{64,80},{80,64},{96,112},{112,96},{1... | collective-permute-start | bytes 393224 | tf_op jit(solution)/shard_map/ppermute | solution.py:25
  41.6 4.7 %collective-permute-start.4 = (bf16[256,256]{1,0:T(8,128)(2,1)S(1)}, bf16[256,256]{1,0:T(8,128)(2,1)S(1)}, u32[]{:S(2)}, u32[]{:S(2)}) collective-permute-start(bf16[256,256]{1,0:T(8,128)(2,1)S(1)} %shard_map.111.refs_0_), channel_id=1, source_target_pairs={{0,32},{16,48},{32,0},{48,16},{64,96},{80,112},{96,64},{112,80},{1... | collective-permute-start | bytes 393224 | tf_op jit(solution)/shard_map/ppermute | solution.py:25
  46.3 1.9 collective-permute-start.5
  48.2 18.8 %collective-permute-start.9 = (bf16[16,4096]{1,0:T(8,128)(2,1)S(1)}, bf16[16,4096]{1,0:T(8,128)(2,1)S(1)}, u32[]{:S(2)}, u32[]{:S(2)}) collective-permute-start(bf16[16,4096]{1,0:T(8,128)(2,1)S(1)} %get-tuple-element.34.refs_0_.refs_2_), channel_id=1, source_target_pairs={{0,2},{2,0},{1,3},{3,1},{4,6},{6,4},{5,7},{7,5},{8,10},{10,8},{9,1... | collective-permute-start | bytes 393224 | tf_op jit(solution)/shard_map/ppermute | solution.py:25
  67.0 0.0 collective-permute-done.4.refs_2_
  67.1 0.0 collective-permute-done.5.refs_3_
  67.1 4.7 %collective-permute-start.6 = (bf16[1024,256]{1,0:T(8,128)(2,1)S(1)}, bf16[1024,256]{1,0:T(8,128)(2,1)S(1)}, u32[]{:S(2)}, u32[]{:S(2)}) collective-permute-start(bf16[1024,256]{1,0:T(8,128)(2,1)S(1)} %shard_map.112.refs_0_.w_own), channel_id=1, source_target_pairs={{0,512},{256,768},{512,0},{768,256},{1,513},{257,769},{513,1},{769... | collective-permute-start | bytes 1572872 | tf_op jit(solution)/shard_map/ppermute | solution.py:30
  71.8 2.2 collective-permute-start.7
  74.0 4.3 %collective-permute-start.8 = (bf16[1024,256]{1,0:T(8,128)(2,1)S(1)}, bf16[1024,256]{1,0:T(8,128)(2,1)S(1)}, u32[]{:S(2)}, u32[]{:S(2)}) collective-permute-start(bf16[1024,256]{1,0:T(8,128)(2,1)S(1)} %shard_map.112.refs_0_.w_own), channel_id=1, source_target_pairs={{0,768},{256,0},{512,256},{768,512},{1,769},{257,1},{513,257},{769... | collective-permute-start | bytes 1572872 | tf_op jit(solution)/shard_map/ppermute | solution.py:30
  78.3 0.0 copy-start.4
  78.3 0.0 copy-start.5
  78.4 17.2 %collective-permute-done.7.refs_0_.w_left = bf16[1024,256]{1,0:T(8,128)(2,1)S(1)} collective-permute-done((bf16[1024,256]{1,0:T(8,128)(2,1)S(1)}, bf16[1024,256]{1,0:T(8,128)(2,1)S(1)}, u32[]{:S(2)}, u32[]{:S(2)}) %collective-permute-start.7) | collective-permute-done | bytes 524320 | tf_op jit(solution)/shard_map/ppermute | solution.py:30
  95.6 3.2 %collective-permute-start.10 = (bf16[32,4096]{1,0:T(8,128)(2,1)S(1)}, bf16[32,4096]{1,0:T(8,128)(2,1)S(1)}, u32[]{:S(2)}, u32[]{:S(2)}) collective-permute-start(bf16[32,4096]{1,0:T(8,128)(2,1)S(1)} %shard_map.114.refs_1_), channel_id=1, source_target_pairs={{0,4},{4,8},{8,12},{12,0},{1,5},{5,9},{9,13},{13,1},{2,6},{6,10},{... | collective-permute-start | bytes 786440 | tf_op jit(solution)/shard_map/ppermute | solution.py:30
  98.8 3.4 %collective-permute-start.11 = (bf16[32,4096]{1,0:T(8,128)(2,1)S(1)}, bf16[32,4096]{1,0:T(8,128)(2,1)S(1)}, u32[]{:S(2)}, u32[]{:S(2)}) collective-permute-start(bf16[32,4096]{1,0:T(8,128)(2,1)S(1)} %shard_map.114.refs_1_), channel_id=1, source_target_pairs={{0,12},{4,0},{8,4},{12,8},{1,13},{5,1},{9,5},{13,9},{2,14},{6,2},{... | collective-permute-start | bytes 786440 | tf_op jit(solution)/shard_map/ppermute | solution.py:30
  102.2 3.5 %collective-permute-start.12 = (bf16[32,4096]{1,0:T(8,128)(2,1)S(1)}, bf16[32,4096]{1,0:T(8,128)(2,1)S(1)}, u32[]{:S(2)}, u32[]{:S(2)}) collective-permute-start(bf16[32,4096]{1,0:T(8,128)(2,1)S(1)} %shard_map.114.refs_1_), channel_id=1, source_target_pairs={{0,8},{4,12},{8,0},{12,4},{1,9},{5,13},{9,1},{13,5},{2,10},{6,14},... | collective-permute-start | bytes 786440 | tf_op jit(solution)/shard_map/ppermute | solution.py:30
  105.8 0.4 collective-permute-done.10.refs_2_
  106.1 1.5 collective-permute-done.11.refs_3_
  107.7 4.6 %collective-permute-done.12.refs_4_ = bf16[32,4096]{1,0:T(8,128)(2,1)S(1)} collective-permute-done((bf16[32,4096]{1,0:T(8,128)(2,1)S(1)}, bf16[32,4096]{1,0:T(8,128)(2,1)S(1)}, u32[]{:S(2)}, u32[]{:S(2)}) %collective-permute-start.12) | collective-permute-done | bytes 262176 | tf_op jit(solution)/shard_map/ppermute | solution.py:30
  112.3 0.1 shard_map.115.t0
  112.4 3.9 %collective-permute-start.13 = (bf16[128,4096]{1,0:T(8,128)(2,1)S(1)}, bf16[128,4096]{1,0:T(8,128)(2,1)S(1)}, u32[]{:S(2)}, u32[]{:S(2)}) collective-permute-start(bf16[128,4096]{1,0:T(8,128)(2,1)S(1)} %shard_map.115.t0), channel_id=1, source_target_pairs={{0,1},{1,0},{2,3},{3,2},{4,5},{5,4},{6,7},{7,6},{8,9},{9,8},{10,11... | collective-permute-start | bytes 3145736 | tf_op jit(solution)/shard_map/ppermute | solution.py:25
  116.3 0.1 stack.23.ids
  116.4 2.2 collective-permute-done.13.t1
  118.6 1.0 copy-done.1
  119.6 1.0 copy-done.3
  120.7 1.5 shard_map.116
  122.2 2.3 collective-permute-start.14
  124.5 0.9 collective-permute-done.14.other_ref
  125.4 1.9 shard_map.117
  127.3 2.2 collective-permute-start.15
  129.5 0.9 collective-permute-done.15.got_ref
  130.4 1.5 shard_map.118
  131.9 1.0 copy-done.9
  132.9 3.4 %shard_map.119.after = bf16[4,1024,256]{2,1,0:T(8,128)(2,1)} custom-call(s32[5]{0:T(128)S(1)} %stack.23.ids, bf16[128,4096]{1,0:T(8,128)(2,1)S(1)} %shard_map.115.t0, bf16[128,4096]{1,0:T(8,128)(2,1)S(1)} %collective-permute-done.13.t1, bf16[256,256]{1,0:T(8,128)(2,1)S(1)} %get-tuple-element.43.dj_ref), custom_call_target="tpu_custom_call" | custom-call | flops 536870912 | bytes 4194304 | tf_op jit(solution)/shard_map/pallas_call | solution.py:246
  136.2 4.0 %all-to-all-start = ((bf16[4,1024,256]{2,1,0:T(8,128)(2,1)}), bf16[4,1024,256]{2,1,0:T(8,128)(2,1)S(1)}, u32[]{:S(2)}, u32[]{:S(2)}) async-start(bf16[4,1024,256]{2,1,0:T(8,128)(2,1)} %shard_map.119.after), calls=%async_computation | async-start | bytes 4194304 | tf_op jit(solution)/shard_map/all_to_all | solution.py:344
  140.3 2.5 %collective-permute-start.16 = (bf16[128,4096]{1,0:T(8,128)(2,1)}, bf16[128,4096]{1,0:T(8,128)(2,1)S(1)}, u32[]{:S(2)}, u32[]{:S(2)}) collective-permute-start(bf16[128,4096]{1,0:T(8,128)(2,1)} %copy-done.9), channel_id=1, source_target_pairs={{0,1},{1,0},{2,3},{3,2},{4,5},{5,4},{6,7},{7,6},{8,9},{9,8},{10,11... | collective-permute-start | bytes 3145736 | tf_op jit(solution)/shard_map/ppermute | solution.py:25
  142.8 2.5 %collective-permute-done.16.got = bf16[128,4096]{1,0:T(8,128)(2,1)S(1)} collective-permute-done((bf16[128,4096]{1,0:T(8,128)(2,1)}, bf16[128,4096]{1,0:T(8,128)(2,1)S(1)}, u32[]{:S(2)}, u32[]{:S(2)}) %collective-permute-start.16) | collective-permute-done | bytes 1048608 | tf_op jit(solution)/shard_map/ppermute | solution.py:25
  145.3 0.2 shard_map.120
  145.5 5.3 %collective-permute-start.17 = (bf16[32,4096]{1,0:T(8,128)(2,1)S(1)}, bf16[32,4096]{1,0:T(8,128)(2,1)S(1)}, u32[]{:S(2)}, u32[]{:S(2)}) collective-permute-start(bf16[32,4096]{1,0:T(8,128)(2,1)S(1)} %get-tuple-element.47), channel_id=1, source_target_pairs={{0,12},{4,0},{8,4},{12,8},{1,13},{5,1},{9,5},{13,9},{2,14},{6,2},{... | collective-permute-start | bytes 786440 | tf_op jit(solution)/shard_map/ppermute | solution.py:30
  150.8 1.9 collective-permute-start.18
  152.8 3.1 %collective-permute-start.19 = (bf16[32,4096]{1,0:T(8,128)(2,1)S(1)}, bf16[32,4096]{1,0:T(8,128)(2,1)S(1)}, u32[]{:S(2)}, u32[]{:S(2)}) collective-permute-start(bf16[32,4096]{1,0:T(8,128)(2,1)S(1)} %get-tuple-element.49), channel_id=1, source_target_pairs={{0,8},{4,12},{8,0},{12,4},{1,9},{5,13},{9,1},{13,5},{2,10},{6,14},... | collective-permute-start | bytes 786440 | tf_op jit(solution)/shard_map/ppermute | solution.py:30
  155.9 0.7 collective-permute-done.17.left
  156.5 10.2 %collective-permute-done.18.right = bf16[32,4096]{1,0:T(8,128)(2,1)S(1)} collective-permute-done((bf16[32,4096]{1,0:T(8,128)(2,1)S(1)}, bf16[32,4096]{1,0:T(8,128)(2,1)S(1)}, u32[]{:S(2)}, u32[]{:S(2)}) %collective-permute-start.18) | collective-permute-done | bytes 262176 | tf_op jit(solution)/shard_map/ppermute | solution.py:30
  166.7 0.1 shard_map.121
  166.9 0.3 shard_map.123
  167.1 3.1 %collective-permute-start.21 = (bf16[256,256]{1,0:T(8,128)(2,1)S(1)}, bf16[256,256]{1,0:T(8,128)(2,1)S(1)}, u32[]{:S(2)}, u32[]{:S(2)}) collective-permute-start(bf16[256,256]{1,0:T(8,128)(2,1)S(1)} %get-tuple-element.53), channel_id=1, source_target_pairs={{0,48},{16,32},{32,16},{48,0},{64,112},{80,96},{96,80},{112,64},{1... | collective-permute-start | bytes 393224 | tf_op jit(solution)/shard_map/ppermute | solution.py:25
  170.2 1.9 collective-permute-start.22
  172.1 4.3 %collective-permute-start.23 = (bf16[256,256]{1,0:T(8,128)(2,1)S(1)}, bf16[256,256]{1,0:T(8,128)(2,1)S(1)}, u32[]{:S(2)}, u32[]{:S(2)}) collective-permute-start(bf16[256,256]{1,0:T(8,128)(2,1)S(1)} %get-tuple-element.55), channel_id=1, source_target_pairs={{0,16},{16,0},{32,48},{48,32},{64,80},{80,64},{96,112},{112,96},{1... | collective-permute-start | bytes 393224 | tf_op jit(solution)/shard_map/ppermute | solution.py:25
  176.4 17.5 %collective-permute-start.20 = (bf16[16,4096]{1,0:T(8,128)(2,1)S(1)}, bf16[16,4096]{1,0:T(8,128)(2,1)S(1)}, u32[]{:S(2)}, u32[]{:S(2)}) collective-permute-start(bf16[16,4096]{1,0:T(8,128)(2,1)S(1)} %get-tuple-element.51.refs_0_), channel_id=1, source_target_pairs={{0,2},{2,0},{1,3},{3,1},{4,6},{6,4},{5,7},{7,5},{8,10},{10,8},{9,1... | collective-permute-start | bytes 393224 | tf_op jit(solution)/shard_map/ppermute | solution.py:25
  193.9 0.1 shard_map.124
  194.0 1.9 collective-permute-start.24
  195.9 5.7 %collective-permute-start.25 = (bf16[64,256]{1,0:T(8,128)(2,1)S(1)}, bf16[64,256]{1,0:T(8,128)(2,1)S(1)}, u32[]{:S(2)}, u32[]{:S(2)}) collective-permute-start(bf16[64,256]{1,0:T(8,128)(2,1)S(1)} %get-tuple-element.58), channel_id=1, source_target_pairs={{0,128},{16,144},{32,160},{48,176},{64,192},{80,208},{96,224},{112... | collective-permute-start | bytes 98312 | tf_op jit(solution)/shard_map/ppermute | solution.py:25
  201.7 13.3 %collective-permute-start.26 = (bf16[64,256]{1,0:T(8,128)(2,1)S(1)}, bf16[64,256]{1,0:T(8,128)(2,1)S(1)}, u32[]{:S(2)}, u32[]{:S(2)}) collective-permute-start(bf16[64,256]{1,0:T(8,128)(2,1)S(1)} %get-tuple-element.59), channel_id=1, source_target_pairs={{0,64},{16,80},{32,96},{48,112},{64,0},{80,16},{96,32},{112,48},{1... | collective-permute-start | bytes 98312 | tf_op jit(solution)/shard_map/ppermute | solution.py:25
  215.0 0.8 shard_map.122
  215.9 13.0 %collective-permute-done.24.a = bf16[64,256]{1,0:T(8,128)(2,1)S(1)} collective-permute-done((bf16[64,256]{1,0:T(8,128)(2,1)S(1)}, bf16[64,256]{1,0:T(8,128)(2,1)S(1)}, u32[]{:S(2)}, u32[]{:S(2)}) %collective-permute-start.24) | collective-permute-done | bytes 32800 | tf_op jit(solution)/shard_map/ppermute | solution.py:25
  228.8 0.7 shard_map.125
  (30 shorter events, 0.1 us)
Async XLA Ops:
  1.5 28.1 %collective-permute-start = (bf16[64,256]{1,0:T(8,128)(2,1)S(1)}, bf16[64,256]{1,0:T(8,128)(2,1)S(1)}, u32[]{:S(2)}, u32[]{:S(2)}) collective-permute-start(bf16[64,256]{1,0:T(8,128)(2,1)S(1)} %pad_maximum_fusion.refs_4_), channel_id=1, source_target_pairs={{0,192},{16,208},{32,224},{48,240},{64,128},{80,144},{96,160},{112... | collective-permute-start | bytes 98312 | tf_op jit(solution)/shard_map/ppermute | solution.py:25
  24.4 13.5 %collective-permute-start.1 = (bf16[64,256]{1,0:T(8,128)(2,1)S(1)}, bf16[64,256]{1,0:T(8,128)(2,1)S(1)}, u32[]{:S(2)}, u32[]{:S(2)}) collective-permute-start(bf16[64,256]{1,0:T(8,128)(2,1)S(1)} %pad_maximum_fusion.refs_4_), channel_id=1, source_target_pairs={{0,128},{16,144},{32,160},{48,176},{64,192},{80,208},{96,224},{112... | collective-permute-start | bytes 98312 | tf_op jit(solution)/shard_map/ppermute | solution.py:25
  26.3 11.6 %collective-permute-start.2 = (bf16[64,256]{1,0:T(8,128)(2,1)S(1)}, bf16[64,256]{1,0:T(8,128)(2,1)S(1)}, u32[]{:S(2)}, u32[]{:S(2)}) collective-permute-start(bf16[64,256]{1,0:T(8,128)(2,1)S(1)} %pad_maximum_fusion.refs_4_), channel_id=1, source_target_pairs={{0,64},{16,80},{32,96},{48,112},{64,0},{80,16},{96,32},{112,48},{1... | collective-permute-start | bytes 98312 | tf_op jit(solution)/shard_map/ppermute | solution.py:25
  28.5 0.9 copy-start.6
  37.9 29.1 %collective-permute-start.3 = (bf16[256,256]{1,0:T(8,128)(2,1)S(1)}, bf16[256,256]{1,0:T(8,128)(2,1)S(1)}, u32[]{:S(2)}, u32[]{:S(2)}) collective-permute-start(bf16[256,256]{1,0:T(8,128)(2,1)S(1)} %shard_map.111.refs_0_), channel_id=1, source_target_pairs={{0,16},{16,0},{32,48},{48,32},{64,80},{80,64},{96,112},{112,96},{1... | collective-permute-start | bytes 393224 | tf_op jit(solution)/shard_map/ppermute | solution.py:25
  41.6 25.5 %collective-permute-start.4 = (bf16[256,256]{1,0:T(8,128)(2,1)S(1)}, bf16[256,256]{1,0:T(8,128)(2,1)S(1)}, u32[]{:S(2)}, u32[]{:S(2)}) collective-permute-start(bf16[256,256]{1,0:T(8,128)(2,1)S(1)} %shard_map.111.refs_0_), channel_id=1, source_target_pairs={{0,32},{16,48},{32,0},{48,16},{64,96},{80,112},{96,64},{112,80},{1... | collective-permute-start | bytes 393224 | tf_op jit(solution)/shard_map/ppermute | solution.py:25
  46.3 20.8 %collective-permute-start.5 = (bf16[256,256]{1,0:T(8,128)(2,1)S(1)}, bf16[256,256]{1,0:T(8,128)(2,1)S(1)}, u32[]{:S(2)}, u32[]{:S(2)}) collective-permute-start(bf16[256,256]{1,0:T(8,128)(2,1)S(1)} %shard_map.111.refs_0_), channel_id=1, source_target_pairs={{0,48},{16,32},{32,16},{48,0},{64,112},{80,96},{96,80},{112,64},{1... | collective-permute-start | bytes 393224 | tf_op jit(solution)/shard_map/ppermute | solution.py:25
  48.2 30.1 %collective-permute-start.9 = (bf16[16,4096]{1,0:T(8,128)(2,1)S(1)}, bf16[16,4096]{1,0:T(8,128)(2,1)S(1)}, u32[]{:S(2)}, u32[]{:S(2)}) collective-permute-start(bf16[16,4096]{1,0:T(8,128)(2,1)S(1)} %get-tuple-element.34.refs_0_.refs_2_), channel_id=1, source_target_pairs={{0,2},{2,0},{1,3},{3,1},{4,6},{6,4},{5,7},{7,5},{8,10},{10,8},{9,1... | collective-permute-start | bytes 393224 | tf_op jit(solution)/shard_map/ppermute | solution.py:25
  67.1 11.2 %copy-start.2 = (bf16[1024,256]{1,0:T(8,128)(2,1)}, bf16[1024,256]{1,0:T(8,128)(2,1)S(1)}, u32[]{:S(2)}) copy-start(bf16[1024,256]{1,0:T(8,128)(2,1)S(1)} %shard_map.112.refs_0_.w_own) | copy-start | bytes 1572868
  67.1 38.6 %collective-permute-start.6 = (bf16[1024,256]{1,0:T(8,128)(2,1)S(1)}, bf16[1024,256]{1,0:T(8,128)(2,1)S(1)}, u32[]{:S(2)}, u32[]{:S(2)}) collective-permute-start(bf16[1024,256]{1,0:T(8,128)(2,1)S(1)} %shard_map.112.refs_0_.w_own), channel_id=1, source_target_pairs={{0,512},{256,768},{512,0},{768,256},{1,513},{257,769},{513,1},{769... | collective-permute-start | bytes 1572872 | tf_op jit(solution)/shard_map/ppermute | solution.py:30
  71.8 23.8 %collective-permute-start.7 = (bf16[1024,256]{1,0:T(8,128)(2,1)S(1)}, bf16[1024,256]{1,0:T(8,128)(2,1)S(1)}, u32[]{:S(2)}, u32[]{:S(2)}) collective-permute-start(bf16[1024,256]{1,0:T(8,128)(2,1)S(1)} %shard_map.112.refs_0_.w_own), channel_id=1, source_target_pairs={{0,256},{256,512},{512,768},{768,0},{1,257},{257,513},{513,769},{7... | collective-permute-start | bytes 1572872 | tf_op jit(solution)/shard_map/ppermute | solution.py:30
  74.0 21.6 %collective-permute-start.8 = (bf16[1024,256]{1,0:T(8,128)(2,1)S(1)}, bf16[1024,256]{1,0:T(8,128)(2,1)S(1)}, u32[]{:S(2)}, u32[]{:S(2)}) collective-permute-start(bf16[1024,256]{1,0:T(8,128)(2,1)S(1)} %shard_map.112.refs_0_.w_own), channel_id=1, source_target_pairs={{0,768},{256,0},{512,256},{768,512},{1,769},{257,1},{513,257},{769... | collective-permute-start | bytes 1572872 | tf_op jit(solution)/shard_map/ppermute | solution.py:30
  78.3 40.3 %copy-start.4 = (f32[256,128]{1,0:T(8,128)S(1)}, f32[256,128]{1,0:T(8,128)}, u32[]{:S(2)}) copy-start(f32[256,128]{1,0:T(8,128)} %constant.24.clone.cos) | copy-start | bytes 393220
  78.3 40.3 %copy-start.5 = (f32[256,128]{1,0:T(8,128)S(1)}, f32[256,128]{1,0:T(8,128)}, u32[]{:S(2)}) copy-start(f32[256,128]{1,0:T(8,128)} %constant.25.clone.sin) | copy-start | bytes 393220
  95.6 16.8 %copy-start = (bf16[1024,256]{1,0:T(8,128)(2,1)}, bf16[1024,256]{1,0:T(8,128)(2,1)S(1)}, u32[]{:S(2)}) copy-start(bf16[1024,256]{1,0:T(8,128)(2,1)S(1)} %collective-permute-done.8.refs_1_.w_right) | copy-start | bytes 1572868
  95.6 10.5 %collective-permute-start.10 = (bf16[32,4096]{1,0:T(8,128)(2,1)S(1)}, bf16[32,4096]{1,0:T(8,128)(2,1)S(1)}, u32[]{:S(2)}, u32[]{:S(2)}) collective-permute-start(bf16[32,4096]{1,0:T(8,128)(2,1)S(1)} %shard_map.114.refs_1_), channel_id=1, source_target_pairs={{0,4},{4,8},{8,12},{12,0},{1,5},{5,9},{9,13},{13,1},{2,6},{6,10},{... | collective-permute-start | bytes 786440 | tf_op jit(solution)/shard_map/ppermute | solution.py:30
  98.8 8.8 %collective-permute-start.11 = (bf16[32,4096]{1,0:T(8,128)(2,1)S(1)}, bf16[32,4096]{1,0:T(8,128)(2,1)S(1)}, u32[]{:S(2)}, u32[]{:S(2)}) collective-permute-start(bf16[32,4096]{1,0:T(8,128)(2,1)S(1)} %shard_map.114.refs_1_), channel_id=1, source_target_pairs={{0,12},{4,0},{8,4},{12,8},{1,13},{5,1},{9,5},{13,9},{2,14},{6,2},{... | collective-permute-start | bytes 786440 | tf_op jit(solution)/shard_map/ppermute | solution.py:30
  102.2 10.1 %collective-permute-start.12 = (bf16[32,4096]{1,0:T(8,128)(2,1)S(1)}, bf16[32,4096]{1,0:T(8,128)(2,1)S(1)}, u32[]{:S(2)}, u32[]{:S(2)}) collective-permute-start(bf16[32,4096]{1,0:T(8,128)(2,1)S(1)} %shard_map.114.refs_1_), channel_id=1, source_target_pairs={{0,8},{4,12},{8,0},{12,4},{1,9},{5,13},{9,1},{13,5},{2,10},{6,14},... | collective-permute-start | bytes 786440 | tf_op jit(solution)/shard_map/ppermute | solution.py:30
  112.4 6.2 %collective-permute-start.13 = (bf16[128,4096]{1,0:T(8,128)(2,1)S(1)}, bf16[128,4096]{1,0:T(8,128)(2,1)S(1)}, u32[]{:S(2)}, u32[]{:S(2)}) collective-permute-start(bf16[128,4096]{1,0:T(8,128)(2,1)S(1)} %shard_map.115.t0), channel_id=1, source_target_pairs={{0,1},{1,0},{2,3},{3,2},{4,5},{5,4},{6,7},{7,6},{8,9},{9,8},{10,11... | collective-permute-start | bytes 3145736 | tf_op jit(solution)/shard_map/ppermute | solution.py:25
  118.6 1.0 copy-start.1
  119.6 1.0 copy-start.3
  120.7 4.7 %copy-start.8 = (bf16[256,128]{1,0:T(8,128)(2,1)S(1)}, bf16[256,128]{1,0:T(8,128)(2,1)}, u32[]{:S(2)}) copy-start(bf16[256,128]{1,0:T(8,128)(2,1)} %d_ctx_ref.1) | copy-start | bytes 196612
  122.2 3.2 %collective-permute-start.14 = (bf16[256,128]{1,0:T(8,128)(2,1)S(1)}, bf16[256,128]{1,0:T(8,128)(2,1)S(1)}, u32[]{:S(2)}, u32[]{:S(2)}) collective-permute-start(bf16[256,128]{1,0:T(8,128)(2,1)S(1)} %get-tuple-element.36.mine_ref), channel_id=1, source_target_pairs={{0,1},{1,0},{2,3},{3,2},{4,5},{5,4},{6,7},{7,6},{8,9},{9,8},{10,11... | collective-permute-start | bytes 196616 | tf_op jit(solution)/shard_map/ppermute | solution.py:25
  127.3 3.1 %collective-permute-start.15 = (bf16[256,128]{1,0:T(8,128)(2,1)S(1)}, bf16[256,128]{1,0:T(8,128)(2,1)S(1)}, u32[]{:S(2)}, u32[]{:S(2)}) collective-permute-start(bf16[256,128]{1,0:T(8,128)(2,1)S(1)} %get-tuple-element.41), channel_id=1, source_target_pairs={{0,1},{1,0},{2,3},{3,2},{4,5},{5,4},{6,7},{7,6},{8,9},{9,8},{10,11... | collective-permute-start | bytes 196616 | tf_op jit(solution)/shard_map/ppermute | solution.py:25
  131.9 1.0 copy-start.9
  136.2 30.6 %all-to-all-start = ((bf16[4,1024,256]{2,1,0:T(8,128)(2,1)}), bf16[4,1024,256]{2,1,0:T(8,128)(2,1)S(1)}, u32[]{:S(2)}, u32[]{:S(2)}) async-start(bf16[4,1024,256]{2,1,0:T(8,128)(2,1)} %shard_map.119.after), calls=%async_computation | async-start | bytes 4194304 | tf_op jit(solution)/shard_map/all_to_all | solution.py:344
  140.3 5.0 %collective-permute-start.16 = (bf16[128,4096]{1,0:T(8,128)(2,1)}, bf16[128,4096]{1,0:T(8,128)(2,1)S(1)}, u32[]{:S(2)}, u32[]{:S(2)}) collective-permute-start(bf16[128,4096]{1,0:T(8,128)(2,1)} %copy-done.9), channel_id=1, source_target_pairs={{0,1},{1,0},{2,3},{3,2},{4,5},{5,4},{6,7},{7,6},{8,9},{9,8},{10,11... | collective-permute-start | bytes 3145736 | tf_op jit(solution)/shard_map/ppermute | solution.py:25
  145.5 11.0 %collective-permute-start.17 = (bf16[32,4096]{1,0:T(8,128)(2,1)S(1)}, bf16[32,4096]{1,0:T(8,128)(2,1)S(1)}, u32[]{:S(2)}, u32[]{:S(2)}) collective-permute-start(bf16[32,4096]{1,0:T(8,128)(2,1)S(1)} %get-tuple-element.47), channel_id=1, source_target_pairs={{0,12},{4,0},{8,4},{12,8},{1,13},{5,1},{9,5},{13,9},{2,14},{6,2},{... | collective-permute-start | bytes 786440 | tf_op jit(solution)/shard_map/ppermute | solution.py:30
  150.8 15.9 %collective-permute-start.18 = (bf16[32,4096]{1,0:T(8,128)(2,1)S(1)}, bf16[32,4096]{1,0:T(8,128)(2,1)S(1)}, u32[]{:S(2)}, u32[]{:S(2)}) collective-permute-start(bf16[32,4096]{1,0:T(8,128)(2,1)S(1)} %get-tuple-element.48), channel_id=1, source_target_pairs={{0,4},{4,8},{8,12},{12,0},{1,5},{5,9},{9,13},{13,1},{2,6},{6,10},{... | collective-permute-start | bytes 786440 | tf_op jit(solution)/shard_map/ppermute | solution.py:30
  152.8 14.0 %collective-permute-start.19 = (bf16[32,4096]{1,0:T(8,128)(2,1)S(1)}, bf16[32,4096]{1,0:T(8,128)(2,1)S(1)}, u32[]{:S(2)}, u32[]{:S(2)}) collective-permute-start(bf16[32,4096]{1,0:T(8,128)(2,1)S(1)} %get-tuple-element.49), channel_id=1, source_target_pairs={{0,8},{4,12},{8,0},{12,4},{1,9},{5,13},{9,1},{13,5},{2,10},{6,14},... | collective-permute-start | bytes 786440 | tf_op jit(solution)/shard_map/ppermute | solution.py:30
  166.7 48.3 %copy-start.7 = (bf16[16,4096]{1,0:T(8,128)(2,1)S(1)}, bf16[16,4096]{1,0:T(8,128)(2,1)}, u32[]{:S(2)}) copy-start(bf16[16,4096]{1,0:T(8,128)(2,1)} %tokens.3) | copy-start | bytes 393220
  167.1 26.8 %collective-permute-start.21 = (bf16[256,256]{1,0:T(8,128)(2,1)S(1)}, bf16[256,256]{1,0:T(8,128)(2,1)S(1)}, u32[]{:S(2)}, u32[]{:S(2)}) collective-permute-start(bf16[256,256]{1,0:T(8,128)(2,1)S(1)} %get-tuple-element.53), channel_id=1, source_target_pairs={{0,48},{16,32},{32,16},{48,0},{64,112},{80,96},{96,80},{112,64},{1... | collective-permute-start | bytes 393224 | tf_op jit(solution)/shard_map/ppermute | solution.py:25
  170.2 23.7 %collective-permute-start.22 = (bf16[256,256]{1,0:T(8,128)(2,1)S(1)}, bf16[256,256]{1,0:T(8,128)(2,1)S(1)}, u32[]{:S(2)}, u32[]{:S(2)}) collective-permute-start(bf16[256,256]{1,0:T(8,128)(2,1)S(1)} %get-tuple-element.54), channel_id=1, source_target_pairs={{0,32},{16,48},{32,0},{48,16},{64,96},{80,112},{96,64},{112,80},{1... | collective-permute-start | bytes 393224 | tf_op jit(solution)/shard_map/ppermute | solution.py:25
  172.1 21.8 %collective-permute-start.23 = (bf16[256,256]{1,0:T(8,128)(2,1)S(1)}, bf16[256,256]{1,0:T(8,128)(2,1)S(1)}, u32[]{:S(2)}, u32[]{:S(2)}) collective-permute-start(bf16[256,256]{1,0:T(8,128)(2,1)S(1)} %get-tuple-element.55), channel_id=1, source_target_pairs={{0,16},{16,0},{32,48},{48,32},{64,80},{80,64},{96,112},{112,96},{1... | collective-permute-start | bytes 393224 | tf_op jit(solution)/shard_map/ppermute | solution.py:25
  176.4 38.6 %collective-permute-start.20 = (bf16[16,4096]{1,0:T(8,128)(2,1)S(1)}, bf16[16,4096]{1,0:T(8,128)(2,1)S(1)}, u32[]{:S(2)}, u32[]{:S(2)}) collective-permute-start(bf16[16,4096]{1,0:T(8,128)(2,1)S(1)} %get-tuple-element.51.refs_0_), channel_id=1, source_target_pairs={{0,2},{2,0},{1,3},{3,1},{4,6},{6,4},{5,7},{7,5},{8,10},{10,8},{9,1... | collective-permute-start | bytes 393224 | tf_op jit(solution)/shard_map/ppermute | solution.py:25
  194.0 34.8 %collective-permute-start.24 = (bf16[64,256]{1,0:T(8,128)(2,1)S(1)}, bf16[64,256]{1,0:T(8,128)(2,1)S(1)}, u32[]{:S(2)}, u32[]{:S(2)}) collective-permute-start(bf16[64,256]{1,0:T(8,128)(2,1)S(1)} %get-tuple-element.57), channel_id=1, source_target_pairs={{0,192},{16,208},{32,224},{48,240},{64,128},{80,144},{96,160},{112... | collective-permute-start | bytes 98312 | tf_op jit(solution)/shard_map/ppermute | solution.py:25
  195.9 32.9 %collective-permute-start.25 = (bf16[64,256]{1,0:T(8,128)(2,1)S(1)}, bf16[64,256]{1,0:T(8,128)(2,1)S(1)}, u32[]{:S(2)}, u32[]{:S(2)}) collective-permute-start(bf16[64,256]{1,0:T(8,128)(2,1)S(1)} %get-tuple-element.58), channel_id=1, source_target_pairs={{0,128},{16,144},{32,160},{48,176},{64,192},{80,208},{96,224},{112... | collective-permute-start | bytes 98312 | tf_op jit(solution)/shard_map/ppermute | solution.py:25
  201.7 27.2 %collective-permute-start.26 = (bf16[64,256]{1,0:T(8,128)(2,1)S(1)}, bf16[64,256]{1,0:T(8,128)(2,1)S(1)}, u32[]{:S(2)}, u32[]{:S(2)}) collective-permute-start(bf16[64,256]{1,0:T(8,128)(2,1)S(1)} %get-tuple-element.59), channel_id=1, source_target_pairs={{0,64},{16,80},{32,96},{48,112},{64,0},{80,16},{96,32},{112,48},{1... | collective-permute-start | bytes 98312 | tf_op jit(solution)/shard_map/ppermute | solution.py:25

commit v6 on v5

--- a/solution.py
+++ b/solution.py
@@ -14,9 +14,10 @@
 SHIFTS = (0, -1, 1, 2)
 VMEM_LIMIT = 20 * 1024 * 1024
 
-AXES = ("x", "zl", "y", "zh", "co")
-SIZES = (4, 16, 4, 2, 2)
-DP = ("x", "zl")
+AXES = ("x", "za", "zb", "y", "zh", "co")
+SIZES = (4, 4, 4, 4, 2, 2)
+ZL = ("za", "zb")
+DP = ("x", "za", "zb")
 TENSOR = ("y", "zh", "co")
 
 
@@ -39,10 +40,6 @@
 
 def spread(block, axis, step):
     return tuple(flipped(block, axis, k * step) for k in range(1, RADIX))
-
-
-def collect(blocks, axis, step):
-    return [flipped(block, axis, k * step) for k, block in reversed(list(enumerate(blocks, 1)))]
 
 
 def ring_gather(block, axis):
@@ -106,18 +103,17 @@
         out[...] = added(own[cut, :], left[cut, :], right[cut, :], far[cut, :]).astype(out.dtype)
 
 
-def scatter_sum_kernel(first, blocks, *refs):
-    parts, outs = refs[first:-blocks], refs[-blocks:]
-    if len(parts) == 1:
-        parts = [parts[0].at[entry] for entry in range(parts[0].shape[0])]
-    count = outs[0].shape[0]
-    for place, out in enumerate(outs):
+def scatter_stack_kernel(first, step, *refs):
+    ids, stack, out = refs[first:]
+    blocks, count = out.shape[:2]
+    mine = ids[1] // step % blocks
+    for place in range(blocks):
         cut = slice(place * count, (place + 1) * count)
-        out[...] = added(*(part[cut, :] for part in parts)).astype(out.dtype)
-
-
-def weights_out_kernel(own, a, b, c, q_out, k_out, v_out):
-    total = added(own[...], a[...], b[...], c[...])
+        out[mine ^ place] = added(*(stack[entry, cut, :] for entry in range(stack.shape[0]))).astype(out.dtype)
+
+
+def weights_out_kernel(parts, q_out, k_out, v_out):
+    total = added(*(parts[entry] for entry in range(parts.shape[0])))
     head, half = q_out.shape[1], k_out.shape[1]
     q_out[...] = total[:, :head]
     k_out[...] = total[:, head : head + half]
@@ -263,30 +259,30 @@
     return out
 
 
-def scatter_sum(blocks, *parts, after=()):
-    shape = (parts[0].shape[-2] // blocks, parts[0].shape[-1])
-    return call(
-        functools.partial(scatter_sum_kernel, len(after), blocks),
-        [(shape, jnp.float32)] + [(shape, jnp.bfloat16)] * (blocks - 1),
-        *parts, after=after, moved=16 * blocks * shape[0] * shape[1],
-    )
+def scatter_stack(ids, step, stack, after=()):
+    count = stack.shape[1] // RADIX
+    (out,) = call(
+        functools.partial(scatter_stack_kernel, len(after), step), [((RADIX, count, stack.shape[2]), jnp.bfloat16)],
+        ids, stack, after=after, moved=10 * stack.shape[1] * stack.shape[2],
+    )
+    return out
 
 
 def shards(tokens, q_weight, k_weight, v_weight, d_context):
     head = q_weight.shape[1]
     count, width = tokens.shape
-    zs = SIZES[1]
+    zs = SIZES[1] * SIZES[2]
     b16, f32 = jnp.bfloat16, jnp.float32
     product = 64 * count * width * head
-    ids = jnp.stack([lax.axis_index(a) for a in AXES]).astype(jnp.int32)
+    ids = jnp.stack([lax.axis_index(a) for a in ("x", ZL, "y", "zh", "co")]).astype(jnp.int32)
 
     weights = jnp.concatenate([q_weight, k_weight, v_weight], axis=1)
     inv_wide, normed = call(
         norm_kernel, [((count, 128), f32), ((count, width), b16)], tokens,
         flops=4 * count * width, moved=4 * count * width,
     )
-    near = rows(*spread(weights, "zl", RADIX)[::-1], weights, after=(normed,), last_first=True)
-    whole = rows(near, *spread(near, "zl", 1))
+    near = rows(*spread(weights, ZL, RADIX)[::-1], weights, after=(normed,), last_first=True)
+    whole = rows(near, *spread(near, ZL, 1))
     w_pieces = (whole, *ring_gather(whole, "x"))
     far = rows(flipped(normed, "zh", 1), after=(whole,), flops=40 * product)
     pair = rows(normed, far, after=w_pieces[1:3])
@@ -341,13 +337,14 @@
         flops=40 * product, moved=12 * count * width,
     )
 
-    kept, *sent = scatter_sum(RADIX, lax.all_to_all(g_blocks, "x", 0, 0), after=(sent_t,))
-    kept, *sent = scatter_sum(RADIX, kept, *collect(sent, "zl", 1))
-    cut = kept.shape[0]
+    near = scatter_stack(ids, 1, lax.all_to_all(g_blocks, "x", 0, 0), after=(sent_t,))
+    far = scatter_stack(ids, RADIX, lax.all_to_all(near, "zb", 0, 0))
+    grads = lax.all_to_all(far, "za", 0, 0)
+    cut = grads.shape[1]
     grads = call(
         weights_out_kernel,
         [((cut, head), f32), ((cut, head // 2), f32), ((cut, head // 2), f32)],
-        kept, *collect(sent, "zl", RADIX),
+        grads,
         moved=24 * cut * head,
     )
     return (context, grad_tokens, *grads)

time: 231 us -> 230 us (level)
  the two profiles are of different devices: /device:TPU:1 before, /device:TPU:96 now
where the time goes in v6:
time: 230 us; the launch traced here: 229 us
  starting transfers between devices  126 us (55%)
  waiting for transfers between devices  83.7 us (36%)
  Pallas kernels  13.2 us (6%)
  local copies, waits for them, and re-layouts  4.09 us (2%)
    ppermute x12, starting transfers between devices, flipped(): return lax.ppermute(value, axis, [(s, s ^ mask) for s in range(size)])  78.4 us
    ppermute x12, waiting for transfers between devices, flipped(): return lax.ppermute(value, axis, [(s, s ^ mask) for s in range(size)])  36 us
    ppermute x9, starting transfers between devices, shifted(): lax.ppermute(value, axis, [(s, (s + step) % size) for s in range(size)])  33.8 us
    ppermute x9, waiting for transfers between devices, shifted(): lax.ppermute(value, axis, [(s, (s + step) % size) for s in range(size)])  20.4 us
    all_to_all x1, waiting for transfers between devices, shards(): far = scatter_stack(ids, RADIX, lax.all_to_all(near, 'zb', 0, 0))  16.3 us
    pallas_call x16, Pallas kernels, call(): pl.pallas_call(kernel, out_shape=[jax.ShapeDtypeStruct(s, t) for s, t in...  13.2 us
    all_to_all x1, waiting for transfers between devices, shards(): grads = lax.all_to_all(far, 'za', 0, 0)  11 us
    all_to_all x1, starting transfers between devices, shards(): far = scatter_stack(ids, RADIX, lax.all_to_all(near, 'zb', 0, 0))  5.83 us
  transfers between devices with their start and end apart: 24, of which 16 were waited for; matrix products, arithmetic and copies ran while one was open for 0% of the time, Pallas kernels for 1%

profile of v6, /device:TPU:96, one launch (start us, length us, event | category | flops | bytes accessed | tf_op | source)
XLA Modules:
  0.0 228.6 jit_solution(11167491141237442538)
XLA Ops:
  0.6 0.8 pad_maximum_fusion.refs_4_
  1.5 22.3 %collective-permute-start = (bf16[64,256]{1,0:T(8,128)(2,1)S(1)}, bf16[64,256]{1,0:T(8,128)(2,1)S(1)}, u32[]{:S(2)}, u32[]{:S(2)}) collective-permute-start(bf16[64,256]{1,0:T(8,128)(2,1)S(1)} %pad_maximum_fusion.refs_4_), channel_id=1, source_target_pairs={{0,192},{16,208},{32,224},{48,240},{64,128},{80,144},{96,160},{112... | collective-permute-start | bytes 98312 | tf_op jit(solution)/shard_map/ppermute | solution.py:26
  23.8 1.9 collective-permute-start.1
  25.7 2.5 %collective-permute-start.2 = (bf16[64,256]{1,0:T(8,128)(2,1)S(1)}, bf16[64,256]{1,0:T(8,128)(2,1)S(1)}, u32[]{:S(2)}, u32[]{:S(2)}) collective-permute-start(bf16[64,256]{1,0:T(8,128)(2,1)S(1)} %pad_maximum_fusion.refs_4_), channel_id=1, source_target_pairs={{0,64},{16,80},{32,96},{48,112},{64,0},{80,16},{96,32},{112,48},{1... | collective-permute-start | bytes 98312 | tf_op jit(solution)/shard_map/ppermute | solution.py:26
  28.2 0.0 copy-start.6
  28.2 0.9 copy-done.6
  29.1 0.1 shard_map.110
  29.3 0.0 collective-permute-done.refs_1_
  29.3 9.2 %collective-permute-done.1.refs_2_ = bf16[64,256]{1,0:T(8,128)(2,1)S(1)} collective-permute-done((bf16[64,256]{1,0:T(8,128)(2,1)S(1)}, bf16[64,256]{1,0:T(8,128)(2,1)S(1)}, u32[]{:S(2)}, u32[]{:S(2)}) %collective-permute-start.1) | collective-permute-done | bytes 32800 | tf_op jit(solution)/shard_map/ppermute | solution.py:26
  38.4 0.0 collective-permute-done.2.refs_3_
  38.5 2.3 collective-permute-start.3
  40.7 1.9 collective-permute-start.4
  42.6 5.9 %collective-permute-start.5 = (bf16[256,256]{1,0:T(8,128)(2,1)S(1)}, bf16[256,256]{1,0:T(8,128)(2,1)S(1)}, u32[]{:S(2)}, u32[]{:S(2)}) collective-permute-start(bf16[256,256]{1,0:T(8,128)(2,1)S(1)} %shard_map.111.refs_0_), channel_id=1, source_target_pairs={{0,48},{16,32},{32,16},{48,0},{64,112},{80,96},{96,80},{112,64},{1... | collective-permute-start | bytes 393224 | tf_op jit(solution)/shard_map/ppermute | solution.py:26
  48.6 15.5 %collective-permute-start.9 = (bf16[16,4096]{1,0:T(8,128)(2,1)S(1)}, bf16[16,4096]{1,0:T(8,128)(2,1)S(1)}, u32[]{:S(2)}, u32[]{:S(2)}) collective-permute-start(bf16[16,4096]{1,0:T(8,128)(2,1)S(1)} %get-tuple-element.26.refs_0_.refs_2_), channel_id=1, source_target_pairs={{0,2},{2,0},{1,3},{3,1},{4,6},{6,4},{5,7},{7,5},{8,10},{10,8},{9,1... | collective-permute-start | bytes 393224 | tf_op jit(solution)/shard_map/ppermute | solution.py:26
  64.2 4.9 %collective-permute-start.6 = (bf16[1024,256]{1,0:T(8,128)(2,1)S(1)}, bf16[1024,256]{1,0:T(8,128)(2,1)S(1)}, u32[]{:S(2)}, u32[]{:S(2)}) collective-permute-start(bf16[1024,256]{1,0:T(8,128)(2,1)S(1)} %shard_map.112.refs_0_.w_own), channel_id=1, source_target_pairs={{0,512},{256,768},{512,0},{768,256},{1,513},{257,769},{513,1},{769... | collective-permute-start | bytes 1572872 | tf_op jit(solution)/shard_map/ppermute | solution.py:31
  69.1 2.5 %collective-permute-start.7 = (bf16[1024,256]{1,0:T(8,128)(2,1)S(1)}, bf16[1024,256]{1,0:T(8,128)(2,1)S(1)}, u32[]{:S(2)}, u32[]{:S(2)}) collective-permute-start(bf16[1024,256]{1,0:T(8,128)(2,1)S(1)} %shard_map.112.refs_0_.w_own), channel_id=1, source_target_pairs={{0,256},{256,512},{512,768},{768,0},{1,257},{257,513},{513,769},{7... | collective-permute-start | bytes 1572872 | tf_op jit(solution)/shard_map/ppermute | solution.py:31
  71.6 4.6 %collective-permute-start.8 = (bf16[1024,256]{1,0:T(8,128)(2,1)S(1)}, bf16[1024,256]{1,0:T(8,128)(2,1)S(1)}, u32[]{:S(2)}, u32[]{:S(2)}) collective-permute-start(bf16[1024,256]{1,0:T(8,128)(2,1)S(1)} %shard_map.112.refs_0_.w_own), channel_id=1, source_target_pairs={{0,768},{256,0},{512,256},{768,512},{1,769},{257,1},{513,257},{769... | collective-permute-start | bytes 1572872 | tf_op jit(solution)/shard_map/ppermute | solution.py:31
  76.2 13.5 %collective-permute-done.9.refs_1_ = bf16[16,4096]{1,0:T(8,128)(2,1)S(1)} collective-permute-done((bf16[16,4096]{1,0:T(8,128)(2,1)S(1)}, bf16[16,4096]{1,0:T(8,128)(2,1)S(1)}, u32[]{:S(2)}, u32[]{:S(2)}) %collective-permute-start.9) | collective-permute-done | bytes 131104 | tf_op jit(solution)/shard_map/ppermute | solution.py:26
  89.7 0.0 copy-start.4
  89.7 0.0 copy-start.5
  89.8 1.6 collective-permute-done.7.refs_0_.w_left
  91.4 0.1 collective-permute-done.8.refs_1_.w_right
  91.5 3.5 %collective-permute-start.10 = (bf16[32,4096]{1,0:T(8,128)(2,1)S(1)}, bf16[32,4096]{1,0:T(8,128)(2,1)S(1)}, u32[]{:S(2)}, u32[]{:S(2)}) collective-permute-start(bf16[32,4096]{1,0:T(8,128)(2,1)S(1)} %shard_map.114.refs_1_), channel_id=1, source_target_pairs={{0,4},{4,8},{8,12},{12,0},{1,5},{5,9},{9,13},{13,1},{2,6},{6,10},{... | collective-permute-start | bytes 786440 | tf_op jit(solution)/shard_map/ppermute | solution.py:31
  95.0 3.6 %collective-permute-start.11 = (bf16[32,4096]{1,0:T(8,128)(2,1)S(1)}, bf16[32,4096]{1,0:T(8,128)(2,1)S(1)}, u32[]{:S(2)}, u32[]{:S(2)}) collective-permute-start(bf16[32,4096]{1,0:T(8,128)(2,1)S(1)} %shard_map.114.refs_1_), channel_id=1, source_target_pairs={{0,12},{4,0},{8,4},{12,8},{1,13},{5,1},{9,5},{13,9},{2,14},{6,2},{... | collective-permute-start | bytes 786440 | tf_op jit(solution)/shard_map/ppermute | solution.py:31
  98.6 3.9 %collective-permute-start.12 = (bf16[32,4096]{1,0:T(8,128)(2,1)S(1)}, bf16[32,4096]{1,0:T(8,128)(2,1)S(1)}, u32[]{:S(2)}, u32[]{:S(2)}) collective-permute-start(bf16[32,4096]{1,0:T(8,128)(2,1)S(1)} %shard_map.114.refs_1_), channel_id=1, source_target_pairs={{0,8},{4,12},{8,0},{12,4},{1,9},{5,13},{9,1},{13,5},{2,10},{6,14},... | collective-permute-start | bytes 786440 | tf_op jit(solution)/shard_map/ppermute | solution.py:31
  102.5 0.3 collective-permute-done.10.refs_2_
  102.8 3.3 %collective-permute-done.11.refs_3_ = bf16[32,4096]{1,0:T(8,128)(2,1)S(1)} collective-permute-done((bf16[32,4096]{1,0:T(8,128)(2,1)S(1)}, bf16[32,4096]{1,0:T(8,128)(2,1)S(1)}, u32[]{:S(2)}, u32[]{:S(2)}) %collective-permute-start.11) | collective-permute-done | bytes 262176 | tf_op jit(solution)/shard_map/ppermute | solution.py:31
  106.2 3.5 %collective-permute-done.12.refs_4_ = bf16[32,4096]{1,0:T(8,128)(2,1)S(1)} collective-permute-done((bf16[32,4096]{1,0:T(8,128)(2,1)S(1)}, bf16[32,4096]{1,0:T(8,128)(2,1)S(1)}, u32[]{:S(2)}, u32[]{:S(2)}) %collective-permute-start.12) | collective-permute-done | bytes 262176 | tf_op jit(solution)/shard_map/ppermute | solution.py:31
  109.6 0.1 shard_map.115.t0
  109.7 1.9 collective-permute-start.13
  111.6 0.1 stack.23.ids.refs_1_.refs_0_
  111.7 2.5 %collective-permute-done.13.t1 = bf16[128,4096]{1,0:T(8,128)(2,1)S(1)} collective-permute-done((bf16[128,4096]{1,0:T(8,128)(2,1)S(1)}, bf16[128,4096]{1,0:T(8,128)(2,1)S(1)}, u32[]{:S(2)}, u32[]{:S(2)}) %collective-permute-start.13) | collective-permute-done | bytes 1048608 | tf_op jit(solution)/shard_map/ppermute | solution.py:26
  114.3 1.0 copy-done.1
  115.3 1.0 copy-done.3
  116.4 1.5 shard_map.116
  117.9 2.0 collective-permute-start.14
  119.9 1.1 collective-permute-done.14.other_ref
  121.0 1.9 shard_map.117
  122.9 2.1 collective-permute-start.15
  125.0 1.1 collective-permute-done.15.got_ref
  126.1 1.5 shard_map.118
  127.6 1.0 copy-done.9
  128.6 3.4 %shard_map.119.after = bf16[4,1024,256]{2,1,0:T(8,128)(2,1)} custom-call(s32[5]{0:T(128)S(1)} %stack.23.ids.refs_1_.refs_0_, bf16[128,4096]{1,0:T(8,128)(2,1)S(1)} %shard_map.115.t0, bf16[128,4096]{1,0:T(8,128)(2,1)S(1)} %collective-permute-done.13.t1, bf16[256,256]{1,0:T(8,128)(2,1)S(1)} %get-tuple-element.35.dj_ref), custom_call_target="tpu_custom_call" | custom-call | flops 536870912 | bytes 4194304 | tf_op jit(solution)/shard_map/pallas_call | solution.py:242
  131.9 4.3 %all-to-all-start = ((bf16[4,1024,256]{2,1,0:T(8,128)(2,1)}), bf16[4,1024,256]{2,1,0:T(8,128)(2,1)S(1)}, u32[]{:S(2)}, u32[]{:S(2)}) async-start(bf16[4,1024,256]{2,1,0:T(8,128)(2,1)} %shard_map.119.after), calls=%async_computation | async-start | bytes 4194304 | tf_op jit(solution)/shard_map/all_to_all | solution.py:340
  136.2 1.9 collective-permute-start.16
  138.2 2.8 %collective-permute-done.16.got = bf16[128,4096]{1,0:T(8,128)(2,1)S(1)} collective-permute-done((bf16[128,4096]{1,0:T(8,128)(2,1)}, bf16[128,4096]{1,0:T(8,128)(2,1)S(1)}, u32[]{:S(2)}, u32[]{:S(2)}) %collective-permute-start.16) | collective-permute-done | bytes 1048608 | tf_op jit(solution)/shard_map/ppermute | solution.py:26
  141.0 0.2 shard_map.120
  141.2 5.6 %collective-permute-start.17 = (bf16[32,4096]{1,0:T(8,128)(2,1)S(1)}, bf16[32,4096]{1,0:T(8,128)(2,1)S(1)}, u32[]{:S(2)}, u32[]{:S(2)}) collective-permute-start(bf16[32,4096]{1,0:T(8,128)(2,1)S(1)} %get-tuple-element.39), channel_id=1, source_target_pairs={{0,12},{4,0},{8,4},{12,8},{1,13},{5,1},{9,5},{13,9},{2,14},{6,2},{... | collective-permute-start | bytes 786440 | tf_op jit(solution)/shard_map/ppermute | solution.py:31
  146.8 1.9 collective-permute-start.18
  148.8 3.4 %collective-permute-start.19 = (bf16[32,4096]{1,0:T(8,128)(2,1)S(1)}, bf16[32,4096]{1,0:T(8,128)(2,1)S(1)}, u32[]{:S(2)}, u32[]{:S(2)}) collective-permute-start(bf16[32,4096]{1,0:T(8,128)(2,1)S(1)} %get-tuple-element.41), channel_id=1, source_target_pairs={{0,8},{4,12},{8,0},{12,4},{1,9},{5,13},{9,1},{13,5},{2,10},{6,14},... | collective-permute-start | bytes 786440 | tf_op jit(solution)/shard_map/ppermute | solution.py:31
  152.1 0.6 collective-permute-done.17.left
  152.8 10.8 %collective-permute-done.18.right = bf16[32,4096]{1,0:T(8,128)(2,1)S(1)} collective-permute-done((bf16[32,4096]{1,0:T(8,128)(2,1)S(1)}, bf16[32,4096]{1,0:T(8,128)(2,1)S(1)}, u32[]{:S(2)}, u32[]{:S(2)}) %collective-permute-start.18) | collective-permute-done | bytes 262176 | tf_op jit(solution)/shard_map/ppermute | solution.py:31
  163.6 0.1 shard_map.121
  163.8 0.0 copy-start.7
  163.8 1.6 shard_map.123
  165.3 5.8 %all-to-all-start.1 = ((bf16[4,256,256]{2,1,0:T(8,128)(2,1)}), bf16[4,256,256]{2,1,0:T(8,128)(2,1)S(1)}, u32[]{:S(2)}, u32[]{:S(2)}) async-start(bf16[4,256,256]{2,1,0:T(8,128)(2,1)} %shard_map.123), calls=%async_computation.1 | async-start | bytes 1048576 | tf_op jit(solution)/shard_map/all_to_all | solution.py:341
  171.2 18.2 %collective-permute-start.20 = (bf16[16,4096]{1,0:T(8,128)(2,1)S(1)}, bf16[16,4096]{1,0:T(8,128)(2,1)S(1)}, u32[]{:S(2)}, u32[]{:S(2)}) collective-permute-start(bf16[16,4096]{1,0:T(8,128)(2,1)S(1)} %get-tuple-element.43.refs_0_), channel_id=1, source_target_pairs={{0,2},{2,0},{1,3},{3,1},{4,6},{6,4},{5,7},{7,5},{8,10},{10,8},{9,1... | collective-permute-start | bytes 393224 | tf_op jit(solution)/shard_map/ppermute | solution.py:26
  189.4 16.3 %all-to-all-done.1.refs_1_ = bf16[4,256,256]{2,1,0:T(8,128)(2,1)S(1)} async-done(((bf16[4,256,256]{2,1,0:T(8,128)(2,1)}), bf16[4,256,256]{2,1,0:T(8,128)(2,1)S(1)}, u32[]{:S(2)}, u32[]{:S(2)}) %all-to-all-start.1) | async-done | bytes 524320 | tf_op jit(solution)/shard_map/all_to_all | solution.py:341
  205.7 1.2 shard_map.124
  206.9 3.3 %all-to-all-start.2 = ((bf16[4,64,256]{2,1,0:T(8,128)(2,1)}), bf16[4,64,256]{2,1,0:T(8,128)(2,1)S(1)}, u32[]{:S(2)}, u32[]{:S(2)}) async-start(bf16[4,64,256]{2,1,0:T(8,128)(2,1)} %shard_map.124), calls=%async_computation.2 | async-start | bytes 262144 | tf_op jit(solution)/shard_map/all_to_all | solution.py:342
  210.3 5.8 %collective-permute-done.20.got = bf16[16,4096]{1,0:T(8,128)(2,1)S(1)} collective-permute-done((bf16[16,4096]{1,0:T(8,128)(2,1)S(1)}, bf16[16,4096]{1,0:T(8,128)(2,1)S(1)}, u32[]{:S(2)}, u32[]{:S(2)}) %collective-permute-start.20) | collective-permute-done | bytes 131104 | tf_op jit(solution)/shard_map/ppermute | solution.py:26
  216.0 0.8 shard_map.122
  216.9 11.0 %all-to-all-done.2.parts = bf16[4,64,256]{2,1,0:T(8,128)(2,1)S(1)} async-done(((bf16[4,64,256]{2,1,0:T(8,128)(2,1)}), bf16[4,64,256]{2,1,0:T(8,128)(2,1)S(1)}, u32[]{:S(2)}, u32[]{:S(2)}) %all-to-all-start.2) | async-done | bytes 131104 | tf_op jit(solution)/shard_map/all_to_all | solution.py:342
  227.9 0.7 shard_map.125
  (22 shorter events, 0.1 us)
Async XLA Ops:
  1.5 27.8 %collective-permute-start = (bf16[64,256]{1,0:T(8,128)(2,1)S(1)}, bf16[64,256]{1,0:T(8,128)(2,1)S(1)}, u32[]{:S(2)}, u32[]{:S(2)}) collective-permute-start(bf16[64,256]{1,0:T(8,128)(2,1)S(1)} %pad_maximum_fusion.refs_4_), channel_id=1, source_target_pairs={{0,192},{16,208},{32,224},{48,240},{64,128},{80,144},{96,160},{112... | collective-permute-start | bytes 98312 | tf_op jit(solution)/shard_map/ppermute | solution.py:26
  23.8 14.6 %collective-permute-start.1 = (bf16[64,256]{1,0:T(8,128)(2,1)S(1)}, bf16[64,256]{1,0:T(8,128)(2,1)S(1)}, u32[]{:S(2)}, u32[]{:S(2)}) collective-permute-start(bf16[64,256]{1,0:T(8,128)(2,1)S(1)} %pad_maximum_fusion.refs_4_), channel_id=1, source_target_pairs={{0,128},{16,144},{32,160},{48,176},{64,192},{80,208},{96,224},{112... | collective-permute-start | bytes 98312 | tf_op jit(solution)/shard_map/ppermute | solution.py:26
  25.7 12.7 %collective-permute-start.2 = (bf16[64,256]{1,0:T(8,128)(2,1)S(1)}, bf16[64,256]{1,0:T(8,128)(2,1)S(1)}, u32[]{:S(2)}, u32[]{:S(2)}) collective-permute-start(bf16[64,256]{1,0:T(8,128)(2,1)S(1)} %pad_maximum_fusion.refs_4_), channel_id=1, source_target_pairs={{0,64},{16,80},{32,96},{48,112},{64,0},{80,16},{96,32},{112,48},{1... | collective-permute-start | bytes 98312 | tf_op jit(solution)/shard_map/ppermute | solution.py:26
  28.2 0.9 copy-start.6
  38.5 25.7 %collective-permute-start.3 = (bf16[256,256]{1,0:T(8,128)(2,1)S(1)}, bf16[256,256]{1,0:T(8,128)(2,1)S(1)}, u32[]{:S(2)}, u32[]{:S(2)}) collective-permute-start(bf16[256,256]{1,0:T(8,128)(2,1)S(1)} %shard_map.111.refs_0_), channel_id=1, source_target_pairs={{0,16},{16,0},{32,48},{48,32},{64,80},{80,64},{96,112},{112,96},{1... | collective-permute-start | bytes 393224 | tf_op jit(solution)/shard_map/ppermute | solution.py:26
  40.7 23.4 %collective-permute-start.4 = (bf16[256,256]{1,0:T(8,128)(2,1)S(1)}, bf16[256,256]{1,0:T(8,128)(2,1)S(1)}, u32[]{:S(2)}, u32[]{:S(2)}) collective-permute-start(bf16[256,256]{1,0:T(8,128)(2,1)S(1)} %shard_map.111.refs_0_), channel_id=1, source_target_pairs={{0,32},{16,48},{32,0},{48,16},{64,96},{80,112},{96,64},{112,80},{1... | collective-permute-start | bytes 393224 | tf_op jit(solution)/shard_map/ppermute | solution.py:26
  42.6 21.5 %collective-permute-start.5 = (bf16[256,256]{1,0:T(8,128)(2,1)S(1)}, bf16[256,256]{1,0:T(8,128)(2,1)S(1)}, u32[]{:S(2)}, u32[]{:S(2)}) collective-permute-start(bf16[256,256]{1,0:T(8,128)(2,1)S(1)} %shard_map.111.refs_0_), channel_id=1, source_target_pairs={{0,48},{16,32},{32,16},{48,0},{64,112},{80,96},{96,80},{112,64},{1... | collective-permute-start | bytes 393224 | tf_op jit(solution)/shard_map/ppermute | solution.py:26
  48.6 41.1 %collective-permute-start.9 = (bf16[16,4096]{1,0:T(8,128)(2,1)S(1)}, bf16[16,4096]{1,0:T(8,128)(2,1)S(1)}, u32[]{:S(2)}, u32[]{:S(2)}) collective-permute-start(bf16[16,4096]{1,0:T(8,128)(2,1)S(1)} %get-tuple-element.26.refs_0_.refs_2_), channel_id=1, source_target_pairs={{0,2},{2,0},{1,3},{3,1},{4,6},{6,4},{5,7},{7,5},{8,10},{10,8},{9,1... | collective-permute-start | bytes 393224 | tf_op jit(solution)/shard_map/ppermute | solution.py:26
  64.2 25.5 %copy-start.2 = (bf16[1024,256]{1,0:T(8,128)(2,1)}, bf16[1024,256]{1,0:T(8,128)(2,1)S(1)}, u32[]{:S(2)}) copy-start(bf16[1024,256]{1,0:T(8,128)(2,1)S(1)} %shard_map.112.refs_0_.w_own) | copy-start | bytes 1572868
  64.2 38.3 %collective-permute-start.6 = (bf16[1024,256]{1,0:T(8,128)(2,1)S(1)}, bf16[1024,256]{1,0:T(8,128)(2,1)S(1)}, u32[]{:S(2)}, u32[]{:S(2)}) collective-permute-start(bf16[1024,256]{1,0:T(8,128)(2,1)S(1)} %shard_map.112.refs_0_.w_own), channel_id=1, source_target_pairs={{0,512},{256,768},{512,0},{768,256},{1,513},{257,769},{513,1},{769... | collective-permute-start | bytes 1572872 | tf_op jit(solution)/shard_map/ppermute | solution.py:31
  69.1 22.3 %collective-permute-start.7 = (bf16[1024,256]{1,0:T(8,128)(2,1)S(1)}, bf16[1024,256]{1,0:T(8,128)(2,1)S(1)}, u32[]{:S(2)}, u32[]{:S(2)}) collective-permute-start(bf16[1024,256]{1,0:T(8,128)(2,1)S(1)} %shard_map.112.refs_0_.w_own), channel_id=1, source_target_pairs={{0,256},{256,512},{512,768},{768,0},{1,257},{257,513},{513,769},{7... | collective-permute-start | bytes 1572872 | tf_op jit(solution)/shard_map/ppermute | solution.py:31
  71.6 19.9 %collective-permute-start.8 = (bf16[1024,256]{1,0:T(8,128)(2,1)S(1)}, bf16[1024,256]{1,0:T(8,128)(2,1)S(1)}, u32[]{:S(2)}, u32[]{:S(2)}) collective-permute-start(bf16[1024,256]{1,0:T(8,128)(2,1)S(1)} %shard_map.112.refs_0_.w_own), channel_id=1, source_target_pairs={{0,768},{256,0},{512,256},{768,512},{1,769},{257,1},{513,257},{769... | collective-permute-start | bytes 1572872 | tf_op jit(solution)/shard_map/ppermute | solution.py:31
  89.7 24.5 %copy-start.4 = (f32[256,128]{1,0:T(8,128)S(1)}, f32[256,128]{1,0:T(8,128)}, u32[]{:S(2)}) copy-start(f32[256,128]{1,0:T(8,128)} %constant.29.clone.cos) | copy-start | bytes 393220
  89.7 24.5 %copy-start.5 = (f32[256,128]{1,0:T(8,128)S(1)}, f32[256,128]{1,0:T(8,128)}, u32[]{:S(2)}) copy-start(f32[256,128]{1,0:T(8,128)} %constant.30.clone.sin) | copy-start | bytes 393220
  91.5 18.2 %copy-start = (bf16[1024,256]{1,0:T(8,128)(2,1)}, bf16[1024,256]{1,0:T(8,128)(2,1)S(1)}, u32[]{:S(2)}) copy-start(bf16[1024,256]{1,0:T(8,128)(2,1)S(1)} %collective-permute-done.8.refs_1_.w_right) | copy-start | bytes 1572868
  91.5 11.3 %collective-permute-start.10 = (bf16[32,4096]{1,0:T(8,128)(2,1)S(1)}, bf16[32,4096]{1,0:T(8,128)(2,1)S(1)}, u32[]{:S(2)}, u32[]{:S(2)}) collective-permute-start(bf16[32,4096]{1,0:T(8,128)(2,1)S(1)} %shard_map.114.refs_1_), channel_id=1, source_target_pairs={{0,4},{4,8},{8,12},{12,0},{1,5},{5,9},{9,13},{13,1},{2,6},{6,10},{... | collective-permute-start | bytes 786440 | tf_op jit(solution)/shard_map/ppermute | solution.py:31
  95.0 11.1 %collective-permute-start.11 = (bf16[32,4096]{1,0:T(8,128)(2,1)S(1)}, bf16[32,4096]{1,0:T(8,128)(2,1)S(1)}, u32[]{:S(2)}, u32[]{:S(2)}) collective-permute-start(bf16[32,4096]{1,0:T(8,128)(2,1)S(1)} %shard_map.114.refs_1_), channel_id=1, source_target_pairs={{0,12},{4,0},{8,4},{12,8},{1,13},{5,1},{9,5},{13,9},{2,14},{6,2},{... | collective-permute-start | bytes 786440 | tf_op jit(solution)/shard_map/ppermute | solution.py:31
  98.6 11.0 %collective-permute-start.12 = (bf16[32,4096]{1,0:T(8,128)(2,1)S(1)}, bf16[32,4096]{1,0:T(8,128)(2,1)S(1)}, u32[]{:S(2)}, u32[]{:S(2)}) collective-permute-start(bf16[32,4096]{1,0:T(8,128)(2,1)S(1)} %shard_map.114.refs_1_), channel_id=1, source_target_pairs={{0,8},{4,12},{8,0},{12,4},{1,9},{5,13},{9,1},{13,5},{2,10},{6,14},... | collective-permute-start | bytes 786440 | tf_op jit(solution)/shard_map/ppermute | solution.py:31
  109.7 4.6 %collective-permute-start.13 = (bf16[128,4096]{1,0:T(8,128)(2,1)S(1)}, bf16[128,4096]{1,0:T(8,128)(2,1)S(1)}, u32[]{:S(2)}, u32[]{:S(2)}) collective-permute-start(bf16[128,4096]{1,0:T(8,128)(2,1)S(1)} %shard_map.115.t0), channel_id=1, source_target_pairs={{0,1},{1,0},{2,3},{3,2},{4,5},{5,4},{6,7},{7,6},{8,9},{9,8},{10,11... | collective-permute-start | bytes 3145736 | tf_op jit(solution)/shard_map/ppermute | solution.py:26
  114.3 1.0 copy-start.1
  115.3 1.0 copy-start.3
  116.4 4.7 %copy-start.8 = (bf16[256,128]{1,0:T(8,128)(2,1)S(1)}, bf16[256,128]{1,0:T(8,128)(2,1)}, u32[]{:S(2)}) copy-start(bf16[256,128]{1,0:T(8,128)(2,1)} %d_ctx_ref.1) | copy-start | bytes 196612
  117.9 3.1 %collective-permute-start.14 = (bf16[256,128]{1,0:T(8,128)(2,1)S(1)}, bf16[256,128]{1,0:T(8,128)(2,1)S(1)}, u32[]{:S(2)}, u32[]{:S(2)}) collective-permute-start(bf16[256,128]{1,0:T(8,128)(2,1)S(1)} %get-tuple-element.28.mine_ref), channel_id=1, source_target_pairs={{0,1},{1,0},{2,3},{3,2},{4,5},{5,4},{6,7},{7,6},{8,9},{9,8},{10,11... | collective-permute-start | bytes 196616 | tf_op jit(solution)/shard_map/ppermute | solution.py:26
  122.9 3.1 %collective-permute-start.15 = (bf16[256,128]{1,0:T(8,128)(2,1)S(1)}, bf16[256,128]{1,0:T(8,128)(2,1)S(1)}, u32[]{:S(2)}, u32[]{:S(2)}) collective-permute-start(bf16[256,128]{1,0:T(8,128)(2,1)S(1)} %get-tuple-element.33), channel_id=1, source_target_pairs={{0,1},{1,0},{2,3},{3,2},{4,5},{5,4},{6,7},{7,6},{8,9},{9,8},{10,11... | collective-permute-start | bytes 196616 | tf_op jit(solution)/shard_map/ppermute | solution.py:26
  127.6 1.0 copy-start.9
  131.9 31.8 %all-to-all-start = ((bf16[4,1024,256]{2,1,0:T(8,128)(2,1)}), bf16[4,1024,256]{2,1,0:T(8,128)(2,1)S(1)}, u32[]{:S(2)}, u32[]{:S(2)}) async-start(bf16[4,1024,256]{2,1,0:T(8,128)(2,1)} %shard_map.119.after), calls=%async_computation | async-start | bytes 4194304 | tf_op jit(solution)/shard_map/all_to_all | solution.py:340
  136.2 4.8 %collective-permute-start.16 = (bf16[128,4096]{1,0:T(8,128)(2,1)}, bf16[128,4096]{1,0:T(8,128)(2,1)S(1)}, u32[]{:S(2)}, u32[]{:S(2)}) collective-permute-start(bf16[128,4096]{1,0:T(8,128)(2,1)} %copy-done.9), channel_id=1, source_target_pairs={{0,1},{1,0},{2,3},{3,2},{4,5},{5,4},{6,7},{7,6},{8,9},{9,8},{10,11... | collective-permute-start | bytes 3145736 | tf_op jit(solution)/shard_map/ppermute | solution.py:26
  141.2 11.6 %collective-permute-start.17 = (bf16[32,4096]{1,0:T(8,128)(2,1)S(1)}, bf16[32,4096]{1,0:T(8,128)(2,1)S(1)}, u32[]{:S(2)}, u32[]{:S(2)}) collective-permute-start(bf16[32,4096]{1,0:T(8,128)(2,1)S(1)} %get-tuple-element.39), channel_id=1, source_target_pairs={{0,12},{4,0},{8,4},{12,8},{1,13},{5,1},{9,5},{13,9},{2,14},{6,2},{... | collective-permute-start | bytes 786440 | tf_op jit(solution)/shard_map/ppermute | solution.py:31
  146.8 16.8 %collective-permute-start.18 = (bf16[32,4096]{1,0:T(8,128)(2,1)S(1)}, bf16[32,4096]{1,0:T(8,128)(2,1)S(1)}, u32[]{:S(2)}, u32[]{:S(2)}) collective-permute-start(bf16[32,4096]{1,0:T(8,128)(2,1)S(1)} %get-tuple-element.40), channel_id=1, source_target_pairs={{0,4},{4,8},{8,12},{12,0},{1,5},{5,9},{9,13},{13,1},{2,6},{6,10},{... | collective-permute-start | bytes 786440 | tf_op jit(solution)/shard_map/ppermute | solution.py:31
  148.8 14.9 %collective-permute-start.19 = (bf16[32,4096]{1,0:T(8,128)(2,1)S(1)}, bf16[32,4096]{1,0:T(8,128)(2,1)S(1)}, u32[]{:S(2)}, u32[]{:S(2)}) collective-permute-start(bf16[32,4096]{1,0:T(8,128)(2,1)S(1)} %get-tuple-element.41), channel_id=1, source_target_pairs={{0,8},{4,12},{8,0},{12,4},{1,9},{5,13},{9,1},{13,5},{2,10},{6,14},... | collective-permute-start | bytes 786440 | tf_op jit(solution)/shard_map/ppermute | solution.py:31
  163.8 52.3 %copy-start.7 = (bf16[16,4096]{1,0:T(8,128)(2,1)S(1)}, bf16[16,4096]{1,0:T(8,128)(2,1)}, u32[]{:S(2)}) copy-start(bf16[16,4096]{1,0:T(8,128)(2,1)} %tokens.3) | copy-start | bytes 393220
  165.3 40.4 %all-to-all-start.1 = ((bf16[4,256,256]{2,1,0:T(8,128)(2,1)}), bf16[4,256,256]{2,1,0:T(8,128)(2,1)S(1)}, u32[]{:S(2)}, u32[]{:S(2)}) async-start(bf16[4,256,256]{2,1,0:T(8,128)(2,1)} %shard_map.123), calls=%async_computation.1 | async-start | bytes 1048576 | tf_op jit(solution)/shard_map/all_to_all | solution.py:341
  171.2 44.9 %collective-permute-start.20 = (bf16[16,4096]{1,0:T(8,128)(2,1)S(1)}, bf16[16,4096]{1,0:T(8,128)(2,1)S(1)}, u32[]{:S(2)}, u32[]{:S(2)}) collective-permute-start(bf16[16,4096]{1,0:T(8,128)(2,1)S(1)} %get-tuple-element.43.refs_0_), channel_id=1, source_target_pairs={{0,2},{2,0},{1,3},{3,1},{4,6},{6,4},{5,7},{7,5},{8,10},{10,8},{9,1... | collective-permute-start | bytes 393224 | tf_op jit(solution)/shard_map/ppermute | solution.py:26
  206.9 20.9 %all-to-all-start.2 = ((bf16[4,64,256]{2,1,0:T(8,128)(2,1)}), bf16[4,64,256]{2,1,0:T(8,128)(2,1)S(1)}, u32[]{:S(2)}, u32[]{:S(2)}) async-start(bf16[4,64,256]{2,1,0:T(8,128)(2,1)} %shard_map.124), calls=%async_computation.2 | async-start | bytes 262144 | tf_op jit(solution)/shard_map/all_to_all | solution.py:342

commit v7 on v6

--- a/solution.py
+++ b/solution.py
@@ -75,11 +75,14 @@
     return y * 4 + (ids[3] ^ zh) * 2 + (ids[4] ^ co)
 
 
-def norm_kernel(tokens, inv_out, normed_out):
+def norm_kernel(ids, tokens, inv_out, normed_out, swap_out):
     inputs = tokens[...].astype(jnp.float32)
     inv = lax.rsqrt(jnp.mean(inputs * inputs, axis=-1, keepdims=True) + 1e-05)
     inv_out[...] = jnp.broadcast_to(inv, inv_out.shape)
     normed_out[...] = (inputs * inv).astype(jnp.bfloat16)
+    count = tokens.shape[0]
+    swap_out[pl.ds(pl.multiple_of((1 - ids[3]) * count, count), count), :] = normed_out[...]
+    swap_out[pl.ds(pl.multiple_of(ids[3] * count, count), count), :] = jnp.zeros_like(normed_out)
 
 
 def rows_kernel(first, order, *refs):
@@ -96,11 +99,12 @@
         out[...] = added(mine[cut, :], got[cut, :]).astype(out.dtype)
 
 
-def pair_kernel(own, left, right, far, keep_out, send_out):
-    count = keep_out.shape[0]
-    for place, out in enumerate((keep_out, send_out)):
+def pair_kernel(ids, own, left, right, far, out):
+    count = out.shape[0] // 2
+    for place in range(2):
         cut = slice(place * count, (place + 1) * count)
-        out[...] = added(own[cut, :], left[cut, :], right[cut, :], far[cut, :]).astype(out.dtype)
+        at = pl.multiple_of((ids[3] ^ place) * count, count)
+        out[pl.ds(at, count), :] = added(own[cut, :], left[cut, :], right[cut, :], far[cut, :]).astype(out.dtype)
 
 
 def scatter_stack_kernel(first, step, *refs):
@@ -120,9 +124,9 @@
     v_out[...] = total[:, head + half :]
 
 
-def tokens_out_kernel(tokens, inv_wide, kept, got, out):
+def tokens_out_kernel(tokens, inv_wide, summed, out):
     inputs = tokens[...].astype(jnp.float32)
-    d_normed = added(kept[...], got[...])
+    d_normed = summed[...].astype(jnp.float32)
     inv = inv_wide[:, :1]
     mean = jnp.mean(inputs * d_normed, axis=-1, keepdims=True)
     out[...] = (inv * d_normed - inputs * (inv * inv * inv) * mean).astype(jnp.bfloat16)
@@ -277,16 +281,16 @@
     ids = jnp.stack([lax.axis_index(a) for a in ("x", ZL, "y", "zh", "co")]).astype(jnp.int32)
 
     weights = jnp.concatenate([q_weight, k_weight, v_weight], axis=1)
-    inv_wide, normed = call(
-        norm_kernel, [((count, 128), f32), ((count, width), b16)], tokens,
+    inv_wide, normed, swap = call(
+        norm_kernel, [((count, 128), f32), ((count, width), b16), ((2 * count, width), b16)], ids, tokens,
         flops=4 * count * width, moved=4 * count * width,
     )
     near = rows(*spread(weights, ZL, RADIX)[::-1], weights, after=(normed,), last_first=True)
     whole = rows(near, *spread(near, ZL, 1))
     w_pieces = (whole, *ring_gather(whole, "x"))
-    far = rows(flipped(normed, "zh", 1), after=(whole,), flops=40 * product)
-    pair = rows(normed, far, after=w_pieces[1:3])
-    t0 = rows(pair, *ring_gather(pair, "y"), after=w_pieces[3:])
+    far = lax.psum_scatter(swap, "zh", scatter_dimension=0, tiled=True)
+    pair = rows(normed, far, after=(whole,), flops=40 * product)
+    t0 = rows(pair, *ring_gather(pair, "y"), after=w_pieces[1:])
     t1 = flipped(t0, "co", 1)
 
     half = t0.shape[0]
@@ -328,12 +332,10 @@
         after=(g_blocks,), moved=24 * half * width,
     )
     y_got = [shifted(sent, "y", shift) for sent, shift in zip(y_sent, SHIFTS[1:])]
-    kept_t, sent_t = call(
-        pair_kernel, [((count, width), f32), ((count, width), b16)], y_own, *y_got, moved=24 * count * width,
-    )
-    from_zh = flipped(sent_t, "zh", 1)
+    (sent_t,) = call(pair_kernel, [((2 * count, width), b16)], ids, y_own, *y_got, moved=24 * count * width)
+    d_normed = lax.psum_scatter(sent_t, "zh", scatter_dimension=0, tiled=True)
     (grad_tokens,) = call(
-        tokens_out_kernel, [((count, width), b16)], tokens, inv_wide, kept_t, from_zh,
+        tokens_out_kernel, [((count, width), b16)], tokens, inv_wide, d_normed,
         flops=40 * product, moved=12 * count * width,
     )
 

time: 230 us -> 256 us (1.11)
  the two profiles are of different devices: /device:TPU:96 before, /device:TPU:1 now
where the time goes in v7:
time: 256 us; the launch traced here: 255 us
  starting transfers between devices  111 us (43%)
  waiting for transfers between devices  109 us (43%)
  Pallas kernels  15.7 us (6%)
  between operations  14.3 us (6%)
  local copies, waits for them, and re-layouts  3.79 us (1%)
    ppermute x10, starting transfers between devices, flipped(): return lax.ppermute(value, axis, [(s, s ^ mask) for s in range(size)])  49.7 us
    ppermute x10, waiting for transfers between devices, flipped(): return lax.ppermute(value, axis, [(s, s ^ mask) for s in range(size)])  38.1 us
    ppermute x9, starting transfers between devices, shifted(): lax.ppermute(value, axis, [(s, (s + step) % size) for s in range(size)])  31.2 us
    reduce_scatter x1, waiting for transfers between devices, shards(): d_normed = lax.psum_scatter(sent_t, 'zh', scatter_dimension=0, tiled=True)  31.1 us
    all_to_all x1, starting transfers between devices, shards(): grads = lax.all_to_all(far, 'za', 0, 0)  20.8 us
    ppermute x9, waiting for transfers between devices, shifted(): lax.ppermute(value, axis, [(s, (s + step) % size) for s in range(size)])  17.3 us
    pallas_call x15, Pallas kernels, call(): pl.pallas_call(kernel, out_shape=[jax.ShapeDtypeStruct(s, t) for s, t in...  15.7 us
    all_to_all x1, waiting for transfers between devices, shards(): far = scatter_stack(ids, RADIX, lax.all_to_all(near, 'zb', 0, 0))  10.8 us
  transfers between devices with their start and end apart: 24, of which 14 were waited for; matrix products, arithmetic and copies ran while one was open for 0% of the time, Pallas kernels for 1%

profile of v7, /device:TPU:1, one launch (start us, length us, event | category | flops | bytes accessed | tf_op | source)
XLA Modules:
  0.0 254.5 jit_solution(14888486791833879667)
XLA Ops:
  7.2 0.0 reduce-scatter.3.cloned.1.call-start
  7.2 0.1 stack.23.ids.refs_1_.refs_0_
  7.3 0.9 copy-done.2
  8.2 1.4 shard_map.110
  9.6 0.0 reduce-scatter.3.cloned.1.call-update
  9.6 0.8 pad_maximum_fusion.refs_4_
  10.5 22.9 %collective-permute-start = (bf16[64,256]{1,0:T(8,128)(2,1)S(1)}, bf16[64,256]{1,0:T(8,128)(2,1)S(1)}, u32[]{:S(2)}, u32[]{:S(2)}) collective-permute-start(bf16[64,256]{1,0:T(8,128)(2,1)S(1)} %pad_maximum_fusion.refs_4_), channel_id=1, source_target_pairs={{0,192},{16,208},{32,224},{48,240},{64,128},{80,144},{96,160},{112... | collective-permute-start | bytes 98312 | tf_op jit(solution)/shard_map/ppermute | solution.py:26
  33.4 1.9 collective-permute-start.1
  35.3 2.2 collective-permute-start.2
  37.5 9.4 %collective-permute-done.1.refs_2_ = bf16[64,256]{1,0:T(8,128)(2,1)S(1)} collective-permute-done((bf16[64,256]{1,0:T(8,128)(2,1)S(1)}, bf16[64,256]{1,0:T(8,128)(2,1)S(1)}, u32[]{:S(2)}, u32[]{:S(2)}) %collective-permute-start.1) | collective-permute-done | bytes 32800 | tf_op jit(solution)/shard_map/ppermute | solution.py:26
  46.9 3.7 %collective-permute-start.3 = (bf16[256,256]{1,0:T(8,128)(2,1)S(1)}, bf16[256,256]{1,0:T(8,128)(2,1)S(1)}, u32[]{:S(2)}, u32[]{:S(2)}) collective-permute-start(bf16[256,256]{1,0:T(8,128)(2,1)S(1)} %shard_map.111.refs_0_), channel_id=1, source_target_pairs={{0,16},{16,0},{32,48},{48,32},{64,80},{80,64},{96,112},{112,96},{1... | collective-permute-start | bytes 393224 | tf_op jit(solution)/shard_map/ppermute | solution.py:26
  50.6 4.7 %collective-permute-start.4 = (bf16[256,256]{1,0:T(8,128)(2,1)S(1)}, bf16[256,256]{1,0:T(8,128)(2,1)S(1)}, u32[]{:S(2)}, u32[]{:S(2)}) collective-permute-start(bf16[256,256]{1,0:T(8,128)(2,1)S(1)} %shard_map.111.refs_0_), channel_id=1, source_target_pairs={{0,32},{16,48},{32,0},{48,16},{64,96},{80,112},{96,64},{112,80},{1... | collective-permute-start | bytes 393224 | tf_op jit(solution)/shard_map/ppermute | solution.py:26
  55.3 1.9 collective-permute-start.5
  57.2 16.9 %collective-permute-done.3.refs_1_ = bf16[256,256]{1,0:T(8,128)(2,1)S(1)} collective-permute-done((bf16[256,256]{1,0:T(8,128)(2,1)S(1)}, bf16[256,256]{1,0:T(8,128)(2,1)S(1)}, u32[]{:S(2)}, u32[]{:S(2)}) %collective-permute-start.3) | collective-permute-done | bytes 131104 | tf_op jit(solution)/shard_map/ppermute | solution.py:26
  74.1 0.0 collective-permute-done.4.refs_2_
  74.1 5.3 %collective-permute-done.5.refs_3_ = bf16[256,256]{1,0:T(8,128)(2,1)S(1)} collective-permute-done((bf16[256,256]{1,0:T(8,128)(2,1)S(1)}, bf16[256,256]{1,0:T(8,128)(2,1)S(1)}, u32[]{:S(2)}, u32[]{:S(2)}) %collective-permute-start.5) | collective-permute-done | bytes 131104 | tf_op jit(solution)/shard_map/ppermute | solution.py:26
  79.4 3.9 %collective-permute-start.6 = (bf16[1024,256]{1,0:T(8,128)(2,1)S(1)}, bf16[1024,256]{1,0:T(8,128)(2,1)S(1)}, u32[]{:S(2)}, u32[]{:S(2)}) collective-permute-start(bf16[1024,256]{1,0:T(8,128)(2,1)S(1)} %shard_map.112.refs_0_.w_own), channel_id=1, source_target_pairs={{0,256},{256,512},{512,768},{768,0},{1,257},{257,513},{513,769},{7... | collective-permute-start | bytes 1572872 | tf_op jit(solution)/shard_map/ppermute | solution.py:31
  83.3 3.2 %collective-permute-start.7 = (bf16[1024,256]{1,0:T(8,128)(2,1)S(1)}, bf16[1024,256]{1,0:T(8,128)(2,1)S(1)}, u32[]{:S(2)}, u32[]{:S(2)}) collective-permute-start(bf16[1024,256]{1,0:T(8,128)(2,1)S(1)} %shard_map.112.refs_0_.w_own), channel_id=1, source_target_pairs={{0,768},{256,0},{512,256},{768,512},{1,769},{257,1},{513,257},{769... | collective-permute-start | bytes 1572872 | tf_op jit(solution)/shard_map/ppermute | solution.py:31
  86.5 3.6 %collective-permute-start.8 = (bf16[1024,256]{1,0:T(8,128)(2,1)S(1)}, bf16[1024,256]{1,0:T(8,128)(2,1)S(1)}, u32[]{:S(2)}, u32[]{:S(2)}) collective-permute-start(bf16[1024,256]{1,0:T(8,128)(2,1)S(1)} %shard_map.112.refs_0_.w_own), channel_id=1, source_target_pairs={{0,512},{256,768},{512,0},{768,256},{1,513},{257,769},{513,1},{769... | collective-permute-start | bytes 1572872 | tf_op jit(solution)/shard_map/ppermute | solution.py:31
  90.1 0.0 reduce-scatter.3.cloned.1.call-done.refs_2_
  90.2 0.9 copy-done.6
  91.1 0.0 copy-start
  91.1 0.0 copy-start.1
  91.1 3.9 %collective-permute-start.9 = (bf16[32,4096]{1,0:T(8,128)(2,1)S(1)}, bf16[32,4096]{1,0:T(8,128)(2,1)S(1)}, u32[]{:S(2)}, u32[]{:S(2)}) collective-permute-start(bf16[32,4096]{1,0:T(8,128)(2,1)S(1)} %shard_map.113.refs_3_), channel_id=1, source_target_pairs={{0,4},{4,8},{8,12},{12,0},{1,5},{5,9},{9,13},{13,1},{2,6},{6,10},{... | collective-permute-start | bytes 786440 | tf_op jit(solution)/shard_map/ppermute | solution.py:31
  95.0 2.8 %collective-permute-start.10 = (bf16[32,4096]{1,0:T(8,128)(2,1)S(1)}, bf16[32,4096]{1,0:T(8,128)(2,1)S(1)}, u32[]{:S(2)}, u32[]{:S(2)}) collective-permute-start(bf16[32,4096]{1,0:T(8,128)(2,1)S(1)} %shard_map.113.refs_3_), channel_id=1, source_target_pairs={{0,12},{4,0},{8,4},{12,8},{1,13},{5,1},{9,5},{13,9},{2,14},{6,2},{... | collective-permute-start | bytes 786440 | tf_op jit(solution)/shard_map/ppermute | solution.py:31
  97.9 3.7 %collective-permute-start.11 = (bf16[32,4096]{1,0:T(8,128)(2,1)S(1)}, bf16[32,4096]{1,0:T(8,128)(2,1)S(1)}, u32[]{:S(2)}, u32[]{:S(2)}) collective-permute-start(bf16[32,4096]{1,0:T(8,128)(2,1)S(1)} %shard_map.113.refs_3_), channel_id=1, source_target_pairs={{0,8},{4,12},{8,0},{12,4},{1,9},{5,13},{9,1},{13,5},{2,10},{6,14},... | collective-permute-start | bytes 786440 | tf_op jit(solution)/shard_map/ppermute | solution.py:31
  101.5 4.7 %collective-permute-done.8.refs_2_.w_far = bf16[1024,256]{1,0:T(8,128)(2,1)S(1)} collective-permute-done((bf16[1024,256]{1,0:T(8,128)(2,1)S(1)}, bf16[1024,256]{1,0:T(8,128)(2,1)S(1)}, u32[]{:S(2)}, u32[]{:S(2)}) %collective-permute-start.8) | collective-permute-done | bytes 524320 | tf_op jit(solution)/shard_map/ppermute | solution.py:31
  106.3 0.0 collective-permute-done.9.refs_4_
  106.3 0.0 collective-permute-done.10.refs_5_
  106.3 1.7 collective-permute-done.11.refs_6_
  108.0 0.1 shard_map.114.t0
  108.1 0.0 copy-start.4
  108.1 5.7 %collective-permute-start.12 = (bf16[128,4096]{1,0:T(8,128)(2,1)S(1)}, bf16[128,4096]{1,0:T(8,128)(2,1)S(1)}, u32[]{:S(2)}, u32[]{:S(2)}) collective-permute-start(bf16[128,4096]{1,0:T(8,128)(2,1)S(1)} %shard_map.114.t0), channel_id=1, source_target_pairs={{0,1},{1,0},{2,3},{3,2},{4,5},{5,4},{6,7},{7,6},{8,9},{9,8},{10,11... | collective-permute-start | bytes 3145736 | tf_op jit(solution)/shard_map/ppermute | solution.py:26
  113.7 2.3 collective-permute-done.12.t1
  116.0 1.5 shard_map.115
  117.5 2.3 collective-permute-start.13
  119.8 0.9 collective-permute-done.13.other_ref
  120.7 1.9 shard_map.116
  122.6 2.2 collective-permute-start.14
  124.8 0.9 collective-permute-done.14.got_ref
  125.7 1.5 shard_map.117
  127.2 1.0 copy-done.5
  128.2 3.4 %shard_map.118.after = bf16[4,1024,256]{2,1,0:T(8,128)(2,1)} custom-call(s32[5]{0:T(128)S(1)} %stack.23.ids.refs_1_.refs_0_, bf16[128,4096]{1,0:T(8,128)(2,1)S(1)} %shard_map.114.t0, bf16[128,4096]{1,0:T(8,128)(2,1)S(1)} %collective-permute-done.12.t1, bf16[256,256]{1,0:T(8,128)(2,1)S(1)} %get-tuple-element.35.dj_ref), custom_call_target="tpu_custom_call" | custom-call | flops 536870912 | bytes 4194304 | tf_op jit(solution)/shard_map/pallas_call | solution.py:246
  131.6 3.6 %all-to-all-start = ((bf16[4,1024,256]{2,1,0:T(8,128)(2,1)}), bf16[4,1024,256]{2,1,0:T(8,128)(2,1)S(1)}, u32[]{:S(2)}, u32[]{:S(2)}) async-start(bf16[4,1024,256]{2,1,0:T(8,128)(2,1)} %shard_map.118.after), calls=%async_computation.2 | async-start | bytes 4194304 | tf_op jit(solution)/shard_map/all_to_all | solution.py:342
  135.2 2.3 collective-permute-start.15
  137.5 2.5 collective-permute-done.15.got
  140.0 0.2 shard_map.119
  140.2 5.1 %collective-permute-start.16 = (bf16[32,4096]{1,0:T(8,128)(2,1)S(1)}, bf16[32,4096]{1,0:T(8,128)(2,1)S(1)}, u32[]{:S(2)}, u32[]{:S(2)}) collective-permute-start(bf16[32,4096]{1,0:T(8,128)(2,1)S(1)} %get-tuple-element.39), channel_id=1, source_target_pairs={{0,12},{4,0},{8,4},{12,8},{1,13},{5,1},{9,5},{13,9},{2,14},{6,2},{... | collective-permute-start | bytes 786440 | tf_op jit(solution)/shard_map/ppermute | solution.py:31
  145.3 1.9 collective-permute-start.17
  147.2 3.1 %collective-permute-start.18 = (bf16[32,4096]{1,0:T(8,128)(2,1)S(1)}, bf16[32,4096]{1,0:T(8,128)(2,1)S(1)}, u32[]{:S(2)}, u32[]{:S(2)}) collective-permute-start(bf16[32,4096]{1,0:T(8,128)(2,1)S(1)} %get-tuple-element.41), channel_id=1, source_target_pairs={{0,8},{4,12},{8,0},{12,4},{1,9},{5,13},{9,1},{13,5},{2,10},{6,14},... | collective-permute-start | bytes 786440 | tf_op jit(solution)/shard_map/ppermute | solution.py:31
  150.3 0.3 collective-permute-done.16.left
  150.5 10.6 %collective-permute-done.17.right = bf16[32,4096]{1,0:T(8,128)(2,1)S(1)} collective-permute-done((bf16[32,4096]{1,0:T(8,128)(2,1)S(1)}, bf16[32,4096]{1,0:T(8,128)(2,1)S(1)}, u32[]{:S(2)}, u32[]{:S(2)}) %collective-permute-start.17) | collective-permute-done | bytes 262176 | tf_op jit(solution)/shard_map/ppermute | solution.py:31
  161.2 1.4 shard_map.120.refs_0_
  162.5 1.6 shard_map.122
  164.1 5.8 %all-to-all-start.1 = ((bf16[4,256,256]{2,1,0:T(8,128)(2,1)}), bf16[4,256,256]{2,1,0:T(8,128)(2,1)S(1)}, u32[]{:S(2)}, u32[]{:S(2)}) async-start(bf16[4,256,256]{2,1,0:T(8,128)(2,1)} %shard_map.122), calls=%async_computation.3 | async-start | bytes 1048576 | tf_op jit(solution)/shard_map/all_to_all | solution.py:343
  169.9 0.7 reduce-scatter.5.cloned.1.call-update
  170.7 10.8 %all-to-all-done.1.refs_1_ = bf16[4,256,256]{2,1,0:T(8,128)(2,1)S(1)} async-done(((bf16[4,256,256]{2,1,0:T(8,128)(2,1)}), bf16[4,256,256]{2,1,0:T(8,128)(2,1)S(1)}, u32[]{:S(2)}, u32[]{:S(2)}) %all-to-all-start.1) | async-done | bytes 524320 | tf_op jit(solution)/shard_map/all_to_all | solution.py:343
  181.5 1.2 shard_map.123
  182.7 20.8 %all-to-all-start.2 = ((bf16[4,64,256]{2,1,0:T(8,128)(2,1)}), bf16[4,64,256]{2,1,0:T(8,128)(2,1)S(1)}, u32[]{:S(2)}, u32[]{:S(2)}) async-start(bf16[4,64,256]{2,1,0:T(8,128)(2,1)} %shard_map.123), calls=%async_computation.4 | async-start | bytes 262144 | tf_op jit(solution)/shard_map/all_to_all | solution.py:344
  203.5 31.1 %reduce-scatter.5.cloned.1.call-done.summed = bf16[16,4096]{1,0:T(8,128)(2,1)} async-done(((bf16[32,4096]{1,0:T(8,128)(2,1)}), bf16[16,4096]{1,0:T(8,128)(2,1)}) %reduce-scatter.5.cloned.1.call-update) | async-done | bytes 131088 | tf_op jit(solution)/shard_map/reduce_scatter | solution.py:336
  234.6 0.9 copy-done.7
  235.5 0.8 shard_map.121
  236.3 10.6 %all-to-all-done.2.parts = bf16[4,64,256]{2,1,0:T(8,128)(2,1)S(1)} async-done(((bf16[4,64,256]{2,1,0:T(8,128)(2,1)}), bf16[4,64,256]{2,1,0:T(8,128)(2,1)S(1)}, u32[]{:S(2)}, u32[]{:S(2)}) %all-to-all-start.2) | async-done | bytes 131104 | tf_op jit(solution)/shard_map/all_to_all | solution.py:344
  247.0 0.7 shard_map.124
  (19 shorter events, 0.1 us)
Async XLA Ops:
  7.2 83.0 %reduce-scatter.3.cloned.1.call-start = ((), (), s32[]{:S(2)}) async-start(), calls=%async_computation.5 | async-start | bytes 393216 | tf_op jit(solution)/shard_map/reduce_scatter | solution.py:291
  7.3 0.9 copy-start.2
  10.5 27.0 %collective-permute-start = (bf16[64,256]{1,0:T(8,128)(2,1)S(1)}, bf16[64,256]{1,0:T(8,128)(2,1)S(1)}, u32[]{:S(2)}, u32[]{:S(2)}) collective-permute-start(bf16[64,256]{1,0:T(8,128)(2,1)S(1)} %pad_maximum_fusion.refs_4_), channel_id=1, source_target_pairs={{0,192},{16,208},{32,224},{48,240},{64,128},{80,144},{96,160},{112... | collective-permute-start | bytes 98312 | tf_op jit(solution)/shard_map/ppermute | solution.py:26
  33.4 13.5 %collective-permute-start.1 = (bf16[64,256]{1,0:T(8,128)(2,1)S(1)}, bf16[64,256]{1,0:T(8,128)(2,1)S(1)}, u32[]{:S(2)}, u32[]{:S(2)}) collective-permute-start(bf16[64,256]{1,0:T(8,128)(2,1)S(1)} %pad_maximum_fusion.refs_4_), channel_id=1, source_target_pairs={{0,128},{16,144},{32,160},{48,176},{64,192},{80,208},{96,224},{112... | collective-permute-start | bytes 98312 | tf_op jit(solution)/shard_map/ppermute | solution.py:26
  35.3 11.6 %collective-permute-start.2 = (bf16[64,256]{1,0:T(8,128)(2,1)S(1)}, bf16[64,256]{1,0:T(8,128)(2,1)S(1)}, u32[]{:S(2)}, u32[]{:S(2)}) collective-permute-start(bf16[64,256]{1,0:T(8,128)(2,1)S(1)} %pad_maximum_fusion.refs_4_), channel_id=1, source_target_pairs={{0,64},{16,80},{32,96},{48,112},{64,0},{80,16},{96,32},{112,48},{1... | collective-permute-start | bytes 98312 | tf_op jit(solution)/shard_map/ppermute | solution.py:26
  46.9 27.2 %collective-permute-start.3 = (bf16[256,256]{1,0:T(8,128)(2,1)S(1)}, bf16[256,256]{1,0:T(8,128)(2,1)S(1)}, u32[]{:S(2)}, u32[]{:S(2)}) collective-permute-start(bf16[256,256]{1,0:T(8,128)(2,1)S(1)} %shard_map.111.refs_0_), channel_id=1, source_target_pairs={{0,16},{16,0},{32,48},{48,32},{64,80},{80,64},{96,112},{112,96},{1... | collective-permute-start | bytes 393224 | tf_op jit(solution)/shard_map/ppermute | solution.py:26
  50.6 23.5 %collective-permute-start.4 = (bf16[256,256]{1,0:T(8,128)(2,1)S(1)}, bf16[256,256]{1,0:T(8,128)(2,1)S(1)}, u32[]{:S(2)}, u32[]{:S(2)}) collective-permute-start(bf16[256,256]{1,0:T(8,128)(2,1)S(1)} %shard_map.111.refs_0_), channel_id=1, source_target_pairs={{0,32},{16,48},{32,0},{48,16},{64,96},{80,112},{96,64},{112,80},{1... | collective-permute-start | bytes 393224 | tf_op jit(solution)/shard_map/ppermute | solution.py:26
  55.3 24.1 %collective-permute-start.5 = (bf16[256,256]{1,0:T(8,128)(2,1)S(1)}, bf16[256,256]{1,0:T(8,128)(2,1)S(1)}, u32[]{:S(2)}, u32[]{:S(2)}) collective-permute-start(bf16[256,256]{1,0:T(8,128)(2,1)S(1)} %shard_map.111.refs_0_), channel_id=1, source_target_pairs={{0,48},{16,32},{32,16},{48,0},{64,112},{80,96},{96,80},{112,64},{1... | collective-permute-start | bytes 393224 | tf_op jit(solution)/shard_map/ppermute | solution.py:26
  79.4 18.5 %collective-permute-start.6 = (bf16[1024,256]{1,0:T(8,128)(2,1)S(1)}, bf16[1024,256]{1,0:T(8,128)(2,1)S(1)}, u32[]{:S(2)}, u32[]{:S(2)}) collective-permute-start(bf16[1024,256]{1,0:T(8,128)(2,1)S(1)} %shard_map.112.refs_0_.w_own), channel_id=1, source_target_pairs={{0,256},{256,512},{512,768},{768,0},{1,257},{257,513},{513,769},{7... | collective-permute-start | bytes 1572872 | tf_op jit(solution)/shard_map/ppermute | solution.py:31
  83.3 18.2 %collective-permute-start.7 = (bf16[1024,256]{1,0:T(8,128)(2,1)S(1)}, bf16[1024,256]{1,0:T(8,128)(2,1)S(1)}, u32[]{:S(2)}, u32[]{:S(2)}) collective-permute-start(bf16[1024,256]{1,0:T(8,128)(2,1)S(1)} %shard_map.112.refs_0_.w_own), channel_id=1, source_target_pairs={{0,768},{256,0},{512,256},{768,512},{1,769},{257,1},{513,257},{769... | collective-permute-start | bytes 1572872 | tf_op jit(solution)/shard_map/ppermute | solution.py:31
  86.5 19.7 %collective-permute-start.8 = (bf16[1024,256]{1,0:T(8,128)(2,1)S(1)}, bf16[1024,256]{1,0:T(8,128)(2,1)S(1)}, u32[]{:S(2)}, u32[]{:S(2)}) collective-permute-start(bf16[1024,256]{1,0:T(8,128)(2,1)S(1)} %shard_map.112.refs_0_.w_own), channel_id=1, source_target_pairs={{0,512},{256,768},{512,0},{768,256},{1,513},{257,769},{513,1},{769... | collective-permute-start | bytes 1572872 | tf_op jit(solution)/shard_map/ppermute | solution.py:31
  90.2 0.9 copy-start.6
  91.1 24.9 %copy-start = (f32[256,128]{1,0:T(8,128)S(1)}, f32[256,128]{1,0:T(8,128)}, u32[]{:S(2)}) copy-start(f32[256,128]{1,0:T(8,128)} %constant.29.clone.cos) | copy-start | bytes 393220
  91.1 24.9 %copy-start.1 = (f32[256,128]{1,0:T(8,128)S(1)}, f32[256,128]{1,0:T(8,128)}, u32[]{:S(2)}) copy-start(f32[256,128]{1,0:T(8,128)} %constant.30.clone.sin) | copy-start | bytes 393220
  91.1 15.2 %collective-permute-start.9 = (bf16[32,4096]{1,0:T(8,128)(2,1)S(1)}, bf16[32,4096]{1,0:T(8,128)(2,1)S(1)}, u32[]{:S(2)}, u32[]{:S(2)}) collective-permute-start(bf16[32,4096]{1,0:T(8,128)(2,1)S(1)} %shard_map.113.refs_3_), channel_id=1, source_target_pairs={{0,4},{4,8},{8,12},{12,0},{1,5},{5,9},{9,13},{13,1},{2,6},{6,10},{... | collective-permute-start | bytes 786440 | tf_op jit(solution)/shard_map/ppermute | solution.py:31
  95.0 11.2 %collective-permute-start.10 = (bf16[32,4096]{1,0:T(8,128)(2,1)S(1)}, bf16[32,4096]{1,0:T(8,128)(2,1)S(1)}, u32[]{:S(2)}, u32[]{:S(2)}) collective-permute-start(bf16[32,4096]{1,0:T(8,128)(2,1)S(1)} %shard_map.113.refs_3_), channel_id=1, source_target_pairs={{0,12},{4,0},{8,4},{12,8},{1,13},{5,1},{9,5},{13,9},{2,14},{6,2},{... | collective-permute-start | bytes 786440 | tf_op jit(solution)/shard_map/ppermute | solution.py:31
  97.9 10.1 %collective-permute-start.11 = (bf16[32,4096]{1,0:T(8,128)(2,1)S(1)}, bf16[32,4096]{1,0:T(8,128)(2,1)S(1)}, u32[]{:S(2)}, u32[]{:S(2)}) collective-permute-start(bf16[32,4096]{1,0:T(8,128)(2,1)S(1)} %shard_map.113.refs_3_), channel_id=1, source_target_pairs={{0,8},{4,12},{8,0},{12,4},{1,9},{5,13},{9,1},{13,5},{2,10},{6,14},... | collective-permute-start | bytes 786440 | tf_op jit(solution)/shard_map/ppermute | solution.py:31
  108.1 12.6 %copy-start.4 = (bf16[256,128]{1,0:T(8,128)(2,1)S(1)}, bf16[256,128]{1,0:T(8,128)(2,1)}, u32[]{:S(2)}) copy-start(bf16[256,128]{1,0:T(8,128)(2,1)} %d_ctx_ref.1) | copy-start | bytes 196612
  108.1 7.9 %collective-permute-start.12 = (bf16[128,4096]{1,0:T(8,128)(2,1)S(1)}, bf16[128,4096]{1,0:T(8,128)(2,1)S(1)}, u32[]{:S(2)}, u32[]{:S(2)}) collective-permute-start(bf16[128,4096]{1,0:T(8,128)(2,1)S(1)} %shard_map.114.t0), channel_id=1, source_target_pairs={{0,1},{1,0},{2,3},{3,2},{4,5},{5,4},{6,7},{7,6},{8,9},{9,8},{10,11... | collective-permute-start | bytes 3145736 | tf_op jit(solution)/shard_map/ppermute | solution.py:26
  117.5 3.2 %collective-permute-start.13 = (bf16[256,128]{1,0:T(8,128)(2,1)S(1)}, bf16[256,128]{1,0:T(8,128)(2,1)S(1)}, u32[]{:S(2)}, u32[]{:S(2)}) collective-permute-start(bf16[256,128]{1,0:T(8,128)(2,1)S(1)} %get-tuple-element.28.mine_ref), channel_id=1, source_target_pairs={{0,1},{1,0},{2,3},{3,2},{4,5},{5,4},{6,7},{7,6},{8,9},{9,8},{10,11... | collective-permute-start | bytes 196616 | tf_op jit(solution)/shard_map/ppermute | solution.py:26
  122.6 3.1 %collective-permute-start.14 = (bf16[256,128]{1,0:T(8,128)(2,1)S(1)}, bf16[256,128]{1,0:T(8,128)(2,1)S(1)}, u32[]{:S(2)}, u32[]{:S(2)}) collective-permute-start(bf16[256,128]{1,0:T(8,128)(2,1)S(1)} %get-tuple-element.33), channel_id=1, source_target_pairs={{0,1},{1,0},{2,3},{3,2},{4,5},{5,4},{6,7},{7,6},{8,9},{9,8},{10,11... | collective-permute-start | bytes 196616 | tf_op jit(solution)/shard_map/ppermute | solution.py:26
  127.2 1.0 copy-start.5
  131.6 31.0 %all-to-all-start = ((bf16[4,1024,256]{2,1,0:T(8,128)(2,1)}), bf16[4,1024,256]{2,1,0:T(8,128)(2,1)S(1)}, u32[]{:S(2)}, u32[]{:S(2)}) async-start(bf16[4,1024,256]{2,1,0:T(8,128)(2,1)} %shard_map.118.after), calls=%async_computation.2 | async-start | bytes 4194304 | tf_op jit(solution)/shard_map/all_to_all | solution.py:342
  135.2 4.8 %collective-permute-start.15 = (bf16[128,4096]{1,0:T(8,128)(2,1)}, bf16[128,4096]{1,0:T(8,128)(2,1)S(1)}, u32[]{:S(2)}, u32[]{:S(2)}) collective-permute-start(bf16[128,4096]{1,0:T(8,128)(2,1)} %copy-done.5), channel_id=1, source_target_pairs={{0,1},{1,0},{2,3},{3,2},{4,5},{5,4},{6,7},{7,6},{8,9},{9,8},{10,11... | collective-permute-start | bytes 3145736 | tf_op jit(solution)/shard_map/ppermute | solution.py:26
  140.2 10.4 %collective-permute-start.16 = (bf16[32,4096]{1,0:T(8,128)(2,1)S(1)}, bf16[32,4096]{1,0:T(8,128)(2,1)S(1)}, u32[]{:S(2)}, u32[]{:S(2)}) collective-permute-start(bf16[32,4096]{1,0:T(8,128)(2,1)S(1)} %get-tuple-element.39), channel_id=1, source_target_pairs={{0,12},{4,0},{8,4},{12,8},{1,13},{5,1},{9,5},{13,9},{2,14},{6,2},{... | collective-permute-start | bytes 786440 | tf_op jit(solution)/shard_map/ppermute | solution.py:31
  145.3 15.9 %collective-permute-start.17 = (bf16[32,4096]{1,0:T(8,128)(2,1)S(1)}, bf16[32,4096]{1,0:T(8,128)(2,1)S(1)}, u32[]{:S(2)}, u32[]{:S(2)}) collective-permute-start(bf16[32,4096]{1,0:T(8,128)(2,1)S(1)} %get-tuple-element.40), channel_id=1, source_target_pairs={{0,4},{4,8},{8,12},{12,0},{1,5},{5,9},{9,13},{13,1},{2,6},{6,10},{... | collective-permute-start | bytes 786440 | tf_op jit(solution)/shard_map/ppermute | solution.py:31
  147.2 14.0 %collective-permute-start.18 = (bf16[32,4096]{1,0:T(8,128)(2,1)S(1)}, bf16[32,4096]{1,0:T(8,128)(2,1)S(1)}, u32[]{:S(2)}, u32[]{:S(2)}) collective-permute-start(bf16[32,4096]{1,0:T(8,128)(2,1)S(1)} %get-tuple-element.41), channel_id=1, source_target_pairs={{0,8},{4,12},{8,0},{12,4},{1,9},{5,13},{9,1},{13,5},{2,10},{6,14},... | collective-permute-start | bytes 786440 | tf_op jit(solution)/shard_map/ppermute | solution.py:31
  162.5 72.1 %copy-start.3 = (bf16[16,4096]{1,0:T(8,128)(2,1)S(1)}, bf16[16,4096]{1,0:T(8,128)(2,1)}, u32[]{:S(2)}) copy-start(bf16[16,4096]{1,0:T(8,128)(2,1)} %tokens.3) | copy-start | bytes 393220
  164.1 17.3 %all-to-all-start.1 = ((bf16[4,256,256]{2,1,0:T(8,128)(2,1)}), bf16[4,256,256]{2,1,0:T(8,128)(2,1)S(1)}, u32[]{:S(2)}, u32[]{:S(2)}) async-start(bf16[4,256,256]{2,1,0:T(8,128)(2,1)} %shard_map.122), calls=%async_computation.3 | async-start | bytes 1048576 | tf_op jit(solution)/shard_map/all_to_all | solution.py:343
  169.9 64.7 %reduce-scatter.5.cloned.1.call-start = ((), (), s32[]{:S(2)}) async-start(), calls=%async_computation.6 | async-start | bytes 393216 | tf_op jit(solution)/shard_map/reduce_scatter | solution.py:336
  182.7 64.3 %all-to-all-start.2 = ((bf16[4,64,256]{2,1,0:T(8,128)(2,1)}), bf16[4,64,256]{2,1,0:T(8,128)(2,1)S(1)}, u32[]{:S(2)}, u32[]{:S(2)}) async-start(bf16[4,64,256]{2,1,0:T(8,128)(2,1)} %shard_map.123), calls=%async_computation.4 | async-start | bytes 262144 | tf_op jit(solution)/shard_map/all_to_all | solution.py:344
  234.6 0.9 copy-start.7
Sparse Core Ops, SparseCore 0:
  11.3 78.3 reduce-scatter.2
  174.5 60.0 reduce-scatter.4

commit v8 on v6

--- a/solution.py
+++ b/solution.py
@@ -82,10 +82,18 @@
     normed_out[...] = (inputs * inv).astype(jnp.bfloat16)
 
 
-def rows_kernel(first, order, *refs):
+def copies_kernel(first, *refs):
     *parts, out = refs[first:]
     count = parts[0].shape[0]
-    for place, ref in enumerate(parts[::order]):
+    for place, ref in enumerate(parts[::-1]):
+        for entry in range(out.shape[0]):
+            out[entry, place * count : (place + 1) * count, :] = ref[...]
+
+
+def rows_kernel(first, *refs):
+    *parts, out = refs[first:]
+    count = parts[0].shape[0]
+    for place, ref in enumerate(parts):
         out[place * count : (place + 1) * count, :] = ref[...]
 
 
@@ -128,15 +136,14 @@
     out[...] = (inv * d_normed - inputs * (inv * inv * inv) * mean).astype(jnp.bfloat16)
 
 
-def project_kernel(zs, ids, t0, t1, w_own, w_left, w_right, w_far, cos, sin, w_out, q_out, kv_out):
-    rows = w_own.shape[0]
+def project_kernel(zs, ids, t0, t1, w_all, cos, sin, w_out, q_out, kv_out):
+    blocks, rows = w_all.shape[:2]
     unit = rows // zs
-    for ring, ref in enumerate((w_own, w_left, w_right, w_far)):
-        block = (ids[0] + SHIFTS[ring] + 4) % 4
+    for block in range(blocks):
         for place in range(zs):
-            z = ids[1] ^ z_offset(place)
+            z = (ids[1] // RADIX ^ place % RADIX) * RADIX + place // RADIX
             at = pl.multiple_of(block * rows + z * unit, unit)
-            w_out[pl.ds(at, unit), :] = ref[place * unit : (place + 1) * unit, :]
+            w_out[pl.ds(at, unit), :] = w_all[block, place * unit : (place + 1) * unit, :]
     totals = []
     for ref in (t0, t1):
         total = None
@@ -250,11 +257,20 @@
     )(*after, *args)
 
 
-def rows(*parts, after=(), last_first=False, flops=0):
+def rows(*parts, after=(), flops=0):
     shape = (len(parts) * parts[0].shape[0], parts[0].shape[1])
     (out,) = call(
-        functools.partial(rows_kernel, len(after), -1 if last_first else 1), [(shape, parts[0].dtype)], *parts, after=after,
+        functools.partial(rows_kernel, len(after)), [(shape, parts[0].dtype)], *parts, after=after,
         flops=flops, moved=4 * shape[0] * shape[1],
+    )
+    return out
+
+
+def copies(entries, *parts, after=()):
+    shape = (entries, len(parts) * parts[0].shape[0], parts[0].shape[1])
+    (out,) = call(
+        functools.partial(copies_kernel, len(after)), [(shape, parts[0].dtype)], *parts, after=after,
+        moved=2 * (entries + 1) * shape[1] * shape[2],
     )
     return out
 
@@ -281,12 +297,13 @@
         norm_kernel, [((count, 128), f32), ((count, width), b16)], tokens,
         flops=4 * count * width, moved=4 * count * width,
     )
-    near = rows(*spread(weights, ZL, RADIX)[::-1], weights, after=(normed,), last_first=True)
-    whole = rows(near, *spread(near, ZL, 1))
-    w_pieces = (whole, *ring_gather(whole, "x"))
+    near = copies(SIZES[2], *spread(weights, ZL, RADIX)[::-1], weights, after=(normed,))
+    near = lax.all_to_all(near, "zb", 0, 0)
+    whole = copies(SIZES[0], near.reshape(-1, near.shape[2]))
     far = rows(flipped(normed, "zh", 1), after=(whole,), flops=40 * product)
-    pair = rows(normed, far, after=w_pieces[1:3])
-    t0 = rows(pair, *ring_gather(pair, "y"), after=w_pieces[3:])
+    pair = rows(normed, far)
+    t0 = rows(pair, *ring_gather(pair, "y"))
+    w_all = lax.all_to_all(whole, "x", 0, 0)
     t1 = flipped(t0, "co", 1)
 
     half = t0.shape[0]
@@ -296,7 +313,7 @@
     w_natural, query, kv_mine = call(
         functools.partial(project_kernel, zs),
         [((width, 2 * head), b16), one_head, one_head],
-        ids, t0, t1, *w_pieces, cosine, sine,
+        ids, t0, t1, w_all, cosine, sine,
         flops=product, moved=6 * width * held,
     )
     kv_other = flipped(kv_mine, "co", 1)

time: 230 us -> 228 us (level)
  the two profiles are of different devices: /device:TPU:96 before, /device:TPU:8 now
where the time goes in v8:
time: 228 us; the launch traced here: 226 us
  starting transfers between devices  115 us (50%)
  waiting for transfers between devices  91.2 us (40%)
  Pallas kernels  16.9 us (7%)
    ppermute x9, starting transfers between devices, flipped(): return lax.ppermute(value, axis, [(s, s ^ mask) for s in range(size)])  66.9 us
    ppermute x9, waiting for transfers between devices, flipped(): return lax.ppermute(value, axis, [(s, s ^ mask) for s in range(size)])  41.9 us
    ppermute x6, starting transfers between devices, shifted(): lax.ppermute(value, axis, [(s, (s + step) % size) for s in range(size)])  21.4 us
    all_to_all x1, waiting for transfers between devices, shards(): far = scatter_stack(ids, RADIX, lax.all_to_all(near, 'zb', 0, 0))  19 us
    pallas_call x16, Pallas kernels, call(): pl.pallas_call(kernel, out_shape=[jax.ShapeDtypeStruct(s, t) for s, t in...  16.9 us
    all_to_all x1, waiting for transfers between devices, shards(): grads = lax.all_to_all(far, 'za', 0, 0)  14.5 us
    ppermute x6, waiting for transfers between devices, shifted(): lax.ppermute(value, axis, [(s, (s + step) % size) for s in range(size)])  11.6 us
    all_to_all x1, starting transfers between devices, shards(): far = scatter_stack(ids, RADIX, lax.all_to_all(near, 'zb', 0, 0))  8.95 us
  transfers between devices with their start and end apart: 20, of which 14 were waited for; matrix products, arithmetic and copies ran while one was open for 0% of the time, Pallas kernels for 2%

profile of v8, /device:TPU:8, one launch (start us, length us, event | category | flops | bytes accessed | tf_op | source)
XLA Modules:
  0.0 226.5 jit_solution(7368947919353235587)
XLA Ops:
  0.6 0.8 pad_maximum_fusion.refs_4_
  1.5 22.3 %collective-permute-start = (bf16[64,256]{1,0:T(8,128)(2,1)S(1)}, bf16[64,256]{1,0:T(8,128)(2,1)S(1)}, u32[]{:S(2)}, u32[]{:S(2)}) collective-permute-start(bf16[64,256]{1,0:T(8,128)(2,1)S(1)} %pad_maximum_fusion.refs_4_), channel_id=1, source_target_pairs={{0,192},{16,208},{32,224},{48,240},{64,128},{80,144},{96,160},{112... | collective-permute-start | bytes 98312 | tf_op jit(solution)/shard_map/ppermute | solution.py:26
  23.8 1.9 collective-permute-start.1
  25.7 2.5 %collective-permute-start.2 = (bf16[64,256]{1,0:T(8,128)(2,1)S(1)}, bf16[64,256]{1,0:T(8,128)(2,1)S(1)}, u32[]{:S(2)}, u32[]{:S(2)}) collective-permute-start(bf16[64,256]{1,0:T(8,128)(2,1)S(1)} %pad_maximum_fusion.refs_4_), channel_id=1, source_target_pairs={{0,64},{16,80},{32,96},{48,112},{64,0},{80,16},{96,32},{112,48},{1... | collective-permute-start | bytes 98312 | tf_op jit(solution)/shard_map/ppermute | solution.py:26
  28.2 0.0 copy-start.2
  28.2 0.9 copy-done.2
  29.1 0.1 shard_map.110
  29.3 0.0 collective-permute-done.refs_1_
  29.3 9.5 %collective-permute-done.1.refs_2_ = bf16[64,256]{1,0:T(8,128)(2,1)S(1)} collective-permute-done((bf16[64,256]{1,0:T(8,128)(2,1)S(1)}, bf16[64,256]{1,0:T(8,128)(2,1)S(1)}, u32[]{:S(2)}, u32[]{:S(2)}) %collective-permute-start.1) | collective-permute-done | bytes 32800 | tf_op jit(solution)/shard_map/ppermute | solution.py:26
  38.8 0.0 collective-permute-done.2.refs_3_
  38.8 0.8 shard_map.111
  39.7 5.4 %all-to-all-start = ((bf16[4,256,256]{2,1,0:T(8,128)(2,1)}), bf16[4,256,256]{2,1,0:T(8,128)(2,1)S(1)}, u32[]{:S(2)}, u32[]{:S(2)}) async-start(bf16[4,256,256]{2,1,0:T(8,128)(2,1)} %shard_map.111), calls=%async_computation | async-start | bytes 1048576 | tf_op jit(solution)/shard_map/all_to_all | solution.py:301
  45.1 16.4 %collective-permute-start.3 = (bf16[16,4096]{1,0:T(8,128)(2,1)S(1)}, bf16[16,4096]{1,0:T(8,128)(2,1)S(1)}, u32[]{:S(2)}, u32[]{:S(2)}) collective-permute-start(bf16[16,4096]{1,0:T(8,128)(2,1)S(1)} %get-tuple-element.26.refs_0_), channel_id=1, source_target_pairs={{0,2},{2,0},{1,3},{3,1},{4,6},{6,4},{5,7},{7,5},{8,10},{10,8},{9,1... | collective-permute-start | bytes 393224 | tf_op jit(solution)/shard_map/ppermute | solution.py:26
  61.4 0.0 all-to-all-done
  61.4 1.5 shard_map.112.refs_0_
  62.9 4.3 %all-to-all-start.1 = ((bf16[4,1024,256]{2,1,0:T(8,128)(2,1)}), bf16[4,1024,256]{2,1,0:T(8,128)(2,1)S(1)}, u32[]{:S(2)}, u32[]{:S(2)}) async-start(bf16[4,1024,256]{2,1,0:T(8,128)(2,1)} %shard_map.112.refs_0_), calls=%async_computation.1 | async-start | bytes 4194304 | tf_op jit(solution)/shard_map/all_to_all | solution.py:306
  67.2 22.1 %collective-permute-done.3.refs_1_ = bf16[16,4096]{1,0:T(8,128)(2,1)S(1)} collective-permute-done((bf16[16,4096]{1,0:T(8,128)(2,1)S(1)}, bf16[16,4096]{1,0:T(8,128)(2,1)S(1)}, u32[]{:S(2)}, u32[]{:S(2)}) %collective-permute-start.3) | collective-permute-done | bytes 131104 | tf_op jit(solution)/shard_map/ppermute | solution.py:26
  89.4 0.0 copy-start
  89.4 0.0 copy-start.1
  89.4 3.6 %collective-permute-start.4 = (bf16[32,4096]{1,0:T(8,128)(2,1)S(1)}, bf16[32,4096]{1,0:T(8,128)(2,1)S(1)}, u32[]{:S(2)}, u32[]{:S(2)}) collective-permute-start(bf16[32,4096]{1,0:T(8,128)(2,1)S(1)} %shard_map.114.refs_0_), channel_id=1, source_target_pairs={{0,4},{4,8},{8,12},{12,0},{1,5},{5,9},{9,13},{13,1},{2,6},{6,10},{... | collective-permute-start | bytes 786440 | tf_op jit(solution)/shard_map/ppermute | solution.py:31
  93.0 2.4 %collective-permute-start.5 = (bf16[32,4096]{1,0:T(8,128)(2,1)S(1)}, bf16[32,4096]{1,0:T(8,128)(2,1)S(1)}, u32[]{:S(2)}, u32[]{:S(2)}) collective-permute-start(bf16[32,4096]{1,0:T(8,128)(2,1)S(1)} %shard_map.114.refs_0_), channel_id=1, source_target_pairs={{0,12},{4,0},{8,4},{12,8},{1,13},{5,1},{9,5},{13,9},{2,14},{6,2},{... | collective-permute-start | bytes 786440 | tf_op jit(solution)/shard_map/ppermute | solution.py:31
  95.4 4.2 %collective-permute-start.6 = (bf16[32,4096]{1,0:T(8,128)(2,1)S(1)}, bf16[32,4096]{1,0:T(8,128)(2,1)S(1)}, u32[]{:S(2)}, u32[]{:S(2)}) collective-permute-start(bf16[32,4096]{1,0:T(8,128)(2,1)S(1)} %shard_map.114.refs_0_), channel_id=1, source_target_pairs={{0,8},{4,12},{8,0},{12,4},{1,9},{5,13},{9,1},{13,5},{2,10},{6,14},... | collective-permute-start | bytes 786440 | tf_op jit(solution)/shard_map/ppermute | solution.py:31
  99.6 0.0 collective-permute-done.4.refs_1_
  99.6 1.7 collective-permute-done.5.refs_2_
  101.3 3.9 %collective-permute-done.6.refs_3_ = bf16[32,4096]{1,0:T(8,128)(2,1)S(1)} collective-permute-done((bf16[32,4096]{1,0:T(8,128)(2,1)S(1)}, bf16[32,4096]{1,0:T(8,128)(2,1)S(1)}, u32[]{:S(2)}, u32[]{:S(2)}) %collective-permute-start.6) | collective-permute-done | bytes 262176 | tf_op jit(solution)/shard_map/ppermute | solution.py:31
  105.2 0.1 shard_map.115.t0
  105.2 1.9 collective-permute-start.7
  107.2 0.1 stack.23.ids.refs_1_.refs_0_
  107.3 2.7 %collective-permute-done.7.t1 = bf16[128,4096]{1,0:T(8,128)(2,1)} collective-permute-done((bf16[128,4096]{1,0:T(8,128)(2,1)S(1)}, bf16[128,4096]{1,0:T(8,128)(2,1)}, u32[]{:S(2)}, u32[]{:S(2)}) %collective-permute-start.7) | collective-permute-done | bytes 1048608 | tf_op jit(solution)/shard_map/ppermute | solution.py:26
  109.9 0.0 all-to-all-done.1.w_all
  109.9 2.2 shard_map.116
  112.2 2.0 collective-permute-start.8
  114.2 1.1 collective-permute-done.8.other_ref
  115.3 0.0 copy-done.4
  115.3 1.9 shard_map.117
  117.2 2.1 collective-permute-start.9
  119.3 1.1 collective-permute-done.9.got_ref
  120.4 1.5 shard_map.118
  121.9 0.0 copy-start.5
  121.9 1.0 copy-done.5
  122.8 4.1 %shard_map.119.after = bf16[4,1024,256]{2,1,0:T(8,128)(2,1)} custom-call(s32[5]{0:T(128)S(1)} %stack.23.ids.refs_1_.refs_0_, bf16[128,4096]{1,0:T(8,128)(2,1)S(1)} %shard_map.115.t0, bf16[128,4096]{1,0:T(8,128)(2,1)} %collective-permute-done.7.t1, bf16[256,256]{1,0:T(8,128)(2,1)S(1)} %get-tuple-element.35.dj_ref), custom_call_target="tpu_custom_call" | custom-call | flops 536870912 | bytes 4194304 | tf_op jit(solution)/shard_map/pallas_call | solution.py:249
  126.9 4.3 %all-to-all-start.2 = ((bf16[4,1024,256]{2,1,0:T(8,128)(2,1)}), bf16[4,1024,256]{2,1,0:T(8,128)(2,1)S(1)}, u32[]{:S(2)}, u32[]{:S(2)}) async-start(bf16[4,1024,256]{2,1,0:T(8,128)(2,1)} %shard_map.119.after), calls=%async_computation.2 | async-start | bytes 4194304 | tf_op jit(solution)/shard_map/all_to_all | solution.py:357
  131.2 1.9 collective-permute-start.10
  133.1 2.8 %collective-permute-done.10.got = bf16[128,4096]{1,0:T(8,128)(2,1)S(1)} collective-permute-done((bf16[128,4096]{1,0:T(8,128)(2,1)}, bf16[128,4096]{1,0:T(8,128)(2,1)S(1)}, u32[]{:S(2)}, u32[]{:S(2)}) %collective-permute-start.10) | collective-permute-done | bytes 1048608 | tf_op jit(solution)/shard_map/ppermute | solution.py:26
  136.0 0.2 shard_map.120
  136.2 3.6 %collective-permute-start.11 = (bf16[32,4096]{1,0:T(8,128)(2,1)S(1)}, bf16[32,4096]{1,0:T(8,128)(2,1)S(1)}, u32[]{:S(2)}, u32[]{:S(2)}) collective-permute-start(bf16[32,4096]{1,0:T(8,128)(2,1)S(1)} %get-tuple-element.39), channel_id=1, source_target_pairs={{0,12},{4,0},{8,4},{12,8},{1,13},{5,1},{9,5},{13,9},{2,14},{6,2},{... | collective-permute-start | bytes 786440 | tf_op jit(solution)/shard_map/ppermute | solution.py:31
  139.8 2.3 %collective-permute-start.12 = (bf16[32,4096]{1,0:T(8,128)(2,1)S(1)}, bf16[32,4096]{1,0:T(8,128)(2,1)S(1)}, u32[]{:S(2)}, u32[]{:S(2)}) collective-permute-start(bf16[32,4096]{1,0:T(8,128)(2,1)S(1)} %get-tuple-element.40), channel_id=1, source_target_pairs={{0,4},{4,8},{8,12},{12,0},{1,5},{5,9},{9,13},{13,1},{2,6},{6,10},{... | collective-permute-start | bytes 786440 | tf_op jit(solution)/shard_map/ppermute | solution.py:31
  142.1 5.4 %collective-permute-start.13 = (bf16[32,4096]{1,0:T(8,128)(2,1)S(1)}, bf16[32,4096]{1,0:T(8,128)(2,1)S(1)}, u32[]{:S(2)}, u32[]{:S(2)}) collective-permute-start(bf16[32,4096]{1,0:T(8,128)(2,1)S(1)} %get-tuple-element.41), channel_id=1, source_target_pairs={{0,8},{4,12},{8,0},{12,4},{1,9},{5,13},{9,1},{13,5},{2,10},{6,14},... | collective-permute-start | bytes 786440 | tf_op jit(solution)/shard_map/ppermute | solution.py:31
  147.5 0.0 collective-permute-done.11.left
  147.5 3.4 %collective-permute-done.12.right = bf16[32,4096]{1,0:T(8,128)(2,1)S(1)} collective-permute-done((bf16[32,4096]{1,0:T(8,128)(2,1)S(1)}, bf16[32,4096]{1,0:T(8,128)(2,1)S(1)}, u32[]{:S(2)}, u32[]{:S(2)}) %collective-permute-start.12) | collective-permute-done | bytes 262176 | tf_op jit(solution)/shard_map/ppermute | solution.py:31
  150.8 2.7 %collective-permute-done.13.far = bf16[32,4096]{1,0:T(8,128)(2,1)S(1)} collective-permute-done((bf16[32,4096]{1,0:T(8,128)(2,1)S(1)}, bf16[32,4096]{1,0:T(8,128)(2,1)S(1)}, u32[]{:S(2)}, u32[]{:S(2)}) %collective-permute-start.13) | collective-permute-done | bytes 262176 | tf_op jit(solution)/shard_map/ppermute | solution.py:31
  153.5 0.1 shard_map.121
  153.6 4.2 %all-to-all-done.2.refs_2_ = bf16[4,1024,256]{2,1,0:T(8,128)(2,1)S(1)} async-done(((bf16[4,1024,256]{2,1,0:T(8,128)(2,1)}), bf16[4,1024,256]{2,1,0:T(8,128)(2,1)S(1)}, u32[]{:S(2)}, u32[]{:S(2)}) %all-to-all-start.2) | async-done | bytes 2097184 | tf_op jit(solution)/shard_map/all_to_all | solution.py:357
  157.9 1.6 shard_map.123
  159.5 8.9 %all-to-all-start.3 = ((bf16[4,256,256]{2,1,0:T(8,128)(2,1)}), bf16[4,256,256]{2,1,0:T(8,128)(2,1)S(1)}, u32[]{:S(2)}, u32[]{:S(2)}) async-start(bf16[4,256,256]{2,1,0:T(8,128)(2,1)} %shard_map.123), calls=%async_computation.3 | async-start | bytes 1048576 | tf_op jit(solution)/shard_map/all_to_all | solution.py:358
  168.4 15.9 %collective-permute-start.14 = (bf16[16,4096]{1,0:T(8,128)(2,1)S(1)}, bf16[16,4096]{1,0:T(8,128)(2,1)S(1)}, u32[]{:S(2)}, u32[]{:S(2)}) collective-permute-start(bf16[16,4096]{1,0:T(8,128)(2,1)S(1)} %get-tuple-element.43.refs_0_), channel_id=1, source_target_pairs={{0,2},{2,0},{1,3},{3,1},{4,6},{6,4},{5,7},{7,5},{8,10},{10,8},{9,1... | collective-permute-start | bytes 393224 | tf_op jit(solution)/shard_map/ppermute | solution.py:26
  184.3 19.0 %all-to-all-done.3.refs_1_ = bf16[4,256,256]{2,1,0:T(8,128)(2,1)S(1)} async-done(((bf16[4,256,256]{2,1,0:T(8,128)(2,1)}), bf16[4,256,256]{2,1,0:T(8,128)(2,1)S(1)}, u32[]{:S(2)}, u32[]{:S(2)}) %all-to-all-start.3) | async-done | bytes 524320 | tf_op jit(solution)/shard_map/all_to_all | solution.py:358
  203.3 1.3 shard_map.124
  204.6 3.3 %all-to-all-start.4 = ((bf16[4,64,256]{2,1,0:T(8,128)(2,1)}), bf16[4,64,256]{2,1,0:T(8,128)(2,1)S(1)}, u32[]{:S(2)}, u32[]{:S(2)}) async-start(bf16[4,64,256]{2,1,0:T(8,128)(2,1)} %shard_map.124), calls=%async_computation.4 | async-start | bytes 262144 | tf_op jit(solution)/shard_map/all_to_all | solution.py:359
  207.9 2.6 %collective-permute-done.14.got = bf16[16,4096]{1,0:T(8,128)(2,1)S(1)} collective-permute-done((bf16[16,4096]{1,0:T(8,128)(2,1)S(1)}, bf16[16,4096]{1,0:T(8,128)(2,1)S(1)}, u32[]{:S(2)}, u32[]{:S(2)}) %collective-permute-start.14) | collective-permute-done | bytes 131104 | tf_op jit(solution)/shard_map/ppermute | solution.py:26
  210.5 0.0 copy-done.3
  210.5 0.8 shard_map.122
  211.3 14.5 %all-to-all-done.4.parts = bf16[4,64,256]{2,1,0:T(8,128)(2,1)S(1)} async-done(((bf16[4,64,256]{2,1,0:T(8,128)(2,1)}), bf16[4,64,256]{2,1,0:T(8,128)(2,1)S(1)}, u32[]{:S(2)}, u32[]{:S(2)}) %all-to-all-start.4) | async-done | bytes 131104 | tf_op jit(solution)/shard_map/all_to_all | solution.py:359
  225.8 0.7 shard_map.125
  (6 shorter events, 0.0 us)
Async XLA Ops:
  1.5 27.8 %collective-permute-start = (bf16[64,256]{1,0:T(8,128)(2,1)S(1)}, bf16[64,256]{1,0:T(8,128)(2,1)S(1)}, u32[]{:S(2)}, u32[]{:S(2)}) collective-permute-start(bf16[64,256]{1,0:T(8,128)(2,1)S(1)} %pad_maximum_fusion.refs_4_), channel_id=1, source_target_pairs={{0,192},{16,208},{32,224},{48,240},{64,128},{80,144},{96,160},{112... | collective-permute-start | bytes 98312 | tf_op jit(solution)/shard_map/ppermute | solution.py:26
  23.8 15.0 %collective-permute-start.1 = (bf16[64,256]{1,0:T(8,128)(2,1)S(1)}, bf16[64,256]{1,0:T(8,128)(2,1)S(1)}, u32[]{:S(2)}, u32[]{:S(2)}) collective-permute-start(bf16[64,256]{1,0:T(8,128)(2,1)S(1)} %pad_maximum_fusion.refs_4_), channel_id=1, source_target_pairs={{0,128},{16,144},{32,160},{48,176},{64,192},{80,208},{96,224},{112... | collective-permute-start | bytes 98312 | tf_op jit(solution)/shard_map/ppermute | solution.py:26
  25.7 13.1 %collective-permute-start.2 = (bf16[64,256]{1,0:T(8,128)(2,1)S(1)}, bf16[64,256]{1,0:T(8,128)(2,1)S(1)}, u32[]{:S(2)}, u32[]{:S(2)}) collective-permute-start(bf16[64,256]{1,0:T(8,128)(2,1)S(1)} %pad_maximum_fusion.refs_4_), channel_id=1, source_target_pairs={{0,64},{16,80},{32,96},{48,112},{64,0},{80,16},{96,32},{112,48},{1... | collective-permute-start | bytes 98312 | tf_op jit(solution)/shard_map/ppermute | solution.py:26
  28.2 0.9 copy-start.2
  39.7 21.8 %all-to-all-start = ((bf16[4,256,256]{2,1,0:T(8,128)(2,1)}), bf16[4,256,256]{2,1,0:T(8,128)(2,1)S(1)}, u32[]{:S(2)}, u32[]{:S(2)}) async-start(bf16[4,256,256]{2,1,0:T(8,128)(2,1)} %shard_map.111), calls=%async_computation | async-start | bytes 1048576 | tf_op jit(solution)/shard_map/all_to_all | solution.py:301
  45.1 44.3 %collective-permute-start.3 = (bf16[16,4096]{1,0:T(8,128)(2,1)S(1)}, bf16[16,4096]{1,0:T(8,128)(2,1)S(1)}, u32[]{:S(2)}, u32[]{:S(2)}) collective-permute-start(bf16[16,4096]{1,0:T(8,128)(2,1)S(1)} %get-tuple-element.26.refs_0_), channel_id=1, source_target_pairs={{0,2},{2,0},{1,3},{3,1},{4,6},{6,4},{5,7},{7,5},{8,10},{10,8},{9,1... | collective-permute-start | bytes 393224 | tf_op jit(solution)/shard_map/ppermute | solution.py:26
  62.9 47.0 %all-to-all-start.1 = ((bf16[4,1024,256]{2,1,0:T(8,128)(2,1)}), bf16[4,1024,256]{2,1,0:T(8,128)(2,1)S(1)}, u32[]{:S(2)}, u32[]{:S(2)}) async-start(bf16[4,1024,256]{2,1,0:T(8,128)(2,1)} %shard_map.112.refs_0_), calls=%async_computation.1 | async-start | bytes 4194304 | tf_op jit(solution)/shard_map/all_to_all | solution.py:306
  89.4 20.6 %copy-start = (f32[256,128]{1,0:T(8,128)S(1)}, f32[256,128]{1,0:T(8,128)}, u32[]{:S(2)}) copy-start(f32[256,128]{1,0:T(8,128)} %constant.29.clone.cos) | copy-start | bytes 393220
  89.4 20.6 %copy-start.1 = (f32[256,128]{1,0:T(8,128)S(1)}, f32[256,128]{1,0:T(8,128)}, u32[]{:S(2)}) copy-start(f32[256,128]{1,0:T(8,128)} %constant.30.clone.sin) | copy-start | bytes 393220
  89.4 10.2 %collective-permute-start.4 = (bf16[32,4096]{1,0:T(8,128)(2,1)S(1)}, bf16[32,4096]{1,0:T(8,128)(2,1)S(1)}, u32[]{:S(2)}, u32[]{:S(2)}) collective-permute-start(bf16[32,4096]{1,0:T(8,128)(2,1)S(1)} %shard_map.114.refs_0_), channel_id=1, source_target_pairs={{0,4},{4,8},{8,12},{12,0},{1,5},{5,9},{9,13},{13,1},{2,6},{6,10},{... | collective-permute-start | bytes 786440 | tf_op jit(solution)/shard_map/ppermute | solution.py:31
  93.0 8.3 %collective-permute-start.5 = (bf16[32,4096]{1,0:T(8,128)(2,1)S(1)}, bf16[32,4096]{1,0:T(8,128)(2,1)S(1)}, u32[]{:S(2)}, u32[]{:S(2)}) collective-permute-start(bf16[32,4096]{1,0:T(8,128)(2,1)S(1)} %shard_map.114.refs_0_), channel_id=1, source_target_pairs={{0,12},{4,0},{8,4},{12,8},{1,13},{5,1},{9,5},{13,9},{2,14},{6,2},{... | collective-permute-start | bytes 786440 | tf_op jit(solution)/shard_map/ppermute | solution.py:31
  95.4 9.8 %collective-permute-start.6 = (bf16[32,4096]{1,0:T(8,128)(2,1)S(1)}, bf16[32,4096]{1,0:T(8,128)(2,1)S(1)}, u32[]{:S(2)}, u32[]{:S(2)}) collective-permute-start(bf16[32,4096]{1,0:T(8,128)(2,1)S(1)} %shard_map.114.refs_0_), channel_id=1, source_target_pairs={{0,8},{4,12},{8,0},{12,4},{1,9},{5,13},{9,1},{13,5},{2,10},{6,14},... | collective-permute-start | bytes 786440 | tf_op jit(solution)/shard_map/ppermute | solution.py:31
  105.2 4.7 %collective-permute-start.7 = (bf16[128,4096]{1,0:T(8,128)(2,1)S(1)}, bf16[128,4096]{1,0:T(8,128)(2,1)}, u32[]{:S(2)}, u32[]{:S(2)}) collective-permute-start(bf16[128,4096]{1,0:T(8,128)(2,1)S(1)} %shard_map.115.t0), channel_id=1, source_target_pairs={{0,1},{1,0},{2,3},{3,2},{4,5},{5,4},{6,7},{7,6},{8,9},{9,8},{10,11... | collective-permute-start | bytes 3145736 | tf_op jit(solution)/shard_map/ppermute | solution.py:26
  107.3 8.0 %copy-start.4 = (bf16[256,128]{1,0:T(8,128)(2,1)S(1)}, bf16[256,128]{1,0:T(8,128)(2,1)}, u32[]{:S(2)}) copy-start(bf16[256,128]{1,0:T(8,128)(2,1)} %d_ctx_ref.1) | copy-start | bytes 196612
  112.2 3.1 %collective-permute-start.8 = (bf16[256,128]{1,0:T(8,128)(2,1)S(1)}, bf16[256,128]{1,0:T(8,128)(2,1)S(1)}, u32[]{:S(2)}, u32[]{:S(2)}) collective-permute-start(bf16[256,128]{1,0:T(8,128)(2,1)S(1)} %get-tuple-element.28.mine_ref), channel_id=1, source_target_pairs={{0,1},{1,0},{2,3},{3,2},{4,5},{5,4},{6,7},{7,6},{8,9},{9,8},{10,11... | collective-permute-start | bytes 196616 | tf_op jit(solution)/shard_map/ppermute | solution.py:26
  117.2 3.1 %collective-permute-start.9 = (bf16[256,128]{1,0:T(8,128)(2,1)S(1)}, bf16[256,128]{1,0:T(8,128)(2,1)S(1)}, u32[]{:S(2)}, u32[]{:S(2)}) collective-permute-start(bf16[256,128]{1,0:T(8,128)(2,1)S(1)} %get-tuple-element.33), channel_id=1, source_target_pairs={{0,1},{1,0},{2,3},{3,2},{4,5},{5,4},{6,7},{7,6},{8,9},{9,8},{10,11... | collective-permute-start | bytes 196616 | tf_op jit(solution)/shard_map/ppermute | solution.py:26
  121.9 1.0 copy-start.5
  126.9 30.9 %all-to-all-start.2 = ((bf16[4,1024,256]{2,1,0:T(8,128)(2,1)}), bf16[4,1024,256]{2,1,0:T(8,128)(2,1)S(1)}, u32[]{:S(2)}, u32[]{:S(2)}) async-start(bf16[4,1024,256]{2,1,0:T(8,128)(2,1)} %shard_map.119.after), calls=%async_computation.2 | async-start | bytes 4194304 | tf_op jit(solution)/shard_map/all_to_all | solution.py:357
  131.2 4.8 %collective-permute-start.10 = (bf16[128,4096]{1,0:T(8,128)(2,1)}, bf16[128,4096]{1,0:T(8,128)(2,1)S(1)}, u32[]{:S(2)}, u32[]{:S(2)}) collective-permute-start(bf16[128,4096]{1,0:T(8,128)(2,1)} %copy-done.5), channel_id=1, source_target_pairs={{0,1},{1,0},{2,3},{3,2},{4,5},{5,4},{6,7},{7,6},{8,9},{9,8},{10,11... | collective-permute-start | bytes 3145736 | tf_op jit(solution)/shard_map/ppermute | solution.py:26
  136.2 11.3 %collective-permute-start.11 = (bf16[32,4096]{1,0:T(8,128)(2,1)S(1)}, bf16[32,4096]{1,0:T(8,128)(2,1)S(1)}, u32[]{:S(2)}, u32[]{:S(2)}) collective-permute-start(bf16[32,4096]{1,0:T(8,128)(2,1)S(1)} %get-tuple-element.39), channel_id=1, source_target_pairs={{0,12},{4,0},{8,4},{12,8},{1,13},{5,1},{9,5},{13,9},{2,14},{6,2},{... | collective-permute-start | bytes 786440 | tf_op jit(solution)/shard_map/ppermute | solution.py:31
  139.8 11.1 %collective-permute-start.12 = (bf16[32,4096]{1,0:T(8,128)(2,1)S(1)}, bf16[32,4096]{1,0:T(8,128)(2,1)S(1)}, u32[]{:S(2)}, u32[]{:S(2)}) collective-permute-start(bf16[32,4096]{1,0:T(8,128)(2,1)S(1)} %get-tuple-element.40), channel_id=1, source_target_pairs={{0,4},{4,8},{8,12},{12,0},{1,5},{5,9},{9,13},{13,1},{2,6},{6,10},{... | collective-permute-start | bytes 786440 | tf_op jit(solution)/shard_map/ppermute | solution.py:31
  142.1 11.4 %collective-permute-start.13 = (bf16[32,4096]{1,0:T(8,128)(2,1)S(1)}, bf16[32,4096]{1,0:T(8,128)(2,1)S(1)}, u32[]{:S(2)}, u32[]{:S(2)}) collective-permute-start(bf16[32,4096]{1,0:T(8,128)(2,1)S(1)} %get-tuple-element.41), channel_id=1, source_target_pairs={{0,8},{4,12},{8,0},{12,4},{1,9},{5,13},{9,1},{13,5},{2,10},{6,14},... | collective-permute-start | bytes 786440 | tf_op jit(solution)/shard_map/ppermute | solution.py:31
  157.9 52.6 %copy-start.3 = (bf16[16,4096]{1,0:T(8,128)(2,1)S(1)}, bf16[16,4096]{1,0:T(8,128)(2,1)}, u32[]{:S(2)}) copy-start(bf16[16,4096]{1,0:T(8,128)(2,1)} %tokens.3) | copy-start | bytes 393220
  159.5 43.9 %all-to-all-start.3 = ((bf16[4,256,256]{2,1,0:T(8,128)(2,1)}), bf16[4,256,256]{2,1,0:T(8,128)(2,1)S(1)}, u32[]{:S(2)}, u32[]{:S(2)}) async-start(bf16[4,256,256]{2,1,0:T(8,128)(2,1)} %shard_map.123), calls=%async_computation.3 | async-start | bytes 1048576 | tf_op jit(solution)/shard_map/all_to_all | solution.py:358
  168.4 42.1 %collective-permute-start.14 = (bf16[16,4096]{1,0:T(8,128)(2,1)S(1)}, bf16[16,4096]{1,0:T(8,128)(2,1)S(1)}, u32[]{:S(2)}, u32[]{:S(2)}) collective-permute-start(bf16[16,4096]{1,0:T(8,128)(2,1)S(1)} %get-tuple-element.43.refs_0_), channel_id=1, source_target_pairs={{0,2},{2,0},{1,3},{3,1},{4,6},{6,4},{5,7},{7,5},{8,10},{10,8},{9,1... | collective-permute-start | bytes 393224 | tf_op jit(solution)/shard_map/ppermute | solution.py:26
  204.6 21.2 %all-to-all-start.4 = ((bf16[4,64,256]{2,1,0:T(8,128)(2,1)}), bf16[4,64,256]{2,1,0:T(8,128)(2,1)S(1)}, u32[]{:S(2)}, u32[]{:S(2)}) async-start(bf16[4,64,256]{2,1,0:T(8,128)(2,1)} %shard_map.124), calls=%async_computation.4 | async-start | bytes 262144 | tf_op jit(solution)/shard_map/all_to_all | solution.py:359

commit v9 on v8

--- a/solution.py
+++ b/solution.py
@@ -70,7 +70,7 @@
 
 
 def sequence_at(place, ids):
-    co, yq, zh = place // 8, place // 2 % 4, place % 2
+    co, zh, yq = place // 8, place // 4 % 2, place % 4
     y = (ids[2] + SHIFTS[yq] + 4) % 4
     return y * 4 + (ids[3] ^ zh) * 2 + (ids[4] ^ co)
 
@@ -98,10 +98,12 @@
 
 
 def part_kernel(after, mine, got, *outs):
-    count = outs[0].shape[0]
+    count = outs[0].shape[0] // 2
     for place, out in enumerate(outs):
-        cut = slice(place * count, (place + 1) * count)
-        out[...] = added(mine[cut, :], got[cut, :]).astype(out.dtype)
+        for zh in range(2):
+            at = (zh * len(outs) + place) * count
+            cut = slice(at, at + count)
+            out[zh * count : (zh + 1) * count, :] = added(mine[cut, :], got[cut, :]).astype(out.dtype)
 
 
 def pair_kernel(own, left, right, far, keep_out, send_out):
@@ -300,9 +302,10 @@
     near = copies(SIZES[2], *spread(weights, ZL, RADIX)[::-1], weights, after=(normed,))
     near = lax.all_to_all(near, "zb", 0, 0)
     whole = copies(SIZES[0], near.reshape(-1, near.shape[2]))
-    far = rows(flipped(normed, "zh", 1), after=(whole,), flops=40 * product)
-    pair = rows(normed, far)
-    t0 = rows(pair, *ring_gather(pair, "y"))
+    own = rows(normed, after=(whole,))
+    own_ring = ring_gather(own, "y")
+    far = rows(flipped(normed, "zh", 1), after=own_ring, flops=40 * product)
+    t0 = rows(own, *own_ring, far, *ring_gather(far, "y"))
     w_all = lax.all_to_all(whole, "x", 0, 0)
     t1 = flipped(t0, "co", 1)
 

time: 228 us -> 230 us (level)
  the two profiles are of different devices: /device:TPU:8 before, /device:TPU:1 now
where the time goes in v9:
time: 230 us; the launch traced here: 229 us
  starting transfers between devices  142 us (62%)
  waiting for transfers between devices  62.9 us (27%)
  Pallas kernels  16.9 us (7%)
  local copies, waits for them, and re-layouts  6.01 us (3%)
    ppermute x9, starting transfers between devices, flipped(): return lax.ppermute(value, axis, [(s, s ^ mask) for s in range(size)])  89.9 us
    ppermute x9, waiting for transfers between devices, flipped(): return lax.ppermute(value, axis, [(s, s ^ mask) for s in range(size)])  35.6 us
    ppermute x9, starting transfers between devices, shifted(): lax.ppermute(value, axis, [(s, (s + step) % size) for s in range(size)])  29.2 us
    pallas_call x16, Pallas kernels, call(): pl.pallas_call(kernel, out_shape=[jax.ShapeDtypeStruct(s, t) for s, t in...  16.9 us
    ppermute x9, waiting for transfers between devices, shifted(): lax.ppermute(value, axis, [(s, (s + step) % size) for s in range(size)])  13.1 us
    all_to_all x1, waiting for transfers between devices, shards(): grads = lax.all_to_all(far, 'za', 0, 0)  12.1 us
    unnamed x24, local copies, waits for them, and re-layouts  5.92 us
    all_to_all x1, starting transfers between devices, shards(): far = scatter_stack(ids, RADIX, lax.all_to_all(near, 'zb', 0, 0))  5.57 us
  transfers between devices with their start and end apart: 23, of which 13 were waited for; matrix products, arithmetic and copies ran while one was open for 0% of the time, Pallas kernels for 2%

profile of v9, /device:TPU:1, one launch (start us, length us, event | category | flops | bytes accessed | tf_op | source)
XLA Modules:
  0.0 229.3 jit_solution(2645671575811916511)
XLA Ops:
  0.6 0.8 pad_maximum_fusion.refs_4_
  1.5 22.9 %collective-permute-start = (bf16[64,256]{1,0:T(8,128)(2,1)S(1)}, bf16[64,256]{1,0:T(8,128)(2,1)S(1)}, u32[]{:S(2)}, u32[]{:S(2)}) collective-permute-start(bf16[64,256]{1,0:T(8,128)(2,1)S(1)} %pad_maximum_fusion.refs_4_), channel_id=1, source_target_pairs={{0,192},{16,208},{32,224},{48,240},{64,128},{80,144},{96,160},{112... | collective-permute-start | bytes 98312 | tf_op jit(solution)/shard_map/ppermute | solution.py:26
  24.4 1.9 collective-permute-start.1
  26.3 2.2 collective-permute-start.2
  28.5 0.0 copy-start.8
  28.5 0.9 copy-done.8
  29.4 0.1 shard_map.110
  29.5 8.3 %collective-permute-done.1.refs_2_ = bf16[64,256]{1,0:T(8,128)(2,1)S(1)} collective-permute-done((bf16[64,256]{1,0:T(8,128)(2,1)S(1)}, bf16[64,256]{1,0:T(8,128)(2,1)S(1)}, u32[]{:S(2)}, u32[]{:S(2)}) %collective-permute-start.1) | collective-permute-done | bytes 32800 | tf_op jit(solution)/shard_map/ppermute | solution.py:26
  37.9 0.0 collective-permute-done.2.refs_3_
  37.9 0.8 shard_map.111
  38.7 5.5 %all-to-all-start = ((bf16[4,256,256]{2,1,0:T(8,128)(2,1)}), bf16[4,256,256]{2,1,0:T(8,128)(2,1)S(1)}, u32[]{:S(2)}, u32[]{:S(2)}) async-start(bf16[4,256,256]{2,1,0:T(8,128)(2,1)} %shard_map.111), calls=%async_computation | async-start | bytes 1048576 | tf_op jit(solution)/shard_map/all_to_all | solution.py:303
  44.2 17.8 %collective-permute-start.6 = (bf16[16,4096]{1,0:T(8,128)(2,1)S(1)}, bf16[16,4096]{1,0:T(8,128)(2,1)S(1)}, u32[]{:S(2)}, u32[]{:S(2)}) collective-permute-start(bf16[16,4096]{1,0:T(8,128)(2,1)S(1)} %get-tuple-element.26.refs_0_.refs_1_), channel_id=1, source_target_pairs={{0,2},{2,0},{1,3},{3,1},{4,6},{6,4},{5,7},{7,5},{8,10},{10,8},{9,1... | collective-permute-start | bytes 393224 | tf_op jit(solution)/shard_map/ppermute | solution.py:26
  62.1 1.5 shard_map.112.refs_0_
  63.5 3.2 %collective-permute-start.3 = (bf16[16,4096]{1,0:T(8,128)(2,1)S(1)}, bf16[16,4096]{1,0:T(8,128)(2,1)S(1)}, u32[]{:S(2)}, u32[]{:S(2)}) collective-permute-start(bf16[16,4096]{1,0:T(8,128)(2,1)S(1)} %shard_map.113.refs_0_), channel_id=1, source_target_pairs={{0,4},{4,8},{8,12},{12,0},{1,5},{5,9},{9,13},{13,1},{2,6},{6,10},{... | collective-permute-start | bytes 393224 | tf_op jit(solution)/shard_map/ppermute | solution.py:31
  66.8 3.4 %collective-permute-start.4 = (bf16[16,4096]{1,0:T(8,128)(2,1)S(1)}, bf16[16,4096]{1,0:T(8,128)(2,1)S(1)}, u32[]{:S(2)}, u32[]{:S(2)}) collective-permute-start(bf16[16,4096]{1,0:T(8,128)(2,1)S(1)} %shard_map.113.refs_0_), channel_id=1, source_target_pairs={{0,12},{4,0},{8,4},{12,8},{1,13},{5,1},{9,5},{13,9},{2,14},{6,2},{... | collective-permute-start | bytes 393224 | tf_op jit(solution)/shard_map/ppermute | solution.py:31
  70.1 3.5 %collective-permute-start.5 = (bf16[16,4096]{1,0:T(8,128)(2,1)S(1)}, bf16[16,4096]{1,0:T(8,128)(2,1)S(1)}, u32[]{:S(2)}, u32[]{:S(2)}) collective-permute-start(bf16[16,4096]{1,0:T(8,128)(2,1)S(1)} %shard_map.113.refs_0_), channel_id=1, source_target_pairs={{0,8},{4,12},{8,0},{12,4},{1,9},{5,13},{9,1},{13,5},{2,10},{6,14},... | collective-permute-start | bytes 393224 | tf_op jit(solution)/shard_map/ppermute | solution.py:31
  73.7 4.0 %all-to-all-start.1 = ((bf16[4,1024,256]{2,1,0:T(8,128)(2,1)}), bf16[4,1024,256]{2,1,0:T(8,128)(2,1)S(1)}, u32[]{:S(2)}, u32[]{:S(2)}) async-start(bf16[4,1024,256]{2,1,0:T(8,128)(2,1)} %shard_map.112.refs_0_), calls=%async_computation.1 | async-start | bytes 4194304 | tf_op jit(solution)/shard_map/all_to_all | solution.py:309
  77.7 2.3 collective-permute-done.6.refs_3_
  80.0 0.0 collective-permute-done.3.refs_0_.refs_1_
  80.0 0.0 collective-permute-done.4.refs_1_.refs_2_
  80.0 0.6 copy-done.4
  80.6 0.1 copy-done.6
  80.7 0.7 copy-done.2
  81.4 3.3 %collective-permute-start.7 = (bf16[16,4096]{1,0:T(8,128)(2,1)S(1)}, bf16[16,4096]{1,0:T(8,128)(2,1)S(1)}, u32[]{:S(2)}, u32[]{:S(2)}) collective-permute-start(bf16[16,4096]{1,0:T(8,128)(2,1)S(1)} %shard_map.114.refs_4_), channel_id=1, source_target_pairs={{0,4},{4,8},{8,12},{12,0},{1,5},{5,9},{9,13},{13,1},{2,6},{6,10},{... | collective-permute-start | bytes 393224 | tf_op jit(solution)/shard_map/ppermute | solution.py:31
  84.7 3.4 %collective-permute-start.8 = (bf16[16,4096]{1,0:T(8,128)(2,1)S(1)}, bf16[16,4096]{1,0:T(8,128)(2,1)S(1)}, u32[]{:S(2)}, u32[]{:S(2)}) collective-permute-start(bf16[16,4096]{1,0:T(8,128)(2,1)S(1)} %shard_map.114.refs_4_), channel_id=1, source_target_pairs={{0,12},{4,0},{8,4},{12,8},{1,13},{5,1},{9,5},{13,9},{2,14},{6,2},{... | collective-permute-start | bytes 393224 | tf_op jit(solution)/shard_map/ppermute | solution.py:31
  88.1 3.5 %collective-permute-start.9 = (bf16[16,4096]{1,0:T(8,128)(2,1)S(1)}, bf16[16,4096]{1,0:T(8,128)(2,1)S(1)}, u32[]{:S(2)}, u32[]{:S(2)}) collective-permute-start(bf16[16,4096]{1,0:T(8,128)(2,1)S(1)} %shard_map.114.refs_4_), channel_id=1, source_target_pairs={{0,8},{4,12},{8,0},{12,4},{1,9},{5,13},{9,1},{13,5},{2,10},{6,14},... | collective-permute-start | bytes 393224 | tf_op jit(solution)/shard_map/ppermute | solution.py:31
  91.6 3.6 %collective-permute-done.9.refs_7_ = bf16[16,4096]{1,0:T(8,128)(2,1)S(1)} collective-permute-done((bf16[16,4096]{1,0:T(8,128)(2,1)S(1)}, bf16[16,4096]{1,0:T(8,128)(2,1)S(1)}, u32[]{:S(2)}, u32[]{:S(2)}) %collective-permute-start.9) | collective-permute-done | bytes 131104 | tf_op jit(solution)/shard_map/ppermute | solution.py:31
  95.3 0.9 copy-done.3
  96.2 0.9 copy-done.5
  97.1 0.9 copy-done.7
  98.0 0.1 shard_map.115.t0
  98.1 14.3 %collective-permute-start.10 = (bf16[128,4096]{1,0:T(8,128)(2,1)S(1)}, bf16[128,4096]{1,0:T(8,128)(2,1)}, u32[]{:S(2)}, u32[]{:S(2)}) collective-permute-start(bf16[128,4096]{1,0:T(8,128)(2,1)S(1)} %shard_map.115.t0), channel_id=1, source_target_pairs={{0,1},{1,0},{2,3},{3,2},{4,5},{5,4},{6,7},{7,6},{8,9},{9,8},{10,11... | collective-permute-start | bytes 3145736 | tf_op jit(solution)/shard_map/ppermute | solution.py:26
  112.4 0.1 stack.23.ids.refs_1_.refs_0_
  112.5 2.3 %collective-permute-done.10.t1 = bf16[128,4096]{1,0:T(8,128)(2,1)} collective-permute-done((bf16[128,4096]{1,0:T(8,128)(2,1)S(1)}, bf16[128,4096]{1,0:T(8,128)(2,1)}, u32[]{:S(2)}, u32[]{:S(2)}) %collective-permute-start.10) | collective-permute-done | bytes 1048608 | tf_op jit(solution)/shard_map/ppermute | solution.py:26
  114.8 2.2 shard_map.116
  117.0 2.3 collective-permute-start.11
  119.3 0.9 collective-permute-done.11.other_ref
  120.2 1.9 shard_map.117
  122.1 2.2 collective-permute-start.12
  124.3 0.9 collective-permute-done.12.got_ref
  125.2 1.5 shard_map.118
  126.7 1.0 copy-done.11
  127.7 4.1 %shard_map.119.after = bf16[4,1024,256]{2,1,0:T(8,128)(2,1)} custom-call(s32[5]{0:T(128)S(1)} %stack.23.ids.refs_1_.refs_0_, bf16[128,4096]{1,0:T(8,128)(2,1)S(1)} %shard_map.115.t0, bf16[128,4096]{1,0:T(8,128)(2,1)} %collective-permute-done.10.t1, bf16[256,256]{1,0:T(8,128)(2,1)S(1)} %get-tuple-element.35.dj_ref), custom_call_target="tpu_custom_call" | custom-call | flops 536870912 | bytes 4194304 | tf_op jit(solution)/shard_map/pallas_call | solution.py:251
  131.8 4.1 %all-to-all-start.2 = ((bf16[4,1024,256]{2,1,0:T(8,128)(2,1)}), bf16[4,1024,256]{2,1,0:T(8,128)(2,1)S(1)}, u32[]{:S(2)}, u32[]{:S(2)}) async-start(bf16[4,1024,256]{2,1,0:T(8,128)(2,1)} %shard_map.119.after), calls=%async_computation.2 | async-start | bytes 4194304 | tf_op jit(solution)/shard_map/all_to_all | solution.py:360
  135.9 2.5 %collective-permute-start.13 = (bf16[128,4096]{1,0:T(8,128)(2,1)}, bf16[128,4096]{1,0:T(8,128)(2,1)S(1)}, u32[]{:S(2)}, u32[]{:S(2)}) collective-permute-start(bf16[128,4096]{1,0:T(8,128)(2,1)} %copy-done.11), channel_id=1, source_target_pairs={{0,1},{1,0},{2,3},{3,2},{4,5},{5,4},{6,7},{7,6},{8,9},{9,8},{10,11... | collective-permute-start | bytes 3145736 | tf_op jit(solution)/shard_map/ppermute | solution.py:26
  138.4 2.5 %collective-permute-done.13.got = bf16[128,4096]{1,0:T(8,128)(2,1)S(1)} collective-permute-done((bf16[128,4096]{1,0:T(8,128)(2,1)}, bf16[128,4096]{1,0:T(8,128)(2,1)S(1)}, u32[]{:S(2)}, u32[]{:S(2)}) %collective-permute-start.13) | collective-permute-done | bytes 1048608 | tf_op jit(solution)/shard_map/ppermute | solution.py:26
  140.9 0.2 shard_map.120
  141.1 3.4 %collective-permute-start.14 = (bf16[32,4096]{1,0:T(8,128)(2,1)S(1)}, bf16[32,4096]{1,0:T(8,128)(2,1)S(1)}, u32[]{:S(2)}, u32[]{:S(2)}) collective-permute-start(bf16[32,4096]{1,0:T(8,128)(2,1)S(1)} %get-tuple-element.39), channel_id=1, source_target_pairs={{0,12},{4,0},{8,4},{12,8},{1,13},{5,1},{9,5},{13,9},{2,14},{6,2},{... | collective-permute-start | bytes 786440 | tf_op jit(solution)/shard_map/ppermute | solution.py:31
  144.6 1.9 collective-permute-start.15
  146.5 3.5 %collective-permute-start.16 = (bf16[32,4096]{1,0:T(8,128)(2,1)S(1)}, bf16[32,4096]{1,0:T(8,128)(2,1)S(1)}, u32[]{:S(2)}, u32[]{:S(2)}) collective-permute-start(bf16[32,4096]{1,0:T(8,128)(2,1)S(1)} %get-tuple-element.41), channel_id=1, source_target_pairs={{0,8},{4,12},{8,0},{12,4},{1,9},{5,13},{9,1},{13,5},{2,10},{6,14},... | collective-permute-start | bytes 786440 | tf_op jit(solution)/shard_map/ppermute | solution.py:31
  150.1 0.5 collective-permute-done.14.left
  150.6 5.3 %collective-permute-done.15.right = bf16[32,4096]{1,0:T(8,128)(2,1)S(1)} collective-permute-done((bf16[32,4096]{1,0:T(8,128)(2,1)S(1)}, bf16[32,4096]{1,0:T(8,128)(2,1)S(1)}, u32[]{:S(2)}, u32[]{:S(2)}) %collective-permute-start.15) | collective-permute-done | bytes 262176 | tf_op jit(solution)/shard_map/ppermute | solution.py:31
  155.9 3.6 %collective-permute-done.16.far = bf16[32,4096]{1,0:T(8,128)(2,1)S(1)} collective-permute-done((bf16[32,4096]{1,0:T(8,128)(2,1)S(1)}, bf16[32,4096]{1,0:T(8,128)(2,1)S(1)}, u32[]{:S(2)}, u32[]{:S(2)}) %collective-permute-start.16) | collective-permute-done | bytes 262176 | tf_op jit(solution)/shard_map/ppermute | solution.py:31
  159.5 0.1 shard_map.121
  159.6 2.0 all-to-all-done.2.refs_2_
  161.7 1.6 shard_map.123
  163.3 5.6 %all-to-all-start.3 = ((bf16[4,256,256]{2,1,0:T(8,128)(2,1)}), bf16[4,256,256]{2,1,0:T(8,128)(2,1)S(1)}, u32[]{:S(2)}, u32[]{:S(2)}) async-start(bf16[4,256,256]{2,1,0:T(8,128)(2,1)} %shard_map.123), calls=%async_computation.3 | async-start | bytes 1048576 | tf_op jit(solution)/shard_map/all_to_all | solution.py:361
  168.9 23.7 %collective-permute-start.17 = (bf16[16,4096]{1,0:T(8,128)(2,1)S(1)}, bf16[16,4096]{1,0:T(8,128)(2,1)S(1)}, u32[]{:S(2)}, u32[]{:S(2)}) collective-permute-start(bf16[16,4096]{1,0:T(8,128)(2,1)S(1)} %get-tuple-element.43.refs_0_), channel_id=1, source_target_pairs={{0,2},{2,0},{1,3},{3,1},{4,6},{6,4},{5,7},{7,5},{8,10},{10,8},{9,1... | collective-permute-start | bytes 393224 | tf_op jit(solution)/shard_map/ppermute | solution.py:26
  192.6 1.3 shard_map.124
  193.9 3.3 %all-to-all-start.4 = ((bf16[4,64,256]{2,1,0:T(8,128)(2,1)}), bf16[4,64,256]{2,1,0:T(8,128)(2,1)S(1)}, u32[]{:S(2)}, u32[]{:S(2)}) async-start(bf16[4,64,256]{2,1,0:T(8,128)(2,1)} %shard_map.124), calls=%async_computation.4 | async-start | bytes 262144 | tf_op jit(solution)/shard_map/all_to_all | solution.py:362
  197.2 18.4 %collective-permute-done.17.got = bf16[16,4096]{1,0:T(8,128)(2,1)S(1)} collective-permute-done((bf16[16,4096]{1,0:T(8,128)(2,1)S(1)}, bf16[16,4096]{1,0:T(8,128)(2,1)S(1)}, u32[]{:S(2)}, u32[]{:S(2)}) %collective-permute-start.17) | collective-permute-done | bytes 131104 | tf_op jit(solution)/shard_map/ppermute | solution.py:26
  215.6 0.8 shard_map.122
  216.5 12.1 %all-to-all-done.4.parts = bf16[4,64,256]{2,1,0:T(8,128)(2,1)S(1)} async-done(((bf16[4,64,256]{2,1,0:T(8,128)(2,1)}), bf16[4,64,256]{2,1,0:T(8,128)(2,1)S(1)}, u32[]{:S(2)}, u32[]{:S(2)}) %all-to-all-start.4) | async-done | bytes 131104 | tf_op jit(solution)/shard_map/all_to_all | solution.py:362
  228.6 0.7 shard_map.125
  (24 shorter events, 0.1 us)
Async XLA Ops:
  1.5 28.1 %collective-permute-start = (bf16[64,256]{1,0:T(8,128)(2,1)S(1)}, bf16[64,256]{1,0:T(8,128)(2,1)S(1)}, u32[]{:S(2)}, u32[]{:S(2)}) collective-permute-start(bf16[64,256]{1,0:T(8,128)(2,1)S(1)} %pad_maximum_fusion.refs_4_), channel_id=1, source_target_pairs={{0,192},{16,208},{32,224},{48,240},{64,128},{80,144},{96,160},{112... | collective-permute-start | bytes 98312 | tf_op jit(solution)/shard_map/ppermute | solution.py:26
  24.4 13.5 %collective-permute-start.1 = (bf16[64,256]{1,0:T(8,128)(2,1)S(1)}, bf16[64,256]{1,0:T(8,128)(2,1)S(1)}, u32[]{:S(2)}, u32[]{:S(2)}) collective-permute-start(bf16[64,256]{1,0:T(8,128)(2,1)S(1)} %pad_maximum_fusion.refs_4_), channel_id=1, source_target_pairs={{0,128},{16,144},{32,160},{48,176},{64,192},{80,208},{96,224},{112... | collective-permute-start | bytes 98312 | tf_op jit(solution)/shard_map/ppermute | solution.py:26
  26.3 11.6 %collective-permute-start.2 = (bf16[64,256]{1,0:T(8,128)(2,1)S(1)}, bf16[64,256]{1,0:T(8,128)(2,1)S(1)}, u32[]{:S(2)}, u32[]{:S(2)}) collective-permute-start(bf16[64,256]{1,0:T(8,128)(2,1)S(1)} %pad_maximum_fusion.refs_4_), channel_id=1, source_target_pairs={{0,64},{16,80},{32,96},{48,112},{64,0},{80,16},{96,32},{112,48},{1... | collective-permute-start | bytes 98312 | tf_op jit(solution)/shard_map/ppermute | solution.py:26
  28.5 0.9 copy-start.8
  38.7 23.3 %all-to-all-start = ((bf16[4,256,256]{2,1,0:T(8,128)(2,1)}), bf16[4,256,256]{2,1,0:T(8,128)(2,1)S(1)}, u32[]{:S(2)}, u32[]{:S(2)}) async-start(bf16[4,256,256]{2,1,0:T(8,128)(2,1)} %shard_map.111), calls=%async_computation | async-start | bytes 1048576 | tf_op jit(solution)/shard_map/all_to_all | solution.py:303
  44.2 35.8 %collective-permute-start.6 = (bf16[16,4096]{1,0:T(8,128)(2,1)S(1)}, bf16[16,4096]{1,0:T(8,128)(2,1)S(1)}, u32[]{:S(2)}, u32[]{:S(2)}) collective-permute-start(bf16[16,4096]{1,0:T(8,128)(2,1)S(1)} %get-tuple-element.26.refs_0_.refs_1_), channel_id=1, source_target_pairs={{0,2},{2,0},{1,3},{3,1},{4,6},{6,4},{5,7},{7,5},{8,10},{10,8},{9,1... | collective-permute-start | bytes 393224 | tf_op jit(solution)/shard_map/ppermute | solution.py:26
  63.5 16.4 %collective-permute-start.3 = (bf16[16,4096]{1,0:T(8,128)(2,1)S(1)}, bf16[16,4096]{1,0:T(8,128)(2,1)S(1)}, u32[]{:S(2)}, u32[]{:S(2)}) collective-permute-start(bf16[16,4096]{1,0:T(8,128)(2,1)S(1)} %shard_map.113.refs_0_), channel_id=1, source_target_pairs={{0,4},{4,8},{8,12},{12,0},{1,5},{5,9},{9,13},{13,1},{2,6},{6,10},{... | collective-permute-start | bytes 393224 | tf_op jit(solution)/shard_map/ppermute | solution.py:31
  66.8 13.2 %collective-permute-start.4 = (bf16[16,4096]{1,0:T(8,128)(2,1)S(1)}, bf16[16,4096]{1,0:T(8,128)(2,1)S(1)}, u32[]{:S(2)}, u32[]{:S(2)}) collective-permute-start(bf16[16,4096]{1,0:T(8,128)(2,1)S(1)} %shard_map.113.refs_0_), channel_id=1, source_target_pairs={{0,12},{4,0},{8,4},{12,8},{1,13},{5,1},{9,5},{13,9},{2,14},{6,2},{... | collective-permute-start | bytes 393224 | tf_op jit(solution)/shard_map/ppermute | solution.py:31
  70.1 9.9 %collective-permute-start.5 = (bf16[16,4096]{1,0:T(8,128)(2,1)S(1)}, bf16[16,4096]{1,0:T(8,128)(2,1)S(1)}, u32[]{:S(2)}, u32[]{:S(2)}) collective-permute-start(bf16[16,4096]{1,0:T(8,128)(2,1)S(1)} %shard_map.113.refs_0_), channel_id=1, source_target_pairs={{0,8},{4,12},{8,0},{12,4},{1,9},{5,13},{9,1},{13,5},{2,10},{6,14},... | collective-permute-start | bytes 393224 | tf_op jit(solution)/shard_map/ppermute | solution.py:31
  73.7 41.1 %all-to-all-start.1 = ((bf16[4,1024,256]{2,1,0:T(8,128)(2,1)}), bf16[4,1024,256]{2,1,0:T(8,128)(2,1)S(1)}, u32[]{:S(2)}, u32[]{:S(2)}) async-start(bf16[4,1024,256]{2,1,0:T(8,128)(2,1)} %shard_map.112.refs_0_), calls=%async_computation.1 | async-start | bytes 4194304 | tf_op jit(solution)/shard_map/all_to_all | solution.py:309
  80.0 0.6 copy-start.4
  80.0 0.7 copy-start.6
  80.7 0.7 copy-start.2
  81.4 33.4 %copy-start = (f32[256,128]{1,0:T(8,128)S(1)}, f32[256,128]{1,0:T(8,128)}, u32[]{:S(2)}) copy-start(f32[256,128]{1,0:T(8,128)} %constant.29.clone.cos) | copy-start | bytes 393220
  81.4 33.4 %copy-start.1 = (f32[256,128]{1,0:T(8,128)S(1)}, f32[256,128]{1,0:T(8,128)}, u32[]{:S(2)}) copy-start(f32[256,128]{1,0:T(8,128)} %constant.30.clone.sin) | copy-start | bytes 393220
  81.4 10.3 %collective-permute-start.7 = (bf16[16,4096]{1,0:T(8,128)(2,1)S(1)}, bf16[16,4096]{1,0:T(8,128)(2,1)S(1)}, u32[]{:S(2)}, u32[]{:S(2)}) collective-permute-start(bf16[16,4096]{1,0:T(8,128)(2,1)S(1)} %shard_map.114.refs_4_), channel_id=1, source_target_pairs={{0,4},{4,8},{8,12},{12,0},{1,5},{5,9},{9,13},{13,1},{2,6},{6,10},{... | collective-permute-start | bytes 393224 | tf_op jit(solution)/shard_map/ppermute | solution.py:31
  84.7 6.9 %collective-permute-start.8 = (bf16[16,4096]{1,0:T(8,128)(2,1)S(1)}, bf16[16,4096]{1,0:T(8,128)(2,1)S(1)}, u32[]{:S(2)}, u32[]{:S(2)}) collective-permute-start(bf16[16,4096]{1,0:T(8,128)(2,1)S(1)} %shard_map.114.refs_4_), channel_id=1, source_target_pairs={{0,12},{4,0},{8,4},{12,8},{1,13},{5,1},{9,5},{13,9},{2,14},{6,2},{... | collective-permute-start | bytes 393224 | tf_op jit(solution)/shard_map/ppermute | solution.py:31
  88.1 7.2 %collective-permute-start.9 = (bf16[16,4096]{1,0:T(8,128)(2,1)S(1)}, bf16[16,4096]{1,0:T(8,128)(2,1)S(1)}, u32[]{:S(2)}, u32[]{:S(2)}) collective-permute-start(bf16[16,4096]{1,0:T(8,128)(2,1)S(1)} %shard_map.114.refs_4_), channel_id=1, source_target_pairs={{0,8},{4,12},{8,0},{12,4},{1,9},{5,13},{9,1},{13,5},{2,10},{6,14},... | collective-permute-start | bytes 393224 | tf_op jit(solution)/shard_map/ppermute | solution.py:31
  95.3 0.9 copy-start.3
  96.2 0.9 copy-start.5
  97.1 0.9 copy-start.7
  98.1 16.7 %collective-permute-start.10 = (bf16[128,4096]{1,0:T(8,128)(2,1)S(1)}, bf16[128,4096]{1,0:T(8,128)(2,1)}, u32[]{:S(2)}, u32[]{:S(2)}) collective-permute-start(bf16[128,4096]{1,0:T(8,128)(2,1)S(1)} %shard_map.115.t0), channel_id=1, source_target_pairs={{0,1},{1,0},{2,3},{3,2},{4,5},{5,4},{6,7},{7,6},{8,9},{9,8},{10,11... | collective-permute-start | bytes 3145736 | tf_op jit(solution)/shard_map/ppermute | solution.py:26
  112.5 7.7 %copy-start.10 = (bf16[256,128]{1,0:T(8,128)(2,1)S(1)}, bf16[256,128]{1,0:T(8,128)(2,1)}, u32[]{:S(2)}) copy-start(bf16[256,128]{1,0:T(8,128)(2,1)} %d_ctx_ref.1) | copy-start | bytes 196612
  117.0 3.2 %collective-permute-start.11 = (bf16[256,128]{1,0:T(8,128)(2,1)S(1)}, bf16[256,128]{1,0:T(8,128)(2,1)S(1)}, u32[]{:S(2)}, u32[]{:S(2)}) collective-permute-start(bf16[256,128]{1,0:T(8,128)(2,1)S(1)} %get-tuple-element.28.mine_ref), channel_id=1, source_target_pairs={{0,1},{1,0},{2,3},{3,2},{4,5},{5,4},{6,7},{7,6},{8,9},{9,8},{10,11... | collective-permute-start | bytes 196616 | tf_op jit(solution)/shard_map/ppermute | solution.py:26
  122.1 3.1 %collective-permute-start.12 = (bf16[256,128]{1,0:T(8,128)(2,1)S(1)}, bf16[256,128]{1,0:T(8,128)(2,1)S(1)}, u32[]{:S(2)}, u32[]{:S(2)}) collective-permute-start(bf16[256,128]{1,0:T(8,128)(2,1)S(1)} %get-tuple-element.33), channel_id=1, source_target_pairs={{0,1},{1,0},{2,3},{3,2},{4,5},{5,4},{6,7},{7,6},{8,9},{9,8},{10,11... | collective-permute-start | bytes 196616 | tf_op jit(solution)/shard_map/ppermute | solution.py:26
  126.7 1.0 copy-start.11
  131.8 29.9 %all-to-all-start.2 = ((bf16[4,1024,256]{2,1,0:T(8,128)(2,1)}), bf16[4,1024,256]{2,1,0:T(8,128)(2,1)S(1)}, u32[]{:S(2)}, u32[]{:S(2)}) async-start(bf16[4,1024,256]{2,1,0:T(8,128)(2,1)} %shard_map.119.after), calls=%async_computation.2 | async-start | bytes 4194304 | tf_op jit(solution)/shard_map/all_to_all | solution.py:360
  135.9 5.0 %collective-permute-start.13 = (bf16[128,4096]{1,0:T(8,128)(2,1)}, bf16[128,4096]{1,0:T(8,128)(2,1)S(1)}, u32[]{:S(2)}, u32[]{:S(2)}) collective-permute-start(bf16[128,4096]{1,0:T(8,128)(2,1)} %copy-done.11), channel_id=1, source_target_pairs={{0,1},{1,0},{2,3},{3,2},{4,5},{5,4},{6,7},{7,6},{8,9},{9,8},{10,11... | collective-permute-start | bytes 3145736 | tf_op jit(solution)/shard_map/ppermute | solution.py:26
  141.1 9.4 %collective-permute-start.14 = (bf16[32,4096]{1,0:T(8,128)(2,1)S(1)}, bf16[32,4096]{1,0:T(8,128)(2,1)S(1)}, u32[]{:S(2)}, u32[]{:S(2)}) collective-permute-start(bf16[32,4096]{1,0:T(8,128)(2,1)S(1)} %get-tuple-element.39), channel_id=1, source_target_pairs={{0,12},{4,0},{8,4},{12,8},{1,13},{5,1},{9,5},{13,9},{2,14},{6,2},{... | collective-permute-start | bytes 786440 | tf_op jit(solution)/shard_map/ppermute | solution.py:31
  144.6 11.3 %collective-permute-start.15 = (bf16[32,4096]{1,0:T(8,128)(2,1)S(1)}, bf16[32,4096]{1,0:T(8,128)(2,1)S(1)}, u32[]{:S(2)}, u32[]{:S(2)}) collective-permute-start(bf16[32,4096]{1,0:T(8,128)(2,1)S(1)} %get-tuple-element.40), channel_id=1, source_target_pairs={{0,4},{4,8},{8,12},{12,0},{1,5},{5,9},{9,13},{13,1},{2,6},{6,10},{... | collective-permute-start | bytes 786440 | tf_op jit(solution)/shard_map/ppermute | solution.py:31
  146.5 13.0 %collective-permute-start.16 = (bf16[32,4096]{1,0:T(8,128)(2,1)S(1)}, bf16[32,4096]{1,0:T(8,128)(2,1)S(1)}, u32[]{:S(2)}, u32[]{:S(2)}) collective-permute-start(bf16[32,4096]{1,0:T(8,128)(2,1)S(1)} %get-tuple-element.41), channel_id=1, source_target_pairs={{0,8},{4,12},{8,0},{12,4},{1,9},{5,13},{9,1},{13,5},{2,10},{6,14},... | collective-permute-start | bytes 786440 | tf_op jit(solution)/shard_map/ppermute | solution.py:31
  161.7 54.0 %copy-start.9 = (bf16[16,4096]{1,0:T(8,128)(2,1)S(1)}, bf16[16,4096]{1,0:T(8,128)(2,1)}, u32[]{:S(2)}) copy-start(bf16[16,4096]{1,0:T(8,128)(2,1)} %tokens.3) | copy-start | bytes 393220
  163.3 29.3 %all-to-all-start.3 = ((bf16[4,256,256]{2,1,0:T(8,128)(2,1)}), bf16[4,256,256]{2,1,0:T(8,128)(2,1)S(1)}, u32[]{:S(2)}, u32[]{:S(2)}) async-start(bf16[4,256,256]{2,1,0:T(8,128)(2,1)} %shard_map.123), calls=%async_computation.3 | async-start | bytes 1048576 | tf_op jit(solution)/shard_map/all_to_all | solution.py:361
  168.9 46.8 %collective-permute-start.17 = (bf16[16,4096]{1,0:T(8,128)(2,1)S(1)}, bf16[16,4096]{1,0:T(8,128)(2,1)S(1)}, u32[]{:S(2)}, u32[]{:S(2)}) collective-permute-start(bf16[16,4096]{1,0:T(8,128)(2,1)S(1)} %get-tuple-element.43.refs_0_), channel_id=1, source_target_pairs={{0,2},{2,0},{1,3},{3,1},{4,6},{6,4},{5,7},{7,5},{8,10},{10,8},{9,1... | collective-permute-start | bytes 393224 | tf_op jit(solution)/shard_map/ppermute | solution.py:26
  193.9 34.7 %all-to-all-start.4 = ((bf16[4,64,256]{2,1,0:T(8,128)(2,1)}), bf16[4,64,256]{2,1,0:T(8,128)(2,1)S(1)}, u32[]{:S(2)}, u32[]{:S(2)}) async-start(bf16[4,64,256]{2,1,0:T(8,128)(2,1)} %shard_map.124), calls=%async_computation.4 | async-start | bytes 262144 | tf_op jit(solution)/shard_map/all_to_all | solution.py:362
